TPU v7x, 32 devices: a whole 2x2x4 slice. The times are simulated.
32 devices in a mesh: param: 8 (over y, x, core), ex: 4 (over z).
Axes of the slice: x: 2, y: 2, z: 4, core: 2. Of those that a mesh axis runs over, the one named last changes fastest.
Arguments:
- activations: bfloat16 [4, 512, 8192], P('ex', None, 'param'), may hold values from -6 to 6
- cotangents: bfloat16 [4, 512, 1024], P('ex', 'param'), may hold values from -0.25 to 0.25
- signs: int32 [8388608], P('param'), may hold values from -1 to 1, as said below
- indices: int32 [32768], replicated, may hold values from 0 to 8388607
Outputs:
- projected: float32 [4, 32768], P('ex', 'param')
Inputs may be any that keep to these rules, and one draw needn't show every extreme that they name: `signs`: every entry is -1 or +1.
All inputs are finite; a program needn't handle non-finite values.
Results may differ from a plain program's by a relative error of at most 0.0003.
Values may be sent and summed in bfloat16 or wider, within the bound.
No kernel may reach another device: no remote copies, remote signals or barrier semaphores. Data moves between devices by JAX's collectives and lax.ppermute only.
A program may use at most 64 MiB of HBM per device.

v0:
```python
import math

import jax
import jax.numpy as jnp
from jax import lax
from jax.sharding import PartitionSpec as P


def swapped(x, axis, distance):
    return lax.ppermute(x, axis, [(i, i ^ 1 << distance) for i in range(lax.axis_size(axis))])


def bit_parity(left, right, bit_count):
    shared = jnp.bitwise_and(left, right)
    total = jnp.zeros_like(shared)
    for position in range(bit_count):
        total = total + jnp.bitwise_and(jnp.right_shift(shared, position), 1)
    return total % 2


def hadamard_table(count):
    row_index = lax.broadcasted_iota(jnp.int32, (count, count), 0)
    col_index = lax.broadcasted_iota(jnp.int32, (count, count), 1)
    parity = bit_parity(row_index, col_index, count.bit_length())
    return (1 - 2 * parity).astype(jnp.float32)


def local_transform(signed):
    examples_here, height, breadth = signed.shape
    highest = lax.Precision.HIGHEST
    span = height * breadth
    inner = min(128, span)
    remaining = span // inner
    middle = min(128, remaining)
    outer = remaining // middle
    blocked = signed.reshape(examples_here, outer, middle, inner)
    blocked = jnp.einsum("eoab,bk->eoak", blocked, hadamard_table(inner), precision=highest)
    blocked = jnp.einsum("eoab,ak->eokb", blocked, hadamard_table(middle), precision=highest)
    blocked = jnp.einsum("eoab,ok->ekab", blocked, hadamard_table(outer), precision=highest)
    return blocked.reshape(examples_here, span)


def on_device(activations, cotangents, signs, indices):
    height = activations.shape[2]
    breadth = cotangents.shape[2]
    parties = lax.axis_size("param")
    my_index = lax.axis_index("param")
    local_span = height * breadth
    gathered = lax.all_gather(cotangents, "param", axis=1, tiled=True)
    gradient = jnp.einsum("etr,etc->erc", activations, gathered, preferred_element_type=jnp.float32)
    signed = gradient * signs.reshape(height, breadth).astype(jnp.float32)
    scale_factor = 1.0 / math.sqrt(local_span * parties)
    local_values = local_transform(signed) * scale_factor
    owner_block = indices // local_span
    offset_within = indices % local_span
    combined = local_values
    for section_bit in range(parties.bit_length() - 1):
        partner = swapped(combined, "param", section_bit)
        upper_half = jnp.bitwise_and(jnp.right_shift(my_index, section_bit), 1) == 1
        combined = jnp.where(upper_half, partner - combined, combined + partner)
    picked_terms = (
        jnp.take(combined, offset_within, axis=1)
        * (owner_block == my_index).astype(jnp.float32)[None, :]
    )
    return lax.psum_scatter(picked_terms, "param", scatter_dimension=1, tiled=True)


def solution(mesh):
    in_specs = (P("ex", None, "param"), P("ex", "param", None), P("param"), P())
    out_specs = P("ex", "param")
    return jax.shard_map(
        on_device, mesh=mesh, in_specs=in_specs, out_specs=out_specs, check_vma=False
    )
```

profile of v0, /device:TPU:0, one launch (start us, length us, event | category | flops | bytes accessed | tf_op | source)
XLA Modules:
  0.0 799.0 jit_solution(3108861063546191415)
XLA Ops:
  6.5 0.7 all-gather.2.cloned.1.call-update
  7.3 4.4 convert_element_type.18
  11.7 4.9 convert_element_type.19
  16.6 18.8 %all-gather.2.cloned.1.call-done = bf16[1,512,1024]{2,1,0:T(8,128)(2,1)} async-done(((bf16[1,64,1024]{2,1,0:T(8,128)(2,1)}), bf16[1,512,1024]{2,1,0:T(8,128)(2,1)}) %all-gather.2.cloned.1.call-update) | async-done | bytes 1048592 | tf_op jit(solution)/shard_map/all_gather | solution.py:49
  35.5 5.8 convolution_multiply_fusion
  41.3 4.9 reshape.51
  46.1 5.7 fusion.15
  51.8 4.1 convolution_bitcast_fusion
  56.0 6.2 fusion.2
  62.2 4.6 copy.10
  66.8 0.3 collective-permute-start
  67.1 7.2 collective-permute-done
  74.3 7.2 broadcast_select_fusion
  81.5 1.5 collective-permute-start.1
  82.9 91.6 %collective-permute-done.1 = f32[1,1048576]{1,0:T(1,128)} collective-permute-done((f32[1,1048576]{1,0:T(1,128)}, f32[1,1048576]{1,0:T(1,128)}, u32[]{:S(2)}, u32[]{:S(2)}) %collective-permute-start.1) | collective-permute-done | bytes 4194336 | tf_op jit(solution)/shard_map/ppermute | solution.py:10
  174.5 7.2 broadcast_select_fusion.1
  181.7 1.4 collective-permute-start.2
  183.2 90.8 %collective-permute-done.2 = f32[1,1048576]{1,0:T(1,128)} collective-permute-done((f32[1,1048576]{1,0:T(1,128)}, f32[1,1048576]{1,0:T(1,128)}, u32[]{:S(2)}, u32[]{:S(2)}) %collective-permute-start.2) | collective-permute-done | bytes 4194336 | tf_op jit(solution)/shard_map/ppermute | solution.py:10
  273.9 7.2 broadcast_select_fusion.2
  281.1 383.7 %gather_fusion = f32[32768]{0:T(1024)S(1)} fusion(f32[1048576]{0:T(1024)} %bitcast.27, s32[32768]{0:T(1024)S(1)} %broadcast_clamp_fusion), kind=kCustom, calls=%fused_computation | custom fusion | bytes 393216 | tf_op jit(solution)/shard_map/jit(_take)/gather | solution.py:62
  664.8 0.2 select_select_fusion
  664.9 8.2 %copy.13 = f32[1,32768]{0,1:T(8,128)} copy(f32[1,32768]{1,0:T(1,128)S(1)} %bitcast.30) | data formatting | bytes 262144
  673.2 116.1 %reduce-scatter.4.cloned.1.call-done = f32[4096,1]{1,0:T(8,128)} async-done(((f32[32768,1]{1,0:T(8,128)}), f32[4096,1]{1,0:T(8,128)}) %reduce-scatter.4.cloned.1.call-update) | async-done | bytes 16400
  789.3 2.8 copy.14
  (10 shorter events, 0.2 us)
Async XLA Ops:
  6.5 28.9 %copy-start = (bf16[1,512,1024]{2,1,0:T(8,128)(2,1)S(1)}, bf16[1,512,1024]{2,1,0:T(8,128)(2,1)}, u32[]{:S(2)}) copy-start(bf16[1,512,1024]{2,1,0:T(8,128)(2,1)} %param.4) | copy-start | bytes 3145732
  6.5 28.9 %all-gather.2.cloned.1.call-start = ((), (), s32[]{:S(2)}) async-start(), calls=%async_computation.1 | async-start | bytes 1179648 | tf_op jit(solution)/shard_map/all_gather | solution.py:49
  7.3 782.1 %reduce-scatter.4.cloned.1.call-start = ((), (), s32[]{:S(2)}) async-start(), calls=%async_computation.2 | async-start | bytes 18874368
  66.8 7.5 collective-permute-start
  81.5 93.1 %collective-permute-start.1 = (f32[1,1048576]{1,0:T(1,128)}, f32[1,1048576]{1,0:T(1,128)}, u32[]{:S(2)}, u32[]{:S(2)}) collective-permute-start(f32[1,1048576]{1,0:T(1,128)} %broadcast_select_fusion), channel_id=1, source_target_pairs={{0,8},{4,12},{8,0},{12,4},{16,24},{20,28},{24,16},{28,20},{1,9},{5... | collective-permute-start | bytes 12582920 | tf_op jit(solution)/shard_map/ppermute | solution.py:10
  82.9 100.2 %copy-start.2 = (s32[32768]{0:T(1024)S(1)}, s32[32768]{0:T(1024)}, u32[]{:S(2)}) copy-start(s32[32768]{0:T(1024)} %param.7) | copy-start | bytes 393220
  181.7 92.3 %collective-permute-start.2 = (f32[1,1048576]{1,0:T(1,128)}, f32[1,1048576]{1,0:T(1,128)}, u32[]{:S(2)}, u32[]{:S(2)}) collective-permute-start(f32[1,1048576]{1,0:T(1,128)} %broadcast_select_fusion.1), channel_id=1, source_target_pairs={{0,16},{4,20},{8,24},{12,28},{16,0},{20,4},{24,8},{28,12},{1,17},{... | collective-permute-start | bytes 12582920 | tf_op jit(solution)/shard_map/ppermute | solution.py:10
  673.2 119.0 %copy-start.1 = (bf16[1,512,1024]{2,1,0:T(8,128)(2,1)S(1)}, bf16[1,512,1024]{2,1,0:T(8,128)(2,1)}, u32[]{:S(2)}) copy-start(bf16[1,512,1024]{2,1,0:T(8,128)(2,1)} %param.4) | copy-start | bytes 3145732
Sparse Core Ops, SparseCore 0:
  9.2 26.1 all-gather.1
  673.3 115.9 reduce-scatter.3
where the time goes:
time: 813 us; the launch traced here: 799 us
  local copies, waits for them, and re-layouts  409 us (50%)
  waiting for transfers between devices  325 us (40%)
  other arithmetic  26.1 us (3%)
  matrix products  21.8 us (3%)
  between operations  13.5 us (2%)
    gather x1, local copies, waits for them, and re-layouts, on_device(): jnp.take(combined, offset_within, axis=1)  384 us
    ppermute x3, waiting for transfers between devices, swapped(): lax.ppermute(x, axis, [(i, i ^ 1 << distance) for i in range(lax.axis_siz...  190 us
    unnamed x3, waiting for transfers between devices  117 us
    select_n x3, other arithmetic, on_device(): combined = jnp.where(upper_half, partner - combined, combined + partner)  21.5 us
    all_gather x1, waiting for transfers between devices, on_device(): gathered = lax.all_gather(cotangents, 'param', axis=1, tiled=True)  18.8 us
  transfers between devices with their start and end apart: 5, of which 5 were waited for; matrix products, arithmetic and copies ran while one was open for 1% of the time, Pallas kernels for 0%

commit v1 on v0

v1 whole, which is shorter than its diff:
```python
import functools
import math

import jax
import jax.numpy as jnp
from jax import lax
from jax.experimental import pallas as pl
from jax.experimental.pallas import tpu as pltpu
from jax.sharding import PartitionSpec as P

LANES = 128
SIDE = 256


def flipped(x, axis, mask):
    return lax.ppermute(x, axis, [(i, i ^ mask) for i in range(lax.axis_size(axis))])


def parity(bits, width):
    shift = 1 << (width - 1).bit_length() >> 1
    while shift:
        bits = bits ^ (bits >> shift)
        shift //= 2
    return bits & 1


def butterfly(parts):
    stride = 1
    while stride < len(parts):
        parts = [
            parts[i] + parts[i + stride] if not i & stride else parts[i - stride] - parts[i]
            for i in range(len(parts))
        ]
        stride *= 2
    return parts


def split(x):
    high = x.astype(jnp.bfloat16)
    return high, (x - high.astype(jnp.float32)).astype(jnp.bfloat16)


def dot(left, right):
    return jnp.dot(left, right, preferred_element_type=jnp.float32)


def sketch_kernel(parties, scale, acts_ref, signs_ref, rows_ref, index_ref, *refs):
    chunk_refs, out_refs = refs[:parties], refs[parties : 2 * parties]
    cots, signed, table, picked, result = refs[2 * parties :]
    me = lax.axis_index("param")
    height = acts_ref.shape[0]
    breadth = signs_ref.shape[1]
    tokens = chunk_refs[0].shape[0]
    for distance in range(parties):
        start = pl.multiple_of((me ^ distance) * tokens, tokens)
        cots[pl.ds(start, tokens), :] = chunk_refs[distance][...]

    row_at = lax.broadcasted_iota(jnp.int32, (SIDE, SIDE), 0)
    col_at = lax.broadcasted_iota(jnp.int32, (SIDE, SIDE), 1)
    hadamard = (1 - 2 * parity(row_at & col_at, 8)).astype(jnp.float32).astype(jnp.bfloat16)

    row_blocks, col_blocks = height // SIDE, breadth // SIDE
    for col in range(col_blocks):
        cols = slice(col * SIDE, (col + 1) * SIDE)
        product = dot(acts_ref[...], cots[:, cols]) * signs_ref[:, cols].astype(jnp.float32)
        parts = butterfly([product[row * SIDE : (row + 1) * SIDE] for row in range(row_blocks)])
        for row in range(row_blocks):
            signed[row * SIDE : (row + 1) * SIDE, cols] = parts[row]
    for row in range(row_blocks):
        rows = slice(row * SIDE, (row + 1) * SIDE)
        parts = butterfly([signed[rows, col * SIDE : (col + 1) * SIDE] for col in range(col_blocks)])
        for col in range(col_blocks):
            high, low = split(parts[col])
            high, low = split(dot(high, hadamard) + dot(low, hadamard))
            done = dot(hadamard, high) + dot(hadamard, low)
            for piece in range(SIDE // LANES):
                at = (col * (SIDE // LANES) + piece) * height + row * SIDE
                table[at : at + SIDE, :] = done[:, piece * LANES : (piece + 1) * LANES]

    groups = index_ref.shape[0]
    sub_at = lax.broadcasted_iota(jnp.int32, (LANES, LANES), 0)

    def group(at, carry):
        for k in range(LANES):
            picked[k : k + 1, :] = table[pl.ds(rows_ref[at * LANES + k], 1), :]
        lane = index_ref[pl.ds(at, 1), :] & (LANES - 1)
        chosen = jnp.where(sub_at == lane, picked[...].T, 0.0)
        result[pl.ds(at, 1), :] = jnp.sum(chosen, axis=0, keepdims=True)
        return carry

    lax.fori_loop(0, groups, group, 0)

    share = groups // parties
    bits = (height * breadth).bit_length() - 1
    for distance in range(parties):
        at = pl.multiple_of((me ^ distance) * share, share)
        owner = index_ref[pl.ds(at, share), :] >> bits
        sign = (1 - 2 * parity(owner & me, parties.bit_length() - 1)).astype(jnp.float32)
        out_refs[distance][...] = result[pl.ds(at, share), :] * (sign * scale)


def on_device(activations, cotangents, signs, indices):
    height = activations.shape[2]
    breadth = cotangents.shape[2]
    parties = lax.axis_size("param")
    samples = indices.shape[0]
    groups = samples // LANES

    chunks = {0: cotangents[0]}
    for distance in range(2, parties, 2):
        chunks[distance] = flipped(chunks[0], "param", distance)
    for distance in range(0, parties, 2):
        chunks[distance + 1] = flipped(chunks[distance], "param", 1)

    acts = activations[0].T
    sign_matrix = signs.reshape(height, breadth).astype(jnp.bfloat16)
    offset = indices & (height * breadth - 1)
    rows = (offset // LANES) % (breadth // LANES) * height + offset // breadth
    vmem = pl.BlockSpec(memory_space=pltpu.VMEM)
    outs = pl.pallas_call(
        functools.partial(sketch_kernel, parties, 1.0 / math.sqrt(height * breadth * parties)),
        out_shape=[jax.ShapeDtypeStruct((groups // parties, LANES), jnp.float32)] * parties,
        in_specs=[vmem, vmem, pl.BlockSpec(memory_space=pltpu.SMEM), vmem] + [vmem] * parties,
        out_specs=[vmem] * parties,
        scratch_shapes=[
            pltpu.VMEM((activations.shape[1], breadth), jnp.bfloat16),
            pltpu.VMEM((height, breadth), jnp.float32),
            pltpu.VMEM((height * breadth // LANES, LANES), jnp.float32),
            pltpu.VMEM((LANES, LANES), jnp.float32),
            pltpu.VMEM((groups, LANES), jnp.float32),
        ],
        compiler_params=pltpu.CompilerParams(vmem_limit_bytes=40 * 1024 * 1024),
        name="sketch",
    )(acts, sign_matrix, rows, indices.reshape(groups, LANES), *[chunks[d] for d in range(parties)])

    total = outs[0]
    for distance in range(1, parties):
        total = total + flipped(outs[distance], "param", distance)
    return total.reshape(1, samples // parties)


def solution(mesh):
    in_specs = (P("ex", None, "param"), P("ex", "param", None), P("param"), P())
    out_specs = P("ex", "param")
    return jax.shard_map(
        on_device, mesh=mesh, in_specs=in_specs, out_specs=out_specs, check_vma=False
    )
```

time: 813 us -> 90.4 us (0.11); the launches traced: 799 us -> 90.2 us
  local copies, waits for them, and re-layouts: 409 us -> 4.37 us
  waiting for transfers between devices: 325 us -> 9.2 us
  Pallas kernels: 0 us -> 59.8 us
  matrix products: 21.8 us -> 0 us
  other arithmetic: 26.1 us -> 5.45 us
  between operations: 13.5 us -> 0.1 us
  starting transfers between devices: 3.17 us -> 11.3 us
    gather x1 -> x0, local copies, waits for them, and re-layouts: 384 us -> none  [on_device(): jnp.take(combined, offset_within, axis=1)]
    ppermute x3 -> x14, waiting for transfers between devices: 190 us -> 9.2 us  [flipped(): lax.ppermute(x, axis, [(i, i ^ mask) for i in range(lax.axis_size(axis))])]
    unnamed x3 -> x0, waiting for transfers between devices: 117 us -> none
    pallas_call x0 -> x1, Pallas kernels: none -> 59.8 us  [on_device(): pl.pallas_call(functools.partial(sketch_kernel, parties, 1.0 / math.sqrt(...]
    dot_general x4 -> x0, matrix products: 21.8 us -> none  [the longest x1 6.21 us: local_transform(): jnp.einsum('eoab,ok->ekab', blocked, hadamard_table(outer), precision=hig...]
    select_n x3 -> x0, other arithmetic: 21.5 us -> none  [on_device(): combined = jnp.where(upper_half, partner - combined, combined + partner)]
    all_gather x1 -> x0, waiting for transfers between devices: 18.8 us -> none  [on_device(): gathered = lax.all_gather(cotangents, 'param', axis=1, tiled=True)]
    unnamed x8 -> x5, local copies, waits for them, and re-layouts: 11.1 us -> 1.55 us
  transfers between devices with their start and end apart: 5 -> 14, of which waited for: 5 -> 5; matrix products, arithmetic and copies ran while one was open for 1% -> 10% of each run, Pallas kernels for 0% -> 0%
where the time goes in v1:
time: 90.4 us; the launch traced here: 90.2 us
  Pallas kernels  59.8 us (66%)
  starting transfers between devices  11.3 us (12%)
  waiting for transfers between devices  9.2 us (10%)
  other arithmetic  5.45 us (6%)
  local copies, waits for them, and re-layouts  4.37 us (5%)
    pallas_call x1, Pallas kernels, on_device(): pl.pallas_call(functools.partial(sketch_kernel, parties, 1.0 / math.sqrt(...  59.8 us
    ppermute x14, starting transfers between devices, flipped(): lax.ppermute(x, axis, [(i, i ^ mask) for i in range(lax.axis_size(axis))])  11.3 us
    ppermute x14, waiting for transfers between devices, flipped(): lax.ppermute(x, axis, [(i, i ^ mask) for i in range(lax.axis_size(axis))])  9.2 us
    convert_element_type x1, other arithmetic, on_device(): sign_matrix = signs.reshape(height, breadth).astype(jnp.bfloat16)  3.72 us
    convert_element_type x1, local copies, waits for them, and re-layouts, on_device(): sign_matrix = signs.reshape(height, breadth).astype(jnp.bfloat16)  2.82 us
  transfers between devices with their start and end apart: 14, of which 5 were waited for; matrix products, arithmetic and copies ran while one was open for 10% of the time, Pallas kernels for 0%

profile of v1, /device:TPU:0, one launch (start us, length us, event | category | flops | bytes accessed | tf_op | source)
XLA Modules:
  0.0 90.2 jit_solution(5814181067710222858)
XLA Ops:
  0.0 2.9 %collective-permute-start.1 = (bf16[64,1024]{1,0:T(8,128)(2,1)}, bf16[64,1024]{1,0:T(8,128)(2,1)}, u32[]{:S(2)}, u32[]{:S(2)}) collective-permute-start(bf16[64,1024]{1,0:T(8,128)(2,1)} %bitcast.8), channel_id=1, source_target_pairs={{0,8},{4,12},{8,0},{12,4},{16,24},{20,28},{24,16},{28,20},{1,9},{5... | collective-permute-start | bytes 393224 | tf_op jit(solution)/shard_map/ppermute | solution.py:16
  2.9 1.5 %collective-permute-start.3 = (bf16[64,1024]{1,0:T(8,128)(2,1)}, bf16[64,1024]{1,0:T(8,128)(2,1)}, u32[]{:S(2)}, u32[]{:S(2)}) collective-permute-start(bf16[64,1024]{1,0:T(8,128)(2,1)} %bitcast.9), channel_id=1, source_target_pairs={{0,16},{4,20},{8,24},{12,28},{16,0},{20,4},{24,8},{28,12},{1,17},{... | collective-permute-start | bytes 393224 | tf_op jit(solution)/shard_map/ppermute | solution.py:16
  4.5 0.0 collective-permute-start.5
  4.5 0.0 collective-permute-start
  4.5 2.7 %collective-permute-done.1.refs_2_ = bf16[64,1024]{1,0:T(8,128)(2,1)} collective-permute-done((bf16[64,1024]{1,0:T(8,128)(2,1)}, bf16[64,1024]{1,0:T(8,128)(2,1)}, u32[]{:S(2)}, u32[]{:S(2)}) %collective-permute-start.1) | collective-permute-done | bytes 131104 | tf_op jit(solution)/shard_map/ppermute | solution.py:16
  7.2 3.9 %collective-permute-done.3.refs_4_ = bf16[64,1024]{1,0:T(8,128)(2,1)} collective-permute-done((bf16[64,1024]{1,0:T(8,128)(2,1)}, bf16[64,1024]{1,0:T(8,128)(2,1)}, u32[]{:S(2)}, u32[]{:S(2)}) %collective-permute-start.3) | collective-permute-done | bytes 131104 | tf_op jit(solution)/shard_map/ppermute | solution.py:16
  11.0 0.5 collective-permute-start.6
  11.5 1.1 %fusion.3.rows_ref = s32[32768]{0:T(1024)S(1)} fusion(s32[32768]{0:T(1024)} %param.7), kind=kLoop, calls=%fused_computation.13 | loop fusion | flops 1277952 | bytes 262144 | tf_op jit(solution)/shard_map/add | solution.py:118
  12.7 3.7 %convert_element_type.5 = bf16[1048576]{0:T(1024)(128)(2,1)} convert(s32[1048576]{0:T(1024)} %param.6) | non-fusion elementwise | flops 1048576 | bytes 6291456 | tf_op jit(solution)/shard_map/convert_element_type | solution.py:116
  16.4 2.8 %convert_element_type.6.signs_ref = bf16[1024,1024]{1,0:T(8,128)(2,1)S(1)} reshape(bf16[1048576]{0:T(1024)(128)(2,1)} %convert_element_type.5) | data formatting | bytes 4194304 | tf_op jit(solution)/shard_map/convert_element_type | solution.py:116
  19.2 0.0 copy-start
  19.2 0.0 copy-start.1
  19.2 1.5 %copy.5 = bf16[1,512,1024]{1,2,0:T(8,128)(2,1)S(1)} copy(bf16[1,512,1024]{2,1,0:T(8,128)(2,1)} %param.4) | data formatting | bytes 2097152 | tf_op args[0]
  20.8 59.8 %sketch.1 = (f32[32,128]{1,0:T(8,128)S(1)}, f32[32,128]{1,0:T(8,128)S(1)}, f32[32,128]{1,0:T(8,128)S(1)}, f32[32,128]{1,0:T(8,128)S(1)}, f32[32,128]{1,0:T(8,128...) custom-call(bf16[1024,512]{1,0:T(8,128)(2,1)S(1)} %bitcast.6, ...), custom_call_target="tpu_custom_call" | custom-call | tf_op jit(solution)/shard_map/sketch/pallas_call | solution.py:120
  80.6 1.6 %collective-permute-start.10 = (f32[32,128]{1,0:T(8,128)S(1)}, f32[32,128]{1,0:T(8,128)S(1)}, u32[]{:S(2)}, u32[]{:S(2)}) collective-permute-start(f32[32,128]{1,0:T(8,128)S(1)} %get-tuple-element.17), channel_id=1, source_target_pairs={{0,16},{4,20},{8,24},{12,28},{16,0},{20,4},{24,8},{28,12},{1,17},{... | collective-permute-start | bytes 49160 | tf_op jit(solution)/shard_map/ppermute | solution.py:16
  82.2 1.3 %collective-permute-start.12 = (f32[32,128]{1,0:T(8,128)S(1)}, f32[32,128]{1,0:T(8,128)S(1)}, u32[]{:S(2)}, u32[]{:S(2)}) collective-permute-start(f32[32,128]{1,0:T(8,128)S(1)} %get-tuple-element.19), channel_id=1, source_target_pairs={{0,24},{4,28},{8,16},{12,20},{16,8},{20,12},{24,0},{28,4},{1,25},{... | collective-permute-start | bytes 49160 | tf_op jit(solution)/shard_map/ppermute | solution.py:16
  83.5 1.5 %collective-permute-start.13 = (f32[32,128]{1,0:T(8,128)S(1)}, f32[32,128]{1,0:T(8,128)S(1)}, u32[]{:S(2)}, u32[]{:S(2)}) collective-permute-start(f32[32,128]{1,0:T(8,128)S(1)} %get-tuple-element.20), channel_id=1, source_target_pairs={{0,28},{4,24},{8,20},{12,16},{16,12},{20,8},{24,4},{28,0},{1,29},{... | collective-permute-start | bytes 49160 | tf_op jit(solution)/shard_map/ppermute | solution.py:16
  85.1 0.2 collective-permute-start.7
  85.2 1.1 %collective-permute-start.8 = (f32[32,128]{1,0:T(8,128)S(1)}, f32[32,128]{1,0:T(8,128)S(1)}, u32[]{:S(2)}, u32[]{:S(2)}) collective-permute-start(f32[32,128]{1,0:T(8,128)S(1)} %get-tuple-element.15), channel_id=1, source_target_pairs={{0,8},{4,12},{8,0},{12,4},{16,24},{20,28},{24,16},{28,20},{1,9},{5... | collective-permute-start | bytes 49160 | tf_op jit(solution)/shard_map/ppermute | solution.py:16
  86.3 0.6 collective-permute-start.9
  86.9 0.7 collective-permute-done.13
  87.6 1.4 %collective-permute-done.8 = f32[32,128]{1,0:T(8,128)S(1)} collective-permute-done((f32[32,128]{1,0:T(8,128)S(1)}, f32[32,128]{1,0:T(8,128)S(1)}, u32[]{:S(2)}, u32[]{:S(2)}) %collective-permute-start.8) | collective-permute-done | bytes 16416 | tf_op jit(solution)/shard_map/ppermute | solution.py:16
  89.0 0.6 collective-permute-done.9
  89.6 0.6 add_add_fusion
  (14 shorter events, 0.0 us)
Async XLA Ops:
  0.0 7.2 %collective-permute-start.1 = (bf16[64,1024]{1,0:T(8,128)(2,1)}, bf16[64,1024]{1,0:T(8,128)(2,1)}, u32[]{:S(2)}, u32[]{:S(2)}) collective-permute-start(bf16[64,1024]{1,0:T(8,128)(2,1)} %bitcast.8), channel_id=1, source_target_pairs={{0,8},{4,12},{8,0},{12,4},{16,24},{20,28},{24,16},{28,20},{1,9},{5... | collective-permute-start | bytes 393224 | tf_op jit(solution)/shard_map/ppermute | solution.py:16
  2.9 8.1 %collective-permute-start.3 = (bf16[64,1024]{1,0:T(8,128)(2,1)}, bf16[64,1024]{1,0:T(8,128)(2,1)}, u32[]{:S(2)}, u32[]{:S(2)}) collective-permute-start(bf16[64,1024]{1,0:T(8,128)(2,1)} %bitcast.9), channel_id=1, source_target_pairs={{0,16},{4,20},{8,24},{12,28},{16,0},{20,4},{24,8},{28,12},{1,17},{... | collective-permute-start | bytes 393224 | tf_op jit(solution)/shard_map/ppermute | solution.py:16
  4.5 6.6 %collective-permute-start.5 = (bf16[64,1024]{1,0:T(8,128)(2,1)}, bf16[64,1024]{1,0:T(8,128)(2,1)}, u32[]{:S(2)}, u32[]{:S(2)}) collective-permute-start(bf16[64,1024]{1,0:T(8,128)(2,1)} %bitcast.10), channel_id=1, source_target_pairs={{0,24},{4,28},{8,16},{12,20},{16,8},{20,12},{24,0},{28,4},{1,25},{... | collective-permute-start | bytes 393224 | tf_op jit(solution)/shard_map/ppermute | solution.py:16
  4.5 16.3 %collective-permute-start = (bf16[64,1024]{1,0:T(8,128)(2,1)}, bf16[64,1024]{1,0:T(8,128)(2,1)}, u32[]{:S(2)}, u32[]{:S(2)}) collective-permute-start(bf16[64,1024]{1,0:T(8,128)(2,1)} %bitcast.11), channel_id=1, source_target_pairs={{0,4},{4,0},{8,12},{12,8},{16,20},{20,16},{24,28},{28,24},{1,5},{5... | collective-permute-start | bytes 393224 | tf_op jit(solution)/shard_map/ppermute | solution.py:16
  7.2 13.6 %collective-permute-start.2 = (bf16[64,1024]{1,0:T(8,128)(2,1)}, bf16[64,1024]{1,0:T(8,128)(2,1)}, u32[]{:S(2)}, u32[]{:S(2)}) collective-permute-start(bf16[64,1024]{1,0:T(8,128)(2,1)} %collective-permute-done.1.refs_2_), channel_id=1, source_target_pairs={{0,4},{4,0},{8,12},{12,8},{16,20},{20,16},{24,28},{28,24},{1,5},{5... | collective-permute-start | bytes 393224 | tf_op jit(solution)/shard_map/ppermute | solution.py:16
  11.0 9.8 %collective-permute-start.4 = (bf16[64,1024]{1,0:T(8,128)(2,1)}, bf16[64,1024]{1,0:T(8,128)(2,1)}, u32[]{:S(2)}, u32[]{:S(2)}) collective-permute-start(bf16[64,1024]{1,0:T(8,128)(2,1)} %collective-permute-done.3.refs_4_), channel_id=1, source_target_pairs={{0,4},{4,0},{8,12},{12,8},{16,20},{20,16},{24,28},{28,24},{1,5},{5... | collective-permute-start | bytes 393224 | tf_op jit(solution)/shard_map/ppermute | solution.py:16
  11.0 9.8 %collective-permute-start.6 = (bf16[64,1024]{1,0:T(8,128)(2,1)}, bf16[64,1024]{1,0:T(8,128)(2,1)}, u32[]{:S(2)}, u32[]{:S(2)}) collective-permute-start(bf16[64,1024]{1,0:T(8,128)(2,1)} %collective-permute-done.5.refs_6_), channel_id=1, source_target_pairs={{0,4},{4,0},{8,12},{12,8},{16,20},{20,16},{24,28},{28,24},{1,5},{5... | collective-permute-start | bytes 393224 | tf_op jit(solution)/shard_map/ppermute | solution.py:16
  19.2 1.6 %copy-start = (s32[32768]{0:T(1024)S(1)}, s32[32768]{0:T(1024)}, u32[]{:S(2)}) copy-start(s32[32768]{0:T(1024)} %param.7) | copy-start | bytes 393220
  19.2 1.6 %copy-start.1 = (bf16[1,64,1024]{2,1,0:T(8,128)(2,1)S(1)}, bf16[1,64,1024]{2,1,0:T(8,128)(2,1)}, u32[]{:S(2)}) copy-start(bf16[1,64,1024]{2,1,0:T(8,128)(2,1)} %param.5) | copy-start | bytes 393220
  80.6 4.6 %collective-permute-start.10 = (f32[32,128]{1,0:T(8,128)S(1)}, f32[32,128]{1,0:T(8,128)S(1)}, u32[]{:S(2)}, u32[]{:S(2)}) collective-permute-start(f32[32,128]{1,0:T(8,128)S(1)} %get-tuple-element.17), channel_id=1, source_target_pairs={{0,16},{4,20},{8,24},{12,28},{16,0},{20,4},{24,8},{28,12},{1,17},{... | collective-permute-start | bytes 49160 | tf_op jit(solution)/shard_map/ppermute | solution.py:16
  82.2 4.1 %collective-permute-start.11 = (f32[32,128]{1,0:T(8,128)S(1)}, f32[32,128]{1,0:T(8,128)S(1)}, u32[]{:S(2)}, u32[]{:S(2)}) collective-permute-start(f32[32,128]{1,0:T(8,128)S(1)} %get-tuple-element.18), channel_id=1, source_target_pairs={{0,20},{4,16},{8,28},{12,24},{16,4},{20,0},{24,12},{28,8},{1,21},{... | collective-permute-start | bytes 49160 | tf_op jit(solution)/shard_map/ppermute | solution.py:16
  82.2 4.7 %collective-permute-start.12 = (f32[32,128]{1,0:T(8,128)S(1)}, f32[32,128]{1,0:T(8,128)S(1)}, u32[]{:S(2)}, u32[]{:S(2)}) collective-permute-start(f32[32,128]{1,0:T(8,128)S(1)} %get-tuple-element.19), channel_id=1, source_target_pairs={{0,24},{4,28},{8,16},{12,20},{16,8},{20,12},{24,0},{28,4},{1,25},{... | collective-permute-start | bytes 49160 | tf_op jit(solution)/shard_map/ppermute | solution.py:16
  83.5 4.1 %collective-permute-start.13 = (f32[32,128]{1,0:T(8,128)S(1)}, f32[32,128]{1,0:T(8,128)S(1)}, u32[]{:S(2)}, u32[]{:S(2)}) collective-permute-start(f32[32,128]{1,0:T(8,128)S(1)} %get-tuple-element.20), channel_id=1, source_target_pairs={{0,28},{4,24},{8,20},{12,16},{16,12},{20,8},{24,4},{28,0},{1,29},{... | collective-permute-start | bytes 49160 | tf_op jit(solution)/shard_map/ppermute | solution.py:16
  85.1 2.5 %collective-permute-start.7 = (f32[32,128]{1,0:T(8,128)S(1)}, f32[32,128]{1,0:T(8,128)S(1)}, u32[]{:S(2)}, u32[]{:S(2)}) collective-permute-start(f32[32,128]{1,0:T(8,128)S(1)} %get-tuple-element.14), channel_id=1, source_target_pairs={{0,4},{4,0},{8,12},{12,8},{16,20},{20,16},{24,28},{28,24},{1,5},{5... | collective-permute-start | bytes 49160 | tf_op jit(solution)/shard_map/ppermute | solution.py:16
  85.2 3.7 %collective-permute-start.8 = (f32[32,128]{1,0:T(8,128)S(1)}, f32[32,128]{1,0:T(8,128)S(1)}, u32[]{:S(2)}, u32[]{:S(2)}) collective-permute-start(f32[32,128]{1,0:T(8,128)S(1)} %get-tuple-element.15), channel_id=1, source_target_pairs={{0,8},{4,12},{8,0},{12,4},{16,24},{20,28},{24,16},{28,20},{1,9},{5... | collective-permute-start | bytes 49160 | tf_op jit(solution)/shard_map/ppermute | solution.py:16
  86.3 3.2 %collective-permute-start.9 = (f32[32,128]{1,0:T(8,128)S(1)}, f32[32,128]{1,0:T(8,128)S(1)}, u32[]{:S(2)}, u32[]{:S(2)}) collective-permute-start(f32[32,128]{1,0:T(8,128)S(1)} %get-tuple-element.16), channel_id=1, source_target_pairs={{0,12},{4,8},{8,4},{12,0},{16,28},{20,24},{24,20},{28,16},{1,13},{... | collective-permute-start | bytes 49160 | tf_op jit(solution)/shard_map/ppermute | solution.py:16

commit v2 on v1

--- a/solution.py
+++ b/solution.py
@@ -44,9 +44,9 @@
     return jnp.dot(left, right, preferred_element_type=jnp.float32)
 
 
-def sketch_kernel(parties, scale, acts_ref, signs_ref, rows_ref, index_ref, *refs):
-    chunk_refs, out_refs = refs[:parties], refs[parties : 2 * parties]
-    cots, signed, table, picked, result = refs[2 * parties :]
+def transform_kernel(parties, acts_ref, signs_ref, *refs):
+    chunk_refs = refs[:parties]
+    table, cots, signed = refs[parties:]
     me = lax.axis_index("param")
     height = acts_ref.shape[0]
     breadth = signs_ref.shape[1]
@@ -77,12 +77,17 @@
                 at = (col * (SIDE // LANES) + piece) * height + row * SIDE
                 table[at : at + SIDE, :] = done[:, piece * LANES : (piece + 1) * LANES]
 
+
+def gather_kernel(parties, scale, table, rows_ref, index_ref, *refs):
+    out_refs = refs[:parties]
+    picked, result = refs[parties:]
+    me = lax.axis_index("param")
     groups = index_ref.shape[0]
     sub_at = lax.broadcasted_iota(jnp.int32, (LANES, LANES), 0)
 
     def group(at, carry):
         for k in range(LANES):
-            picked[k : k + 1, :] = table[pl.ds(rows_ref[at * LANES + k], 1), :]
+            picked[k : k + 1, :] = table[rows_ref[at * LANES + k]]
         lane = index_ref[pl.ds(at, 1), :] & (LANES - 1)
         chosen = jnp.where(sub_at == lane, picked[...].T, 0.0)
         result[pl.ds(at, 1), :] = jnp.sum(chosen, axis=0, keepdims=True)
@@ -91,7 +96,7 @@
     lax.fori_loop(0, groups, group, 0)
 
     share = groups // parties
-    bits = (height * breadth).bit_length() - 1
+    bits = (table.shape[0] * LANES).bit_length() - 1
     for distance in range(parties):
         at = pl.multiple_of((me ^ distance) * share, share)
         owner = index_ref[pl.ds(at, share), :] >> bits
@@ -117,21 +122,31 @@
     offset = indices & (height * breadth - 1)
     rows = (offset // LANES) % (breadth // LANES) * height + offset // breadth
     vmem = pl.BlockSpec(memory_space=pltpu.VMEM)
-    outs = pl.pallas_call(
-        functools.partial(sketch_kernel, parties, 1.0 / math.sqrt(height * breadth * parties)),
-        out_shape=[jax.ShapeDtypeStruct((groups // parties, LANES), jnp.float32)] * parties,
-        in_specs=[vmem, vmem, pl.BlockSpec(memory_space=pltpu.SMEM), vmem] + [vmem] * parties,
-        out_specs=[vmem] * parties,
+    table_rows = height * breadth // LANES
+    table = pl.pallas_call(
+        functools.partial(transform_kernel, parties),
+        out_shape=jax.ShapeDtypeStruct((table_rows, LANES), jnp.float32),
+        in_specs=[vmem] * (2 + parties),
+        out_specs=vmem,
         scratch_shapes=[
             pltpu.VMEM((activations.shape[1], breadth), jnp.bfloat16),
             pltpu.VMEM((height, breadth), jnp.float32),
-            pltpu.VMEM((height * breadth // LANES, LANES), jnp.float32),
+        ],
+        compiler_params=pltpu.CompilerParams(vmem_limit_bytes=32 * 1024 * 1024),
+        name="transform",
+    )(acts, sign_matrix, *[chunks[d] for d in range(parties)])
+    outs = pl.pallas_call(
+        functools.partial(gather_kernel, parties, 1.0 / math.sqrt(height * breadth * parties)),
+        out_shape=[jax.ShapeDtypeStruct((groups // parties, LANES), jnp.float32)] * parties,
+        in_specs=[vmem, pl.BlockSpec(memory_space=pltpu.SMEM), vmem],
+        out_specs=[vmem] * parties,
+        scratch_shapes=[
             pltpu.VMEM((LANES, LANES), jnp.float32),
             pltpu.VMEM((groups, LANES), jnp.float32),
         ],
-        compiler_params=pltpu.CompilerParams(vmem_limit_bytes=40 * 1024 * 1024),
-        name="sketch",
-    )(acts, sign_matrix, rows, indices.reshape(groups, LANES), *[chunks[d] for d in range(parties)])
+        compiler_params=pltpu.CompilerParams(vmem_limit_bytes=32 * 1024 * 1024),
+        name="gather",
+    )(table.reshape(table_rows, 1, LANES), rows, indices.reshape(groups, LANES))
 
     total = outs[0]
     for distance in range(1, parties):

time: 90.4 us -> 91.7 us (1.014)
  Pallas kernels: 59.8 us -> 61.1 us
    pallas_call x1 -> x2, Pallas kernels: 59.8 us -> 61.1 us  [the longest x1 55.3 us: on_device(): pl.pallas_call(functools.partial(gather_kernel, parties, 1.0 / math.sqrt(...]
where the time goes in v2:
time: 91.7 us; the launch traced here: 91.4 us
  Pallas kernels  61.1 us (67%)
  starting transfers between devices  11.3 us (12%)
  waiting for transfers between devices  9.18 us (10%)
  other arithmetic  5.45 us (6%)
  local copies, waits for them, and re-layouts  4.36 us (5%)
    pallas_call x1, Pallas kernels, on_device(): pl.pallas_call(functools.partial(gather_kernel, parties, 1.0 / math.sqrt(...  55.3 us
    ppermute x14, starting transfers between devices, flipped(): lax.ppermute(x, axis, [(i, i ^ mask) for i in range(lax.axis_size(axis))])  11.3 us
    ppermute x14, waiting for transfers between devices, flipped(): lax.ppermute(x, axis, [(i, i ^ mask) for i in range(lax.axis_size(axis))])  9.18 us
    pallas_call x1, Pallas kernels, on_device(): pl.pallas_call(functools.partial(transform_kernel, parties), out_shape=ja...  5.78 us
    convert_element_type x1, other arithmetic, on_device(): sign_matrix = signs.reshape(height, breadth).astype(jnp.bfloat16)  3.72 us
    convert_element_type x1, local copies, waits for them, and re-layouts, on_device(): sign_matrix = signs.reshape(height, breadth).astype(jnp.bfloat16)  2.86 us
  transfers between devices with their start and end apart: 14, of which 5 were waited for; matrix products, arithmetic and copies ran while one was open for 10% of the time, Pallas kernels for 0%

profile of v2, /device:TPU:0, one launch (start us, length us, event | category | flops | bytes accessed | tf_op | source)
XLA Modules:
  0.0 91.4 jit_solution(11017222311659199465)
XLA Ops:
  0.0 2.9 %collective-permute-start.1 = (bf16[64,1024]{1,0:T(8,128)(2,1)}, bf16[64,1024]{1,0:T(8,128)(2,1)S(1)}, u32[]{:S(2)}, u32[]{:S(2)}) collective-permute-start(bf16[64,1024]{1,0:T(8,128)(2,1)} %bitcast.10), channel_id=1, source_target_pairs={{0,8},{4,12},{8,0},{12,4},{16,24},{20,28},{24,16},{28,20},{1,9},{5... | collective-permute-start | bytes 393224 | tf_op jit(solution)/shard_map/ppermute | solution.py:16
  2.9 1.5 %collective-permute-start.3 = (bf16[64,1024]{1,0:T(8,128)(2,1)}, bf16[64,1024]{1,0:T(8,128)(2,1)}, u32[]{:S(2)}, u32[]{:S(2)}) collective-permute-start(bf16[64,1024]{1,0:T(8,128)(2,1)} %bitcast.11), channel_id=1, source_target_pairs={{0,16},{4,20},{8,24},{12,28},{16,0},{20,4},{24,8},{28,12},{1,17},{... | collective-permute-start | bytes 393224 | tf_op jit(solution)/shard_map/ppermute | solution.py:16
  4.5 2.7 %collective-permute-done.1.refs_2_ = bf16[64,1024]{1,0:T(8,128)(2,1)S(1)} collective-permute-done((bf16[64,1024]{1,0:T(8,128)(2,1)}, bf16[64,1024]{1,0:T(8,128)(2,1)S(1)}, u32[]{:S(2)}, u32[]{:S(2)}) %collective-permute-start.1) | collective-permute-done | bytes 131104 | tf_op jit(solution)/shard_map/ppermute | solution.py:16
  7.2 3.9 %collective-permute-done.3.refs_4_ = bf16[64,1024]{1,0:T(8,128)(2,1)} collective-permute-done((bf16[64,1024]{1,0:T(8,128)(2,1)}, bf16[64,1024]{1,0:T(8,128)(2,1)}, u32[]{:S(2)}, u32[]{:S(2)}) %collective-permute-start.3) | collective-permute-done | bytes 131104 | tf_op jit(solution)/shard_map/ppermute | solution.py:16
  11.0 0.0 collective-permute-done.5.refs_6_
  11.0 0.5 collective-permute-start.6
  11.5 1.1 %fusion.3.rows_ref = s32[32768]{0:T(1024)S(1)} fusion(s32[32768]{0:T(1024)} %param.7), kind=kLoop, calls=%fused_computation.13 | loop fusion | flops 1277952 | bytes 262144 | tf_op jit(solution)/shard_map/add | solution.py:123
  12.7 3.7 %convert_element_type.5 = bf16[1048576]{0:T(1024)(128)(2,1)} convert(s32[1048576]{0:T(1024)} %param.6) | non-fusion elementwise | flops 1048576 | bytes 6291456 | tf_op jit(solution)/shard_map/convert_element_type | solution.py:121
  16.4 2.9 %convert_element_type.6.signs_ref = bf16[1024,1024]{1,0:T(8,128)(2,1)S(1)} reshape(bf16[1048576]{0:T(1024)(128)(2,1)} %convert_element_type.5) | data formatting | bytes 4194304 | tf_op jit(solution)/shard_map/convert_element_type | solution.py:121
  19.2 1.5 %copy.5 = bf16[1,512,1024]{1,2,0:T(8,128)(2,1)S(1)} copy(bf16[1,512,1024]{2,1,0:T(8,128)(2,1)} %param.4) | data formatting | bytes 2097152 | tf_op args[0]
  20.7 0.0 collective-permute-done.refs_1_
  20.8 0.0 copy-start
  20.8 5.8 %transform.1 = f32[8192,128]{1,0:T(8,128)S(1)} custom-call(bf16[1024,512]{1,0:T(8,128)(2,1)S(1)} %bitcast.8, bf16[1024,1024]{1,0:T(8,128)(2,1)S(1)} %convert_element_type.6.signs_ref, bf16[64,1024]{1,0:T(8,128)(2,1)S(1)} %bitcast.14, bf16[64,1024]{1,0:T(8,128)(2,1)} %collective-permute-done.refs_1_, bf16[64,1024]{1,0:T(8,128)(2,1)S(1)} %collective-permute-done.1.refs_2_, ...), custom_call_target="tpu_custom_call" | custom-call | tf_op jit(solution)/shard_map/transform/pallas_call | solution.py:126
  26.6 55.3 %gather.1 = (f32[32,128]{1,0:T(8,128)S(1)}, f32[32,128]{1,0:T(8,128)S(1)}, f32[32,128]{1,0:T(8,128)S(1)}, f32[32,128]{1,0:T(8,128)S(1)}, f32[32,128]{1,0:T(8,128...) custom-call(f32[8192,1,128]{2,1,0:T(1,128)S(1)} %bitcast.7, ...), custom_call_target="tpu_custom_call" | custom-call | tf_op jit(solution)/shard_map/gather/pallas_call | solution.py:138
  81.9 1.6 %collective-permute-start.10 = (f32[32,128]{1,0:T(8,128)S(1)}, f32[32,128]{1,0:T(8,128)S(1)}, u32[]{:S(2)}, u32[]{:S(2)}) collective-permute-start(f32[32,128]{1,0:T(8,128)S(1)} %get-tuple-element.17), channel_id=1, source_target_pairs={{0,16},{4,20},{8,24},{12,28},{16,0},{20,4},{24,8},{28,12},{1,17},{... | collective-permute-start | bytes 49160 | tf_op jit(solution)/shard_map/ppermute | solution.py:16
  83.5 1.3 %collective-permute-start.12 = (f32[32,128]{1,0:T(8,128)S(1)}, f32[32,128]{1,0:T(8,128)S(1)}, u32[]{:S(2)}, u32[]{:S(2)}) collective-permute-start(f32[32,128]{1,0:T(8,128)S(1)} %get-tuple-element.19), channel_id=1, source_target_pairs={{0,24},{4,28},{8,16},{12,20},{16,8},{20,12},{24,0},{28,4},{1,25},{... | collective-permute-start | bytes 49160 | tf_op jit(solution)/shard_map/ppermute | solution.py:16
  84.8 1.6 %collective-permute-start.13 = (f32[32,128]{1,0:T(8,128)S(1)}, f32[32,128]{1,0:T(8,128)S(1)}, u32[]{:S(2)}, u32[]{:S(2)}) collective-permute-start(f32[32,128]{1,0:T(8,128)S(1)} %get-tuple-element.20), channel_id=1, source_target_pairs={{0,28},{4,24},{8,20},{12,16},{16,12},{20,8},{24,4},{28,0},{1,29},{... | collective-permute-start | bytes 49160 | tf_op jit(solution)/shard_map/ppermute | solution.py:16
  86.4 0.2 collective-permute-start.7
  86.5 1.0 %collective-permute-start.8 = (f32[32,128]{1,0:T(8,128)S(1)}, f32[32,128]{1,0:T(8,128)S(1)}, u32[]{:S(2)}, u32[]{:S(2)}) collective-permute-start(f32[32,128]{1,0:T(8,128)S(1)} %get-tuple-element.15), channel_id=1, source_target_pairs={{0,8},{4,12},{8,0},{12,4},{16,24},{20,28},{24,16},{28,20},{1,9},{5... | collective-permute-start | bytes 49160 | tf_op jit(solution)/shard_map/ppermute | solution.py:16
  87.6 0.6 collective-permute-start.9
  88.2 0.6 collective-permute-done.13
  88.9 1.4 %collective-permute-done.8 = f32[32,128]{1,0:T(8,128)S(1)} collective-permute-done((f32[32,128]{1,0:T(8,128)S(1)}, f32[32,128]{1,0:T(8,128)S(1)}, u32[]{:S(2)}, u32[]{:S(2)}) %collective-permute-start.8) | collective-permute-done | bytes 16416 | tf_op jit(solution)/shard_map/ppermute | solution.py:16
  90.3 0.6 collective-permute-done.9
  90.8 0.6 add_add_fusion
  (15 shorter events, 0.0 us)
Async XLA Ops:
  0.0 7.2 %collective-permute-start.1 = (bf16[64,1024]{1,0:T(8,128)(2,1)}, bf16[64,1024]{1,0:T(8,128)(2,1)S(1)}, u32[]{:S(2)}, u32[]{:S(2)}) collective-permute-start(bf16[64,1024]{1,0:T(8,128)(2,1)} %bitcast.10), channel_id=1, source_target_pairs={{0,8},{4,12},{8,0},{12,4},{16,24},{20,28},{24,16},{28,20},{1,9},{5... | collective-permute-start | bytes 393224 | tf_op jit(solution)/shard_map/ppermute | solution.py:16
  2.9 8.1 %collective-permute-start.3 = (bf16[64,1024]{1,0:T(8,128)(2,1)}, bf16[64,1024]{1,0:T(8,128)(2,1)}, u32[]{:S(2)}, u32[]{:S(2)}) collective-permute-start(bf16[64,1024]{1,0:T(8,128)(2,1)} %bitcast.11), channel_id=1, source_target_pairs={{0,16},{4,20},{8,24},{12,28},{16,0},{20,4},{24,8},{28,12},{1,17},{... | collective-permute-start | bytes 393224 | tf_op jit(solution)/shard_map/ppermute | solution.py:16
  4.5 6.6 %collective-permute-start.5 = (bf16[64,1024]{1,0:T(8,128)(2,1)}, bf16[64,1024]{1,0:T(8,128)(2,1)}, u32[]{:S(2)}, u32[]{:S(2)}) collective-permute-start(bf16[64,1024]{1,0:T(8,128)(2,1)} %bitcast.12), channel_id=1, source_target_pairs={{0,24},{4,28},{8,16},{12,20},{16,8},{20,12},{24,0},{28,4},{1,25},{... | collective-permute-start | bytes 393224 | tf_op jit(solution)/shard_map/ppermute | solution.py:16
  4.5 16.3 %collective-permute-start = (bf16[64,1024]{1,0:T(8,128)(2,1)}, bf16[64,1024]{1,0:T(8,128)(2,1)}, u32[]{:S(2)}, u32[]{:S(2)}) collective-permute-start(bf16[64,1024]{1,0:T(8,128)(2,1)} %bitcast.13), channel_id=1, source_target_pairs={{0,4},{4,0},{8,12},{12,8},{16,20},{20,16},{24,28},{28,24},{1,5},{5... | collective-permute-start | bytes 393224 | tf_op jit(solution)/shard_map/ppermute | solution.py:16
  7.2 13.6 %collective-permute-start.2 = (bf16[64,1024]{1,0:T(8,128)(2,1)S(1)}, bf16[64,1024]{1,0:T(8,128)(2,1)}, u32[]{:S(2)}, u32[]{:S(2)}) collective-permute-start(bf16[64,1024]{1,0:T(8,128)(2,1)S(1)} %collective-permute-done.1.refs_2_), channel_id=1, source_target_pairs={{0,4},{4,0},{8,12},{12,8},{16,20},{20,16},{24,28},{28,24},{1,5},{5... | collective-permute-start | bytes 393224 | tf_op jit(solution)/shard_map/ppermute | solution.py:16
  11.0 9.7 %collective-permute-start.4 = (bf16[64,1024]{1,0:T(8,128)(2,1)}, bf16[64,1024]{1,0:T(8,128)(2,1)}, u32[]{:S(2)}, u32[]{:S(2)}) collective-permute-start(bf16[64,1024]{1,0:T(8,128)(2,1)} %collective-permute-done.3.refs_4_), channel_id=1, source_target_pairs={{0,4},{4,0},{8,12},{12,8},{16,20},{20,16},{24,28},{28,24},{1,5},{5... | collective-permute-start | bytes 393224 | tf_op jit(solution)/shard_map/ppermute | solution.py:16
  11.0 9.7 %collective-permute-start.6 = (bf16[64,1024]{1,0:T(8,128)(2,1)}, bf16[64,1024]{1,0:T(8,128)(2,1)}, u32[]{:S(2)}, u32[]{:S(2)}) collective-permute-start(bf16[64,1024]{1,0:T(8,128)(2,1)} %collective-permute-done.5.refs_6_), channel_id=1, source_target_pairs={{0,4},{4,0},{8,12},{12,8},{16,20},{20,16},{24,28},{28,24},{1,5},{5... | collective-permute-start | bytes 393224 | tf_op jit(solution)/shard_map/ppermute | solution.py:16
  16.4 4.4 %copy-start.1 = (bf16[1,64,1024]{2,1,0:T(8,128)(2,1)S(1)}, bf16[1,64,1024]{2,1,0:T(8,128)(2,1)}, u32[]{:S(2)}) copy-start(bf16[1,64,1024]{2,1,0:T(8,128)(2,1)} %param.5) | copy-start | bytes 393220
  20.8 5.8 %copy-start = (s32[32768]{0:T(1024)S(1)}, s32[32768]{0:T(1024)}, u32[]{:S(2)}) copy-start(s32[32768]{0:T(1024)} %param.7) | copy-start | bytes 393220
  81.9 4.6 %collective-permute-start.10 = (f32[32,128]{1,0:T(8,128)S(1)}, f32[32,128]{1,0:T(8,128)S(1)}, u32[]{:S(2)}, u32[]{:S(2)}) collective-permute-start(f32[32,128]{1,0:T(8,128)S(1)} %get-tuple-element.17), channel_id=1, source_target_pairs={{0,16},{4,20},{8,24},{12,28},{16,0},{20,4},{24,8},{28,12},{1,17},{... | collective-permute-start | bytes 49160 | tf_op jit(solution)/shard_map/ppermute | solution.py:16
  83.5 4.1 %collective-permute-start.11 = (f32[32,128]{1,0:T(8,128)S(1)}, f32[32,128]{1,0:T(8,128)S(1)}, u32[]{:S(2)}, u32[]{:S(2)}) collective-permute-start(f32[32,128]{1,0:T(8,128)S(1)} %get-tuple-element.18), channel_id=1, source_target_pairs={{0,20},{4,16},{8,28},{12,24},{16,4},{20,0},{24,12},{28,8},{1,21},{... | collective-permute-start | bytes 49160 | tf_op jit(solution)/shard_map/ppermute | solution.py:16
  83.5 4.7 %collective-permute-start.12 = (f32[32,128]{1,0:T(8,128)S(1)}, f32[32,128]{1,0:T(8,128)S(1)}, u32[]{:S(2)}, u32[]{:S(2)}) collective-permute-start(f32[32,128]{1,0:T(8,128)S(1)} %get-tuple-element.19), channel_id=1, source_target_pairs={{0,24},{4,28},{8,16},{12,20},{16,8},{20,12},{24,0},{28,4},{1,25},{... | collective-permute-start | bytes 49160 | tf_op jit(solution)/shard_map/ppermute | solution.py:16
  84.8 4.1 %collective-permute-start.13 = (f32[32,128]{1,0:T(8,128)S(1)}, f32[32,128]{1,0:T(8,128)S(1)}, u32[]{:S(2)}, u32[]{:S(2)}) collective-permute-start(f32[32,128]{1,0:T(8,128)S(1)} %get-tuple-element.20), channel_id=1, source_target_pairs={{0,28},{4,24},{8,20},{12,16},{16,12},{20,8},{24,4},{28,0},{1,29},{... | collective-permute-start | bytes 49160 | tf_op jit(solution)/shard_map/ppermute | solution.py:16
  86.4 2.5 %collective-permute-start.7 = (f32[32,128]{1,0:T(8,128)S(1)}, f32[32,128]{1,0:T(8,128)S(1)}, u32[]{:S(2)}, u32[]{:S(2)}) collective-permute-start(f32[32,128]{1,0:T(8,128)S(1)} %get-tuple-element.14), channel_id=1, source_target_pairs={{0,4},{4,0},{8,12},{12,8},{16,20},{20,16},{24,28},{28,24},{1,5},{5... | collective-permute-start | bytes 49160 | tf_op jit(solution)/shard_map/ppermute | solution.py:16
  86.5 3.7 %collective-permute-start.8 = (f32[32,128]{1,0:T(8,128)S(1)}, f32[32,128]{1,0:T(8,128)S(1)}, u32[]{:S(2)}, u32[]{:S(2)}) collective-permute-start(f32[32,128]{1,0:T(8,128)S(1)} %get-tuple-element.15), channel_id=1, source_target_pairs={{0,8},{4,12},{8,0},{12,4},{16,24},{20,28},{24,16},{28,20},{1,9},{5... | collective-permute-start | bytes 49160 | tf_op jit(solution)/shard_map/ppermute | solution.py:16
  87.6 3.2 %collective-permute-start.9 = (f32[32,128]{1,0:T(8,128)S(1)}, f32[32,128]{1,0:T(8,128)S(1)}, u32[]{:S(2)}, u32[]{:S(2)}) collective-permute-start(f32[32,128]{1,0:T(8,128)S(1)} %get-tuple-element.16), channel_id=1, source_target_pairs={{0,12},{4,8},{8,4},{12,0},{16,28},{20,24},{24,20},{28,16},{1,13},{... | collective-permute-start | bytes 49160 | tf_op jit(solution)/shard_map/ppermute | solution.py:16

commit v3 on v2

--- a/solution.py
+++ b/solution.py
@@ -80,20 +80,27 @@
 
 def gather_kernel(parties, scale, table, rows_ref, index_ref, *refs):
     out_refs = refs[:parties]
-    picked, result = refs[parties:]
+    result, *picked = refs[parties:]
     me = lax.axis_index("param")
     groups = index_ref.shape[0]
+    depth = len(picked)
     sub_at = lax.broadcasted_iota(jnp.int32, (LANES, LANES), 0)
 
-    def group(at, carry):
-        for k in range(LANES):
-            picked[k : k + 1, :] = table[rows_ref[at * LANES + k]]
+    def choose(at, rows):
         lane = index_ref[pl.ds(at, 1), :] & (LANES - 1)
-        chosen = jnp.where(sub_at == lane, picked[...].T, 0.0)
+        chosen = jnp.where(sub_at == lane, rows[...].T, 0.0)
         result[pl.ds(at, 1), :] = jnp.sum(chosen, axis=0, keepdims=True)
+
+    def step(at, carry):
+        for slot in range(depth):
+            group = at * depth + slot
+            choose(jnp.maximum(group - 1, 0), picked[slot - 1])
+            for k in range(LANES):
+                picked[slot][k : k + 1, :] = table[rows_ref[group * LANES + k]]
         return carry
 
-    lax.fori_loop(0, groups, group, 0)
+    lax.fori_loop(0, groups // depth, step, 0)
+    choose(groups - 1, picked[-1])
 
     share = groups // parties
     bits = (table.shape[0] * LANES).bit_length() - 1
@@ -140,10 +147,8 @@
         out_shape=[jax.ShapeDtypeStruct((groups // parties, LANES), jnp.float32)] * parties,
         in_specs=[vmem, pl.BlockSpec(memory_space=pltpu.SMEM), vmem],
         out_specs=[vmem] * parties,
-        scratch_shapes=[
-            pltpu.VMEM((LANES, LANES), jnp.float32),
-            pltpu.VMEM((groups, LANES), jnp.float32),
-        ],
+        scratch_shapes=[pltpu.VMEM((groups, LANES), jnp.float32)]
+        + [pltpu.VMEM((LANES, LANES), jnp.float32)] * 4,
         compiler_params=pltpu.CompilerParams(vmem_limit_bytes=32 * 1024 * 1024),
         name="gather",
     )(table.reshape(table_rows, 1, LANES), rows, indices.reshape(groups, LANES))

time: 91.7 us -> 75.4 us (0.82)
  Pallas kernels: 61.1 us -> 44.8 us
    pallas_call x1, Pallas kernels: 55.3 us -> 39 us  [on_device(): pl.pallas_call(functools.partial(gather_kernel, parties, 1.0 / math.sqrt(...]
  transfers between devices with their start and end apart: 14 -> 14, of which waited for: 5 -> 5; matrix products, arithmetic and copies ran while one was open for 10% -> 12% of each run, Pallas kernels for 0% -> 0%
where the time goes in v3:
time: 75.4 us; the launch traced here: 75.1 us
  Pallas kernels  44.8 us (59%)
  starting transfers between devices  11.3 us (15%)
  waiting for transfers between devices  9.18 us (12%)
  other arithmetic  5.45 us (7%)
  local copies, waits for them, and re-layouts  4.36 us (6%)
    pallas_call x1, Pallas kernels, on_device(): pl.pallas_call(functools.partial(gather_kernel, parties, 1.0 / math.sqrt(...  39 us
    ppermute x14, starting transfers between devices, flipped(): lax.ppermute(x, axis, [(i, i ^ mask) for i in range(lax.axis_size(axis))])  11.3 us
    ppermute x14, waiting for transfers between devices, flipped(): lax.ppermute(x, axis, [(i, i ^ mask) for i in range(lax.axis_size(axis))])  9.18 us
    pallas_call x1, Pallas kernels, on_device(): pl.pallas_call(functools.partial(transform_kernel, parties), out_shape=ja...  5.78 us
    convert_element_type x1, other arithmetic, on_device(): sign_matrix = signs.reshape(height, breadth).astype(jnp.bfloat16)  3.72 us
    convert_element_type x1, local copies, waits for them, and re-layouts, on_device(): sign_matrix = signs.reshape(height, breadth).astype(jnp.bfloat16)  2.86 us
  transfers between devices with their start and end apart: 14, of which 5 were waited for; matrix products, arithmetic and copies ran while one was open for 12% of the time, Pallas kernels for 0%

profile of v3, /device:TPU:0, one launch (start us, length us, event | category | flops | bytes accessed | tf_op | source)
XLA Modules:
  0.0 75.1 jit_solution(13973217515874776816)
XLA Ops:
  0.0 2.9 %collective-permute-start.1 = (bf16[64,1024]{1,0:T(8,128)(2,1)}, bf16[64,1024]{1,0:T(8,128)(2,1)S(1)}, u32[]{:S(2)}, u32[]{:S(2)}) collective-permute-start(bf16[64,1024]{1,0:T(8,128)(2,1)} %bitcast.10), channel_id=1, source_target_pairs={{0,8},{4,12},{8,0},{12,4},{16,24},{20,28},{24,16},{28,20},{1,9},{5... | collective-permute-start | bytes 393224 | tf_op jit(solution)/shard_map/ppermute | solution.py:16
  2.9 1.5 %collective-permute-start.3 = (bf16[64,1024]{1,0:T(8,128)(2,1)}, bf16[64,1024]{1,0:T(8,128)(2,1)}, u32[]{:S(2)}, u32[]{:S(2)}) collective-permute-start(bf16[64,1024]{1,0:T(8,128)(2,1)} %bitcast.11), channel_id=1, source_target_pairs={{0,16},{4,20},{8,24},{12,28},{16,0},{20,4},{24,8},{28,12},{1,17},{... | collective-permute-start | bytes 393224 | tf_op jit(solution)/shard_map/ppermute | solution.py:16
  4.5 2.7 %collective-permute-done.1.refs_2_ = bf16[64,1024]{1,0:T(8,128)(2,1)S(1)} collective-permute-done((bf16[64,1024]{1,0:T(8,128)(2,1)}, bf16[64,1024]{1,0:T(8,128)(2,1)S(1)}, u32[]{:S(2)}, u32[]{:S(2)}) %collective-permute-start.1) | collective-permute-done | bytes 131104 | tf_op jit(solution)/shard_map/ppermute | solution.py:16
  7.2 3.9 %collective-permute-done.3.refs_4_ = bf16[64,1024]{1,0:T(8,128)(2,1)} collective-permute-done((bf16[64,1024]{1,0:T(8,128)(2,1)}, bf16[64,1024]{1,0:T(8,128)(2,1)}, u32[]{:S(2)}, u32[]{:S(2)}) %collective-permute-start.3) | collective-permute-done | bytes 131104 | tf_op jit(solution)/shard_map/ppermute | solution.py:16
  11.0 0.0 collective-permute-done.5.refs_6_
  11.0 0.5 collective-permute-start.6
  11.5 1.1 %fusion.3.rows_ref = s32[32768]{0:T(1024)S(1)} fusion(s32[32768]{0:T(1024)} %param.7), kind=kLoop, calls=%fused_computation.13 | loop fusion | flops 1277952 | bytes 262144 | tf_op jit(solution)/shard_map/add | solution.py:130
  12.7 3.7 %convert_element_type.5 = bf16[1048576]{0:T(1024)(128)(2,1)} convert(s32[1048576]{0:T(1024)} %param.6) | non-fusion elementwise | flops 1048576 | bytes 6291456 | tf_op jit(solution)/shard_map/convert_element_type | solution.py:128
  16.4 2.9 %convert_element_type.6.signs_ref = bf16[1024,1024]{1,0:T(8,128)(2,1)S(1)} reshape(bf16[1048576]{0:T(1024)(128)(2,1)} %convert_element_type.5) | data formatting | bytes 4194304 | tf_op jit(solution)/shard_map/convert_element_type | solution.py:128
  19.2 1.5 %copy.5 = bf16[1,512,1024]{1,2,0:T(8,128)(2,1)S(1)} copy(bf16[1,512,1024]{2,1,0:T(8,128)(2,1)} %param.4) | data formatting | bytes 2097152 | tf_op args[0]
  20.7 0.0 collective-permute-done.refs_1_
  20.8 0.0 copy-start
  20.8 5.8 %transform.1 = f32[8192,128]{1,0:T(8,128)S(1)} custom-call(bf16[1024,512]{1,0:T(8,128)(2,1)S(1)} %bitcast.8, bf16[1024,1024]{1,0:T(8,128)(2,1)S(1)} %convert_element_type.6.signs_ref, bf16[64,1024]{1,0:T(8,128)(2,1)S(1)} %bitcast.14, bf16[64,1024]{1,0:T(8,128)(2,1)} %collective-permute-done.refs_1_, bf16[64,1024]{1,0:T(8,128)(2,1)S(1)} %collective-permute-done.1.refs_2_, ...), custom_call_target="tpu_custom_call" | custom-call | tf_op jit(solution)/shard_map/transform/pallas_call | solution.py:133
  26.6 39.0 %gather.1 = (f32[32,128]{1,0:T(8,128)S(1)}, f32[32,128]{1,0:T(8,128)S(1)}, f32[32,128]{1,0:T(8,128)S(1)}, f32[32,128]{1,0:T(8,128)S(1)}, f32[32,128]{1,0:T(8,128...) custom-call(f32[8192,1,128]{2,1,0:T(1,128)S(1)} %bitcast.7, ...), custom_call_target="tpu_custom_call" | custom-call | tf_op jit(solution)/shard_map/gather/pallas_call | solution.py:145
  65.6 1.6 %collective-permute-start.10 = (f32[32,128]{1,0:T(8,128)S(1)}, f32[32,128]{1,0:T(8,128)S(1)}, u32[]{:S(2)}, u32[]{:S(2)}) collective-permute-start(f32[32,128]{1,0:T(8,128)S(1)} %get-tuple-element.17), channel_id=1, source_target_pairs={{0,16},{4,20},{8,24},{12,28},{16,0},{20,4},{24,8},{28,12},{1,17},{... | collective-permute-start | bytes 49160 | tf_op jit(solution)/shard_map/ppermute | solution.py:16
  67.2 1.3 %collective-permute-start.12 = (f32[32,128]{1,0:T(8,128)S(1)}, f32[32,128]{1,0:T(8,128)S(1)}, u32[]{:S(2)}, u32[]{:S(2)}) collective-permute-start(f32[32,128]{1,0:T(8,128)S(1)} %get-tuple-element.19), channel_id=1, source_target_pairs={{0,24},{4,28},{8,16},{12,20},{16,8},{20,12},{24,0},{28,4},{1,25},{... | collective-permute-start | bytes 49160 | tf_op jit(solution)/shard_map/ppermute | solution.py:16
  68.5 1.6 %collective-permute-start.13 = (f32[32,128]{1,0:T(8,128)S(1)}, f32[32,128]{1,0:T(8,128)S(1)}, u32[]{:S(2)}, u32[]{:S(2)}) collective-permute-start(f32[32,128]{1,0:T(8,128)S(1)} %get-tuple-element.20), channel_id=1, source_target_pairs={{0,28},{4,24},{8,20},{12,16},{16,12},{20,8},{24,4},{28,0},{1,29},{... | collective-permute-start | bytes 49160 | tf_op jit(solution)/shard_map/ppermute | solution.py:16
  70.1 0.2 collective-permute-start.7
  70.2 1.0 %collective-permute-start.8 = (f32[32,128]{1,0:T(8,128)S(1)}, f32[32,128]{1,0:T(8,128)S(1)}, u32[]{:S(2)}, u32[]{:S(2)}) collective-permute-start(f32[32,128]{1,0:T(8,128)S(1)} %get-tuple-element.15), channel_id=1, source_target_pairs={{0,8},{4,12},{8,0},{12,4},{16,24},{20,28},{24,16},{28,20},{1,9},{5... | collective-permute-start | bytes 49160 | tf_op jit(solution)/shard_map/ppermute | solution.py:16
  71.3 0.6 collective-permute-start.9
  71.9 0.6 collective-permute-done.13
  72.6 1.4 %collective-permute-done.8 = f32[32,128]{1,0:T(8,128)S(1)} collective-permute-done((f32[32,128]{1,0:T(8,128)S(1)}, f32[32,128]{1,0:T(8,128)S(1)}, u32[]{:S(2)}, u32[]{:S(2)}) %collective-permute-start.8) | collective-permute-done | bytes 16416 | tf_op jit(solution)/shard_map/ppermute | solution.py:16
  74.0 0.6 collective-permute-done.9
  74.5 0.6 add_add_fusion
  (15 shorter events, 0.0 us)
Async XLA Ops:
  0.0 7.2 %collective-permute-start.1 = (bf16[64,1024]{1,0:T(8,128)(2,1)}, bf16[64,1024]{1,0:T(8,128)(2,1)S(1)}, u32[]{:S(2)}, u32[]{:S(2)}) collective-permute-start(bf16[64,1024]{1,0:T(8,128)(2,1)} %bitcast.10), channel_id=1, source_target_pairs={{0,8},{4,12},{8,0},{12,4},{16,24},{20,28},{24,16},{28,20},{1,9},{5... | collective-permute-start | bytes 393224 | tf_op jit(solution)/shard_map/ppermute | solution.py:16
  2.9 8.1 %collective-permute-start.3 = (bf16[64,1024]{1,0:T(8,128)(2,1)}, bf16[64,1024]{1,0:T(8,128)(2,1)}, u32[]{:S(2)}, u32[]{:S(2)}) collective-permute-start(bf16[64,1024]{1,0:T(8,128)(2,1)} %bitcast.11), channel_id=1, source_target_pairs={{0,16},{4,20},{8,24},{12,28},{16,0},{20,4},{24,8},{28,12},{1,17},{... | collective-permute-start | bytes 393224 | tf_op jit(solution)/shard_map/ppermute | solution.py:16
  4.5 6.6 %collective-permute-start.5 = (bf16[64,1024]{1,0:T(8,128)(2,1)}, bf16[64,1024]{1,0:T(8,128)(2,1)}, u32[]{:S(2)}, u32[]{:S(2)}) collective-permute-start(bf16[64,1024]{1,0:T(8,128)(2,1)} %bitcast.12), channel_id=1, source_target_pairs={{0,24},{4,28},{8,16},{12,20},{16,8},{20,12},{24,0},{28,4},{1,25},{... | collective-permute-start | bytes 393224 | tf_op jit(solution)/shard_map/ppermute | solution.py:16
  4.5 16.3 %collective-permute-start = (bf16[64,1024]{1,0:T(8,128)(2,1)}, bf16[64,1024]{1,0:T(8,128)(2,1)}, u32[]{:S(2)}, u32[]{:S(2)}) collective-permute-start(bf16[64,1024]{1,0:T(8,128)(2,1)} %bitcast.13), channel_id=1, source_target_pairs={{0,4},{4,0},{8,12},{12,8},{16,20},{20,16},{24,28},{28,24},{1,5},{5... | collective-permute-start | bytes 393224 | tf_op jit(solution)/shard_map/ppermute | solution.py:16
  7.2 13.6 %collective-permute-start.2 = (bf16[64,1024]{1,0:T(8,128)(2,1)S(1)}, bf16[64,1024]{1,0:T(8,128)(2,1)}, u32[]{:S(2)}, u32[]{:S(2)}) collective-permute-start(bf16[64,1024]{1,0:T(8,128)(2,1)S(1)} %collective-permute-done.1.refs_2_), channel_id=1, source_target_pairs={{0,4},{4,0},{8,12},{12,8},{16,20},{20,16},{24,28},{28,24},{1,5},{5... | collective-permute-start | bytes 393224 | tf_op jit(solution)/shard_map/ppermute | solution.py:16
  11.0 9.7 %collective-permute-start.4 = (bf16[64,1024]{1,0:T(8,128)(2,1)}, bf16[64,1024]{1,0:T(8,128)(2,1)}, u32[]{:S(2)}, u32[]{:S(2)}) collective-permute-start(bf16[64,1024]{1,0:T(8,128)(2,1)} %collective-permute-done.3.refs_4_), channel_id=1, source_target_pairs={{0,4},{4,0},{8,12},{12,8},{16,20},{20,16},{24,28},{28,24},{1,5},{5... | collective-permute-start | bytes 393224 | tf_op jit(solution)/shard_map/ppermute | solution.py:16
  11.0 9.7 %collective-permute-start.6 = (bf16[64,1024]{1,0:T(8,128)(2,1)}, bf16[64,1024]{1,0:T(8,128)(2,1)}, u32[]{:S(2)}, u32[]{:S(2)}) collective-permute-start(bf16[64,1024]{1,0:T(8,128)(2,1)} %collective-permute-done.5.refs_6_), channel_id=1, source_target_pairs={{0,4},{4,0},{8,12},{12,8},{16,20},{20,16},{24,28},{28,24},{1,5},{5... | collective-permute-start | bytes 393224 | tf_op jit(solution)/shard_map/ppermute | solution.py:16
  16.4 4.4 %copy-start.1 = (bf16[1,64,1024]{2,1,0:T(8,128)(2,1)S(1)}, bf16[1,64,1024]{2,1,0:T(8,128)(2,1)}, u32[]{:S(2)}) copy-start(bf16[1,64,1024]{2,1,0:T(8,128)(2,1)} %param.5) | copy-start | bytes 393220
  20.8 5.8 %copy-start = (s32[32768]{0:T(1024)S(1)}, s32[32768]{0:T(1024)}, u32[]{:S(2)}) copy-start(s32[32768]{0:T(1024)} %param.7) | copy-start | bytes 393220
  65.6 4.6 %collective-permute-start.10 = (f32[32,128]{1,0:T(8,128)S(1)}, f32[32,128]{1,0:T(8,128)S(1)}, u32[]{:S(2)}, u32[]{:S(2)}) collective-permute-start(f32[32,128]{1,0:T(8,128)S(1)} %get-tuple-element.17), channel_id=1, source_target_pairs={{0,16},{4,20},{8,24},{12,28},{16,0},{20,4},{24,8},{28,12},{1,17},{... | collective-permute-start | bytes 49160 | tf_op jit(solution)/shard_map/ppermute | solution.py:16
  67.2 4.1 %collective-permute-start.11 = (f32[32,128]{1,0:T(8,128)S(1)}, f32[32,128]{1,0:T(8,128)S(1)}, u32[]{:S(2)}, u32[]{:S(2)}) collective-permute-start(f32[32,128]{1,0:T(8,128)S(1)} %get-tuple-element.18), channel_id=1, source_target_pairs={{0,20},{4,16},{8,28},{12,24},{16,4},{20,0},{24,12},{28,8},{1,21},{... | collective-permute-start | bytes 49160 | tf_op jit(solution)/shard_map/ppermute | solution.py:16
  67.2 4.7 %collective-permute-start.12 = (f32[32,128]{1,0:T(8,128)S(1)}, f32[32,128]{1,0:T(8,128)S(1)}, u32[]{:S(2)}, u32[]{:S(2)}) collective-permute-start(f32[32,128]{1,0:T(8,128)S(1)} %get-tuple-element.19), channel_id=1, source_target_pairs={{0,24},{4,28},{8,16},{12,20},{16,8},{20,12},{24,0},{28,4},{1,25},{... | collective-permute-start | bytes 49160 | tf_op jit(solution)/shard_map/ppermute | solution.py:16
  68.5 4.1 %collective-permute-start.13 = (f32[32,128]{1,0:T(8,128)S(1)}, f32[32,128]{1,0:T(8,128)S(1)}, u32[]{:S(2)}, u32[]{:S(2)}) collective-permute-start(f32[32,128]{1,0:T(8,128)S(1)} %get-tuple-element.20), channel_id=1, source_target_pairs={{0,28},{4,24},{8,20},{12,16},{16,12},{20,8},{24,4},{28,0},{1,29},{... | collective-permute-start | bytes 49160 | tf_op jit(solution)/shard_map/ppermute | solution.py:16
  70.1 2.5 %collective-permute-start.7 = (f32[32,128]{1,0:T(8,128)S(1)}, f32[32,128]{1,0:T(8,128)S(1)}, u32[]{:S(2)}, u32[]{:S(2)}) collective-permute-start(f32[32,128]{1,0:T(8,128)S(1)} %get-tuple-element.14), channel_id=1, source_target_pairs={{0,4},{4,0},{8,12},{12,8},{16,20},{20,16},{24,28},{28,24},{1,5},{5... | collective-permute-start | bytes 49160 | tf_op jit(solution)/shard_map/ppermute | solution.py:16
  70.2 3.7 %collective-permute-start.8 = (f32[32,128]{1,0:T(8,128)S(1)}, f32[32,128]{1,0:T(8,128)S(1)}, u32[]{:S(2)}, u32[]{:S(2)}) collective-permute-start(f32[32,128]{1,0:T(8,128)S(1)} %get-tuple-element.15), channel_id=1, source_target_pairs={{0,8},{4,12},{8,0},{12,4},{16,24},{20,28},{24,16},{28,20},{1,9},{5... | collective-permute-start | bytes 49160 | tf_op jit(solution)/shard_map/ppermute | solution.py:16
  71.3 3.2 %collective-permute-start.9 = (f32[32,128]{1,0:T(8,128)S(1)}, f32[32,128]{1,0:T(8,128)S(1)}, u32[]{:S(2)}, u32[]{:S(2)}) collective-permute-start(f32[32,128]{1,0:T(8,128)S(1)} %get-tuple-element.16), channel_id=1, source_target_pairs={{0,12},{4,8},{8,4},{12,0},{16,28},{20,24},{24,20},{28,16},{1,13},{... | collective-permute-start | bytes 49160 | tf_op jit(solution)/shard_map/ppermute | solution.py:16

commit v4 on v3

--- a/solution.py
+++ b/solution.py
@@ -95,8 +95,9 @@
         for slot in range(depth):
             group = at * depth + slot
             choose(jnp.maximum(group - 1, 0), picked[slot - 1])
+            single = picked[slot].reshape(LANES, 1, LANES)
             for k in range(LANES):
-                picked[slot][k : k + 1, :] = table[rows_ref[group * LANES + k]]
+                single[k] = table[rows_ref[group * LANES + k]]
         return carry
 
     lax.fori_loop(0, groups // depth, step, 0)

time: 75.4 us -> 75.4 us (level)
  no operation moved by 1% of the time
where the time goes in v4:
time: 75.4 us; the launch traced here: 75.1 us
  Pallas kernels  44.8 us (59%)
  starting transfers between devices  11.3 us (15%)
  waiting for transfers between devices  9.18 us (12%)
  other arithmetic  5.45 us (7%)
  local copies, waits for them, and re-layouts  4.36 us (6%)
    pallas_call x1, Pallas kernels, on_device(): pl.pallas_call(functools.partial(gather_kernel, parties, 1.0 / math.sqrt(...  39 us
    ppermute x14, starting transfers between devices, flipped(): lax.ppermute(x, axis, [(i, i ^ mask) for i in range(lax.axis_size(axis))])  11.3 us
    ppermute x14, waiting for transfers between devices, flipped(): lax.ppermute(x, axis, [(i, i ^ mask) for i in range(lax.axis_size(axis))])  9.18 us
    pallas_call x1, Pallas kernels, on_device(): pl.pallas_call(functools.partial(transform_kernel, parties), out_shape=ja...  5.78 us
    convert_element_type x1, other arithmetic, on_device(): sign_matrix = signs.reshape(height, breadth).astype(jnp.bfloat16)  3.72 us
    convert_element_type x1, local copies, waits for them, and re-layouts, on_device(): sign_matrix = signs.reshape(height, breadth).astype(jnp.bfloat16)  2.86 us
  transfers between devices with their start and end apart: 14, of which 5 were waited for; matrix products, arithmetic and copies ran while one was open for 12% of the time, Pallas kernels for 0%

profile of v4, /device:TPU:0, one launch (start us, length us, event | category | flops | bytes accessed | tf_op | source)
XLA Modules:
  0.0 75.1 jit_solution(13973217515874776816)
XLA Ops:
  0.0 2.9 %collective-permute-start.1 = (bf16[64,1024]{1,0:T(8,128)(2,1)}, bf16[64,1024]{1,0:T(8,128)(2,1)S(1)}, u32[]{:S(2)}, u32[]{:S(2)}) collective-permute-start(bf16[64,1024]{1,0:T(8,128)(2,1)} %bitcast.10), channel_id=1, source_target_pairs={{0,8},{4,12},{8,0},{12,4},{16,24},{20,28},{24,16},{28,20},{1,9},{5... | collective-permute-start | bytes 393224 | tf_op jit(solution)/shard_map/ppermute | solution.py:16
  2.9 1.5 %collective-permute-start.3 = (bf16[64,1024]{1,0:T(8,128)(2,1)}, bf16[64,1024]{1,0:T(8,128)(2,1)}, u32[]{:S(2)}, u32[]{:S(2)}) collective-permute-start(bf16[64,1024]{1,0:T(8,128)(2,1)} %bitcast.11), channel_id=1, source_target_pairs={{0,16},{4,20},{8,24},{12,28},{16,0},{20,4},{24,8},{28,12},{1,17},{... | collective-permute-start | bytes 393224 | tf_op jit(solution)/shard_map/ppermute | solution.py:16
  4.5 2.7 %collective-permute-done.1.refs_2_ = bf16[64,1024]{1,0:T(8,128)(2,1)S(1)} collective-permute-done((bf16[64,1024]{1,0:T(8,128)(2,1)}, bf16[64,1024]{1,0:T(8,128)(2,1)S(1)}, u32[]{:S(2)}, u32[]{:S(2)}) %collective-permute-start.1) | collective-permute-done | bytes 131104 | tf_op jit(solution)/shard_map/ppermute | solution.py:16
  7.2 3.9 %collective-permute-done.3.refs_4_ = bf16[64,1024]{1,0:T(8,128)(2,1)} collective-permute-done((bf16[64,1024]{1,0:T(8,128)(2,1)}, bf16[64,1024]{1,0:T(8,128)(2,1)}, u32[]{:S(2)}, u32[]{:S(2)}) %collective-permute-start.3) | collective-permute-done | bytes 131104 | tf_op jit(solution)/shard_map/ppermute | solution.py:16
  11.0 0.0 collective-permute-done.5.refs_6_
  11.0 0.5 collective-permute-start.6
  11.5 1.1 %fusion.3.rows_ref = s32[32768]{0:T(1024)S(1)} fusion(s32[32768]{0:T(1024)} %param.7), kind=kLoop, calls=%fused_computation.13 | loop fusion | flops 1277952 | bytes 262144 | tf_op jit(solution)/shard_map/add | solution.py:131
  12.7 3.7 %convert_element_type.5 = bf16[1048576]{0:T(1024)(128)(2,1)} convert(s32[1048576]{0:T(1024)} %param.6) | non-fusion elementwise | flops 1048576 | bytes 6291456 | tf_op jit(solution)/shard_map/convert_element_type | solution.py:129
  16.4 2.9 %convert_element_type.6.signs_ref = bf16[1024,1024]{1,0:T(8,128)(2,1)S(1)} reshape(bf16[1048576]{0:T(1024)(128)(2,1)} %convert_element_type.5) | data formatting | bytes 4194304 | tf_op jit(solution)/shard_map/convert_element_type | solution.py:129
  19.2 1.5 %copy.5 = bf16[1,512,1024]{1,2,0:T(8,128)(2,1)S(1)} copy(bf16[1,512,1024]{2,1,0:T(8,128)(2,1)} %param.4) | data formatting | bytes 2097152 | tf_op args[0]
  20.7 0.0 collective-permute-done.refs_1_
  20.8 0.0 copy-start
  20.8 5.8 %transform.1 = f32[8192,128]{1,0:T(8,128)S(1)} custom-call(bf16[1024,512]{1,0:T(8,128)(2,1)S(1)} %bitcast.8, bf16[1024,1024]{1,0:T(8,128)(2,1)S(1)} %convert_element_type.6.signs_ref, bf16[64,1024]{1,0:T(8,128)(2,1)S(1)} %bitcast.14, bf16[64,1024]{1,0:T(8,128)(2,1)} %collective-permute-done.refs_1_, bf16[64,1024]{1,0:T(8,128)(2,1)S(1)} %collective-permute-done.1.refs_2_, ...), custom_call_target="tpu_custom_call" | custom-call | tf_op jit(solution)/shard_map/transform/pallas_call | solution.py:134
  26.6 39.0 %gather.1 = (f32[32,128]{1,0:T(8,128)S(1)}, f32[32,128]{1,0:T(8,128)S(1)}, f32[32,128]{1,0:T(8,128)S(1)}, f32[32,128]{1,0:T(8,128)S(1)}, f32[32,128]{1,0:T(8,128...) custom-call(f32[8192,1,128]{2,1,0:T(1,128)S(1)} %bitcast.7, ...), custom_call_target="tpu_custom_call" | custom-call | tf_op jit(solution)/shard_map/gather/pallas_call | solution.py:146
  65.6 1.6 %collective-permute-start.10 = (f32[32,128]{1,0:T(8,128)S(1)}, f32[32,128]{1,0:T(8,128)S(1)}, u32[]{:S(2)}, u32[]{:S(2)}) collective-permute-start(f32[32,128]{1,0:T(8,128)S(1)} %get-tuple-element.17), channel_id=1, source_target_pairs={{0,16},{4,20},{8,24},{12,28},{16,0},{20,4},{24,8},{28,12},{1,17},{... | collective-permute-start | bytes 49160 | tf_op jit(solution)/shard_map/ppermute | solution.py:16
  67.2 1.3 %collective-permute-start.12 = (f32[32,128]{1,0:T(8,128)S(1)}, f32[32,128]{1,0:T(8,128)S(1)}, u32[]{:S(2)}, u32[]{:S(2)}) collective-permute-start(f32[32,128]{1,0:T(8,128)S(1)} %get-tuple-element.19), channel_id=1, source_target_pairs={{0,24},{4,28},{8,16},{12,20},{16,8},{20,12},{24,0},{28,4},{1,25},{... | collective-permute-start | bytes 49160 | tf_op jit(solution)/shard_map/ppermute | solution.py:16
  68.5 1.6 %collective-permute-start.13 = (f32[32,128]{1,0:T(8,128)S(1)}, f32[32,128]{1,0:T(8,128)S(1)}, u32[]{:S(2)}, u32[]{:S(2)}) collective-permute-start(f32[32,128]{1,0:T(8,128)S(1)} %get-tuple-element.20), channel_id=1, source_target_pairs={{0,28},{4,24},{8,20},{12,16},{16,12},{20,8},{24,4},{28,0},{1,29},{... | collective-permute-start | bytes 49160 | tf_op jit(solution)/shard_map/ppermute | solution.py:16
  70.1 0.2 collective-permute-start.7
  70.2 1.0 %collective-permute-start.8 = (f32[32,128]{1,0:T(8,128)S(1)}, f32[32,128]{1,0:T(8,128)S(1)}, u32[]{:S(2)}, u32[]{:S(2)}) collective-permute-start(f32[32,128]{1,0:T(8,128)S(1)} %get-tuple-element.15), channel_id=1, source_target_pairs={{0,8},{4,12},{8,0},{12,4},{16,24},{20,28},{24,16},{28,20},{1,9},{5... | collective-permute-start | bytes 49160 | tf_op jit(solution)/shard_map/ppermute | solution.py:16
  71.3 0.6 collective-permute-start.9
  71.9 0.6 collective-permute-done.13
  72.6 1.4 %collective-permute-done.8 = f32[32,128]{1,0:T(8,128)S(1)} collective-permute-done((f32[32,128]{1,0:T(8,128)S(1)}, f32[32,128]{1,0:T(8,128)S(1)}, u32[]{:S(2)}, u32[]{:S(2)}) %collective-permute-start.8) | collective-permute-done | bytes 16416 | tf_op jit(solution)/shard_map/ppermute | solution.py:16
  74.0 0.6 collective-permute-done.9
  74.5 0.6 add_add_fusion
  (15 shorter events, 0.0 us)
Async XLA Ops:
  0.0 7.2 %collective-permute-start.1 = (bf16[64,1024]{1,0:T(8,128)(2,1)}, bf16[64,1024]{1,0:T(8,128)(2,1)S(1)}, u32[]{:S(2)}, u32[]{:S(2)}) collective-permute-start(bf16[64,1024]{1,0:T(8,128)(2,1)} %bitcast.10), channel_id=1, source_target_pairs={{0,8},{4,12},{8,0},{12,4},{16,24},{20,28},{24,16},{28,20},{1,9},{5... | collective-permute-start | bytes 393224 | tf_op jit(solution)/shard_map/ppermute | solution.py:16
  2.9 8.1 %collective-permute-start.3 = (bf16[64,1024]{1,0:T(8,128)(2,1)}, bf16[64,1024]{1,0:T(8,128)(2,1)}, u32[]{:S(2)}, u32[]{:S(2)}) collective-permute-start(bf16[64,1024]{1,0:T(8,128)(2,1)} %bitcast.11), channel_id=1, source_target_pairs={{0,16},{4,20},{8,24},{12,28},{16,0},{20,4},{24,8},{28,12},{1,17},{... | collective-permute-start | bytes 393224 | tf_op jit(solution)/shard_map/ppermute | solution.py:16
  4.5 6.6 %collective-permute-start.5 = (bf16[64,1024]{1,0:T(8,128)(2,1)}, bf16[64,1024]{1,0:T(8,128)(2,1)}, u32[]{:S(2)}, u32[]{:S(2)}) collective-permute-start(bf16[64,1024]{1,0:T(8,128)(2,1)} %bitcast.12), channel_id=1, source_target_pairs={{0,24},{4,28},{8,16},{12,20},{16,8},{20,12},{24,0},{28,4},{1,25},{... | collective-permute-start | bytes 393224 | tf_op jit(solution)/shard_map/ppermute | solution.py:16
  4.5 16.3 %collective-permute-start = (bf16[64,1024]{1,0:T(8,128)(2,1)}, bf16[64,1024]{1,0:T(8,128)(2,1)}, u32[]{:S(2)}, u32[]{:S(2)}) collective-permute-start(bf16[64,1024]{1,0:T(8,128)(2,1)} %bitcast.13), channel_id=1, source_target_pairs={{0,4},{4,0},{8,12},{12,8},{16,20},{20,16},{24,28},{28,24},{1,5},{5... | collective-permute-start | bytes 393224 | tf_op jit(solution)/shard_map/ppermute | solution.py:16
  7.2 13.6 %collective-permute-start.2 = (bf16[64,1024]{1,0:T(8,128)(2,1)S(1)}, bf16[64,1024]{1,0:T(8,128)(2,1)}, u32[]{:S(2)}, u32[]{:S(2)}) collective-permute-start(bf16[64,1024]{1,0:T(8,128)(2,1)S(1)} %collective-permute-done.1.refs_2_), channel_id=1, source_target_pairs={{0,4},{4,0},{8,12},{12,8},{16,20},{20,16},{24,28},{28,24},{1,5},{5... | collective-permute-start | bytes 393224 | tf_op jit(solution)/shard_map/ppermute | solution.py:16
  11.0 9.7 %collective-permute-start.4 = (bf16[64,1024]{1,0:T(8,128)(2,1)}, bf16[64,1024]{1,0:T(8,128)(2,1)}, u32[]{:S(2)}, u32[]{:S(2)}) collective-permute-start(bf16[64,1024]{1,0:T(8,128)(2,1)} %collective-permute-done.3.refs_4_), channel_id=1, source_target_pairs={{0,4},{4,0},{8,12},{12,8},{16,20},{20,16},{24,28},{28,24},{1,5},{5... | collective-permute-start | bytes 393224 | tf_op jit(solution)/shard_map/ppermute | solution.py:16
  11.0 9.7 %collective-permute-start.6 = (bf16[64,1024]{1,0:T(8,128)(2,1)}, bf16[64,1024]{1,0:T(8,128)(2,1)}, u32[]{:S(2)}, u32[]{:S(2)}) collective-permute-start(bf16[64,1024]{1,0:T(8,128)(2,1)} %collective-permute-done.5.refs_6_), channel_id=1, source_target_pairs={{0,4},{4,0},{8,12},{12,8},{16,20},{20,16},{24,28},{28,24},{1,5},{5... | collective-permute-start | bytes 393224 | tf_op jit(solution)/shard_map/ppermute | solution.py:16
  16.4 4.4 %copy-start.1 = (bf16[1,64,1024]{2,1,0:T(8,128)(2,1)S(1)}, bf16[1,64,1024]{2,1,0:T(8,128)(2,1)}, u32[]{:S(2)}) copy-start(bf16[1,64,1024]{2,1,0:T(8,128)(2,1)} %param.5) | copy-start | bytes 393220
  20.8 5.8 %copy-start = (s32[32768]{0:T(1024)S(1)}, s32[32768]{0:T(1024)}, u32[]{:S(2)}) copy-start(s32[32768]{0:T(1024)} %param.7) | copy-start | bytes 393220
  65.6 4.6 %collective-permute-start.10 = (f32[32,128]{1,0:T(8,128)S(1)}, f32[32,128]{1,0:T(8,128)S(1)}, u32[]{:S(2)}, u32[]{:S(2)}) collective-permute-start(f32[32,128]{1,0:T(8,128)S(1)} %get-tuple-element.17), channel_id=1, source_target_pairs={{0,16},{4,20},{8,24},{12,28},{16,0},{20,4},{24,8},{28,12},{1,17},{... | collective-permute-start | bytes 49160 | tf_op jit(solution)/shard_map/ppermute | solution.py:16
  67.2 4.1 %collective-permute-start.11 = (f32[32,128]{1,0:T(8,128)S(1)}, f32[32,128]{1,0:T(8,128)S(1)}, u32[]{:S(2)}, u32[]{:S(2)}) collective-permute-start(f32[32,128]{1,0:T(8,128)S(1)} %get-tuple-element.18), channel_id=1, source_target_pairs={{0,20},{4,16},{8,28},{12,24},{16,4},{20,0},{24,12},{28,8},{1,21},{... | collective-permute-start | bytes 49160 | tf_op jit(solution)/shard_map/ppermute | solution.py:16
  67.2 4.7 %collective-permute-start.12 = (f32[32,128]{1,0:T(8,128)S(1)}, f32[32,128]{1,0:T(8,128)S(1)}, u32[]{:S(2)}, u32[]{:S(2)}) collective-permute-start(f32[32,128]{1,0:T(8,128)S(1)} %get-tuple-element.19), channel_id=1, source_target_pairs={{0,24},{4,28},{8,16},{12,20},{16,8},{20,12},{24,0},{28,4},{1,25},{... | collective-permute-start | bytes 49160 | tf_op jit(solution)/shard_map/ppermute | solution.py:16
  68.5 4.1 %collective-permute-start.13 = (f32[32,128]{1,0:T(8,128)S(1)}, f32[32,128]{1,0:T(8,128)S(1)}, u32[]{:S(2)}, u32[]{:S(2)}) collective-permute-start(f32[32,128]{1,0:T(8,128)S(1)} %get-tuple-element.20), channel_id=1, source_target_pairs={{0,28},{4,24},{8,20},{12,16},{16,12},{20,8},{24,4},{28,0},{1,29},{... | collective-permute-start | bytes 49160 | tf_op jit(solution)/shard_map/ppermute | solution.py:16
  70.1 2.5 %collective-permute-start.7 = (f32[32,128]{1,0:T(8,128)S(1)}, f32[32,128]{1,0:T(8,128)S(1)}, u32[]{:S(2)}, u32[]{:S(2)}) collective-permute-start(f32[32,128]{1,0:T(8,128)S(1)} %get-tuple-element.14), channel_id=1, source_target_pairs={{0,4},{4,0},{8,12},{12,8},{16,20},{20,16},{24,28},{28,24},{1,5},{5... | collective-permute-start | bytes 49160 | tf_op jit(solution)/shard_map/ppermute | solution.py:16
  70.2 3.7 %collective-permute-start.8 = (f32[32,128]{1,0:T(8,128)S(1)}, f32[32,128]{1,0:T(8,128)S(1)}, u32[]{:S(2)}, u32[]{:S(2)}) collective-permute-start(f32[32,128]{1,0:T(8,128)S(1)} %get-tuple-element.15), channel_id=1, source_target_pairs={{0,8},{4,12},{8,0},{12,4},{16,24},{20,28},{24,16},{28,20},{1,9},{5... | collective-permute-start | bytes 49160 | tf_op jit(solution)/shard_map/ppermute | solution.py:16
  71.3 3.2 %collective-permute-start.9 = (f32[32,128]{1,0:T(8,128)S(1)}, f32[32,128]{1,0:T(8,128)S(1)}, u32[]{:S(2)}, u32[]{:S(2)}) collective-permute-start(f32[32,128]{1,0:T(8,128)S(1)} %get-tuple-element.16), channel_id=1, source_target_pairs={{0,12},{4,8},{8,4},{12,0},{16,28},{20,24},{24,20},{28,16},{1,13},{... | collective-permute-start | bytes 49160 | tf_op jit(solution)/shard_map/ppermute | solution.py:16

commit v5 on v4

--- a/solution.py
+++ b/solution.py
@@ -10,6 +10,7 @@
 
 LANES = 128
 SIDE = 256
+BATCH = 16
 
 
 def flipped(x, axis, mask):
@@ -96,8 +97,10 @@
             group = at * depth + slot
             choose(jnp.maximum(group - 1, 0), picked[slot - 1])
             single = picked[slot].reshape(LANES, 1, LANES)
-            for k in range(LANES):
-                single[k] = table[rows_ref[group * LANES + k]]
+            for first in range(0, LANES, BATCH):
+                rows = [table[rows_ref[group * LANES + first + k]] for k in range(BATCH)]
+                for k in range(BATCH):
+                    single[first + k] = rows[k]
         return carry
 
     lax.fori_loop(0, groups // depth, step, 0)

time: 75.4 us -> 75.4 us (level)
  no operation moved by 1% of the time
where the time goes in v5:
time: 75.4 us; the launch traced here: 75.1 us
  Pallas kernels  44.8 us (59%)
  starting transfers between devices  11.3 us (15%)
  waiting for transfers between devices  9.18 us (12%)
  other arithmetic  5.45 us (7%)
  local copies, waits for them, and re-layouts  4.36 us (6%)
    pallas_call x1, Pallas kernels, on_device(): pl.pallas_call(functools.partial(gather_kernel, parties, 1.0 / math.sqrt(...  39 us
    ppermute x14, starting transfers between devices, flipped(): lax.ppermute(x, axis, [(i, i ^ mask) for i in range(lax.axis_size(axis))])  11.3 us
    ppermute x14, waiting for transfers between devices, flipped(): lax.ppermute(x, axis, [(i, i ^ mask) for i in range(lax.axis_size(axis))])  9.18 us
    pallas_call x1, Pallas kernels, on_device(): pl.pallas_call(functools.partial(transform_kernel, parties), out_shape=ja...  5.78 us
    convert_element_type x1, other arithmetic, on_device(): sign_matrix = signs.reshape(height, breadth).astype(jnp.bfloat16)  3.72 us
    convert_element_type x1, local copies, waits for them, and re-layouts, on_device(): sign_matrix = signs.reshape(height, breadth).astype(jnp.bfloat16)  2.86 us
  transfers between devices with their start and end apart: 14, of which 5 were waited for; matrix products, arithmetic and copies ran while one was open for 12% of the time, Pallas kernels for 0%

profile of v5, /device:TPU:0, one launch (start us, length us, event | category | flops | bytes accessed | tf_op | source)
XLA Modules:
  0.0 75.1 jit_solution(9656492025928781944)
XLA Ops:
  0.0 2.9 %collective-permute-start.1 = (bf16[64,1024]{1,0:T(8,128)(2,1)}, bf16[64,1024]{1,0:T(8,128)(2,1)S(1)}, u32[]{:S(2)}, u32[]{:S(2)}) collective-permute-start(bf16[64,1024]{1,0:T(8,128)(2,1)} %bitcast.10), channel_id=1, source_target_pairs={{0,8},{4,12},{8,0},{12,4},{16,24},{20,28},{24,16},{28,20},{1,9},{5... | collective-permute-start | bytes 393224 | tf_op jit(solution)/shard_map/ppermute | solution.py:17
  2.9 1.5 %collective-permute-start.3 = (bf16[64,1024]{1,0:T(8,128)(2,1)}, bf16[64,1024]{1,0:T(8,128)(2,1)}, u32[]{:S(2)}, u32[]{:S(2)}) collective-permute-start(bf16[64,1024]{1,0:T(8,128)(2,1)} %bitcast.11), channel_id=1, source_target_pairs={{0,16},{4,20},{8,24},{12,28},{16,0},{20,4},{24,8},{28,12},{1,17},{... | collective-permute-start | bytes 393224 | tf_op jit(solution)/shard_map/ppermute | solution.py:17
  4.5 2.7 %collective-permute-done.1.refs_2_ = bf16[64,1024]{1,0:T(8,128)(2,1)S(1)} collective-permute-done((bf16[64,1024]{1,0:T(8,128)(2,1)}, bf16[64,1024]{1,0:T(8,128)(2,1)S(1)}, u32[]{:S(2)}, u32[]{:S(2)}) %collective-permute-start.1) | collective-permute-done | bytes 131104 | tf_op jit(solution)/shard_map/ppermute | solution.py:17
  7.2 3.9 %collective-permute-done.3.refs_4_ = bf16[64,1024]{1,0:T(8,128)(2,1)} collective-permute-done((bf16[64,1024]{1,0:T(8,128)(2,1)}, bf16[64,1024]{1,0:T(8,128)(2,1)}, u32[]{:S(2)}, u32[]{:S(2)}) %collective-permute-start.3) | collective-permute-done | bytes 131104 | tf_op jit(solution)/shard_map/ppermute | solution.py:17
  11.0 0.0 collective-permute-done.5.refs_6_
  11.0 0.5 collective-permute-start.6
  11.5 1.1 %fusion.3.rows_ref = s32[32768]{0:T(1024)S(1)} fusion(s32[32768]{0:T(1024)} %param.7), kind=kLoop, calls=%fused_computation.13 | loop fusion | flops 1277952 | bytes 262144 | tf_op jit(solution)/shard_map/add | solution.py:134
  12.7 3.7 %convert_element_type.5 = bf16[1048576]{0:T(1024)(128)(2,1)} convert(s32[1048576]{0:T(1024)} %param.6) | non-fusion elementwise | flops 1048576 | bytes 6291456 | tf_op jit(solution)/shard_map/convert_element_type | solution.py:132
  16.4 2.9 %convert_element_type.6.signs_ref = bf16[1024,1024]{1,0:T(8,128)(2,1)S(1)} reshape(bf16[1048576]{0:T(1024)(128)(2,1)} %convert_element_type.5) | data formatting | bytes 4194304 | tf_op jit(solution)/shard_map/convert_element_type | solution.py:132
  19.2 1.5 %copy.5 = bf16[1,512,1024]{1,2,0:T(8,128)(2,1)S(1)} copy(bf16[1,512,1024]{2,1,0:T(8,128)(2,1)} %param.4) | data formatting | bytes 2097152 | tf_op args[0]
  20.7 0.0 collective-permute-done.refs_1_
  20.8 0.0 copy-start
  20.8 5.8 %transform.1 = f32[8192,128]{1,0:T(8,128)S(1)} custom-call(bf16[1024,512]{1,0:T(8,128)(2,1)S(1)} %bitcast.8, bf16[1024,1024]{1,0:T(8,128)(2,1)S(1)} %convert_element_type.6.signs_ref, bf16[64,1024]{1,0:T(8,128)(2,1)S(1)} %bitcast.14, bf16[64,1024]{1,0:T(8,128)(2,1)} %collective-permute-done.refs_1_, bf16[64,1024]{1,0:T(8,128)(2,1)S(1)} %collective-permute-done.1.refs_2_, ...), custom_call_target="tpu_custom_call" | custom-call | tf_op jit(solution)/shard_map/transform/pallas_call | solution.py:137
  26.6 39.0 %gather.1 = (f32[32,128]{1,0:T(8,128)S(1)}, f32[32,128]{1,0:T(8,128)S(1)}, f32[32,128]{1,0:T(8,128)S(1)}, f32[32,128]{1,0:T(8,128)S(1)}, f32[32,128]{1,0:T(8,128...) custom-call(f32[8192,1,128]{2,1,0:T(1,128)S(1)} %bitcast.7, ...), custom_call_target="tpu_custom_call" | custom-call | tf_op jit(solution)/shard_map/gather/pallas_call | solution.py:149
  65.6 1.6 %collective-permute-start.10 = (f32[32,128]{1,0:T(8,128)S(1)}, f32[32,128]{1,0:T(8,128)S(1)}, u32[]{:S(2)}, u32[]{:S(2)}) collective-permute-start(f32[32,128]{1,0:T(8,128)S(1)} %get-tuple-element.17), channel_id=1, source_target_pairs={{0,16},{4,20},{8,24},{12,28},{16,0},{20,4},{24,8},{28,12},{1,17},{... | collective-permute-start | bytes 49160 | tf_op jit(solution)/shard_map/ppermute | solution.py:17
  67.2 1.3 %collective-permute-start.12 = (f32[32,128]{1,0:T(8,128)S(1)}, f32[32,128]{1,0:T(8,128)S(1)}, u32[]{:S(2)}, u32[]{:S(2)}) collective-permute-start(f32[32,128]{1,0:T(8,128)S(1)} %get-tuple-element.19), channel_id=1, source_target_pairs={{0,24},{4,28},{8,16},{12,20},{16,8},{20,12},{24,0},{28,4},{1,25},{... | collective-permute-start | bytes 49160 | tf_op jit(solution)/shard_map/ppermute | solution.py:17
  68.5 1.6 %collective-permute-start.13 = (f32[32,128]{1,0:T(8,128)S(1)}, f32[32,128]{1,0:T(8,128)S(1)}, u32[]{:S(2)}, u32[]{:S(2)}) collective-permute-start(f32[32,128]{1,0:T(8,128)S(1)} %get-tuple-element.20), channel_id=1, source_target_pairs={{0,28},{4,24},{8,20},{12,16},{16,12},{20,8},{24,4},{28,0},{1,29},{... | collective-permute-start | bytes 49160 | tf_op jit(solution)/shard_map/ppermute | solution.py:17
  70.1 0.2 collective-permute-start.7
  70.2 1.0 %collective-permute-start.8 = (f32[32,128]{1,0:T(8,128)S(1)}, f32[32,128]{1,0:T(8,128)S(1)}, u32[]{:S(2)}, u32[]{:S(2)}) collective-permute-start(f32[32,128]{1,0:T(8,128)S(1)} %get-tuple-element.15), channel_id=1, source_target_pairs={{0,8},{4,12},{8,0},{12,4},{16,24},{20,28},{24,16},{28,20},{1,9},{5... | collective-permute-start | bytes 49160 | tf_op jit(solution)/shard_map/ppermute | solution.py:17
  71.3 0.6 collective-permute-start.9
  71.9 0.6 collective-permute-done.13
  72.6 1.4 %collective-permute-done.8 = f32[32,128]{1,0:T(8,128)S(1)} collective-permute-done((f32[32,128]{1,0:T(8,128)S(1)}, f32[32,128]{1,0:T(8,128)S(1)}, u32[]{:S(2)}, u32[]{:S(2)}) %collective-permute-start.8) | collective-permute-done | bytes 16416 | tf_op jit(solution)/shard_map/ppermute | solution.py:17
  74.0 0.6 collective-permute-done.9
  74.5 0.6 add_add_fusion
  (15 shorter events, 0.0 us)
Async XLA Ops:
  0.0 7.2 %collective-permute-start.1 = (bf16[64,1024]{1,0:T(8,128)(2,1)}, bf16[64,1024]{1,0:T(8,128)(2,1)S(1)}, u32[]{:S(2)}, u32[]{:S(2)}) collective-permute-start(bf16[64,1024]{1,0:T(8,128)(2,1)} %bitcast.10), channel_id=1, source_target_pairs={{0,8},{4,12},{8,0},{12,4},{16,24},{20,28},{24,16},{28,20},{1,9},{5... | collective-permute-start | bytes 393224 | tf_op jit(solution)/shard_map/ppermute | solution.py:17
  2.9 8.1 %collective-permute-start.3 = (bf16[64,1024]{1,0:T(8,128)(2,1)}, bf16[64,1024]{1,0:T(8,128)(2,1)}, u32[]{:S(2)}, u32[]{:S(2)}) collective-permute-start(bf16[64,1024]{1,0:T(8,128)(2,1)} %bitcast.11), channel_id=1, source_target_pairs={{0,16},{4,20},{8,24},{12,28},{16,0},{20,4},{24,8},{28,12},{1,17},{... | collective-permute-start | bytes 393224 | tf_op jit(solution)/shard_map/ppermute | solution.py:17
  4.5 6.6 %collective-permute-start.5 = (bf16[64,1024]{1,0:T(8,128)(2,1)}, bf16[64,1024]{1,0:T(8,128)(2,1)}, u32[]{:S(2)}, u32[]{:S(2)}) collective-permute-start(bf16[64,1024]{1,0:T(8,128)(2,1)} %bitcast.12), channel_id=1, source_target_pairs={{0,24},{4,28},{8,16},{12,20},{16,8},{20,12},{24,0},{28,4},{1,25},{... | collective-permute-start | bytes 393224 | tf_op jit(solution)/shard_map/ppermute | solution.py:17
  4.5 16.3 %collective-permute-start = (bf16[64,1024]{1,0:T(8,128)(2,1)}, bf16[64,1024]{1,0:T(8,128)(2,1)}, u32[]{:S(2)}, u32[]{:S(2)}) collective-permute-start(bf16[64,1024]{1,0:T(8,128)(2,1)} %bitcast.13), channel_id=1, source_target_pairs={{0,4},{4,0},{8,12},{12,8},{16,20},{20,16},{24,28},{28,24},{1,5},{5... | collective-permute-start | bytes 393224 | tf_op jit(solution)/shard_map/ppermute | solution.py:17
  7.2 13.6 %collective-permute-start.2 = (bf16[64,1024]{1,0:T(8,128)(2,1)S(1)}, bf16[64,1024]{1,0:T(8,128)(2,1)}, u32[]{:S(2)}, u32[]{:S(2)}) collective-permute-start(bf16[64,1024]{1,0:T(8,128)(2,1)S(1)} %collective-permute-done.1.refs_2_), channel_id=1, source_target_pairs={{0,4},{4,0},{8,12},{12,8},{16,20},{20,16},{24,28},{28,24},{1,5},{5... | collective-permute-start | bytes 393224 | tf_op jit(solution)/shard_map/ppermute | solution.py:17
  11.0 9.7 %collective-permute-start.4 = (bf16[64,1024]{1,0:T(8,128)(2,1)}, bf16[64,1024]{1,0:T(8,128)(2,1)}, u32[]{:S(2)}, u32[]{:S(2)}) collective-permute-start(bf16[64,1024]{1,0:T(8,128)(2,1)} %collective-permute-done.3.refs_4_), channel_id=1, source_target_pairs={{0,4},{4,0},{8,12},{12,8},{16,20},{20,16},{24,28},{28,24},{1,5},{5... | collective-permute-start | bytes 393224 | tf_op jit(solution)/shard_map/ppermute | solution.py:17
  11.0 9.7 %collective-permute-start.6 = (bf16[64,1024]{1,0:T(8,128)(2,1)}, bf16[64,1024]{1,0:T(8,128)(2,1)}, u32[]{:S(2)}, u32[]{:S(2)}) collective-permute-start(bf16[64,1024]{1,0:T(8,128)(2,1)} %collective-permute-done.5.refs_6_), channel_id=1, source_target_pairs={{0,4},{4,0},{8,12},{12,8},{16,20},{20,16},{24,28},{28,24},{1,5},{5... | collective-permute-start | bytes 393224 | tf_op jit(solution)/shard_map/ppermute | solution.py:17
  16.4 4.4 %copy-start.1 = (bf16[1,64,1024]{2,1,0:T(8,128)(2,1)S(1)}, bf16[1,64,1024]{2,1,0:T(8,128)(2,1)}, u32[]{:S(2)}) copy-start(bf16[1,64,1024]{2,1,0:T(8,128)(2,1)} %param.5) | copy-start | bytes 393220
  20.8 5.8 %copy-start = (s32[32768]{0:T(1024)S(1)}, s32[32768]{0:T(1024)}, u32[]{:S(2)}) copy-start(s32[32768]{0:T(1024)} %param.7) | copy-start | bytes 393220
  65.6 4.6 %collective-permute-start.10 = (f32[32,128]{1,0:T(8,128)S(1)}, f32[32,128]{1,0:T(8,128)S(1)}, u32[]{:S(2)}, u32[]{:S(2)}) collective-permute-start(f32[32,128]{1,0:T(8,128)S(1)} %get-tuple-element.17), channel_id=1, source_target_pairs={{0,16},{4,20},{8,24},{12,28},{16,0},{20,4},{24,8},{28,12},{1,17},{... | collective-permute-start | bytes 49160 | tf_op jit(solution)/shard_map/ppermute | solution.py:17
  67.2 4.1 %collective-permute-start.11 = (f32[32,128]{1,0:T(8,128)S(1)}, f32[32,128]{1,0:T(8,128)S(1)}, u32[]{:S(2)}, u32[]{:S(2)}) collective-permute-start(f32[32,128]{1,0:T(8,128)S(1)} %get-tuple-element.18), channel_id=1, source_target_pairs={{0,20},{4,16},{8,28},{12,24},{16,4},{20,0},{24,12},{28,8},{1,21},{... | collective-permute-start | bytes 49160 | tf_op jit(solution)/shard_map/ppermute | solution.py:17
  67.2 4.7 %collective-permute-start.12 = (f32[32,128]{1,0:T(8,128)S(1)}, f32[32,128]{1,0:T(8,128)S(1)}, u32[]{:S(2)}, u32[]{:S(2)}) collective-permute-start(f32[32,128]{1,0:T(8,128)S(1)} %get-tuple-element.19), channel_id=1, source_target_pairs={{0,24},{4,28},{8,16},{12,20},{16,8},{20,12},{24,0},{28,4},{1,25},{... | collective-permute-start | bytes 49160 | tf_op jit(solution)/shard_map/ppermute | solution.py:17
  68.5 4.1 %collective-permute-start.13 = (f32[32,128]{1,0:T(8,128)S(1)}, f32[32,128]{1,0:T(8,128)S(1)}, u32[]{:S(2)}, u32[]{:S(2)}) collective-permute-start(f32[32,128]{1,0:T(8,128)S(1)} %get-tuple-element.20), channel_id=1, source_target_pairs={{0,28},{4,24},{8,20},{12,16},{16,12},{20,8},{24,4},{28,0},{1,29},{... | collective-permute-start | bytes 49160 | tf_op jit(solution)/shard_map/ppermute | solution.py:17
  70.1 2.5 %collective-permute-start.7 = (f32[32,128]{1,0:T(8,128)S(1)}, f32[32,128]{1,0:T(8,128)S(1)}, u32[]{:S(2)}, u32[]{:S(2)}) collective-permute-start(f32[32,128]{1,0:T(8,128)S(1)} %get-tuple-element.14), channel_id=1, source_target_pairs={{0,4},{4,0},{8,12},{12,8},{16,20},{20,16},{24,28},{28,24},{1,5},{5... | collective-permute-start | bytes 49160 | tf_op jit(solution)/shard_map/ppermute | solution.py:17
  70.2 3.7 %collective-permute-start.8 = (f32[32,128]{1,0:T(8,128)S(1)}, f32[32,128]{1,0:T(8,128)S(1)}, u32[]{:S(2)}, u32[]{:S(2)}) collective-permute-start(f32[32,128]{1,0:T(8,128)S(1)} %get-tuple-element.15), channel_id=1, source_target_pairs={{0,8},{4,12},{8,0},{12,4},{16,24},{20,28},{24,16},{28,20},{1,9},{5... | collective-permute-start | bytes 49160 | tf_op jit(solution)/shard_map/ppermute | solution.py:17
  71.3 3.2 %collective-permute-start.9 = (f32[32,128]{1,0:T(8,128)S(1)}, f32[32,128]{1,0:T(8,128)S(1)}, u32[]{:S(2)}, u32[]{:S(2)}) collective-permute-start(f32[32,128]{1,0:T(8,128)S(1)} %get-tuple-element.16), channel_id=1, source_target_pairs={{0,12},{4,8},{8,4},{12,0},{16,28},{20,24},{24,20},{28,16},{1,13},{... | collective-permute-start | bytes 49160 | tf_op jit(solution)/shard_map/ppermute | solution.py:17

commit v6 on v5

--- a/solution.py
+++ b/solution.py
@@ -86,11 +86,14 @@
     groups = index_ref.shape[0]
     depth = len(picked)
     sub_at = lax.broadcasted_iota(jnp.int32, (LANES, LANES), 0)
+    diagonal = sub_at == lax.broadcasted_iota(jnp.int32, (LANES, LANES), 1)
 
     def choose(at, rows):
         lane = index_ref[pl.ds(at, 1), :] & (LANES - 1)
-        chosen = jnp.where(sub_at == lane, rows[...].T, 0.0)
-        result[pl.ds(at, 1), :] = jnp.sum(chosen, axis=0, keepdims=True)
+        mask = jnp.where(sub_at == lane, 1.0, 0.0).astype(jnp.bfloat16)
+        both = jnp.concatenate(split(rows[...]), axis=1)
+        pairs = dot(both, jnp.concatenate([mask, mask], axis=0))
+        result[pl.ds(at, 1), :] = jnp.sum(jnp.where(diagonal, pairs, 0.0), axis=0, keepdims=True)
 
     def step(at, carry):
         for slot in range(depth):

time: 75.4 us -> 79 us (1.048)
  Pallas kernels: 44.8 us -> 48.4 us
    pallas_call x1, Pallas kernels: 39 us -> 42.6 us  [on_device(): pl.pallas_call(functools.partial(gather_kernel, parties, 1.0 / math.sqrt(...]
where the time goes in v6:
time: 79 us; the launch traced here: 78.8 us
  Pallas kernels  48.4 us (61%)
  starting transfers between devices  11.3 us (14%)
  waiting for transfers between devices  9.18 us (12%)
  other arithmetic  5.45 us (7%)
  local copies, waits for them, and re-layouts  4.36 us (6%)
    pallas_call x1, Pallas kernels, on_device(): pl.pallas_call(functools.partial(gather_kernel, parties, 1.0 / math.sqrt(...  42.6 us
    ppermute x14, starting transfers between devices, flipped(): lax.ppermute(x, axis, [(i, i ^ mask) for i in range(lax.axis_size(axis))])  11.3 us
    ppermute x14, waiting for transfers between devices, flipped(): lax.ppermute(x, axis, [(i, i ^ mask) for i in range(lax.axis_size(axis))])  9.18 us
    pallas_call x1, Pallas kernels, on_device(): pl.pallas_call(functools.partial(transform_kernel, parties), out_shape=ja...  5.78 us
    convert_element_type x1, other arithmetic, on_device(): sign_matrix = signs.reshape(height, breadth).astype(jnp.bfloat16)  3.72 us
    convert_element_type x1, local copies, waits for them, and re-layouts, on_device(): sign_matrix = signs.reshape(height, breadth).astype(jnp.bfloat16)  2.86 us
  transfers between devices with their start and end apart: 14, of which 5 were waited for; matrix products, arithmetic and copies ran while one was open for 12% of the time, Pallas kernels for 0%

profile of v6, /device:TPU:0, one launch (start us, length us, event | category | flops | bytes accessed | tf_op | source)
XLA Modules:
  0.0 78.8 jit_solution(9255289105536234461)
XLA Ops:
  0.0 2.9 %collective-permute-start.1 = (bf16[64,1024]{1,0:T(8,128)(2,1)}, bf16[64,1024]{1,0:T(8,128)(2,1)S(1)}, u32[]{:S(2)}, u32[]{:S(2)}) collective-permute-start(bf16[64,1024]{1,0:T(8,128)(2,1)} %bitcast.10), channel_id=1, source_target_pairs={{0,8},{4,12},{8,0},{12,4},{16,24},{20,28},{24,16},{28,20},{1,9},{5... | collective-permute-start | bytes 393224 | tf_op jit(solution)/shard_map/ppermute | solution.py:17
  2.9 1.5 %collective-permute-start.3 = (bf16[64,1024]{1,0:T(8,128)(2,1)}, bf16[64,1024]{1,0:T(8,128)(2,1)}, u32[]{:S(2)}, u32[]{:S(2)}) collective-permute-start(bf16[64,1024]{1,0:T(8,128)(2,1)} %bitcast.11), channel_id=1, source_target_pairs={{0,16},{4,20},{8,24},{12,28},{16,0},{20,4},{24,8},{28,12},{1,17},{... | collective-permute-start | bytes 393224 | tf_op jit(solution)/shard_map/ppermute | solution.py:17
  4.5 2.7 %collective-permute-done.1.refs_2_ = bf16[64,1024]{1,0:T(8,128)(2,1)S(1)} collective-permute-done((bf16[64,1024]{1,0:T(8,128)(2,1)}, bf16[64,1024]{1,0:T(8,128)(2,1)S(1)}, u32[]{:S(2)}, u32[]{:S(2)}) %collective-permute-start.1) | collective-permute-done | bytes 131104 | tf_op jit(solution)/shard_map/ppermute | solution.py:17
  7.2 3.9 %collective-permute-done.3.refs_4_ = bf16[64,1024]{1,0:T(8,128)(2,1)} collective-permute-done((bf16[64,1024]{1,0:T(8,128)(2,1)}, bf16[64,1024]{1,0:T(8,128)(2,1)}, u32[]{:S(2)}, u32[]{:S(2)}) %collective-permute-start.3) | collective-permute-done | bytes 131104 | tf_op jit(solution)/shard_map/ppermute | solution.py:17
  11.0 0.0 collective-permute-done.5.refs_6_
  11.0 0.5 collective-permute-start.6
  11.5 1.1 %fusion.3.rows_ref = s32[32768]{0:T(1024)S(1)} fusion(s32[32768]{0:T(1024)} %param.7), kind=kLoop, calls=%fused_computation.13 | loop fusion | flops 1277952 | bytes 262144 | tf_op jit(solution)/shard_map/add | solution.py:137
  12.7 3.7 %convert_element_type.5 = bf16[1048576]{0:T(1024)(128)(2,1)} convert(s32[1048576]{0:T(1024)} %param.6) | non-fusion elementwise | flops 1048576 | bytes 6291456 | tf_op jit(solution)/shard_map/convert_element_type | solution.py:135
  16.4 2.9 %convert_element_type.6.signs_ref = bf16[1024,1024]{1,0:T(8,128)(2,1)S(1)} reshape(bf16[1048576]{0:T(1024)(128)(2,1)} %convert_element_type.5) | data formatting | bytes 4194304 | tf_op jit(solution)/shard_map/convert_element_type | solution.py:135
  19.2 1.5 %copy.5 = bf16[1,512,1024]{1,2,0:T(8,128)(2,1)S(1)} copy(bf16[1,512,1024]{2,1,0:T(8,128)(2,1)} %param.4) | data formatting | bytes 2097152 | tf_op args[0]
  20.7 0.0 collective-permute-done.refs_1_
  20.8 0.0 copy-start
  20.8 5.8 %transform.1 = f32[8192,128]{1,0:T(8,128)S(1)} custom-call(bf16[1024,512]{1,0:T(8,128)(2,1)S(1)} %bitcast.8, bf16[1024,1024]{1,0:T(8,128)(2,1)S(1)} %convert_element_type.6.signs_ref, bf16[64,1024]{1,0:T(8,128)(2,1)S(1)} %bitcast.14, bf16[64,1024]{1,0:T(8,128)(2,1)} %collective-permute-done.refs_1_, bf16[64,1024]{1,0:T(8,128)(2,1)S(1)} %collective-permute-done.1.refs_2_, ...), custom_call_target="tpu_custom_call" | custom-call | tf_op jit(solution)/shard_map/transform/pallas_call | solution.py:140
  26.6 42.6 %gather.1 = (f32[32,128]{1,0:T(8,128)S(1)}, f32[32,128]{1,0:T(8,128)S(1)}, f32[32,128]{1,0:T(8,128)S(1)}, f32[32,128]{1,0:T(8,128)S(1)}, f32[32,128]{1,0:T(8,128...) custom-call(f32[8192,1,128]{2,1,0:T(1,128)S(1)} %bitcast.7, ...), custom_call_target="tpu_custom_call" | custom-call | tf_op jit(solution)/shard_map/gather/pallas_call | solution.py:152
  69.2 1.6 %collective-permute-start.10 = (f32[32,128]{1,0:T(8,128)S(1)}, f32[32,128]{1,0:T(8,128)S(1)}, u32[]{:S(2)}, u32[]{:S(2)}) collective-permute-start(f32[32,128]{1,0:T(8,128)S(1)} %get-tuple-element.17), channel_id=1, source_target_pairs={{0,16},{4,20},{8,24},{12,28},{16,0},{20,4},{24,8},{28,12},{1,17},{... | collective-permute-start | bytes 49160 | tf_op jit(solution)/shard_map/ppermute | solution.py:17
  70.8 1.3 %collective-permute-start.12 = (f32[32,128]{1,0:T(8,128)S(1)}, f32[32,128]{1,0:T(8,128)S(1)}, u32[]{:S(2)}, u32[]{:S(2)}) collective-permute-start(f32[32,128]{1,0:T(8,128)S(1)} %get-tuple-element.19), channel_id=1, source_target_pairs={{0,24},{4,28},{8,16},{12,20},{16,8},{20,12},{24,0},{28,4},{1,25},{... | collective-permute-start | bytes 49160 | tf_op jit(solution)/shard_map/ppermute | solution.py:17
  72.1 1.6 %collective-permute-start.13 = (f32[32,128]{1,0:T(8,128)S(1)}, f32[32,128]{1,0:T(8,128)S(1)}, u32[]{:S(2)}, u32[]{:S(2)}) collective-permute-start(f32[32,128]{1,0:T(8,128)S(1)} %get-tuple-element.20), channel_id=1, source_target_pairs={{0,28},{4,24},{8,20},{12,16},{16,12},{20,8},{24,4},{28,0},{1,29},{... | collective-permute-start | bytes 49160 | tf_op jit(solution)/shard_map/ppermute | solution.py:17
  73.7 0.2 collective-permute-start.7
  73.8 1.0 %collective-permute-start.8 = (f32[32,128]{1,0:T(8,128)S(1)}, f32[32,128]{1,0:T(8,128)S(1)}, u32[]{:S(2)}, u32[]{:S(2)}) collective-permute-start(f32[32,128]{1,0:T(8,128)S(1)} %get-tuple-element.15), channel_id=1, source_target_pairs={{0,8},{4,12},{8,0},{12,4},{16,24},{20,28},{24,16},{28,20},{1,9},{5... | collective-permute-start | bytes 49160 | tf_op jit(solution)/shard_map/ppermute | solution.py:17
  74.9 0.6 collective-permute-start.9
  75.5 0.6 collective-permute-done.13
  76.2 1.4 %collective-permute-done.8 = f32[32,128]{1,0:T(8,128)S(1)} collective-permute-done((f32[32,128]{1,0:T(8,128)S(1)}, f32[32,128]{1,0:T(8,128)S(1)}, u32[]{:S(2)}, u32[]{:S(2)}) %collective-permute-start.8) | collective-permute-done | bytes 16416 | tf_op jit(solution)/shard_map/ppermute | solution.py:17
  77.6 0.6 collective-permute-done.9
  78.1 0.6 add_add_fusion
  (15 shorter events, 0.0 us)
Async XLA Ops:
  0.0 7.2 %collective-permute-start.1 = (bf16[64,1024]{1,0:T(8,128)(2,1)}, bf16[64,1024]{1,0:T(8,128)(2,1)S(1)}, u32[]{:S(2)}, u32[]{:S(2)}) collective-permute-start(bf16[64,1024]{1,0:T(8,128)(2,1)} %bitcast.10), channel_id=1, source_target_pairs={{0,8},{4,12},{8,0},{12,4},{16,24},{20,28},{24,16},{28,20},{1,9},{5... | collective-permute-start | bytes 393224 | tf_op jit(solution)/shard_map/ppermute | solution.py:17
  2.9 8.1 %collective-permute-start.3 = (bf16[64,1024]{1,0:T(8,128)(2,1)}, bf16[64,1024]{1,0:T(8,128)(2,1)}, u32[]{:S(2)}, u32[]{:S(2)}) collective-permute-start(bf16[64,1024]{1,0:T(8,128)(2,1)} %bitcast.11), channel_id=1, source_target_pairs={{0,16},{4,20},{8,24},{12,28},{16,0},{20,4},{24,8},{28,12},{1,17},{... | collective-permute-start | bytes 393224 | tf_op jit(solution)/shard_map/ppermute | solution.py:17
  4.5 6.6 %collective-permute-start.5 = (bf16[64,1024]{1,0:T(8,128)(2,1)}, bf16[64,1024]{1,0:T(8,128)(2,1)}, u32[]{:S(2)}, u32[]{:S(2)}) collective-permute-start(bf16[64,1024]{1,0:T(8,128)(2,1)} %bitcast.12), channel_id=1, source_target_pairs={{0,24},{4,28},{8,16},{12,20},{16,8},{20,12},{24,0},{28,4},{1,25},{... | collective-permute-start | bytes 393224 | tf_op jit(solution)/shard_map/ppermute | solution.py:17
  4.5 16.3 %collective-permute-start = (bf16[64,1024]{1,0:T(8,128)(2,1)}, bf16[64,1024]{1,0:T(8,128)(2,1)}, u32[]{:S(2)}, u32[]{:S(2)}) collective-permute-start(bf16[64,1024]{1,0:T(8,128)(2,1)} %bitcast.13), channel_id=1, source_target_pairs={{0,4},{4,0},{8,12},{12,8},{16,20},{20,16},{24,28},{28,24},{1,5},{5... | collective-permute-start | bytes 393224 | tf_op jit(solution)/shard_map/ppermute | solution.py:17
  7.2 13.6 %collective-permute-start.2 = (bf16[64,1024]{1,0:T(8,128)(2,1)S(1)}, bf16[64,1024]{1,0:T(8,128)(2,1)}, u32[]{:S(2)}, u32[]{:S(2)}) collective-permute-start(bf16[64,1024]{1,0:T(8,128)(2,1)S(1)} %collective-permute-done.1.refs_2_), channel_id=1, source_target_pairs={{0,4},{4,0},{8,12},{12,8},{16,20},{20,16},{24,28},{28,24},{1,5},{5... | collective-permute-start | bytes 393224 | tf_op jit(solution)/shard_map/ppermute | solution.py:17
  11.0 9.7 %collective-permute-start.4 = (bf16[64,1024]{1,0:T(8,128)(2,1)}, bf16[64,1024]{1,0:T(8,128)(2,1)}, u32[]{:S(2)}, u32[]{:S(2)}) collective-permute-start(bf16[64,1024]{1,0:T(8,128)(2,1)} %collective-permute-done.3.refs_4_), channel_id=1, source_target_pairs={{0,4},{4,0},{8,12},{12,8},{16,20},{20,16},{24,28},{28,24},{1,5},{5... | collective-permute-start | bytes 393224 | tf_op jit(solution)/shard_map/ppermute | solution.py:17
  11.0 9.7 %collective-permute-start.6 = (bf16[64,1024]{1,0:T(8,128)(2,1)}, bf16[64,1024]{1,0:T(8,128)(2,1)}, u32[]{:S(2)}, u32[]{:S(2)}) collective-permute-start(bf16[64,1024]{1,0:T(8,128)(2,1)} %collective-permute-done.5.refs_6_), channel_id=1, source_target_pairs={{0,4},{4,0},{8,12},{12,8},{16,20},{20,16},{24,28},{28,24},{1,5},{5... | collective-permute-start | bytes 393224 | tf_op jit(solution)/shard_map/ppermute | solution.py:17
  16.4 4.4 %copy-start.1 = (bf16[1,64,1024]{2,1,0:T(8,128)(2,1)S(1)}, bf16[1,64,1024]{2,1,0:T(8,128)(2,1)}, u32[]{:S(2)}) copy-start(bf16[1,64,1024]{2,1,0:T(8,128)(2,1)} %param.5) | copy-start | bytes 393220
  20.8 5.8 %copy-start = (s32[32768]{0:T(1024)S(1)}, s32[32768]{0:T(1024)}, u32[]{:S(2)}) copy-start(s32[32768]{0:T(1024)} %param.7) | copy-start | bytes 393220
  69.2 4.6 %collective-permute-start.10 = (f32[32,128]{1,0:T(8,128)S(1)}, f32[32,128]{1,0:T(8,128)S(1)}, u32[]{:S(2)}, u32[]{:S(2)}) collective-permute-start(f32[32,128]{1,0:T(8,128)S(1)} %get-tuple-element.17), channel_id=1, source_target_pairs={{0,16},{4,20},{8,24},{12,28},{16,0},{20,4},{24,8},{28,12},{1,17},{... | collective-permute-start | bytes 49160 | tf_op jit(solution)/shard_map/ppermute | solution.py:17
  70.8 4.1 %collective-permute-start.11 = (f32[32,128]{1,0:T(8,128)S(1)}, f32[32,128]{1,0:T(8,128)S(1)}, u32[]{:S(2)}, u32[]{:S(2)}) collective-permute-start(f32[32,128]{1,0:T(8,128)S(1)} %get-tuple-element.18), channel_id=1, source_target_pairs={{0,20},{4,16},{8,28},{12,24},{16,4},{20,0},{24,12},{28,8},{1,21},{... | collective-permute-start | bytes 49160 | tf_op jit(solution)/shard_map/ppermute | solution.py:17
  70.8 4.7 %collective-permute-start.12 = (f32[32,128]{1,0:T(8,128)S(1)}, f32[32,128]{1,0:T(8,128)S(1)}, u32[]{:S(2)}, u32[]{:S(2)}) collective-permute-start(f32[32,128]{1,0:T(8,128)S(1)} %get-tuple-element.19), channel_id=1, source_target_pairs={{0,24},{4,28},{8,16},{12,20},{16,8},{20,12},{24,0},{28,4},{1,25},{... | collective-permute-start | bytes 49160 | tf_op jit(solution)/shard_map/ppermute | solution.py:17
  72.1 4.1 %collective-permute-start.13 = (f32[32,128]{1,0:T(8,128)S(1)}, f32[32,128]{1,0:T(8,128)S(1)}, u32[]{:S(2)}, u32[]{:S(2)}) collective-permute-start(f32[32,128]{1,0:T(8,128)S(1)} %get-tuple-element.20), channel_id=1, source_target_pairs={{0,28},{4,24},{8,20},{12,16},{16,12},{20,8},{24,4},{28,0},{1,29},{... | collective-permute-start | bytes 49160 | tf_op jit(solution)/shard_map/ppermute | solution.py:17
  73.7 2.5 %collective-permute-start.7 = (f32[32,128]{1,0:T(8,128)S(1)}, f32[32,128]{1,0:T(8,128)S(1)}, u32[]{:S(2)}, u32[]{:S(2)}) collective-permute-start(f32[32,128]{1,0:T(8,128)S(1)} %get-tuple-element.14), channel_id=1, source_target_pairs={{0,4},{4,0},{8,12},{12,8},{16,20},{20,16},{24,28},{28,24},{1,5},{5... | collective-permute-start | bytes 49160 | tf_op jit(solution)/shard_map/ppermute | solution.py:17
  73.8 3.7 %collective-permute-start.8 = (f32[32,128]{1,0:T(8,128)S(1)}, f32[32,128]{1,0:T(8,128)S(1)}, u32[]{:S(2)}, u32[]{:S(2)}) collective-permute-start(f32[32,128]{1,0:T(8,128)S(1)} %get-tuple-element.15), channel_id=1, source_target_pairs={{0,8},{4,12},{8,0},{12,4},{16,24},{20,28},{24,16},{28,20},{1,9},{5... | collective-permute-start | bytes 49160 | tf_op jit(solution)/shard_map/ppermute | solution.py:17
  74.9 3.2 %collective-permute-start.9 = (f32[32,128]{1,0:T(8,128)S(1)}, f32[32,128]{1,0:T(8,128)S(1)}, u32[]{:S(2)}, u32[]{:S(2)}) collective-permute-start(f32[32,128]{1,0:T(8,128)S(1)} %get-tuple-element.16), channel_id=1, source_target_pairs={{0,12},{4,8},{8,4},{12,0},{16,28},{20,24},{24,20},{28,16},{1,13},{... | collective-permute-start | bytes 49160 | tf_op jit(solution)/shard_map/ppermute | solution.py:17

commit v7 on v3

--- a/solution.py
+++ b/solution.py
@@ -10,6 +10,7 @@
 
 LANES = 128
 SIDE = 256
+SUBLANES = 8
 
 
 def flipped(x, axis, mask):
@@ -95,15 +96,20 @@
         for slot in range(depth):
             group = at * depth + slot
             choose(jnp.maximum(group - 1, 0), picked[slot - 1])
-            for k in range(LANES):
-                picked[slot][k : k + 1, :] = table[rows_ref[group * LANES + k]]
+            for first in range(0, LANES, SUBLANES):
+                at_rows = [rows_ref[group * LANES + first + k] for k in range(SUBLANES)]
+                copies = [table[pl.ds(row, SUBLANES, stride=0), :] for row in at_rows]
+                merged = copies[0]
+                for k in range(1, SUBLANES):
+                    merged = jnp.where(sub_at[:SUBLANES] == k, copies[k], merged)
+                picked[slot][first : first + SUBLANES, :] = merged
         return carry
 
     lax.fori_loop(0, groups // depth, step, 0)
     choose(groups - 1, picked[-1])
 
     share = groups // parties
-    bits = (table.shape[0] * LANES).bit_length() - 1
+    bits = ((table.shape[0] - SUBLANES) * LANES).bit_length() - 1
     for distance in range(parties):
         at = pl.multiple_of((me ^ distance) * share, share)
         owner = index_ref[pl.ds(at, share), :] >> bits
@@ -132,7 +138,7 @@
     table_rows = height * breadth // LANES
     table = pl.pallas_call(
         functools.partial(transform_kernel, parties),
-        out_shape=jax.ShapeDtypeStruct((table_rows, LANES), jnp.float32),
+        out_shape=jax.ShapeDtypeStruct((table_rows + SUBLANES, LANES), jnp.float32),
         in_specs=[vmem] * (2 + parties),
         out_specs=vmem,
         scratch_shapes=[
@@ -151,7 +157,7 @@
         + [pltpu.VMEM((LANES, LANES), jnp.float32)] * 4,
         compiler_params=pltpu.CompilerParams(vmem_limit_bytes=32 * 1024 * 1024),
         name="gather",
-    )(table.reshape(table_rows, 1, LANES), rows, indices.reshape(groups, LANES))
+    )(table, rows, indices.reshape(groups, LANES))
 
     total = outs[0]
     for distance in range(1, parties):

time: 75.4 us -> 70 us (0.928)
  Pallas kernels: 44.8 us -> 39.3 us
    pallas_call x1, Pallas kernels: 39 us -> 33.6 us  [on_device(): pl.pallas_call(functools.partial(gather_kernel, parties, 1.0 / math.sqrt(...]
  transfers between devices with their start and end apart: 14 -> 14, of which waited for: 5 -> 5; matrix products, arithmetic and copies ran while one was open for 12% -> 13% of each run, Pallas kernels for 0% -> 0%
where the time goes in v7:
time: 70 us; the launch traced here: 69.7 us
  Pallas kernels  39.3 us (56%)
  starting transfers between devices  11.3 us (16%)
  waiting for transfers between devices  9.18 us (13%)
  other arithmetic  5.45 us (8%)
  local copies, waits for them, and re-layouts  4.36 us (6%)
    pallas_call x1, Pallas kernels, on_device(): pl.pallas_call(functools.partial(gather_kernel, parties, 1.0 / math.sqrt(...  33.6 us
    ppermute x14, starting transfers between devices, flipped(): lax.ppermute(x, axis, [(i, i ^ mask) for i in range(lax.axis_size(axis))])  11.3 us
    ppermute x14, waiting for transfers between devices, flipped(): lax.ppermute(x, axis, [(i, i ^ mask) for i in range(lax.axis_size(axis))])  9.18 us
    pallas_call x1, Pallas kernels, on_device(): pl.pallas_call(functools.partial(transform_kernel, parties), out_shape=ja...  5.78 us
    convert_element_type x1, other arithmetic, on_device(): sign_matrix = signs.reshape(height, breadth).astype(jnp.bfloat16)  3.72 us
    convert_element_type x1, local copies, waits for them, and re-layouts, on_device(): sign_matrix = signs.reshape(height, breadth).astype(jnp.bfloat16)  2.86 us
    unnamed x5, local copies, waits for them, and re-layouts  1.51 us
  transfers between devices with their start and end apart: 14, of which 5 were waited for; matrix products, arithmetic and copies ran while one was open for 13% of the time, Pallas kernels for 0%

profile of v7, /device:TPU:0, one launch (start us, length us, event | category | flops | bytes accessed | tf_op | source)
XLA Modules:
  0.0 69.7 jit_solution(4381610870511648247)
XLA Ops:
  0.0 2.9 %collective-permute-start.1 = (bf16[64,1024]{1,0:T(8,128)(2,1)}, bf16[64,1024]{1,0:T(8,128)(2,1)S(1)}, u32[]{:S(2)}, u32[]{:S(2)}) collective-permute-start(bf16[64,1024]{1,0:T(8,128)(2,1)} %bitcast.8), channel_id=1, source_target_pairs={{0,8},{4,12},{8,0},{12,4},{16,24},{20,28},{24,16},{28,20},{1,9},{5... | collective-permute-start | bytes 393224 | tf_op jit(solution)/shard_map/ppermute | solution.py:17
  2.9 1.5 %collective-permute-start.3 = (bf16[64,1024]{1,0:T(8,128)(2,1)}, bf16[64,1024]{1,0:T(8,128)(2,1)}, u32[]{:S(2)}, u32[]{:S(2)}) collective-permute-start(bf16[64,1024]{1,0:T(8,128)(2,1)} %bitcast.9), channel_id=1, source_target_pairs={{0,16},{4,20},{8,24},{12,28},{16,0},{20,4},{24,8},{28,12},{1,17},{... | collective-permute-start | bytes 393224 | tf_op jit(solution)/shard_map/ppermute | solution.py:17
  4.5 2.7 %collective-permute-done.1.refs_2_ = bf16[64,1024]{1,0:T(8,128)(2,1)S(1)} collective-permute-done((bf16[64,1024]{1,0:T(8,128)(2,1)}, bf16[64,1024]{1,0:T(8,128)(2,1)S(1)}, u32[]{:S(2)}, u32[]{:S(2)}) %collective-permute-start.1) | collective-permute-done | bytes 131104 | tf_op jit(solution)/shard_map/ppermute | solution.py:17
  7.2 3.9 %collective-permute-done.3.refs_4_ = bf16[64,1024]{1,0:T(8,128)(2,1)} collective-permute-done((bf16[64,1024]{1,0:T(8,128)(2,1)}, bf16[64,1024]{1,0:T(8,128)(2,1)}, u32[]{:S(2)}, u32[]{:S(2)}) %collective-permute-start.3) | collective-permute-done | bytes 131104 | tf_op jit(solution)/shard_map/ppermute | solution.py:17
  11.0 0.0 collective-permute-done.5.refs_6_
  11.0 0.5 collective-permute-start.6
  11.5 1.1 %fusion.3.rows_ref = s32[32768]{0:T(1024)S(1)} fusion(s32[32768]{0:T(1024)} %param.7), kind=kLoop, calls=%fused_computation.13 | loop fusion | flops 1277952 | bytes 262144 | tf_op jit(solution)/shard_map/add | solution.py:136
  12.7 3.7 %convert_element_type.5 = bf16[1048576]{0:T(1024)(128)(2,1)} convert(s32[1048576]{0:T(1024)} %param.6) | non-fusion elementwise | flops 1048576 | bytes 6291456 | tf_op jit(solution)/shard_map/convert_element_type | solution.py:134
  16.4 2.9 %convert_element_type.6.signs_ref = bf16[1024,1024]{1,0:T(8,128)(2,1)S(1)} reshape(bf16[1048576]{0:T(1024)(128)(2,1)} %convert_element_type.5) | data formatting | bytes 4194304 | tf_op jit(solution)/shard_map/convert_element_type | solution.py:134
  19.2 1.5 %copy.5 = bf16[1,512,1024]{1,2,0:T(8,128)(2,1)S(1)} copy(bf16[1,512,1024]{2,1,0:T(8,128)(2,1)} %param.4) | data formatting | bytes 2097152 | tf_op args[0]
  20.7 0.0 collective-permute-done.refs_1_
  20.8 0.0 copy-start
  20.8 5.8 %transform.1.table = f32[8200,128]{1,0:T(8,128)S(1)} custom-call(bf16[1024,512]{1,0:T(8,128)(2,1)S(1)} %bitcast.6, bf16[1024,1024]{1,0:T(8,128)(2,1)S(1)} %convert_element_type.6.signs_ref, bf16[64,1024]{1,0:T(8,128)(2,1)S(1)} %bitcast.12, bf16[64,1024]{1,0:T(8,128)(2,1)} %collective-permute-done.refs_1_, ...), custom_call_target="tpu_custom_call" | custom-call | tf_op jit(solution)/shard_map/transform/pallas_call | solution.py:139
  26.6 33.6 %gather.1 = (f32[32,128]{1,0:T(8,128)S(1)}, f32[32,128]{1,0:T(8,128)S(1)}, f32[32,128]{1,0:T(8,128)S(1)}, f32[32,128]{1,0:T(8,128)S(1)}, f32[32,128]{1,0:T(8,128...) custom-call(f32[8200,128]{1,0:T(8,128)S(1)} %transform.1.table, ...), custom_call_target="tpu_custom_call" | custom-call | tf_op jit(solution)/shard_map/gather/pallas_call | solution.py:151
  60.2 1.6 %collective-permute-start.10 = (f32[32,128]{1,0:T(8,128)S(1)}, f32[32,128]{1,0:T(8,128)S(1)}, u32[]{:S(2)}, u32[]{:S(2)}) collective-permute-start(f32[32,128]{1,0:T(8,128)S(1)} %get-tuple-element.17), channel_id=1, source_target_pairs={{0,16},{4,20},{8,24},{12,28},{16,0},{20,4},{24,8},{28,12},{1,17},{... | collective-permute-start | bytes 49160 | tf_op jit(solution)/shard_map/ppermute | solution.py:17
  61.8 1.3 %collective-permute-start.12 = (f32[32,128]{1,0:T(8,128)S(1)}, f32[32,128]{1,0:T(8,128)S(1)}, u32[]{:S(2)}, u32[]{:S(2)}) collective-permute-start(f32[32,128]{1,0:T(8,128)S(1)} %get-tuple-element.19), channel_id=1, source_target_pairs={{0,24},{4,28},{8,16},{12,20},{16,8},{20,12},{24,0},{28,4},{1,25},{... | collective-permute-start | bytes 49160 | tf_op jit(solution)/shard_map/ppermute | solution.py:17
  63.1 1.6 %collective-permute-start.13 = (f32[32,128]{1,0:T(8,128)S(1)}, f32[32,128]{1,0:T(8,128)S(1)}, u32[]{:S(2)}, u32[]{:S(2)}) collective-permute-start(f32[32,128]{1,0:T(8,128)S(1)} %get-tuple-element.20), channel_id=1, source_target_pairs={{0,28},{4,24},{8,20},{12,16},{16,12},{20,8},{24,4},{28,0},{1,29},{... | collective-permute-start | bytes 49160 | tf_op jit(solution)/shard_map/ppermute | solution.py:17
  64.6 0.2 collective-permute-start.7
  64.8 1.0 %collective-permute-start.8 = (f32[32,128]{1,0:T(8,128)S(1)}, f32[32,128]{1,0:T(8,128)S(1)}, u32[]{:S(2)}, u32[]{:S(2)}) collective-permute-start(f32[32,128]{1,0:T(8,128)S(1)} %get-tuple-element.15), channel_id=1, source_target_pairs={{0,8},{4,12},{8,0},{12,4},{16,24},{20,28},{24,16},{28,20},{1,9},{5... | collective-permute-start | bytes 49160 | tf_op jit(solution)/shard_map/ppermute | solution.py:17
  65.9 0.6 collective-permute-start.9
  66.5 0.6 collective-permute-done.13
  67.1 1.4 %collective-permute-done.8 = f32[32,128]{1,0:T(8,128)S(1)} collective-permute-done((f32[32,128]{1,0:T(8,128)S(1)}, f32[32,128]{1,0:T(8,128)S(1)}, u32[]{:S(2)}, u32[]{:S(2)}) %collective-permute-start.8) | collective-permute-done | bytes 16416 | tf_op jit(solution)/shard_map/ppermute | solution.py:17
  68.5 0.6 collective-permute-done.9
  69.1 0.6 add_add_fusion
  (15 shorter events, 0.0 us)
Async XLA Ops:
  0.0 7.2 %collective-permute-start.1 = (bf16[64,1024]{1,0:T(8,128)(2,1)}, bf16[64,1024]{1,0:T(8,128)(2,1)S(1)}, u32[]{:S(2)}, u32[]{:S(2)}) collective-permute-start(bf16[64,1024]{1,0:T(8,128)(2,1)} %bitcast.8), channel_id=1, source_target_pairs={{0,8},{4,12},{8,0},{12,4},{16,24},{20,28},{24,16},{28,20},{1,9},{5... | collective-permute-start | bytes 393224 | tf_op jit(solution)/shard_map/ppermute | solution.py:17
  2.9 8.1 %collective-permute-start.3 = (bf16[64,1024]{1,0:T(8,128)(2,1)}, bf16[64,1024]{1,0:T(8,128)(2,1)}, u32[]{:S(2)}, u32[]{:S(2)}) collective-permute-start(bf16[64,1024]{1,0:T(8,128)(2,1)} %bitcast.9), channel_id=1, source_target_pairs={{0,16},{4,20},{8,24},{12,28},{16,0},{20,4},{24,8},{28,12},{1,17},{... | collective-permute-start | bytes 393224 | tf_op jit(solution)/shard_map/ppermute | solution.py:17
  4.5 6.6 %collective-permute-start.5 = (bf16[64,1024]{1,0:T(8,128)(2,1)}, bf16[64,1024]{1,0:T(8,128)(2,1)}, u32[]{:S(2)}, u32[]{:S(2)}) collective-permute-start(bf16[64,1024]{1,0:T(8,128)(2,1)} %bitcast.10), channel_id=1, source_target_pairs={{0,24},{4,28},{8,16},{12,20},{16,8},{20,12},{24,0},{28,4},{1,25},{... | collective-permute-start | bytes 393224 | tf_op jit(solution)/shard_map/ppermute | solution.py:17
  4.5 16.3 %collective-permute-start = (bf16[64,1024]{1,0:T(8,128)(2,1)}, bf16[64,1024]{1,0:T(8,128)(2,1)}, u32[]{:S(2)}, u32[]{:S(2)}) collective-permute-start(bf16[64,1024]{1,0:T(8,128)(2,1)} %bitcast.11), channel_id=1, source_target_pairs={{0,4},{4,0},{8,12},{12,8},{16,20},{20,16},{24,28},{28,24},{1,5},{5... | collective-permute-start | bytes 393224 | tf_op jit(solution)/shard_map/ppermute | solution.py:17
  7.2 13.6 %collective-permute-start.2 = (bf16[64,1024]{1,0:T(8,128)(2,1)S(1)}, bf16[64,1024]{1,0:T(8,128)(2,1)}, u32[]{:S(2)}, u32[]{:S(2)}) collective-permute-start(bf16[64,1024]{1,0:T(8,128)(2,1)S(1)} %collective-permute-done.1.refs_2_), channel_id=1, source_target_pairs={{0,4},{4,0},{8,12},{12,8},{16,20},{20,16},{24,28},{28,24},{1,5},{5... | collective-permute-start | bytes 393224 | tf_op jit(solution)/shard_map/ppermute | solution.py:17
  11.0 9.7 %collective-permute-start.4 = (bf16[64,1024]{1,0:T(8,128)(2,1)}, bf16[64,1024]{1,0:T(8,128)(2,1)}, u32[]{:S(2)}, u32[]{:S(2)}) collective-permute-start(bf16[64,1024]{1,0:T(8,128)(2,1)} %collective-permute-done.3.refs_4_), channel_id=1, source_target_pairs={{0,4},{4,0},{8,12},{12,8},{16,20},{20,16},{24,28},{28,24},{1,5},{5... | collective-permute-start | bytes 393224 | tf_op jit(solution)/shard_map/ppermute | solution.py:17
  11.0 9.7 %collective-permute-start.6 = (bf16[64,1024]{1,0:T(8,128)(2,1)}, bf16[64,1024]{1,0:T(8,128)(2,1)}, u32[]{:S(2)}, u32[]{:S(2)}) collective-permute-start(bf16[64,1024]{1,0:T(8,128)(2,1)} %collective-permute-done.5.refs_6_), channel_id=1, source_target_pairs={{0,4},{4,0},{8,12},{12,8},{16,20},{20,16},{24,28},{28,24},{1,5},{5... | collective-permute-start | bytes 393224 | tf_op jit(solution)/shard_map/ppermute | solution.py:17
  16.4 4.4 %copy-start.1 = (bf16[1,64,1024]{2,1,0:T(8,128)(2,1)S(1)}, bf16[1,64,1024]{2,1,0:T(8,128)(2,1)}, u32[]{:S(2)}) copy-start(bf16[1,64,1024]{2,1,0:T(8,128)(2,1)} %param.5) | copy-start | bytes 393220
  20.8 5.8 %copy-start = (s32[32768]{0:T(1024)S(1)}, s32[32768]{0:T(1024)}, u32[]{:S(2)}) copy-start(s32[32768]{0:T(1024)} %param.7) | copy-start | bytes 393220
  60.2 4.6 %collective-permute-start.10 = (f32[32,128]{1,0:T(8,128)S(1)}, f32[32,128]{1,0:T(8,128)S(1)}, u32[]{:S(2)}, u32[]{:S(2)}) collective-permute-start(f32[32,128]{1,0:T(8,128)S(1)} %get-tuple-element.17), channel_id=1, source_target_pairs={{0,16},{4,20},{8,24},{12,28},{16,0},{20,4},{24,8},{28,12},{1,17},{... | collective-permute-start | bytes 49160 | tf_op jit(solution)/shard_map/ppermute | solution.py:17
  61.8 4.1 %collective-permute-start.11 = (f32[32,128]{1,0:T(8,128)S(1)}, f32[32,128]{1,0:T(8,128)S(1)}, u32[]{:S(2)}, u32[]{:S(2)}) collective-permute-start(f32[32,128]{1,0:T(8,128)S(1)} %get-tuple-element.18), channel_id=1, source_target_pairs={{0,20},{4,16},{8,28},{12,24},{16,4},{20,0},{24,12},{28,8},{1,21},{... | collective-permute-start | bytes 49160 | tf_op jit(solution)/shard_map/ppermute | solution.py:17
  61.8 4.7 %collective-permute-start.12 = (f32[32,128]{1,0:T(8,128)S(1)}, f32[32,128]{1,0:T(8,128)S(1)}, u32[]{:S(2)}, u32[]{:S(2)}) collective-permute-start(f32[32,128]{1,0:T(8,128)S(1)} %get-tuple-element.19), channel_id=1, source_target_pairs={{0,24},{4,28},{8,16},{12,20},{16,8},{20,12},{24,0},{28,4},{1,25},{... | collective-permute-start | bytes 49160 | tf_op jit(solution)/shard_map/ppermute | solution.py:17
  63.1 4.1 %collective-permute-start.13 = (f32[32,128]{1,0:T(8,128)S(1)}, f32[32,128]{1,0:T(8,128)S(1)}, u32[]{:S(2)}, u32[]{:S(2)}) collective-permute-start(f32[32,128]{1,0:T(8,128)S(1)} %get-tuple-element.20), channel_id=1, source_target_pairs={{0,28},{4,24},{8,20},{12,16},{16,12},{20,8},{24,4},{28,0},{1,29},{... | collective-permute-start | bytes 49160 | tf_op jit(solution)/shard_map/ppermute | solution.py:17
  64.6 2.5 %collective-permute-start.7 = (f32[32,128]{1,0:T(8,128)S(1)}, f32[32,128]{1,0:T(8,128)S(1)}, u32[]{:S(2)}, u32[]{:S(2)}) collective-permute-start(f32[32,128]{1,0:T(8,128)S(1)} %get-tuple-element.14), channel_id=1, source_target_pairs={{0,4},{4,0},{8,12},{12,8},{16,20},{20,16},{24,28},{28,24},{1,5},{5... | collective-permute-start | bytes 49160 | tf_op jit(solution)/shard_map/ppermute | solution.py:17
  64.8 3.7 %collective-permute-start.8 = (f32[32,128]{1,0:T(8,128)S(1)}, f32[32,128]{1,0:T(8,128)S(1)}, u32[]{:S(2)}, u32[]{:S(2)}) collective-permute-start(f32[32,128]{1,0:T(8,128)S(1)} %get-tuple-element.15), channel_id=1, source_target_pairs={{0,8},{4,12},{8,0},{12,4},{16,24},{20,28},{24,16},{28,20},{1,9},{5... | collective-permute-start | bytes 49160 | tf_op jit(solution)/shard_map/ppermute | solution.py:17
  65.9 3.2 %collective-permute-start.9 = (f32[32,128]{1,0:T(8,128)S(1)}, f32[32,128]{1,0:T(8,128)S(1)}, u32[]{:S(2)}, u32[]{:S(2)}) collective-permute-start(f32[32,128]{1,0:T(8,128)S(1)} %get-tuple-element.16), channel_id=1, source_target_pairs={{0,12},{4,8},{8,4},{12,0},{16,28},{20,24},{24,20},{28,16},{1,13},{... | collective-permute-start | bytes 49160 | tf_op jit(solution)/shard_map/ppermute | solution.py:17

commit v8 on v7

v8 whole, which is shorter than its diff:
```python
import functools
import math

import jax
import jax.numpy as jnp
from jax import lax
from jax.experimental import pallas as pl
from jax.experimental.pallas import tpu as pltpu
from jax.sharding import PartitionSpec as P

LANES = 128
SIDE = 256
SUBLANES = 8
LIMIT = 32 * 1024 * 1024


def flipped(x, axis, mask):
    return lax.ppermute(x, axis, [(i, i ^ mask) for i in range(lax.axis_size(axis))])


def parity(bits, width):
    shift = 1 << (width - 1).bit_length() >> 1
    while shift:
        bits = bits ^ (bits >> shift)
        shift //= 2
    return bits & 1


def butterfly(parts):
    stride = 1
    while stride < len(parts):
        parts = [
            parts[i] + parts[i + stride] if not i & stride else parts[i - stride] - parts[i]
            for i in range(len(parts))
        ]
        stride *= 2
    return parts


def split(x):
    high = x.astype(jnp.bfloat16)
    return high, (x - high.astype(jnp.float32)).astype(jnp.bfloat16)


def dot(left, right):
    return jnp.dot(left, right, preferred_element_type=jnp.float32)


def prepare_kernel(breadth, acts_ref, signs_ref, index_ref, packed_ref, rows_ref):
    spread = breadth // LANES
    rows = packed_ref.shape[0]
    for piece in range(spread):
        part = signs_ref[pl.ds(piece, rows, stride=spread), :]
        packed_ref[:, piece * LANES : (piece + 1) * LANES] = part.astype(jnp.float32).astype(jnp.bfloat16)
    packed_ref[:, breadth:] = acts_ref[...].T
    height = rows * pl.num_programs(0)
    index = index_ref[...]
    at_row = (index // LANES) % spread * height + index // breadth % height
    half = index // (breadth * height) % 2
    rows_ref[...] = half * (spread * height) + at_row


def transform_kernel(parties, own_ref, other_ref, *refs):
    chunk_refs = refs[:parties]
    table, cots, total, change = refs[parties:]
    me = lax.axis_index("param")
    height, breadth = total.shape
    tokens = chunk_refs[0].shape[0]
    for distance in range(parties):
        start = pl.multiple_of((me ^ distance) * tokens, tokens)
        cots[pl.ds(start, tokens), :] = chunk_refs[distance][...]

    row_at = lax.broadcasted_iota(jnp.int32, (SIDE, SIDE), 0)
    col_at = lax.broadcasted_iota(jnp.int32, (SIDE, SIDE), 1)
    hadamard = (1 - 2 * parity(row_at & col_at, 8)).astype(jnp.float32).astype(jnp.bfloat16)

    row_blocks, col_blocks = height // SIDE, breadth // SIDE
    for col in range(col_blocks):
        cols = slice(col * SIDE, (col + 1) * SIDE)
        own, other = [
            dot(ref[:, breadth:], cots[:, cols]) * ref[:, cols].astype(jnp.float32)
            for ref in (own_ref, other_ref)
        ]
        for signed, product in ((total, own + other), (change, own - other)):
            parts = butterfly([product[row * SIDE : (row + 1) * SIDE] for row in range(row_blocks)])
            for row in range(row_blocks):
                signed[row * SIDE : (row + 1) * SIDE, cols] = parts[row]
    for half, signed in enumerate((total, change)):
        for row in range(row_blocks):
            rows = slice(row * SIDE, (row + 1) * SIDE)
            parts = butterfly([signed[rows, col * SIDE : (col + 1) * SIDE] for col in range(col_blocks)])
            for col in range(col_blocks):
                high, low = split(parts[col])
                high, low = split(dot(high, hadamard) + dot(low, hadamard))
                done = dot(hadamard, high) + dot(hadamard, low)
                for piece in range(SIDE // LANES):
                    at = (half * (breadth // LANES) + col * (SIDE // LANES) + piece) * height + row * SIDE
                    table[at : at + SIDE, :] = done[:, piece * LANES : (piece + 1) * LANES]


def gather_kernel(parties, scale, table, rows_ref, index_ref, *refs):
    out_refs = refs[: parties // 2]
    result, *picked = refs[parties // 2 :]
    me = lax.axis_index("param")
    share = index_ref.shape[0] // parties
    groups = share * len(out_refs)
    depth = len(picked)
    sub_at = lax.broadcasted_iota(jnp.int32, (LANES, LANES), 0)

    def place(group):
        return (me ^ (group // share * 2)) * share + group % share

    def choose(group, rows):
        lane = index_ref[pl.ds(place(group), 1), :] & (LANES - 1)
        chosen = jnp.where(sub_at == lane, rows[...].T, 0.0)
        result[pl.ds(group, 1), :] = jnp.sum(chosen, axis=0, keepdims=True)

    def step(at, carry):
        for slot in range(depth):
            group = at * depth + slot
            choose(jnp.maximum(group - 1, 0), picked[slot - 1])
            base = place(group) * LANES
            for first in range(0, LANES, SUBLANES):
                at_rows = [rows_ref[base + first + k] for k in range(SUBLANES)]
                copies = [table[pl.ds(row, SUBLANES, stride=0), :] for row in at_rows]
                merged = copies[0]
                for k in range(1, SUBLANES):
                    merged = jnp.where(sub_at[:SUBLANES] == k, copies[k], merged)
                picked[slot][first : first + SUBLANES, :] = merged
        return carry

    lax.fori_loop(0, groups // depth, step, 0)
    choose(groups - 1, picked[-1])

    bits = ((table.shape[0] - SUBLANES) // 2 * LANES).bit_length() - 1
    for step_at, out_ref in enumerate(out_refs):
        at = pl.multiple_of((me ^ (2 * step_at)) * share, share)
        owner = index_ref[pl.ds(at, share), :] >> bits
        sign = (1 - 2 * parity(owner & me, parties.bit_length() - 1)).astype(jnp.float32)
        out_ref[...] = result[step_at * share : (step_at + 1) * share, :] * (sign * scale)


def on_device(activations, cotangents, signs, indices):
    tokens, height = activations.shape[1:]
    breadth = cotangents.shape[2]
    parties = lax.axis_size("param")
    samples = indices.shape[0]
    groups = samples // LANES
    table_rows = height * breadth // LANES
    vmem = pl.BlockSpec(memory_space=pltpu.VMEM)
    limit = pltpu.CompilerParams(vmem_limit_bytes=LIMIT)

    chunks = {0: cotangents[0]}
    for distance in range(2, parties, 2):
        chunks[distance] = flipped(chunks[0], "param", distance)

    steps = height // LANES
    packed, rows = pl.pallas_call(
        functools.partial(prepare_kernel, breadth),
        grid=(steps,),
        out_shape=[
            jax.ShapeDtypeStruct((height, breadth + tokens), jnp.bfloat16),
            jax.ShapeDtypeStruct((groups, LANES), jnp.int32),
        ],
        in_specs=[
            pl.BlockSpec((tokens, LANES), lambda at: (0, at)),
            pl.BlockSpec((table_rows // steps, LANES), lambda at: (at, 0)),
            pl.BlockSpec((groups // steps, LANES), lambda at: (at, 0)),
        ],
        out_specs=[
            pl.BlockSpec((LANES, breadth + tokens), lambda at: (at, 0)),
            pl.BlockSpec((groups // steps, LANES), lambda at: (at, 0)),
        ],
        compiler_params=limit,
        name="prepare",
    )(activations[0], signs.reshape(table_rows, LANES), indices.reshape(groups, LANES))
    other = flipped(packed, "param", 1)

    for distance in range(0, parties, 2):
        chunks[distance + 1] = flipped(chunks[distance], "param", 1)

    table = pl.pallas_call(
        functools.partial(transform_kernel, parties),
        out_shape=jax.ShapeDtypeStruct((2 * table_rows + SUBLANES, LANES), jnp.float32),
        in_specs=[vmem] * (2 + parties),
        out_specs=vmem,
        scratch_shapes=[
            pltpu.VMEM((tokens, breadth), jnp.bfloat16),
            pltpu.VMEM((height, breadth), jnp.float32),
            pltpu.VMEM((height, breadth), jnp.float32),
        ],
        compiler_params=limit,
        name="transform",
    )(packed, other, *[chunks[d] for d in range(parties)])
    outs = pl.pallas_call(
        functools.partial(gather_kernel, parties, 1.0 / math.sqrt(height * breadth * parties)),
        out_shape=[jax.ShapeDtypeStruct((groups // parties, LANES), jnp.float32)] * (parties // 2),
        in_specs=[vmem, pl.BlockSpec(memory_space=pltpu.SMEM), vmem],
        out_specs=[vmem] * (parties // 2),
        scratch_shapes=[pltpu.VMEM((groups // 2, LANES), jnp.float32)]
        + [pltpu.VMEM((LANES, LANES), jnp.float32)] * 4,
        compiler_params=limit,
        name="gather",
    )(table, rows.reshape(samples), indices.reshape(groups, LANES))

    total = outs[0]
    for step_at in range(1, parties // 2):
        total = total + flipped(outs[step_at], "param", 2 * step_at)
    return total.reshape(1, samples // parties)


def solution(mesh):
    in_specs = (P("ex", None, "param"), P("ex", "param", None), P("param"), P())
    out_specs = P("ex", "param")
    return jax.shard_map(
        on_device, mesh=mesh, in_specs=in_specs, out_specs=out_specs, check_vma=False
    )
```

time: 70 us -> 54 us (0.77)
  Pallas kernels: 39.3 us -> 29.3 us
  other arithmetic: 5.45 us -> 0.61 us
  starting transfers between devices: 11.3 us -> 8.48 us
  waiting for transfers between devices: 9.18 us -> 11 us
    pallas_call x1, Pallas kernels: 33.6 us -> 19.1 us  [on_device(): pl.pallas_call(functools.partial(gather_kernel, parties, 1.0 / math.sqrt(...]
    convert_element_type x1 -> x0, other arithmetic: 3.72 us -> none  [on_device(): sign_matrix = signs.reshape(height, breadth).astype(jnp.bfloat16)]
    convert_element_type x1 -> x0, local copies, waits for them, and re-layouts: 2.86 us -> none  [on_device(): sign_matrix = signs.reshape(height, breadth).astype(jnp.bfloat16)]
    ppermute x14 -> x11, starting transfers between devices: 11.3 us -> 8.48 us  [flipped(): lax.ppermute(x, axis, [(i, i ^ mask) for i in range(lax.axis_size(axis))])]
    unnamed x5 -> x8, local copies, waits for them, and re-layouts: 1.51 us -> 4.32 us
    pallas_call x1, Pallas kernels: 5.78 us -> 8.57 us  [on_device(): pl.pallas_call(functools.partial(transform_kernel, parties), out_shape=ja...]
    ppermute x14 -> x11, waiting for transfers between devices: 9.18 us -> 11 us  [flipped(): lax.ppermute(x, axis, [(i, i ^ mask) for i in range(lax.axis_size(axis))])]
    pallas_call x0 -> x1, Pallas kernels: none -> 1.63 us  [on_device(): pl.pallas_call(functools.partial(prepare_kernel, breadth), grid=(steps,),...]
  transfers between devices with their start and end apart: 14 -> 11, of which waited for: 5 -> 8; matrix products, arithmetic and copies ran while one was open for 13% -> 0% of each run, Pallas kernels for 0% -> 0%
where the time goes in v8:
time: 54 us; the launch traced here: 53.8 us
  Pallas kernels  29.3 us (54%)
  waiting for transfers between devices  11 us (20%)
  starting transfers between devices  8.48 us (16%)
  local copies, waits for them, and re-layouts  4.32 us (8%)
  other arithmetic  0.61 us (1%)
    pallas_call x1, Pallas kernels, on_device(): pl.pallas_call(functools.partial(gather_kernel, parties, 1.0 / math.sqrt(...  19.1 us
    ppermute x11, waiting for transfers between devices, flipped(): lax.ppermute(x, axis, [(i, i ^ mask) for i in range(lax.axis_size(axis))])  11 us
    pallas_call x1, Pallas kernels, on_device(): pl.pallas_call(functools.partial(transform_kernel, parties), out_shape=ja...  8.57 us
    ppermute x11, starting transfers between devices, flipped(): lax.ppermute(x, axis, [(i, i ^ mask) for i in range(lax.axis_size(axis))])  8.48 us
    unnamed x8, local copies, waits for them, and re-layouts  4.32 us
    pallas_call x1, Pallas kernels, on_device(): pl.pallas_call(functools.partial(prepare_kernel, breadth), grid=(steps,),...  1.63 us
  transfers between devices with their start and end apart: 11, of which 8 were waited for; matrix products, arithmetic and copies ran while one was open for 0% of the time, Pallas kernels for 0%

profile of v8, /device:TPU:0, one launch (start us, length us, event | category | flops | bytes accessed | tf_op | source)
XLA Modules:
  0.0 53.8 jit_solution(6851578682728004022)
XLA Ops:
  0.0 2.2 %copy-done = s32[1048576]{0:T(1024)S(1)} copy-done((s32[1048576]{0:T(1024)S(1)}, s32[1048576]{0:T(1024)}, u32[]{:S(2)}) %copy-start) | copy-done | bytes 4194328
  2.2 1.2 %copy-done.1 = bf16[1,512,1024]{2,1,0:T(8,128)(2,1)S(1)} copy-done((bf16[1,512,1024]{2,1,0:T(8,128)(2,1)S(1)}, bf16[1,512,1024]{2,1,0:T(8,128)(2,1)}, u32[]{:S(2)}) %copy-start.1) | copy-done | bytes 1048600
  3.4 0.9 %copy-done.2 = s32[32768]{0:T(1024)S(1)} copy-done((s32[32768]{0:T(1024)S(1)}, s32[32768]{0:T(1024)}, u32[]{:S(2)}) %copy-start.2) | copy-done | bytes 131096
  4.3 1.6 %prepare.1 = (bf16[1024,1536]{1,0:T(8,128)(2,1)S(1)}, s32[256,128]{1,0:T(8,128)S(1)}) custom-call(bf16[512,1024]{1,0:T(8,128)(2,1)S(1)} %bitcast.7, s32[8192,128]{1,0:T(8,128)S(1)} %bitcast.6, s32[256,128]{1,0:T(8,128)S(1)} %bitcast.8), custom_call_target="tpu_custom_call" | custom-call | tf_op jit(solution)/shard_map/prepare/pallas_call | solution.py:158
  6.0 0.5 collective-permute-start
  6.5 3.5 %collective-permute-start.6 = (bf16[64,1024]{1,0:T(8,128)(2,1)S(1)}, bf16[64,1024]{1,0:T(8,128)(2,1)S(1)}, u32[]{:S(2)}, u32[]{:S(2)}) collective-permute-start(bf16[64,1024]{1,0:T(8,128)(2,1)S(1)} %bitcast.10), channel_id=1, source_target_pairs={{0,24},{4,28},{8,16},{12,20},{16,8},{20,12},{24,0},{28,4},{1,25},{... | collective-permute-start | bytes 393224 | tf_op jit(solution)/shard_map/ppermute | solution.py:18
  10.0 0.5 collective-permute-start.4
  10.5 0.1 collective-permute-start.2
  10.7 3.5 %collective-permute-done.6.refs_6_ = bf16[64,1024]{1,0:T(8,128)(2,1)S(1)} collective-permute-done((bf16[64,1024]{1,0:T(8,128)(2,1)S(1)}, bf16[64,1024]{1,0:T(8,128)(2,1)S(1)}, u32[]{:S(2)}, u32[]{:S(2)}) %collective-permute-start.6) | collective-permute-done | bytes 131104 | tf_op jit(solution)/shard_map/ppermute | solution.py:18
  14.2 2.7 %collective-permute-done.4.refs_4_ = bf16[64,1024]{1,0:T(8,128)(2,1)S(1)} collective-permute-done((bf16[64,1024]{1,0:T(8,128)(2,1)S(1)}, bf16[64,1024]{1,0:T(8,128)(2,1)S(1)}, u32[]{:S(2)}, u32[]{:S(2)}) %collective-permute-start.4) | collective-permute-done | bytes 131104 | tf_op jit(solution)/shard_map/ppermute | solution.py:18
  16.9 0.0 collective-permute-start.5
  16.9 0.3 collective-permute-done.2.refs_2_
  17.2 0.2 collective-permute-start.3
  17.4 0.8 %collective-permute-done.5.refs_5_ = bf16[64,1024]{1,0:T(8,128)(2,1)S(1)} collective-permute-done((bf16[64,1024]{1,0:T(8,128)(2,1)S(1)}, bf16[64,1024]{1,0:T(8,128)(2,1)S(1)}, u32[]{:S(2)}, u32[]{:S(2)}) %collective-permute-start.5) | collective-permute-done | bytes 131104 | tf_op jit(solution)/shard_map/ppermute | solution.py:18
  18.2 0.3 collective-permute-done.3.refs_3_
  18.6 8.6 %transform.1.table = f32[16392,128]{1,0:T(8,128)S(1)} custom-call(bf16[1024,1536]{1,0:T(8,128)(2,1)S(1)} %get-tuple-element.11.own_ref, bf16[1024,1536]{1,0:T(8,128)(2,1)S(1)} %collective-permute-done.other_ref, bf16[64,1024]{1,0:T(8,128)(2,1)S(1)} %bitcast.14, bf16[64,1024]{1,0:T(8,128)(2,1)S(1)} %collective-permute-done.1.refs_1_, ...), custom_call_target="tpu_custom_call" | custom-call | tf_op jit(solution)/shard_map/transform/pallas_call | solution.py:182
  27.1 19.1 %gather.1 = (f32[32,128]{1,0:T(8,128)S(1)}, f32[32,128]{1,0:T(8,128)S(1)}, f32[32,128]{1,0:T(8,128)S(1)}, f32[32,128]{1,0:T(8,128)S(1)}) custom-call(f32[16392,128]{1,0:T(8,128)S(1)} %transform.1.table, s32[32768]{0:T(1024)S(1)} %bitcast.15, s32[256,128]{1,0:T(8,128)S(1)} %bitcast.9), custom_call_target="tpu_custom_call" | custom-call | tf_op jit(solution)/shard_map/gather/pallas_call | solution.py:195
  46.3 1.6 %collective-permute-start.8 = (f32[32,128]{1,0:T(8,128)S(1)}, f32[32,128]{1,0:T(8,128)S(1)}, u32[]{:S(2)}, u32[]{:S(2)}) collective-permute-start(f32[32,128]{1,0:T(8,128)S(1)} %get-tuple-element.14), channel_id=1, source_target_pairs={{0,8},{4,12},{8,0},{12,4},{16,24},{20,28},{24,16},{28,20},{1,9},{5... | collective-permute-start | bytes 49160 | tf_op jit(solution)/shard_map/ppermute | solution.py:18
  47.9 0.6 %collective-permute-start.9 = (f32[32,128]{1,0:T(8,128)S(1)}, f32[32,128]{1,0:T(8,128)S(1)}, u32[]{:S(2)}, u32[]{:S(2)}) collective-permute-start(f32[32,128]{1,0:T(8,128)S(1)} %get-tuple-element.15), channel_id=1, source_target_pairs={{0,16},{4,20},{8,24},{12,28},{16,0},{20,4},{24,8},{28,12},{1,17},{... | collective-permute-start | bytes 49160 | tf_op jit(solution)/shard_map/ppermute | solution.py:18
  48.5 1.3 %collective-permute-start.10 = (f32[32,128]{1,0:T(8,128)S(1)}, f32[32,128]{1,0:T(8,128)S(1)}, u32[]{:S(2)}, u32[]{:S(2)}) collective-permute-start(f32[32,128]{1,0:T(8,128)S(1)} %get-tuple-element.16), channel_id=1, source_target_pairs={{0,24},{4,28},{8,16},{12,20},{16,8},{20,12},{24,0},{28,4},{1,25},{... | collective-permute-start | bytes 49160 | tf_op jit(solution)/shard_map/ppermute | solution.py:18
  49.8 0.2 collective-permute-done.8
  50.1 1.6 %collective-permute-done.9 = f32[32,128]{1,0:T(8,128)S(1)} collective-permute-done((f32[32,128]{1,0:T(8,128)S(1)}, f32[32,128]{1,0:T(8,128)S(1)}, u32[]{:S(2)}, u32[]{:S(2)}) %collective-permute-start.9) | collective-permute-done | bytes 16416 | tf_op jit(solution)/shard_map/ppermute | solution.py:18
  51.7 1.5 %collective-permute-done.10 = f32[32,128]{1,0:T(8,128)S(1)} collective-permute-done((f32[32,128]{1,0:T(8,128)S(1)}, f32[32,128]{1,0:T(8,128)S(1)}, u32[]{:S(2)}, u32[]{:S(2)}) %collective-permute-start.10) | collective-permute-done | bytes 16416 | tf_op jit(solution)/shard_map/ppermute | solution.py:18
  53.2 0.6 %add_add_fusion = f32[32,128]{1,0:T(8,128)} fusion(f32[32,128]{1,0:T(8,128)S(1)} %collective-permute-done.10, f32[32,128]{1,0:T(8,128)S(1)} %collective-permute-done.9, f32[32,128]{1,0:T(8,128)S(1)} %get-tuple-element.13, f32[32,128]{1,0:T(8,128)S(1)} %collective-permute-done.8), kind=kLoop, calls=%fused_computation | loop fusion | flops 12288 | bytes 81920 | tf_op jit(solution)/shard_map/add | solution.py:208
  (10 shorter events, 0.0 us)
Async XLA Ops:
  0.0 2.2 %copy-start = (s32[1048576]{0:T(1024)S(1)}, s32[1048576]{0:T(1024)}, u32[]{:S(2)}) copy-start(s32[1048576]{0:T(1024)} %param.6) | copy-start | bytes 12582916
  2.2 1.2 %copy-start.1 = (bf16[1,512,1024]{2,1,0:T(8,128)(2,1)S(1)}, bf16[1,512,1024]{2,1,0:T(8,128)(2,1)}, u32[]{:S(2)}) copy-start(bf16[1,512,1024]{2,1,0:T(8,128)(2,1)} %param.4) | copy-start | bytes 3145732
  3.4 0.9 %copy-start.2 = (s32[32768]{0:T(1024)S(1)}, s32[32768]{0:T(1024)}, u32[]{:S(2)}) copy-start(s32[32768]{0:T(1024)} %param.7) | copy-start | bytes 393220
  4.3 2.2 %copy-start.3 = (bf16[1,64,1024]{2,1,0:T(8,128)(2,1)S(1)}, bf16[1,64,1024]{2,1,0:T(8,128)(2,1)}, u32[]{:S(2)}) copy-start(bf16[1,64,1024]{2,1,0:T(8,128)(2,1)} %param.5) | copy-start | bytes 393220
  6.0 12.6 %collective-permute-start = (bf16[1024,1536]{1,0:T(8,128)(2,1)S(1)}, bf16[1024,1536]{1,0:T(8,128)(2,1)S(1)}, u32[]{:S(2)}, u32[]{:S(2)}) collective-permute-start(bf16[1024,1536]{1,0:T(8,128)(2,1)S(1)} %get-tuple-element.11.own_ref), channel_id=1, source_target_pairs={{0,4},{4,0},{8,12},{12,8},{16,20},{20,16},{24,28},{28,24},{1,5},{5... | collective-permute-start | bytes 9437192 | tf_op jit(solution)/shard_map/ppermute | solution.py:18
  6.5 7.7 %collective-permute-start.6 = (bf16[64,1024]{1,0:T(8,128)(2,1)S(1)}, bf16[64,1024]{1,0:T(8,128)(2,1)S(1)}, u32[]{:S(2)}, u32[]{:S(2)}) collective-permute-start(bf16[64,1024]{1,0:T(8,128)(2,1)S(1)} %bitcast.10), channel_id=1, source_target_pairs={{0,24},{4,28},{8,16},{12,20},{16,8},{20,12},{24,0},{28,4},{1,25},{... | collective-permute-start | bytes 393224 | tf_op jit(solution)/shard_map/ppermute | solution.py:18
  10.0 6.9 %collective-permute-start.4 = (bf16[64,1024]{1,0:T(8,128)(2,1)S(1)}, bf16[64,1024]{1,0:T(8,128)(2,1)S(1)}, u32[]{:S(2)}, u32[]{:S(2)}) collective-permute-start(bf16[64,1024]{1,0:T(8,128)(2,1)S(1)} %bitcast.11), channel_id=1, source_target_pairs={{0,16},{4,20},{8,24},{12,28},{16,0},{20,4},{24,8},{28,12},{1,17},{... | collective-permute-start | bytes 393224 | tf_op jit(solution)/shard_map/ppermute | solution.py:18
  10.5 6.7 %collective-permute-start.2 = (bf16[64,1024]{1,0:T(8,128)(2,1)S(1)}, bf16[64,1024]{1,0:T(8,128)(2,1)S(1)}, u32[]{:S(2)}, u32[]{:S(2)}) collective-permute-start(bf16[64,1024]{1,0:T(8,128)(2,1)S(1)} %bitcast.12), channel_id=1, source_target_pairs={{0,8},{4,12},{8,0},{12,4},{16,24},{20,28},{24,16},{28,20},{1,9},{5... | collective-permute-start | bytes 393224 | tf_op jit(solution)/shard_map/ppermute | solution.py:18
  10.7 6.8 %collective-permute-start.1 = (bf16[64,1024]{1,0:T(8,128)(2,1)S(1)}, bf16[64,1024]{1,0:T(8,128)(2,1)S(1)}, u32[]{:S(2)}, u32[]{:S(2)}) collective-permute-start(bf16[64,1024]{1,0:T(8,128)(2,1)S(1)} %bitcast.13), channel_id=1, source_target_pairs={{0,4},{4,0},{8,12},{12,8},{16,20},{20,16},{24,28},{28,24},{1,5},{5... | collective-permute-start | bytes 393224 | tf_op jit(solution)/shard_map/ppermute | solution.py:18
  14.2 3.2 %collective-permute-start.7 = (bf16[64,1024]{1,0:T(8,128)(2,1)S(1)}, bf16[64,1024]{1,0:T(8,128)(2,1)S(1)}, u32[]{:S(2)}, u32[]{:S(2)}) collective-permute-start(bf16[64,1024]{1,0:T(8,128)(2,1)S(1)} %collective-permute-done.6.refs_6_), channel_id=1, source_target_pairs={{0,4},{4,0},{8,12},{12,8},{16,20},{20,16},{24,28},{28,24},{1,5},{5... | collective-permute-start | bytes 393224 | tf_op jit(solution)/shard_map/ppermute | solution.py:18
  16.9 1.3 %collective-permute-start.5 = (bf16[64,1024]{1,0:T(8,128)(2,1)S(1)}, bf16[64,1024]{1,0:T(8,128)(2,1)S(1)}, u32[]{:S(2)}, u32[]{:S(2)}) collective-permute-start(bf16[64,1024]{1,0:T(8,128)(2,1)S(1)} %collective-permute-done.4.refs_4_), channel_id=1, source_target_pairs={{0,4},{4,0},{8,12},{12,8},{16,20},{20,16},{24,28},{28,24},{1,5},{5... | collective-permute-start | bytes 393224 | tf_op jit(solution)/shard_map/ppermute | solution.py:18
  17.2 1.3 %collective-permute-start.3 = (bf16[64,1024]{1,0:T(8,128)(2,1)S(1)}, bf16[64,1024]{1,0:T(8,128)(2,1)S(1)}, u32[]{:S(2)}, u32[]{:S(2)}) collective-permute-start(bf16[64,1024]{1,0:T(8,128)(2,1)S(1)} %collective-permute-done.2.refs_2_), channel_id=1, source_target_pairs={{0,4},{4,0},{8,12},{12,8},{16,20},{20,16},{24,28},{28,24},{1,5},{5... | collective-permute-start | bytes 393224 | tf_op jit(solution)/shard_map/ppermute | solution.py:18
  46.3 3.8 %collective-permute-start.8 = (f32[32,128]{1,0:T(8,128)S(1)}, f32[32,128]{1,0:T(8,128)S(1)}, u32[]{:S(2)}, u32[]{:S(2)}) collective-permute-start(f32[32,128]{1,0:T(8,128)S(1)} %get-tuple-element.14), channel_id=1, source_target_pairs={{0,8},{4,12},{8,0},{12,4},{16,24},{20,28},{24,16},{28,20},{1,9},{5... | collective-permute-start | bytes 49160 | tf_op jit(solution)/shard_map/ppermute | solution.py:18
  47.9 3.7 %collective-permute-start.9 = (f32[32,128]{1,0:T(8,128)S(1)}, f32[32,128]{1,0:T(8,128)S(1)}, u32[]{:S(2)}, u32[]{:S(2)}) collective-permute-start(f32[32,128]{1,0:T(8,128)S(1)} %get-tuple-element.15), channel_id=1, source_target_pairs={{0,16},{4,20},{8,24},{12,28},{16,0},{20,4},{24,8},{28,12},{1,17},{... | collective-permute-start | bytes 49160 | tf_op jit(solution)/shard_map/ppermute | solution.py:18
  48.5 4.6 %collective-permute-start.10 = (f32[32,128]{1,0:T(8,128)S(1)}, f32[32,128]{1,0:T(8,128)S(1)}, u32[]{:S(2)}, u32[]{:S(2)}) collective-permute-start(f32[32,128]{1,0:T(8,128)S(1)} %get-tuple-element.16), channel_id=1, source_target_pairs={{0,24},{4,28},{8,16},{12,20},{16,8},{20,12},{24,0},{28,4},{1,25},{... | collective-permute-start | bytes 49160 | tf_op jit(solution)/shard_map/ppermute | solution.py:18

commit v9 on v8

v9 whole, which is shorter than its diff:
```python
import functools
import math

import jax
import jax.numpy as jnp
from jax import lax
from jax.experimental import pallas as pl
from jax.experimental.pallas import tpu as pltpu
from jax.sharding import PartitionSpec as P

LANES = 128
LANE_BITS = 7
SIDE = 256
SUBLANES = 8
LIMIT = 40 * 1024 * 1024


def flipped(x, axis, mask):
    return lax.ppermute(x, axis, [(i, i ^ mask) for i in range(lax.axis_size(axis))])


def parity(bits, width):
    shift = 1 << (width - 1).bit_length() >> 1
    while shift:
        bits = bits ^ (bits >> shift)
        shift //= 2
    return bits & 1


def butterfly(parts):
    stride = 1
    while stride < len(parts):
        parts = [
            parts[i] + parts[i + stride] if not i & stride else parts[i - stride] - parts[i]
            for i in range(len(parts))
        ]
        stride *= 2
    return parts


def split(x):
    high = x.astype(jnp.bfloat16)
    return high, (x - high.astype(jnp.float32)).astype(jnp.bfloat16)


def dot(left, right):
    return jnp.dot(left, right, preferred_element_type=jnp.float32)


def prepare_kernel(acts_ref, signs_ref, index_ref, turned_ref, signs_out_ref, rows_ref):
    rows, breadth = signs_out_ref.shape
    spread = breadth // LANES
    for piece in range(spread):
        part = signs_ref[pl.ds(piece, rows, stride=spread), :]
        signs_out_ref[:, piece * LANES : (piece + 1) * LANES] = part.astype(jnp.float32).astype(jnp.bfloat16)
    turned_ref[...] = acts_ref[...].T
    height = rows * pl.num_programs(0)
    index = index_ref[...]
    at_row = ((index >> LANE_BITS) & (spread - 1)) * height + ((index // breadth) & (height - 1))
    half = (index // (breadth * height)) & 1
    rows_ref[...] = half * (spread * height) + at_row


def sketch_kernel(parties, scale, own_turned, own_signs, other_acts, other_signs, index_ref, rows_hbm, *refs):
    outs = parties // 2
    chunk_refs, out_refs, scratch = refs[:parties], refs[parties : parties + outs], refs[parties + outs :]
    table, cots, other_turned, total, change, result, rows_ref, rows_sems, *picked = scratch
    me = lax.axis_index("param")
    height, breadth = total.shape
    spread = breadth // LANES
    tokens = chunk_refs[0].shape[0]
    share = index_ref.shape[0] // parties

    def index_of(out):
        return index_ref[pl.ds(pl.multiple_of((me ^ (2 * out)) * share, share), share), :]

    copies = []
    for out in range(outs):
        source = rows_hbm.at[pl.ds(pl.multiple_of((me ^ (2 * out)) * share, share), share), :]
        target = rows_ref.at[pl.ds(out * share, share), :]
        copies.append(pltpu.make_async_copy(source, target, rows_sems.at[out]))
    for copy in copies:
        copy.start()

    for distance in range(parties):
        start = pl.multiple_of((me ^ distance) * tokens, tokens)
        cots[pl.ds(start, tokens), :] = chunk_refs[distance][...]
    other_turned[...] = other_acts[...].T

    row_at = lax.broadcasted_iota(jnp.int32, (SIDE, SIDE), 0)
    col_at = lax.broadcasted_iota(jnp.int32, (SIDE, SIDE), 1)
    hadamard = (1 - 2 * parity(row_at & col_at, 8)).astype(jnp.float32).astype(jnp.bfloat16)

    row_blocks, col_blocks, pieces = height // SIDE, breadth // SIDE, SIDE // LANES
    for col in range(col_blocks):
        cols = slice(col * SIDE, (col + 1) * SIDE)
        own = dot(own_turned[...], cots[:, cols]) * own_signs[:, cols].astype(jnp.float32)
        strips = [other_signs[pl.ds(col * pieces + piece, height, stride=spread), :] for piece in range(pieces)]
        other = dot(other_turned[...], cots[:, cols]) * jnp.concatenate(strips, axis=1).astype(jnp.float32)
        for signed, product in ((total, own + other), (change, own - other)):
            parts = butterfly([product[row * SIDE : (row + 1) * SIDE] for row in range(row_blocks)])
            for row in range(row_blocks):
                signed[row * SIDE : (row + 1) * SIDE, cols] = parts[row]
    for half, signed in enumerate((total, change)):
        for row in range(row_blocks):
            rows = slice(row * SIDE, (row + 1) * SIDE)
            parts = butterfly([signed[rows, col * SIDE : (col + 1) * SIDE] for col in range(col_blocks)])
            for col in range(col_blocks):
                high, low = split(parts[col])
                high, low = split(dot(high, hadamard) + dot(low, hadamard))
                done = dot(hadamard, high) + dot(hadamard, low)
                for piece in range(pieces):
                    at = (half * spread + col * pieces + piece) * height + row * SIDE
                    table[at : at + SIDE, :] = done[:, piece * LANES : (piece + 1) * LANES]

    for copy in copies:
        copy.wait()
    groups = share * outs
    depth = len(picked)
    sub_at = lax.broadcasted_iota(jnp.int32, (LANES, LANES), 0)

    def choose(group, rows):
        place = (me ^ (group // share * 2)) * share + group % share
        lane = index_ref[pl.ds(place, 1), :] & (LANES - 1)
        chosen = jnp.where(sub_at == lane, rows[...].T, 0.0)
        result[pl.ds(group, 1), :] = jnp.sum(chosen, axis=0, keepdims=True)

    def step(at, carry):
        for slot in range(depth):
            group = at * depth + slot
            choose(jnp.maximum(group - 1, 0), picked[slot - 1])
            for first in range(0, LANES, SUBLANES):
                at_rows = [rows_ref[group, first + k] for k in range(SUBLANES)]
                lines = [table[pl.ds(row, SUBLANES, stride=0), :] for row in at_rows]
                merged = lines[0]
                for k in range(1, SUBLANES):
                    merged = jnp.where(sub_at[:SUBLANES] == k, lines[k], merged)
                picked[slot][first : first + SUBLANES, :] = merged
        return carry

    lax.fori_loop(0, groups // depth, step, 0)
    choose(groups - 1, picked[-1])

    bits = (height * breadth).bit_length() - 1
    for out, out_ref in enumerate(out_refs):
        sign = (1 - 2 * parity((index_of(out) >> bits) & me, parties.bit_length() - 1)).astype(jnp.float32)
        out_ref[...] = result[out * share : (out + 1) * share, :] * (sign * scale)


def on_device(activations, cotangents, signs, indices):
    tokens, height = activations.shape[1:]
    breadth = cotangents.shape[2]
    parties = lax.axis_size("param")
    samples = indices.shape[0]
    groups = samples // LANES
    table_rows = height * breadth // LANES
    outs = parties // 2
    vmem = pl.BlockSpec(memory_space=pltpu.VMEM)

    chunks = {0: cotangents[0]}
    for distance in range(2, parties, 2):
        chunks[distance] = flipped(chunks[0], "param", distance)
    for distance in range(0, parties, 2):
        chunks[distance + 1] = flipped(chunks[distance], "param", 1)
    acts = activations[0]
    sign_rows = signs.reshape(table_rows, LANES)
    index_rows = indices.reshape(groups, LANES)
    other_acts, other_signs = flipped(acts, "param", 1), flipped(sign_rows, "param", 1)

    steps = height // LANES
    turned, sign_matrix, rows = pl.pallas_call(
        prepare_kernel,
        grid=(steps,),
        out_shape=[
            jax.ShapeDtypeStruct((height, tokens), jnp.bfloat16),
            jax.ShapeDtypeStruct((height, breadth), jnp.bfloat16),
            jax.ShapeDtypeStruct((groups, LANES), jnp.int32),
        ],
        in_specs=[
            pl.BlockSpec((tokens, LANES), lambda at: (0, at)),
            pl.BlockSpec((table_rows // steps, LANES), lambda at: (at, 0)),
            pl.BlockSpec((groups // steps, LANES), lambda at: (at, 0)),
        ],
        out_specs=[
            pl.BlockSpec((LANES, tokens), lambda at: (at, 0)),
            pl.BlockSpec((LANES, breadth), lambda at: (at, 0)),
            pl.BlockSpec((groups // steps, LANES), lambda at: (at, 0)),
        ],
        compiler_params=pltpu.CompilerParams(vmem_limit_bytes=LIMIT),
        cost_estimate=pl.CostEstimate(flops=0, bytes_accessed=8 * height * breadth, transcendentals=0),
        name="prepare",
    )(acts, sign_rows, index_rows)

    sums = pl.pallas_call(
        functools.partial(sketch_kernel, parties, 1.0 / math.sqrt(height * breadth * parties)),
        out_shape=[jax.ShapeDtypeStruct((groups // parties, LANES), jnp.float32)] * outs,
        in_specs=[vmem] * 5 + [pl.BlockSpec(memory_space=pl.ANY)] + [vmem] * parties,
        out_specs=[vmem] * outs,
        scratch_shapes=[
            pltpu.VMEM((2 * table_rows + SUBLANES, LANES), jnp.float32),
            pltpu.VMEM((tokens, breadth), jnp.bfloat16),
            pltpu.VMEM((height, tokens), jnp.bfloat16),
            pltpu.VMEM((height, breadth), jnp.float32),
            pltpu.VMEM((height, breadth), jnp.float32),
            pltpu.VMEM((groups // 2, LANES), jnp.float32),
            pltpu.SMEM((groups // 2, LANES), jnp.int32),
            pltpu.SemaphoreType.DMA((outs,)),
        ]
        + [pltpu.VMEM((LANES, LANES), jnp.float32)] * 4,
        compiler_params=pltpu.CompilerParams(vmem_limit_bytes=LIMIT),
        name="sketch",
    )(
        turned,
        sign_matrix,
        other_acts,
        other_signs,
        index_rows,
        rows,
        *[chunks[d] for d in range(parties)],
    )

    total = sums[0]
    for out in range(1, outs):
        total = total + flipped(sums[out], "param", 2 * out)
    return total.reshape(1, samples // parties)


def solution(mesh):
    in_specs = (P("ex", None, "param"), P("ex", "param", None), P("param"), P())
    out_specs = P("ex", "param")
    return jax.shard_map(
        on_device, mesh=mesh, in_specs=in_specs, out_specs=out_specs, check_vma=False
    )
```

time: 54 us -> 50 us (0.926)
  Pallas kernels: 29.3 us -> 25.9 us
  waiting for transfers between devices: 11 us -> 9.86 us
  starting transfers between devices: 8.48 us -> 9.05 us
    pallas_call x3 -> x2, Pallas kernels: 29.3 us -> 25.9 us  [the longest x1 24.4 us: on_device(): pl.pallas_call(functools.partial(sketch_kernel, parties, 1.0 / math.sqrt(...]
    ppermute x11 -> x12, waiting for transfers between devices: 11 us -> 9.86 us  [flipped(): lax.ppermute(x, axis, [(i, i ^ mask) for i in range(lax.axis_size(axis))])]
    ppermute x11 -> x12, starting transfers between devices: 8.48 us -> 9.05 us  [flipped(): lax.ppermute(x, axis, [(i, i ^ mask) for i in range(lax.axis_size(axis))])]
  transfers between devices with their start and end apart: 11 -> 12, of which waited for: 8 -> 6; matrix products, arithmetic and copies ran while one was open for 0% -> 0% of each run, Pallas kernels for 0% -> 3%
where the time goes in v9:
time: 50 us; the launch traced here: 49.8 us
  Pallas kernels  25.9 us (52%)
  waiting for transfers between devices  9.86 us (20%)
  starting transfers between devices  9.05 us (18%)
  local copies, waits for them, and re-layouts  4.32 us (9%)
  other arithmetic  0.61 us (1%)
    pallas_call x1, Pallas kernels, on_device(): pl.pallas_call(functools.partial(sketch_kernel, parties, 1.0 / math.sqrt(...  24.4 us
    ppermute x12, waiting for transfers between devices, flipped(): lax.ppermute(x, axis, [(i, i ^ mask) for i in range(lax.axis_size(axis))])  9.86 us
    ppermute x12, starting transfers between devices, flipped(): lax.ppermute(x, axis, [(i, i ^ mask) for i in range(lax.axis_size(axis))])  9.05 us
    unnamed x8, local copies, waits for them, and re-layouts  4.32 us
    pallas_call x1, Pallas kernels, on_device(): pl.pallas_call(prepare_kernel, grid=(steps,), out_shape=[jax.ShapeDtypeSt...  1.46 us
  transfers between devices with their start and end apart: 12, of which 6 were waited for; matrix products, arithmetic and copies ran while one was open for 0% of the time, Pallas kernels for 3%

profile of v9, /device:TPU:0, one launch (start us, length us, event | category | flops | bytes accessed | tf_op | source)
XLA Modules:
  0.0 49.8 jit_solution(15938100814100306396)
XLA Ops:
  0.0 0.5 collective-permute-start.1
  0.5 0.1 collective-permute-start
  0.5 3.9 %collective-permute-start.7 = (bf16[64,1024]{1,0:T(8,128)(2,1)}, bf16[64,1024]{1,0:T(8,128)(2,1)S(1)}, u32[]{:S(2)}, u32[]{:S(2)}) collective-permute-start(bf16[64,1024]{1,0:T(8,128)(2,1)} %bitcast.11), channel_id=1, source_target_pairs={{0,24},{4,28},{8,16},{12,20},{16,8},{20,12},{24,0},{28,4},{1,25},{... | collective-permute-start | bytes 393224 | tf_op jit(solution)/shard_map/ppermute | solution.py:19
  4.4 0.5 %collective-permute-start.5 = (bf16[64,1024]{1,0:T(8,128)(2,1)}, bf16[64,1024]{1,0:T(8,128)(2,1)S(1)}, u32[]{:S(2)}, u32[]{:S(2)}) collective-permute-start(bf16[64,1024]{1,0:T(8,128)(2,1)} %bitcast.12), channel_id=1, source_target_pairs={{0,16},{4,20},{8,24},{12,28},{16,0},{20,4},{24,8},{28,12},{1,17},{... | collective-permute-start | bytes 393224 | tf_op jit(solution)/shard_map/ppermute | solution.py:19
  4.9 0.1 collective-permute-start.3
  5.0 3.7 %collective-permute-done.7.refs_6_ = bf16[64,1024]{1,0:T(8,128)(2,1)S(1)} collective-permute-done((bf16[64,1024]{1,0:T(8,128)(2,1)}, bf16[64,1024]{1,0:T(8,128)(2,1)S(1)}, u32[]{:S(2)}, u32[]{:S(2)}) %collective-permute-start.7) | collective-permute-done | bytes 131104 | tf_op jit(solution)/shard_map/ppermute | solution.py:19
  8.6 0.0 collective-permute-start.2
  8.6 2.4 %collective-permute-done.5.refs_4_ = bf16[64,1024]{1,0:T(8,128)(2,1)S(1)} collective-permute-done((bf16[64,1024]{1,0:T(8,128)(2,1)}, bf16[64,1024]{1,0:T(8,128)(2,1)S(1)}, u32[]{:S(2)}, u32[]{:S(2)}) %collective-permute-start.5) | collective-permute-done | bytes 131104 | tf_op jit(solution)/shard_map/ppermute | solution.py:19
  11.1 0.0 collective-permute-start.8
  11.1 0.2 collective-permute-done.3.refs_2_
  11.4 0.3 collective-permute-start.6
  11.6 0.3 collective-permute-start.4
  11.9 2.2 %copy-done = s32[1048576]{0:T(1024)S(1)} copy-done((s32[1048576]{0:T(1024)S(1)}, s32[1048576]{0:T(1024)}, u32[]{:S(2)}) %copy-start) | copy-done | bytes 4194328
  14.1 1.2 %copy-done.1 = bf16[1,512,1024]{2,1,0:T(8,128)(2,1)S(1)} copy-done((bf16[1,512,1024]{2,1,0:T(8,128)(2,1)S(1)}, bf16[1,512,1024]{2,1,0:T(8,128)(2,1)}, u32[]{:S(2)}) %copy-start.1) | copy-done | bytes 1048600
  15.3 0.9 %copy-done.2 = s32[32768]{0:T(1024)S(1)} copy-done((s32[32768]{0:T(1024)S(1)}, s32[32768]{0:T(1024)}, u32[]{:S(2)}) %copy-start.2) | copy-done | bytes 131096
  16.2 1.5 %prepare.1 = (bf16[1024,512]{1,0:T(8,128)(2,1)S(1)}, bf16[1024,1024]{1,0:T(8,128)(2,1)S(1)}, s32[256,128]{1,0:T(8,128)S(1)}) custom-call(bf16[512,1024]{1,0:T(8,128)(2,1)S(1)} %bitcast.8, s32[8192,128]{1,0:T(8,128)S(1)} %bitcast.6, s32[256,128]{1,0:T(8,128)S(1)} %bitcast.9), custom_call_target="tpu_custom_call" | custom-call | bytes 8388608 | tf_op jit(solution)/shard_map/prepare/pallas_call | solution.py:171
  17.7 24.4 %sketch.1 = (f32[32,128]{1,0:T(8,128)S(1)}, f32[32,128]{1,0:T(8,128)S(1)}, f32[32,128]{1,0:T(8,128)S(1)}, f32[32,128]{1,0:T(8,128)S(1)}) custom-call(bf16[1024,512]{1,0:T(8,128)(2,1)S(1)} %get-tuple-element.12.own_turned, bf16[1024,1024]{1,0:T(8,128)(2,1)S(1)} %get-tuple-element.13.own_signs, bf16[512,1024]{1,0:T(8,128)(2,1)S(1)} %collective-permute-done.other_acts, ...), custom_call_target="tpu_custom_call" | custom-call | tf_op jit(solution)/shard_map/sketch/pallas_call | solution.py:194
  42.2 1.6 %collective-permute-start.9 = (f32[32,128]{1,0:T(8,128)S(1)}, f32[32,128]{1,0:T(8,128)S(1)}, u32[]{:S(2)}, u32[]{:S(2)}) collective-permute-start(f32[32,128]{1,0:T(8,128)S(1)} %get-tuple-element.16), channel_id=1, source_target_pairs={{0,8},{4,12},{8,0},{12,4},{16,24},{20,28},{24,16},{28,20},{1,9},{5... | collective-permute-start | bytes 49160 | tf_op jit(solution)/shard_map/ppermute | solution.py:19
  43.8 0.8 %collective-permute-start.10 = (f32[32,128]{1,0:T(8,128)S(1)}, f32[32,128]{1,0:T(8,128)S(1)}, u32[]{:S(2)}, u32[]{:S(2)}) collective-permute-start(f32[32,128]{1,0:T(8,128)S(1)} %get-tuple-element.17), channel_id=1, source_target_pairs={{0,16},{4,20},{8,24},{12,28},{16,0},{20,4},{24,8},{28,12},{1,17},{... | collective-permute-start | bytes 49160 | tf_op jit(solution)/shard_map/ppermute | solution.py:19
  44.6 1.1 %collective-permute-start.11 = (f32[32,128]{1,0:T(8,128)S(1)}, f32[32,128]{1,0:T(8,128)S(1)}, u32[]{:S(2)}, u32[]{:S(2)}) collective-permute-start(f32[32,128]{1,0:T(8,128)S(1)} %get-tuple-element.18), channel_id=1, source_target_pairs={{0,24},{4,28},{8,16},{12,20},{16,8},{20,12},{24,0},{28,4},{1,25},{... | collective-permute-start | bytes 49160 | tf_op jit(solution)/shard_map/ppermute | solution.py:19
  45.7 0.2 collective-permute-done.9
  46.0 1.5 %collective-permute-done.10 = f32[32,128]{1,0:T(8,128)S(1)} collective-permute-done((f32[32,128]{1,0:T(8,128)S(1)}, f32[32,128]{1,0:T(8,128)S(1)}, u32[]{:S(2)}, u32[]{:S(2)}) %collective-permute-start.10) | collective-permute-done | bytes 16416 | tf_op jit(solution)/shard_map/ppermute | solution.py:19
  47.5 1.7 %collective-permute-done.11 = f32[32,128]{1,0:T(8,128)S(1)} collective-permute-done((f32[32,128]{1,0:T(8,128)S(1)}, f32[32,128]{1,0:T(8,128)S(1)}, u32[]{:S(2)}, u32[]{:S(2)}) %collective-permute-start.11) | collective-permute-done | bytes 16416 | tf_op jit(solution)/shard_map/ppermute | solution.py:19
  49.2 0.6 %add_add_fusion = f32[32,128]{1,0:T(8,128)} fusion(f32[32,128]{1,0:T(8,128)S(1)} %collective-permute-done.11, f32[32,128]{1,0:T(8,128)S(1)} %collective-permute-done.10, f32[32,128]{1,0:T(8,128)S(1)} %get-tuple-element.15, f32[32,128]{1,0:T(8,128)S(1)} %collective-permute-done.9), kind=kLoop, calls=%fused_computation | loop fusion | flops 12288 | bytes 81920 | tf_op jit(solution)/shard_map/add | solution.py:224
  (11 shorter events, 0.0 us)
Async XLA Ops:
  0.0 17.7 %collective-permute-start.1 = (s32[8192,128]{1,0:T(8,128)}, s32[8192,128]{1,0:T(8,128)S(1)}, u32[]{:S(2)}, u32[]{:S(2)}) collective-permute-start(s32[8192,128]{1,0:T(8,128)} %bitcast.5), channel_id=1, source_target_pairs={{0,4},{4,0},{8,12},{12,8},{16,20},{20,16},{24,28},{28,24},{1,5},{5... | collective-permute-start | bytes 12582920 | tf_op jit(solution)/shard_map/ppermute | solution.py:19
  0.5 17.2 %collective-permute-start = (bf16[512,1024]{1,0:T(8,128)(2,1)}, bf16[512,1024]{1,0:T(8,128)(2,1)S(1)}, u32[]{:S(2)}, u32[]{:S(2)}) collective-permute-start(bf16[512,1024]{1,0:T(8,128)(2,1)} %bitcast.7), channel_id=1, source_target_pairs={{0,4},{4,0},{8,12},{12,8},{16,20},{20,16},{24,28},{28,24},{1,5},{5... | collective-permute-start | bytes 3145736 | tf_op jit(solution)/shard_map/ppermute | solution.py:19
  0.5 8.1 %collective-permute-start.7 = (bf16[64,1024]{1,0:T(8,128)(2,1)}, bf16[64,1024]{1,0:T(8,128)(2,1)S(1)}, u32[]{:S(2)}, u32[]{:S(2)}) collective-permute-start(bf16[64,1024]{1,0:T(8,128)(2,1)} %bitcast.11), channel_id=1, source_target_pairs={{0,24},{4,28},{8,16},{12,20},{16,8},{20,12},{24,0},{28,4},{1,25},{... | collective-permute-start | bytes 393224 | tf_op jit(solution)/shard_map/ppermute | solution.py:19
  4.4 6.7 %collective-permute-start.5 = (bf16[64,1024]{1,0:T(8,128)(2,1)}, bf16[64,1024]{1,0:T(8,128)(2,1)S(1)}, u32[]{:S(2)}, u32[]{:S(2)}) collective-permute-start(bf16[64,1024]{1,0:T(8,128)(2,1)} %bitcast.12), channel_id=1, source_target_pairs={{0,16},{4,20},{8,24},{12,28},{16,0},{20,4},{24,8},{28,12},{1,17},{... | collective-permute-start | bytes 393224 | tf_op jit(solution)/shard_map/ppermute | solution.py:19
  4.9 6.4 %collective-permute-start.3 = (bf16[64,1024]{1,0:T(8,128)(2,1)}, bf16[64,1024]{1,0:T(8,128)(2,1)S(1)}, u32[]{:S(2)}, u32[]{:S(2)}) collective-permute-start(bf16[64,1024]{1,0:T(8,128)(2,1)} %bitcast.13), channel_id=1, source_target_pairs={{0,8},{4,12},{8,0},{12,4},{16,24},{20,28},{24,16},{28,20},{1,9},{5... | collective-permute-start | bytes 393224 | tf_op jit(solution)/shard_map/ppermute | solution.py:19
  8.6 3.0 %collective-permute-start.2 = (bf16[64,1024]{1,0:T(8,128)(2,1)}, bf16[64,1024]{1,0:T(8,128)(2,1)S(1)}, u32[]{:S(2)}, u32[]{:S(2)}) collective-permute-start(bf16[64,1024]{1,0:T(8,128)(2,1)} %bitcast.14), channel_id=1, source_target_pairs={{0,4},{4,0},{8,12},{12,8},{16,20},{20,16},{24,28},{28,24},{1,5},{5... | collective-permute-start | bytes 393224 | tf_op jit(solution)/shard_map/ppermute | solution.py:19
  11.1 6.6 %collective-permute-start.8 = (bf16[64,1024]{1,0:T(8,128)(2,1)S(1)}, bf16[64,1024]{1,0:T(8,128)(2,1)S(1)}, u32[]{:S(2)}, u32[]{:S(2)}) collective-permute-start(bf16[64,1024]{1,0:T(8,128)(2,1)S(1)} %collective-permute-done.7.refs_6_), channel_id=1, source_target_pairs={{0,4},{4,0},{8,12},{12,8},{16,20},{20,16},{24,28},{28,24},{1,5},{5... | collective-permute-start | bytes 393224 | tf_op jit(solution)/shard_map/ppermute | solution.py:19
  11.4 6.3 %collective-permute-start.6 = (bf16[64,1024]{1,0:T(8,128)(2,1)S(1)}, bf16[64,1024]{1,0:T(8,128)(2,1)S(1)}, u32[]{:S(2)}, u32[]{:S(2)}) collective-permute-start(bf16[64,1024]{1,0:T(8,128)(2,1)S(1)} %collective-permute-done.5.refs_4_), channel_id=1, source_target_pairs={{0,4},{4,0},{8,12},{12,8},{16,20},{20,16},{24,28},{28,24},{1,5},{5... | collective-permute-start | bytes 393224 | tf_op jit(solution)/shard_map/ppermute | solution.py:19
  11.6 6.1 %collective-permute-start.4 = (bf16[64,1024]{1,0:T(8,128)(2,1)S(1)}, bf16[64,1024]{1,0:T(8,128)(2,1)S(1)}, u32[]{:S(2)}, u32[]{:S(2)}) collective-permute-start(bf16[64,1024]{1,0:T(8,128)(2,1)S(1)} %collective-permute-done.3.refs_2_), channel_id=1, source_target_pairs={{0,4},{4,0},{8,12},{12,8},{16,20},{20,16},{24,28},{28,24},{1,5},{5... | collective-permute-start | bytes 393224 | tf_op jit(solution)/shard_map/ppermute | solution.py:19
  11.9 2.2 %copy-start = (s32[1048576]{0:T(1024)S(1)}, s32[1048576]{0:T(1024)}, u32[]{:S(2)}) copy-start(s32[1048576]{0:T(1024)} %param.6) | copy-start | bytes 12582916
  14.1 1.2 %copy-start.1 = (bf16[1,512,1024]{2,1,0:T(8,128)(2,1)S(1)}, bf16[1,512,1024]{2,1,0:T(8,128)(2,1)}, u32[]{:S(2)}) copy-start(bf16[1,512,1024]{2,1,0:T(8,128)(2,1)} %param.4) | copy-start | bytes 3145732
  15.3 0.9 %copy-start.2 = (s32[32768]{0:T(1024)S(1)}, s32[32768]{0:T(1024)}, u32[]{:S(2)}) copy-start(s32[32768]{0:T(1024)} %param.7) | copy-start | bytes 393220
  16.2 1.5 %copy-start.3 = (bf16[1,64,1024]{2,1,0:T(8,128)(2,1)S(1)}, bf16[1,64,1024]{2,1,0:T(8,128)(2,1)}, u32[]{:S(2)}) copy-start(bf16[1,64,1024]{2,1,0:T(8,128)(2,1)} %param.5) | copy-start | bytes 393220
  42.2 3.8 %collective-permute-start.9 = (f32[32,128]{1,0:T(8,128)S(1)}, f32[32,128]{1,0:T(8,128)S(1)}, u32[]{:S(2)}, u32[]{:S(2)}) collective-permute-start(f32[32,128]{1,0:T(8,128)S(1)} %get-tuple-element.16), channel_id=1, source_target_pairs={{0,8},{4,12},{8,0},{12,4},{16,24},{20,28},{24,16},{28,20},{1,9},{5... | collective-permute-start | bytes 49160 | tf_op jit(solution)/shard_map/ppermute | solution.py:19
  43.8 3.7 %collective-permute-start.10 = (f32[32,128]{1,0:T(8,128)S(1)}, f32[32,128]{1,0:T(8,128)S(1)}, u32[]{:S(2)}, u32[]{:S(2)}) collective-permute-start(f32[32,128]{1,0:T(8,128)S(1)} %get-tuple-element.17), channel_id=1, source_target_pairs={{0,16},{4,20},{8,24},{12,28},{16,0},{20,4},{24,8},{28,12},{1,17},{... | collective-permute-start | bytes 49160 | tf_op jit(solution)/shard_map/ppermute | solution.py:19
  44.6 4.6 %collective-permute-start.11 = (f32[32,128]{1,0:T(8,128)S(1)}, f32[32,128]{1,0:T(8,128)S(1)}, u32[]{:S(2)}, u32[]{:S(2)}) collective-permute-start(f32[32,128]{1,0:T(8,128)S(1)} %get-tuple-element.18), channel_id=1, source_target_pairs={{0,24},{4,28},{8,16},{12,20},{16,8},{20,12},{24,0},{28,4},{1,25},{... | collective-permute-start | bytes 49160 | tf_op jit(solution)/shard_map/ppermute | solution.py:19

commit v10 on v9

v10 whole, which is shorter than its diff:
```python
import functools
import math

import jax
import jax.numpy as jnp
from jax import lax
from jax.experimental import pallas as pl
from jax.experimental.pallas import tpu as pltpu
from jax.sharding import PartitionSpec as P

LANES = 128
LANE_BITS = 7
SIDE = 256
SUBLANES = 8
LIMIT = 40 * 1024 * 1024


def flipped(x, axis, mask):
    return lax.ppermute(x, axis, [(i, i ^ mask) for i in range(lax.axis_size(axis))])


def parity(bits, width):
    shift = 1 << (width - 1).bit_length() >> 1
    while shift:
        bits = bits ^ (bits >> shift)
        shift //= 2
    return bits & 1


def butterfly(parts):
    stride = 1
    while stride < len(parts):
        parts = [
            parts[i] + parts[i + stride] if not i & stride else parts[i - stride] - parts[i]
            for i in range(len(parts))
        ]
        stride *= 2
    return parts


def split(x):
    high = x.astype(jnp.bfloat16)
    return high, (x - high.astype(jnp.float32)).astype(jnp.bfloat16)


def dot(left, right):
    return jnp.dot(left, right, preferred_element_type=jnp.float32)


def sketch_kernel(parties, scale, index_hbm, own_cots_hbm, own_acts_hbm, own_signs_hbm, other_acts, other_signs, *refs):
    outs = parties // 2
    chunk_refs, out_refs, scratch = refs[: parties - 1], refs[parties - 1 : parties - 1 + outs], refs[parties - 1 + outs :]
    index_ref, own_acts, own_signs, in_sems, *scratch = scratch
    table, cots, turned, total, change, result, rows_vmem, rows_ref, rows_sem, *picked = scratch
    me = lax.axis_index("param")
    height, breadth = total.shape
    spread = breadth // LANES
    tokens = chunk_refs[0].shape[0]
    share = index_ref.shape[0] // parties
    own_start = pl.multiple_of(me * tokens, tokens)
    loads = [
        pltpu.make_async_copy(source, target, in_sems.at[at])
        for at, (source, target) in enumerate(
            (
                (index_hbm, index_ref),
                (own_cots_hbm, cots.at[pl.ds(own_start, tokens), :]),
                (own_acts_hbm, own_acts),
                (own_signs_hbm, own_signs),
            )
        )
    ]
    for load in loads:
        load.start()

    def index_of(out):
        return index_ref[pl.ds(pl.multiple_of((me ^ (2 * out)) * share, share), share), :]

    for distance in range(1, parties):
        start = pl.multiple_of((me ^ distance) * tokens, tokens)
        cots[pl.ds(start, tokens), :] = chunk_refs[distance - 1][...]
    turned[1] = other_acts[...].T

    loads[0].wait()
    for out in range(outs):
        index = index_of(out)
        at_row = ((index >> LANE_BITS) & (spread - 1)) * height + ((index // breadth) & (height - 1))
        half = (index // (breadth * height)) & 1
        rows_vmem[out * share : (out + 1) * share, :] = half * (spread * height) + at_row
    copy = pltpu.make_async_copy(rows_vmem, rows_ref, rows_sem)
    copy.start()

    loads[1].wait()
    loads[2].wait()
    turned[0] = own_acts[...].T
    loads[3].wait()

    row_at = lax.broadcasted_iota(jnp.int32, (SIDE, SIDE), 0)
    col_at = lax.broadcasted_iota(jnp.int32, (SIDE, SIDE), 1)
    hadamard = (1 - 2 * parity(row_at & col_at, 8)).astype(jnp.float32).astype(jnp.bfloat16)

    row_blocks, col_blocks, pieces = height // SIDE, breadth // SIDE, SIDE // LANES
    for col in range(col_blocks):
        cols = slice(col * SIDE, (col + 1) * SIDE)
        products = []
        for side, signs in enumerate((own_signs, other_signs)):
            strips = [signs[pl.ds(col * pieces + piece, height, stride=spread), :] for piece in range(pieces)]
            sign = jnp.concatenate(strips, axis=1).astype(jnp.float32)
            products.append(dot(turned[side], cots[:, cols]) * sign)
        own, other = products
        for signed, product in ((total, own + other), (change, own - other)):
            parts = butterfly([product[row * SIDE : (row + 1) * SIDE] for row in range(row_blocks)])
            for row in range(row_blocks):
                signed[row * SIDE : (row + 1) * SIDE, cols] = parts[row]
    for half, signed in enumerate((total, change)):
        for row in range(row_blocks):
            rows = slice(row * SIDE, (row + 1) * SIDE)
            parts = butterfly([signed[rows, col * SIDE : (col + 1) * SIDE] for col in range(col_blocks)])
            for col in range(col_blocks):
                high, low = split(parts[col])
                high, low = split(dot(high, hadamard) + dot(low, hadamard))
                done = dot(hadamard, high) + dot(hadamard, low)
                for piece in range(pieces):
                    at = (half * spread + col * pieces + piece) * height + row * SIDE
                    table[at : at + SIDE, :] = done[:, piece * LANES : (piece + 1) * LANES]

    copy.wait()
    groups = share * outs
    depth = len(picked)
    sub_at = lax.broadcasted_iota(jnp.int32, (LANES, LANES), 0)

    def choose(group, rows):
        place = (me ^ (group // share * 2)) * share + group % share
        lane = index_ref[pl.ds(place, 1), :] & (LANES - 1)
        chosen = jnp.where(sub_at == lane, rows[...].T, 0.0)
        result[pl.ds(group, 1), :] = jnp.sum(chosen, axis=0, keepdims=True)

    def step(at, carry):
        for slot in range(depth):
            group = at * depth + slot
            choose(jnp.maximum(group - 1, 0), picked[slot - 1])
            for first in range(0, LANES, SUBLANES):
                at_rows = [rows_ref[group, first + k] for k in range(SUBLANES)]
                copies = [table[pl.ds(row, SUBLANES, stride=0), :] for row in at_rows]
                merged = copies[0]
                for k in range(1, SUBLANES):
                    merged = jnp.where(sub_at[:SUBLANES] == k, copies[k], merged)
                picked[slot][first : first + SUBLANES, :] = merged
        return carry

    lax.fori_loop(0, groups // depth, step, 0)
    choose(groups - 1, picked[-1])

    bits = (height * breadth).bit_length() - 1
    for out, out_ref in enumerate(out_refs):
        sign = (1 - 2 * parity((index_of(out) >> bits) & me, parties.bit_length() - 1)).astype(jnp.float32)
        out_ref[...] = result[out * share : (out + 1) * share, :] * (sign * scale)


def on_device(activations, cotangents, signs, indices):
    tokens, height = activations.shape[1:]
    breadth = cotangents.shape[2]
    parties = lax.axis_size("param")
    samples = indices.shape[0]
    groups = samples // LANES
    table_rows = height * breadth // LANES
    outs = parties // 2
    vmem = pl.BlockSpec(memory_space=pltpu.VMEM)

    chunks = {0: cotangents[0]}
    for distance in range(2, parties, 2):
        chunks[distance] = flipped(chunks[0], "param", distance)
    for distance in range(0, parties, 2):
        chunks[distance + 1] = flipped(chunks[distance], "param", 1)
    acts = activations[0]
    sign_rows = signs.reshape(table_rows, LANES)

    sums = pl.pallas_call(
        functools.partial(sketch_kernel, parties, 1.0 / math.sqrt(height * breadth * parties)),
        out_shape=[jax.ShapeDtypeStruct((groups // parties, LANES), jnp.float32)] * outs,
        in_specs=[pl.BlockSpec(memory_space=pltpu.HBM)] * 4 + [vmem] * (1 + parties),
        out_specs=[vmem] * outs,
        scratch_shapes=[
            pltpu.VMEM((groups, LANES), jnp.int32),
            pltpu.VMEM((tokens, height), jnp.bfloat16),
            pltpu.VMEM((table_rows, LANES), jnp.int32),
            pltpu.SemaphoreType.DMA((4,)),
            pltpu.VMEM((2 * table_rows + SUBLANES, LANES), jnp.float32),
            pltpu.VMEM((tokens, breadth), jnp.bfloat16),
            pltpu.VMEM((2, height, tokens), jnp.bfloat16),
            pltpu.VMEM((height, breadth), jnp.float32),
            pltpu.VMEM((height, breadth), jnp.float32),
            pltpu.VMEM((groups // 2, LANES), jnp.float32),
            pltpu.VMEM((groups // 2, LANES), jnp.int32),
            pltpu.SMEM((groups // 2, LANES), jnp.int32),
            pltpu.SemaphoreType.DMA,
        ]
        + [pltpu.VMEM((LANES, LANES), jnp.float32)] * 4,
        compiler_params=pltpu.CompilerParams(vmem_limit_bytes=LIMIT),
        name="sketch",
    )(
        *[
            pltpu.with_memory_space_constraint(x, pltpu.HBM)
            for x in (indices.reshape(groups, LANES), chunks[0], acts, sign_rows)
        ],
        flipped(acts, "param", 1),
        flipped(sign_rows, "param", 1),
        *[chunks[d] for d in range(1, parties)],
    )

    total = sums[0]
    for out in range(1, outs):
        total = total + flipped(sums[out], "param", 2 * out)
    return total.reshape(1, samples // parties)


def solution(mesh):
    in_specs = (P("ex", None, "param"), P("ex", "param", None), P("param"), P())
    out_specs = P("ex", "param")
    return jax.shard_map(
        on_device, mesh=mesh, in_specs=in_specs, out_specs=out_specs, check_vma=False
    )
```

time: 50 us -> 48.1 us (0.962)
  local copies, waits for them, and re-layouts: 4.32 us -> 0 us
  Pallas kernels: 25.9 us -> 27.3 us
  waiting for transfers between devices: 9.86 us -> 11.1 us
    unnamed x8 -> x0, local copies, waits for them, and re-layouts: 4.32 us -> none
    pallas_call x1, Pallas kernels: 24.4 us -> 27.3 us  [on_device(): pl.pallas_call(functools.partial(sketch_kernel, parties, 1.0 / math.sqrt(...]
    pallas_call x1 -> x0, Pallas kernels: 1.46 us -> none  [on_device(): pl.pallas_call(prepare_kernel, grid=(steps,), out_shape=[jax.ShapeDtypeSt...]
    ppermute x12, waiting for transfers between devices: 9.86 us -> 11.1 us  [flipped(): lax.ppermute(x, axis, [(i, i ^ mask) for i in range(lax.axis_size(axis))])]
  transfers between devices with their start and end apart: 12 -> 12, of which waited for: 6 -> 9; matrix products, arithmetic and copies ran while one was open for 0% -> 0% of each run, Pallas kernels for 3% -> 0%
where the time goes in v10:
time: 48.1 us; the launch traced here: 48 us
  Pallas kernels  27.3 us (57%)
  waiting for transfers between devices  11.1 us (23%)
  starting transfers between devices  9.05 us (19%)
  other arithmetic  0.61 us (1%)
    pallas_call x1, Pallas kernels, on_device(): pl.pallas_call(functools.partial(sketch_kernel, parties, 1.0 / math.sqrt(...  27.3 us
    ppermute x12, waiting for transfers between devices, flipped(): lax.ppermute(x, axis, [(i, i ^ mask) for i in range(lax.axis_size(axis))])  11.1 us
    ppermute x12, starting transfers between devices, flipped(): lax.ppermute(x, axis, [(i, i ^ mask) for i in range(lax.axis_size(axis))])  9.05 us
  transfers between devices with their start and end apart: 12, of which 9 were waited for; matrix products, arithmetic and copies ran while one was open for 0% of the time, Pallas kernels for 0%

profile of v10, /device:TPU:0, one launch (start us, length us, event | category | flops | bytes accessed | tf_op | source)
XLA Modules:
  0.0 48.0 jit_solution(17312656258980228296)
XLA Ops:
  0.0 0.5 collective-permute-start.1
  0.5 0.1 collective-permute-start
  0.5 3.9 %collective-permute-start.7 = (bf16[64,1024]{1,0:T(8,128)(2,1)}, bf16[64,1024]{1,0:T(8,128)(2,1)S(1)}, u32[]{:S(2)}, u32[]{:S(2)}) collective-permute-start(bf16[64,1024]{1,0:T(8,128)(2,1)} %bitcast.10), channel_id=1, source_target_pairs={{0,24},{4,28},{8,16},{12,20},{16,8},{20,12},{24,0},{28,4},{1,25},{... | collective-permute-start | bytes 393224 | tf_op jit(solution)/shard_map/ppermute | solution.py:19
  4.4 0.5 %collective-permute-start.5 = (bf16[64,1024]{1,0:T(8,128)(2,1)}, bf16[64,1024]{1,0:T(8,128)(2,1)S(1)}, u32[]{:S(2)}, u32[]{:S(2)}) collective-permute-start(bf16[64,1024]{1,0:T(8,128)(2,1)} %bitcast.11), channel_id=1, source_target_pairs={{0,16},{4,20},{8,24},{12,28},{16,0},{20,4},{24,8},{28,12},{1,17},{... | collective-permute-start | bytes 393224 | tf_op jit(solution)/shard_map/ppermute | solution.py:19
  4.9 0.1 collective-permute-start.3
  5.0 3.7 %collective-permute-done.7.refs_5_ = bf16[64,1024]{1,0:T(8,128)(2,1)S(1)} collective-permute-done((bf16[64,1024]{1,0:T(8,128)(2,1)}, bf16[64,1024]{1,0:T(8,128)(2,1)S(1)}, u32[]{:S(2)}, u32[]{:S(2)}) %collective-permute-start.7) | collective-permute-done | bytes 131104 | tf_op jit(solution)/shard_map/ppermute | solution.py:19
  8.6 2.4 %collective-permute-done.5.refs_3_ = bf16[64,1024]{1,0:T(8,128)(2,1)S(1)} collective-permute-done((bf16[64,1024]{1,0:T(8,128)(2,1)}, bf16[64,1024]{1,0:T(8,128)(2,1)S(1)}, u32[]{:S(2)}, u32[]{:S(2)}) %collective-permute-start.5) | collective-permute-done | bytes 131104 | tf_op jit(solution)/shard_map/ppermute | solution.py:19
  11.1 0.0 collective-permute-start.8
  11.1 0.2 collective-permute-done.3.refs_1_
  11.4 0.3 collective-permute-start.6
  11.6 0.3 collective-permute-start.4
  11.9 0.6 %collective-permute-done.8.refs_6_ = bf16[64,1024]{1,0:T(8,128)(2,1)S(1)} collective-permute-done((bf16[64,1024]{1,0:T(8,128)(2,1)S(1)}, bf16[64,1024]{1,0:T(8,128)(2,1)S(1)}, u32[]{:S(2)}, u32[]{:S(2)}) %collective-permute-start.8) | collective-permute-done | bytes 131104 | tf_op jit(solution)/shard_map/ppermute | solution.py:19
  12.4 0.3 collective-permute-done.6.refs_4_
  12.7 0.3 collective-permute-done.4.refs_2_
  13.0 0.0 collective-permute-done.other_acts
  13.0 0.0 collective-permute-done.1.other_signs
  13.0 27.3 %sketch.1 = (f32[32,128]{1,0:T(8,128)S(1)}, f32[32,128]{1,0:T(8,128)S(1)}, f32[32,128]{1,0:T(8,128)S(1)}, f32[32,128]{1,0:T(8,128)S(1)}) custom-call(s32[256,128]{1,0:T(8,128)} %bitcast.9, bf16[64,1024]{1,0:T(8,128)(2,1)} %bitcast.14, bf16[512,1024]{1,0:T(8,128)(2,1)} %bitcast.8, s32[8192,128]{1,0:T(8,128)} %bitcast.6, ...), custom_call_target="tpu_custom_call" | custom-call | tf_op jit(solution)/shard_map/sketch/pallas_call | solution.py:177
  40.2 1.8 %collective-permute-start.9 = (f32[32,128]{1,0:T(8,128)S(1)}, f32[32,128]{1,0:T(8,128)S(1)}, u32[]{:S(2)}, u32[]{:S(2)}) collective-permute-start(f32[32,128]{1,0:T(8,128)S(1)} %get-tuple-element.10), channel_id=1, source_target_pairs={{0,8},{4,12},{8,0},{12,4},{16,24},{20,28},{24,16},{28,20},{1,9},{5... | collective-permute-start | bytes 49160 | tf_op jit(solution)/shard_map/ppermute | solution.py:19
  42.0 0.8 %collective-permute-start.10 = (f32[32,128]{1,0:T(8,128)S(1)}, f32[32,128]{1,0:T(8,128)S(1)}, u32[]{:S(2)}, u32[]{:S(2)}) collective-permute-start(f32[32,128]{1,0:T(8,128)S(1)} %get-tuple-element.11), channel_id=1, source_target_pairs={{0,16},{4,20},{8,24},{12,28},{16,0},{20,4},{24,8},{28,12},{1,17},{... | collective-permute-start | bytes 49160 | tf_op jit(solution)/shard_map/ppermute | solution.py:19
  42.7 1.0 %collective-permute-start.11 = (f32[32,128]{1,0:T(8,128)S(1)}, f32[32,128]{1,0:T(8,128)S(1)}, u32[]{:S(2)}, u32[]{:S(2)}) collective-permute-start(f32[32,128]{1,0:T(8,128)S(1)} %get-tuple-element.12), channel_id=1, source_target_pairs={{0,24},{4,28},{8,16},{12,20},{16,8},{20,12},{24,0},{28,4},{1,25},{... | collective-permute-start | bytes 49160 | tf_op jit(solution)/shard_map/ppermute | solution.py:19
  43.8 0.2 collective-permute-done.9
  44.0 1.7 %collective-permute-done.10 = f32[32,128]{1,0:T(8,128)S(1)} collective-permute-done((f32[32,128]{1,0:T(8,128)S(1)}, f32[32,128]{1,0:T(8,128)S(1)}, u32[]{:S(2)}, u32[]{:S(2)}) %collective-permute-start.10) | collective-permute-done | bytes 16416 | tf_op jit(solution)/shard_map/ppermute | solution.py:19
  45.7 1.7 %collective-permute-done.11 = f32[32,128]{1,0:T(8,128)S(1)} collective-permute-done((f32[32,128]{1,0:T(8,128)S(1)}, f32[32,128]{1,0:T(8,128)S(1)}, u32[]{:S(2)}, u32[]{:S(2)}) %collective-permute-start.11) | collective-permute-done | bytes 16416 | tf_op jit(solution)/shard_map/ppermute | solution.py:19
  47.4 0.6 %add_add_fusion = f32[32,128]{1,0:T(8,128)} fusion(f32[32,128]{1,0:T(8,128)S(1)} %collective-permute-done.11, f32[32,128]{1,0:T(8,128)S(1)} %collective-permute-done.10, f32[32,128]{1,0:T(8,128)S(1)} %get-tuple-element.9, f32[32,128]{1,0:T(8,128)S(1)} %collective-permute-done.9), kind=kLoop, calls=%fused_computation | loop fusion | flops 12288 | bytes 81920 | tf_op jit(solution)/shard_map/add | solution.py:212
  (2 shorter events, 0.0 us)
Async XLA Ops:
  0.0 13.0 %collective-permute-start.1 = (s32[8192,128]{1,0:T(8,128)}, s32[8192,128]{1,0:T(8,128)S(1)}, u32[]{:S(2)}, u32[]{:S(2)}) collective-permute-start(s32[8192,128]{1,0:T(8,128)} %bitcast.5), channel_id=1, source_target_pairs={{0,4},{4,0},{8,12},{12,8},{16,20},{20,16},{24,28},{28,24},{1,5},{5... | collective-permute-start | bytes 12582920 | tf_op jit(solution)/shard_map/ppermute | solution.py:19
  0.5 12.5 %collective-permute-start = (bf16[512,1024]{1,0:T(8,128)(2,1)}, bf16[512,1024]{1,0:T(8,128)(2,1)S(1)}, u32[]{:S(2)}, u32[]{:S(2)}) collective-permute-start(bf16[512,1024]{1,0:T(8,128)(2,1)} %bitcast.7), channel_id=1, source_target_pairs={{0,4},{4,0},{8,12},{12,8},{16,20},{20,16},{24,28},{28,24},{1,5},{5... | collective-permute-start | bytes 3145736 | tf_op jit(solution)/shard_map/ppermute | solution.py:19
  0.5 8.1 %collective-permute-start.7 = (bf16[64,1024]{1,0:T(8,128)(2,1)}, bf16[64,1024]{1,0:T(8,128)(2,1)S(1)}, u32[]{:S(2)}, u32[]{:S(2)}) collective-permute-start(bf16[64,1024]{1,0:T(8,128)(2,1)} %bitcast.10), channel_id=1, source_target_pairs={{0,24},{4,28},{8,16},{12,20},{16,8},{20,12},{24,0},{28,4},{1,25},{... | collective-permute-start | bytes 393224 | tf_op jit(solution)/shard_map/ppermute | solution.py:19
  4.4 6.7 %collective-permute-start.5 = (bf16[64,1024]{1,0:T(8,128)(2,1)}, bf16[64,1024]{1,0:T(8,128)(2,1)S(1)}, u32[]{:S(2)}, u32[]{:S(2)}) collective-permute-start(bf16[64,1024]{1,0:T(8,128)(2,1)} %bitcast.11), channel_id=1, source_target_pairs={{0,16},{4,20},{8,24},{12,28},{16,0},{20,4},{24,8},{28,12},{1,17},{... | collective-permute-start | bytes 393224 | tf_op jit(solution)/shard_map/ppermute | solution.py:19
  4.9 6.4 %collective-permute-start.3 = (bf16[64,1024]{1,0:T(8,128)(2,1)}, bf16[64,1024]{1,0:T(8,128)(2,1)S(1)}, u32[]{:S(2)}, u32[]{:S(2)}) collective-permute-start(bf16[64,1024]{1,0:T(8,128)(2,1)} %bitcast.12), channel_id=1, source_target_pairs={{0,8},{4,12},{8,0},{12,4},{16,24},{20,28},{24,16},{28,20},{1,9},{5... | collective-permute-start | bytes 393224 | tf_op jit(solution)/shard_map/ppermute | solution.py:19
  8.6 3.0 %collective-permute-start.2 = (bf16[64,1024]{1,0:T(8,128)(2,1)}, bf16[64,1024]{1,0:T(8,128)(2,1)S(1)}, u32[]{:S(2)}, u32[]{:S(2)}) collective-permute-start(bf16[64,1024]{1,0:T(8,128)(2,1)} %bitcast.13), channel_id=1, source_target_pairs={{0,4},{4,0},{8,12},{12,8},{16,20},{20,16},{24,28},{28,24},{1,5},{5... | collective-permute-start | bytes 393224 | tf_op jit(solution)/shard_map/ppermute | solution.py:19
  11.1 1.3 %collective-permute-start.8 = (bf16[64,1024]{1,0:T(8,128)(2,1)S(1)}, bf16[64,1024]{1,0:T(8,128)(2,1)S(1)}, u32[]{:S(2)}, u32[]{:S(2)}) collective-permute-start(bf16[64,1024]{1,0:T(8,128)(2,1)S(1)} %collective-permute-done.7.refs_5_), channel_id=1, source_target_pairs={{0,4},{4,0},{8,12},{12,8},{16,20},{20,16},{24,28},{28,24},{1,5},{5... | collective-permute-start | bytes 393224 | tf_op jit(solution)/shard_map/ppermute | solution.py:19
  11.4 1.3 %collective-permute-start.6 = (bf16[64,1024]{1,0:T(8,128)(2,1)S(1)}, bf16[64,1024]{1,0:T(8,128)(2,1)S(1)}, u32[]{:S(2)}, u32[]{:S(2)}) collective-permute-start(bf16[64,1024]{1,0:T(8,128)(2,1)S(1)} %collective-permute-done.5.refs_3_), channel_id=1, source_target_pairs={{0,4},{4,0},{8,12},{12,8},{16,20},{20,16},{24,28},{28,24},{1,5},{5... | collective-permute-start | bytes 393224 | tf_op jit(solution)/shard_map/ppermute | solution.py:19
  11.6 1.3 %collective-permute-start.4 = (bf16[64,1024]{1,0:T(8,128)(2,1)S(1)}, bf16[64,1024]{1,0:T(8,128)(2,1)S(1)}, u32[]{:S(2)}, u32[]{:S(2)}) collective-permute-start(bf16[64,1024]{1,0:T(8,128)(2,1)S(1)} %collective-permute-done.3.refs_1_), channel_id=1, source_target_pairs={{0,4},{4,0},{8,12},{12,8},{16,20},{20,16},{24,28},{28,24},{1,5},{5... | collective-permute-start | bytes 393224 | tf_op jit(solution)/shard_map/ppermute | solution.py:19
  40.2 3.8 %collective-permute-start.9 = (f32[32,128]{1,0:T(8,128)S(1)}, f32[32,128]{1,0:T(8,128)S(1)}, u32[]{:S(2)}, u32[]{:S(2)}) collective-permute-start(f32[32,128]{1,0:T(8,128)S(1)} %get-tuple-element.10), channel_id=1, source_target_pairs={{0,8},{4,12},{8,0},{12,4},{16,24},{20,28},{24,16},{28,20},{1,9},{5... | collective-permute-start | bytes 49160 | tf_op jit(solution)/shard_map/ppermute | solution.py:19
  42.0 3.7 %collective-permute-start.10 = (f32[32,128]{1,0:T(8,128)S(1)}, f32[32,128]{1,0:T(8,128)S(1)}, u32[]{:S(2)}, u32[]{:S(2)}) collective-permute-start(f32[32,128]{1,0:T(8,128)S(1)} %get-tuple-element.11), channel_id=1, source_target_pairs={{0,16},{4,20},{8,24},{12,28},{16,0},{20,4},{24,8},{28,12},{1,17},{... | collective-permute-start | bytes 49160 | tf_op jit(solution)/shard_map/ppermute | solution.py:19
  42.7 4.6 %collective-permute-start.11 = (f32[32,128]{1,0:T(8,128)S(1)}, f32[32,128]{1,0:T(8,128)S(1)}, u32[]{:S(2)}, u32[]{:S(2)}) collective-permute-start(f32[32,128]{1,0:T(8,128)S(1)} %get-tuple-element.12), channel_id=1, source_target_pairs={{0,24},{4,28},{8,16},{12,20},{16,8},{20,12},{24,0},{28,4},{1,25},{... | collective-permute-start | bytes 49160 | tf_op jit(solution)/shard_map/ppermute | solution.py:19

commit v11 on v9

--- a/solution.py
+++ b/solution.py
@@ -47,13 +47,14 @@
     return jnp.dot(left, right, preferred_element_type=jnp.float32)
 
 
-def prepare_kernel(acts_ref, signs_ref, index_ref, turned_ref, signs_out_ref, rows_ref):
+def prepare_kernel(acts_ref, signs_ref, index_ref, cots_ref, turned_ref, signs_out_ref, rows_ref, cots_out_ref):
     rows, breadth = signs_out_ref.shape
     spread = breadth // LANES
     for piece in range(spread):
         part = signs_ref[pl.ds(piece, rows, stride=spread), :]
         signs_out_ref[:, piece * LANES : (piece + 1) * LANES] = part.astype(jnp.float32).astype(jnp.bfloat16)
     turned_ref[...] = acts_ref[...].T
+    cots_out_ref[...] = cots_ref[...]
     height = rows * pl.num_programs(0)
     index = index_ref[...]
     at_row = ((index >> LANE_BITS) & (spread - 1)) * height + ((index // breadth) & (height - 1))
@@ -63,7 +64,7 @@
 
 def sketch_kernel(parties, scale, own_turned, own_signs, other_acts, other_signs, index_ref, rows_hbm, *refs):
     outs = parties // 2
-    chunk_refs, out_refs, scratch = refs[:parties], refs[parties : parties + outs], refs[parties + outs :]
+    chunk_refs, out_ref, scratch = refs[:parties], refs[parties], refs[parties + 1 :]
     table, cots, other_turned, total, change, result, rows_ref, rows_sems, *picked = scratch
     me = lax.axis_index("param")
     height, breadth = total.shape
@@ -71,12 +72,12 @@
     tokens = chunk_refs[0].shape[0]
     share = index_ref.shape[0] // parties
 
-    def index_of(out):
-        return index_ref[pl.ds(pl.multiple_of((me ^ (2 * out)) * share, share), share), :]
+    def start_of(out):
+        return pl.multiple_of((2 * out + (me & 1)) * share, share)
 
     copies = []
     for out in range(outs):
-        source = rows_hbm.at[pl.ds(pl.multiple_of((me ^ (2 * out)) * share, share), share), :]
+        source = rows_hbm.at[pl.ds(start_of(out), share), :]
         target = rows_ref.at[pl.ds(out * share, share), :]
         copies.append(pltpu.make_async_copy(source, target, rows_sems.at[out]))
     for copy in copies:
@@ -117,11 +118,11 @@
         copy.wait()
     groups = share * outs
     depth = len(picked)
+    singles = table.reshape(table.shape[0], 1, LANES)
     sub_at = lax.broadcasted_iota(jnp.int32, (LANES, LANES), 0)
 
     def choose(group, rows):
-        place = (me ^ (group // share * 2)) * share + group % share
-        lane = index_ref[pl.ds(place, 1), :] & (LANES - 1)
+        lane = index_ref[pl.ds(start_of(group // share) + group % share, 1), :] & (LANES - 1)
         chosen = jnp.where(sub_at == lane, rows[...].T, 0.0)
         result[pl.ds(group, 1), :] = jnp.sum(chosen, axis=0, keepdims=True)
 
@@ -131,7 +132,7 @@
             choose(jnp.maximum(group - 1, 0), picked[slot - 1])
             for first in range(0, LANES, SUBLANES):
                 at_rows = [rows_ref[group, first + k] for k in range(SUBLANES)]
-                lines = [table[pl.ds(row, SUBLANES, stride=0), :] for row in at_rows]
+                lines = [jnp.broadcast_to(singles[row], (SUBLANES, LANES)) for row in at_rows]
                 merged = lines[0]
                 for k in range(1, SUBLANES):
                     merged = jnp.where(sub_at[:SUBLANES] == k, lines[k], merged)
@@ -142,9 +143,10 @@
     choose(groups - 1, picked[-1])
 
     bits = (height * breadth).bit_length() - 1
-    for out, out_ref in enumerate(out_refs):
-        sign = (1 - 2 * parity((index_of(out) >> bits) & me, parties.bit_length() - 1)).astype(jnp.float32)
-        out_ref[...] = result[out * share : (out + 1) * share, :] * (sign * scale)
+    for out in range(outs):
+        owner = index_ref[pl.ds(start_of(out), share), :] >> bits
+        sign = (1 - 2 * parity(owner & me, parties.bit_length() - 1)).astype(jnp.float32)
+        out_ref[out] = result[out * share : (out + 1) * share, :] * (sign * scale)
 
 
 def on_device(activations, cotangents, signs, indices):
@@ -160,42 +162,45 @@
     chunks = {0: cotangents[0]}
     for distance in range(2, parties, 2):
         chunks[distance] = flipped(chunks[0], "param", distance)
-    for distance in range(0, parties, 2):
-        chunks[distance + 1] = flipped(chunks[distance], "param", 1)
     acts = activations[0]
     sign_rows = signs.reshape(table_rows, LANES)
     index_rows = indices.reshape(groups, LANES)
     other_acts, other_signs = flipped(acts, "param", 1), flipped(sign_rows, "param", 1)
 
     steps = height // LANES
-    turned, sign_matrix, rows = pl.pallas_call(
+    turned, sign_matrix, rows, chunks[0] = pl.pallas_call(
         prepare_kernel,
         grid=(steps,),
         out_shape=[
             jax.ShapeDtypeStruct((height, tokens), jnp.bfloat16),
             jax.ShapeDtypeStruct((height, breadth), jnp.bfloat16),
             jax.ShapeDtypeStruct((groups, LANES), jnp.int32),
+            jax.ShapeDtypeStruct(chunks[0].shape, jnp.bfloat16),
         ],
         in_specs=[
             pl.BlockSpec((tokens, LANES), lambda at: (0, at)),
             pl.BlockSpec((table_rows // steps, LANES), lambda at: (at, 0)),
             pl.BlockSpec((groups // steps, LANES), lambda at: (at, 0)),
+            pl.BlockSpec((chunks[0].shape[0], breadth // steps), lambda at: (0, at)),
         ],
         out_specs=[
             pl.BlockSpec((LANES, tokens), lambda at: (at, 0)),
             pl.BlockSpec((LANES, breadth), lambda at: (at, 0)),
             pl.BlockSpec((groups // steps, LANES), lambda at: (at, 0)),
+            pl.BlockSpec((chunks[0].shape[0], breadth // steps), lambda at: (0, at)),
         ],
         compiler_params=pltpu.CompilerParams(vmem_limit_bytes=LIMIT),
         cost_estimate=pl.CostEstimate(flops=0, bytes_accessed=8 * height * breadth, transcendentals=0),
         name="prepare",
-    )(acts, sign_rows, index_rows)
+    )(*[pltpu.with_memory_space_constraint(x, pltpu.HBM) for x in (acts, sign_rows, index_rows, chunks[0])])
+    for distance in range(0, parties, 2):
+        chunks[distance + 1] = flipped(chunks[distance], "param", 1)
 
     sums = pl.pallas_call(
         functools.partial(sketch_kernel, parties, 1.0 / math.sqrt(height * breadth * parties)),
-        out_shape=[jax.ShapeDtypeStruct((groups // parties, LANES), jnp.float32)] * outs,
+        out_shape=jax.ShapeDtypeStruct((outs, groups // parties, LANES), jnp.float32),
         in_specs=[vmem] * 5 + [pl.BlockSpec(memory_space=pl.ANY)] + [vmem] * parties,
-        out_specs=[vmem] * outs,
+        out_specs=vmem,
         scratch_shapes=[
             pltpu.VMEM((2 * table_rows + SUBLANES, LANES), jnp.float32),
             pltpu.VMEM((tokens, breadth), jnp.bfloat16),
@@ -219,10 +224,9 @@
         *[chunks[d] for d in range(parties)],
     )
 
-    total = sums[0]
-    for out in range(1, outs):
-        total = total + flipped(sums[out], "param", 2 * out)
-    return total.reshape(1, samples // parties)
+    same_core = [list(range(core, parties, 2)) for core in range(2)]
+    terms = lax.all_to_all(sums, "param", 0, 0, axis_index_groups=same_core)
+    return jnp.sum(terms, axis=0).reshape(1, samples // parties)
 
 
 def solution(mesh):

time: 50 us -> 47.1 us (0.942)
  blocking collectives: 0 us -> 8.81 us
  waiting for transfers between devices: 9.86 us -> 2.19 us
  local copies, waits for them, and re-layouts: 4.32 us -> 0.01 us
  Pallas kernels: 25.9 us -> 29.7 us
  starting transfers between devices: 9.05 us -> 5.57 us
    all_to_all x0 -> x1, blocking collectives: none -> 8.81 us  [on_device(): terms = lax.all_to_all(sums, 'param', 0, 0, axis_index_groups=same_core)]
    ppermute x12 -> x9, waiting for transfers between devices: 9.86 us -> 2.19 us  [flipped(): lax.ppermute(x, axis, [(i, i ^ mask) for i in range(lax.axis_size(axis))])]
    unnamed x8 -> x2, local copies, waits for them, and re-layouts: 4.32 us -> 0.01 us
    pallas_call x1, Pallas kernels: 1.46 us -> 5.23 us  [on_device(): pl.pallas_call(prepare_kernel, grid=(steps,), out_shape=[jax.ShapeDtypeSt...]
    ppermute x12 -> x9, starting transfers between devices: 9.05 us -> 5.57 us  [flipped(): lax.ppermute(x, axis, [(i, i ^ mask) for i in range(lax.axis_size(axis))])]
    add x1 -> x0, other arithmetic: 0.61 us -> none  [on_device(): total = total + flipped(sums[out], 'param', 2 * out)]
    reduce_sum x0 -> x1, other arithmetic: none -> 0.61 us  [on_device(): return jnp.sum(terms, axis=0).reshape(1, samples // parties)]
  transfers between devices with their start and end apart: 12 -> 9, of which waited for: 6 -> 5; matrix products, arithmetic and copies ran while one was open for 0% -> 0% of each run, Pallas kernels for 3% -> 11%
where the time goes in v11:
time: 47.1 us; the launch traced here: 46.9 us
  Pallas kernels  29.7 us (63%)
  blocking collectives  8.81 us (19%)
  starting transfers between devices  5.57 us (12%)
  waiting for transfers between devices  2.19 us (5%)
  other arithmetic  0.61 us (1%)
    pallas_call x1, Pallas kernels, on_device(): pl.pallas_call(functools.partial(sketch_kernel, parties, 1.0 / math.sqrt(...  24.4 us
    all_to_all x1, blocking collectives, on_device(): terms = lax.all_to_all(sums, 'param', 0, 0, axis_index_groups=same_core)  8.81 us
    ppermute x9, starting transfers between devices, flipped(): lax.ppermute(x, axis, [(i, i ^ mask) for i in range(lax.axis_size(axis))])  5.57 us
    pallas_call x1, Pallas kernels, on_device(): pl.pallas_call(prepare_kernel, grid=(steps,), out_shape=[jax.ShapeDtypeSt...  5.23 us
    ppermute x9, waiting for transfers between devices, flipped(): lax.ppermute(x, axis, [(i, i ^ mask) for i in range(lax.axis_size(axis))])  2.19 us
  transfers between devices with their start and end apart: 9, of which 5 were waited for; matrix products, arithmetic and copies ran while one was open for 0% of the time, Pallas kernels for 11%

profile of v11, /device:TPU:0, one launch (start us, length us, event | category | flops | bytes accessed | tf_op | source)
XLA Modules:
  0.0 46.9 jit_solution(2483284399002733030)
XLA Ops:
  0.0 0.0 copy-start
  0.0 0.5 collective-permute-start.1
  0.5 0.1 collective-permute-start
  0.5 3.9 %collective-permute-start.7 = (bf16[64,1024]{1,0:T(8,128)(2,1)}, bf16[64,1024]{1,0:T(8,128)(2,1)S(1)}, u32[]{:S(2)}, u32[]{:S(2)}) collective-permute-start(bf16[64,1024]{1,0:T(8,128)(2,1)} %bitcast.11), channel_id=1, source_target_pairs={{0,24},{4,28},{8,16},{12,20},{16,8},{20,12},{24,0},{28,4},{1,25},{... | collective-permute-start | bytes 393224 | tf_op jit(solution)/shard_map/ppermute | solution.py:19
  4.4 0.5 %collective-permute-start.5 = (bf16[64,1024]{1,0:T(8,128)(2,1)}, bf16[64,1024]{1,0:T(8,128)(2,1)S(1)}, u32[]{:S(2)}, u32[]{:S(2)}) collective-permute-start(bf16[64,1024]{1,0:T(8,128)(2,1)} %bitcast.12), channel_id=1, source_target_pairs={{0,16},{4,20},{8,24},{12,28},{16,0},{20,4},{24,8},{28,12},{1,17},{... | collective-permute-start | bytes 393224 | tf_op jit(solution)/shard_map/ppermute | solution.py:19
  4.9 0.1 collective-permute-start.3
  5.0 5.2 %prepare.1 = (bf16[1024,512]{1,0:T(8,128)(2,1)S(1)}, bf16[1024,1024]{1,0:T(8,128)(2,1)S(1)}, s32[256,128]{1,0:T(8,128)S(1)}, bf16[64,1024]{1,0:T(8,128)(2,1)S(1)}) custom-call(bf16[512,1024]{1,0:T(8,128)(2,1)} %bitcast.10, s32[8192,128]{1,0:T(8,128)} %bitcast.8, s32[256,128]{1,0:T(8,128)} %bitcast.5, bf16[64,1024]{1,0:T(8,128)(2,1)} %bitcast.14), custom_call_target="tpu_custom_call" | custom-call | bytes 8388608 | tf_op jit(solution)/shard_map/prepare/pallas_call | solution.py:171
  10.2 0.0 collective-permute-done.7.refs_6_
  10.2 0.1 collective-permute-start.2
  10.3 0.8 %collective-permute-done.5.refs_4_ = bf16[64,1024]{1,0:T(8,128)(2,1)S(1)} collective-permute-done((bf16[64,1024]{1,0:T(8,128)(2,1)}, bf16[64,1024]{1,0:T(8,128)(2,1)S(1)}, u32[]{:S(2)}, u32[]{:S(2)}) %collective-permute-start.5) | collective-permute-done | bytes 131104 | tf_op jit(solution)/shard_map/ppermute | solution.py:19
  11.2 0.0 collective-permute-start.8
  11.2 0.3 collective-permute-done.3.refs_2_
  11.4 0.2 collective-permute-start.6
  11.7 0.0 collective-permute-done.2.refs_1_
  11.7 0.3 collective-permute-start.4
  11.9 0.6 %collective-permute-done.8.refs_7_ = bf16[64,1024]{1,0:T(8,128)(2,1)S(1)} collective-permute-done((bf16[64,1024]{1,0:T(8,128)(2,1)S(1)}, bf16[64,1024]{1,0:T(8,128)(2,1)S(1)}, u32[]{:S(2)}, u32[]{:S(2)}) %collective-permute-start.8) | collective-permute-done | bytes 131104 | tf_op jit(solution)/shard_map/ppermute | solution.py:19
  12.5 0.3 collective-permute-done.6.refs_5_
  12.8 0.2 collective-permute-done.4.refs_3_
  13.0 0.0 collective-permute-done.other_acts
  13.0 0.0 collective-permute-done.1.other_signs
  13.0 0.0 copy-done
  13.0 24.4 %sketch.1 = f32[4,32,128]{2,1,0:T(8,128)S(1)} custom-call(bf16[1024,512]{1,0:T(8,128)(2,1)S(1)} %get-tuple-element.9.own_turned, bf16[1024,1024]{1,0:T(8,128)(2,1)S(1)} %get-tuple-element.10.own_signs, bf16[512,1024]{1,0:T(8,128)(2,1)S(1)} %collective-permute-done.other_acts, s32[8192,128]{1,0:T(8,128)S(1)} %collective-permute-done.1.other_signs, ...), custom_call_target="tpu_custom_call" | custom-call | tf_op jit(solution)/shard_map/sketch/pallas_call | solution.py:199
  37.5 8.8 %all_to_all.5 = f32[4,32,128]{2,1,0:T(8,128)S(1)} all-to-all(f32[4,32,128]{2,1,0:T(8,128)S(1)} %sketch.1), channel_id=1, replica_groups={{0,8,16,24},{4,12,20,28},{1,9,17,25},{5,13,21,29},{2,10,18,26},{6,14,22..., dimensions={0} | all-to-all | bytes 131072 | tf_op jit(solution)/shard_map/all_to_all | solution.py:228
  46.3 0.6 %reduce_sum.9 = f32[32,128]{1,0:T(8,128)} reduce(f32[4,32,128]{2,1,0:T(8,128)S(1)} %all_to_all.5, f32[]{:T(128)} %constant.0.clone.1), dimensions={0}, to_apply=%region_0.0 | reduce | flops 12288 | bytes 81924 | tf_op jit(solution)/shard_map/reduce_sum | solution.py:229
Async XLA Ops:
  0.0 13.0 %copy-start = (s32[32768]{0:T(1024)S(1)}, s32[32768]{0:T(1024)}, u32[]{:S(2)}) copy-start(s32[32768]{0:T(1024)} %param.7) | copy-start | bytes 393220
  0.0 13.0 %collective-permute-start.1 = (s32[8192,128]{1,0:T(8,128)}, s32[8192,128]{1,0:T(8,128)S(1)}, u32[]{:S(2)}, u32[]{:S(2)}) collective-permute-start(s32[8192,128]{1,0:T(8,128)} %bitcast.7), channel_id=1, source_target_pairs={{0,4},{4,0},{8,12},{12,8},{16,20},{20,16},{24,28},{28,24},{1,5},{5... | collective-permute-start | bytes 12582920 | tf_op jit(solution)/shard_map/ppermute | solution.py:19
  0.5 12.6 %collective-permute-start = (bf16[512,1024]{1,0:T(8,128)(2,1)}, bf16[512,1024]{1,0:T(8,128)(2,1)S(1)}, u32[]{:S(2)}, u32[]{:S(2)}) collective-permute-start(bf16[512,1024]{1,0:T(8,128)(2,1)} %bitcast.9), channel_id=1, source_target_pairs={{0,4},{4,0},{8,12},{12,8},{16,20},{20,16},{24,28},{28,24},{1,5},{5... | collective-permute-start | bytes 3145736 | tf_op jit(solution)/shard_map/ppermute | solution.py:19
  0.5 9.7 %collective-permute-start.7 = (bf16[64,1024]{1,0:T(8,128)(2,1)}, bf16[64,1024]{1,0:T(8,128)(2,1)S(1)}, u32[]{:S(2)}, u32[]{:S(2)}) collective-permute-start(bf16[64,1024]{1,0:T(8,128)(2,1)} %bitcast.11), channel_id=1, source_target_pairs={{0,24},{4,28},{8,16},{12,20},{16,8},{20,12},{24,0},{28,4},{1,25},{... | collective-permute-start | bytes 393224 | tf_op jit(solution)/shard_map/ppermute | solution.py:19
  4.4 6.7 %collective-permute-start.5 = (bf16[64,1024]{1,0:T(8,128)(2,1)}, bf16[64,1024]{1,0:T(8,128)(2,1)S(1)}, u32[]{:S(2)}, u32[]{:S(2)}) collective-permute-start(bf16[64,1024]{1,0:T(8,128)(2,1)} %bitcast.12), channel_id=1, source_target_pairs={{0,16},{4,20},{8,24},{12,28},{16,0},{20,4},{24,8},{28,12},{1,17},{... | collective-permute-start | bytes 393224 | tf_op jit(solution)/shard_map/ppermute | solution.py:19
  4.9 6.5 %collective-permute-start.3 = (bf16[64,1024]{1,0:T(8,128)(2,1)}, bf16[64,1024]{1,0:T(8,128)(2,1)S(1)}, u32[]{:S(2)}, u32[]{:S(2)}) collective-permute-start(bf16[64,1024]{1,0:T(8,128)(2,1)} %bitcast.13), channel_id=1, source_target_pairs={{0,8},{4,12},{8,0},{12,4},{16,24},{20,28},{24,16},{28,20},{1,9},{5... | collective-permute-start | bytes 393224 | tf_op jit(solution)/shard_map/ppermute | solution.py:19
  10.2 1.4 %collective-permute-start.2 = (bf16[64,1024]{1,0:T(8,128)(2,1)S(1)}, bf16[64,1024]{1,0:T(8,128)(2,1)S(1)}, u32[]{:S(2)}, u32[]{:S(2)}) collective-permute-start(bf16[64,1024]{1,0:T(8,128)(2,1)S(1)} %get-tuple-element.12.refs_0_), channel_id=1, source_target_pairs={{0,4},{4,0},{8,12},{12,8},{16,20},{20,16},{24,28},{28,24},{1,5},{5... | collective-permute-start | bytes 393224 | tf_op jit(solution)/shard_map/ppermute | solution.py:19
  11.2 1.3 %collective-permute-start.8 = (bf16[64,1024]{1,0:T(8,128)(2,1)S(1)}, bf16[64,1024]{1,0:T(8,128)(2,1)S(1)}, u32[]{:S(2)}, u32[]{:S(2)}) collective-permute-start(bf16[64,1024]{1,0:T(8,128)(2,1)S(1)} %collective-permute-done.7.refs_6_), channel_id=1, source_target_pairs={{0,4},{4,0},{8,12},{12,8},{16,20},{20,16},{24,28},{28,24},{1,5},{5... | collective-permute-start | bytes 393224 | tf_op jit(solution)/shard_map/ppermute | solution.py:19
  11.4 1.3 %collective-permute-start.6 = (bf16[64,1024]{1,0:T(8,128)(2,1)S(1)}, bf16[64,1024]{1,0:T(8,128)(2,1)S(1)}, u32[]{:S(2)}, u32[]{:S(2)}) collective-permute-start(bf16[64,1024]{1,0:T(8,128)(2,1)S(1)} %collective-permute-done.5.refs_4_), channel_id=1, source_target_pairs={{0,4},{4,0},{8,12},{12,8},{16,20},{20,16},{24,28},{28,24},{1,5},{5... | collective-permute-start | bytes 393224 | tf_op jit(solution)/shard_map/ppermute | solution.py:19
  11.7 1.3 %collective-permute-start.4 = (bf16[64,1024]{1,0:T(8,128)(2,1)S(1)}, bf16[64,1024]{1,0:T(8,128)(2,1)S(1)}, u32[]{:S(2)}, u32[]{:S(2)}) collective-permute-start(bf16[64,1024]{1,0:T(8,128)(2,1)S(1)} %collective-permute-done.3.refs_2_), channel_id=1, source_target_pairs={{0,4},{4,0},{8,12},{12,8},{16,20},{20,16},{24,28},{28,24},{1,5},{5... | collective-permute-start | bytes 393224 | tf_op jit(solution)/shard_map/ppermute | solution.py:19

commit v12 on v9

--- a/solution.py
+++ b/solution.py
@@ -71,12 +71,12 @@
     tokens = chunk_refs[0].shape[0]
     share = index_ref.shape[0] // parties
 
-    def index_of(out):
-        return index_ref[pl.ds(pl.multiple_of((me ^ (2 * out)) * share, share), share), :]
+    def start_of(out):
+        return pl.multiple_of((me ^ (2 * out)) * share, share)
 
     copies = []
     for out in range(outs):
-        source = rows_hbm.at[pl.ds(pl.multiple_of((me ^ (2 * out)) * share, share), share), :]
+        source = rows_hbm.at[pl.ds(start_of(out), share), :]
         target = rows_ref.at[pl.ds(out * share, share), :]
         copies.append(pltpu.make_async_copy(source, target, rows_sems.at[out]))
     for copy in copies:
@@ -117,11 +117,11 @@
         copy.wait()
     groups = share * outs
     depth = len(picked)
+    singles = table.reshape(table.shape[0], 1, LANES)
     sub_at = lax.broadcasted_iota(jnp.int32, (LANES, LANES), 0)
 
     def choose(group, rows):
-        place = (me ^ (group // share * 2)) * share + group % share
-        lane = index_ref[pl.ds(place, 1), :] & (LANES - 1)
+        lane = index_ref[pl.ds(start_of(group // share) + group % share, 1), :] & (LANES - 1)
         chosen = jnp.where(sub_at == lane, rows[...].T, 0.0)
         result[pl.ds(group, 1), :] = jnp.sum(chosen, axis=0, keepdims=True)
 
@@ -131,7 +131,7 @@
             choose(jnp.maximum(group - 1, 0), picked[slot - 1])
             for first in range(0, LANES, SUBLANES):
                 at_rows = [rows_ref[group, first + k] for k in range(SUBLANES)]
-                lines = [table[pl.ds(row, SUBLANES, stride=0), :] for row in at_rows]
+                lines = [jnp.broadcast_to(singles[row], (SUBLANES, LANES)) for row in at_rows]
                 merged = lines[0]
                 for k in range(1, SUBLANES):
                     merged = jnp.where(sub_at[:SUBLANES] == k, lines[k], merged)
@@ -143,7 +143,8 @@
 
     bits = (height * breadth).bit_length() - 1
     for out, out_ref in enumerate(out_refs):
-        sign = (1 - 2 * parity((index_of(out) >> bits) & me, parties.bit_length() - 1)).astype(jnp.float32)
+        owner = index_ref[pl.ds(start_of(out), share), :] >> bits
+        sign = (1 - 2 * parity(owner & me, parties.bit_length() - 1)).astype(jnp.float32)
         out_ref[...] = result[out * share : (out + 1) * share, :] * (sign * scale)
 
 
@@ -160,8 +161,6 @@
     chunks = {0: cotangents[0]}
     for distance in range(2, parties, 2):
         chunks[distance] = flipped(chunks[0], "param", distance)
-    for distance in range(0, parties, 2):
-        chunks[distance + 1] = flipped(chunks[distance], "param", 1)
     acts = activations[0]
     sign_rows = signs.reshape(table_rows, LANES)
     index_rows = indices.reshape(groups, LANES)
@@ -189,7 +188,10 @@
         compiler_params=pltpu.CompilerParams(vmem_limit_bytes=LIMIT),
         cost_estimate=pl.CostEstimate(flops=0, bytes_accessed=8 * height * breadth, transcendentals=0),
         name="prepare",
-    )(acts, sign_rows, index_rows)
+    )(*[pltpu.with_memory_space_constraint(x, pltpu.HBM) for x in (acts, sign_rows, index_rows)])
+    chunks[0], rows = lax.optimization_barrier((chunks[0], rows))
+    for distance in range(0, parties, 2):
+        chunks[distance + 1] = flipped(chunks[distance], "param", 1)
 
     sums = pl.pallas_call(
         functools.partial(sketch_kernel, parties, 1.0 / math.sqrt(height * breadth * parties)),
@@ -206,7 +208,7 @@
             pltpu.SMEM((groups // 2, LANES), jnp.int32),
             pltpu.SemaphoreType.DMA((outs,)),
         ]
-        + [pltpu.VMEM((LANES, LANES), jnp.float32)] * 4,
+        + [pltpu.VMEM((LANES, LANES), jnp.float32)] * 8,
         compiler_params=pltpu.CompilerParams(vmem_limit_bytes=LIMIT),
         name="sketch",
     )(

time: 50 us -> 45.5 us (0.910)
  local copies, waits for them, and re-layouts: 4.32 us -> 0.01 us
  waiting for transfers between devices: 9.86 us -> 6.79 us
  Pallas kernels: 25.9 us -> 28.7 us
    unnamed x8 -> x4, local copies, waits for them, and re-layouts: 4.32 us -> 0.01 us
    pallas_call x1, Pallas kernels: 1.46 us -> 5.18 us  [on_device(): pl.pallas_call(prepare_kernel, grid=(steps,), out_shape=[jax.ShapeDtypeSt...]
    ppermute x12, waiting for transfers between devices: 9.86 us -> 6.79 us  [flipped(): lax.ppermute(x, axis, [(i, i ^ mask) for i in range(lax.axis_size(axis))])]
    pallas_call x1, Pallas kernels: 24.4 us -> 23.5 us  [on_device(): pl.pallas_call(functools.partial(sketch_kernel, parties, 1.0 / math.sqrt(...]
  transfers between devices with their start and end apart: 12 -> 12, of which waited for: 6 -> 8; matrix products, arithmetic and copies ran while one was open for 0% -> 0% of each run, Pallas kernels for 3% -> 11%
where the time goes in v12:
time: 45.5 us; the launch traced here: 45.3 us
  Pallas kernels  28.7 us (63%)
  starting transfers between devices  9.12 us (20%)
  waiting for transfers between devices  6.79 us (15%)
  other arithmetic  0.61 us (1%)
    pallas_call x1, Pallas kernels, on_device(): pl.pallas_call(functools.partial(sketch_kernel, parties, 1.0 / math.sqrt(...  23.5 us
    ppermute x12, starting transfers between devices, flipped(): lax.ppermute(x, axis, [(i, i ^ mask) for i in range(lax.axis_size(axis))])  9.12 us
    ppermute x12, waiting for transfers between devices, flipped(): lax.ppermute(x, axis, [(i, i ^ mask) for i in range(lax.axis_size(axis))])  6.79 us
    pallas_call x1, Pallas kernels, on_device(): pl.pallas_call(prepare_kernel, grid=(steps,), out_shape=[jax.ShapeDtypeSt...  5.18 us
  transfers between devices with their start and end apart: 12, of which 8 were waited for; matrix products, arithmetic and copies ran while one was open for 0% of the time, Pallas kernels for 11%

profile of v12, /device:TPU:0, one launch (start us, length us, event | category | flops | bytes accessed | tf_op | source)
XLA Modules:
  0.0 45.3 jit_solution(15777445701151430302)
XLA Ops:
  0.0 0.5 %collective-permute-start.1 = (s32[8192,128]{1,0:T(8,128)}, s32[8192,128]{1,0:T(8,128)S(1)}, u32[]{:S(2)}, u32[]{:S(2)}) collective-permute-start(s32[8192,128]{1,0:T(8,128)} %bitcast.12), channel_id=1, source_target_pairs={{0,4},{4,0},{8,12},{12,8},{16,20},{20,16},{24,28},{28,24},{1,5},{5... | collective-permute-start | bytes 12582920 | tf_op jit(solution)/shard_map/ppermute | solution.py:19
  0.5 0.1 collective-permute-start
  0.5 3.9 %collective-permute-start.7 = (bf16[64,1024]{1,0:T(8,128)(2,1)}, bf16[64,1024]{1,0:T(8,128)(2,1)S(1)}, u32[]{:S(2)}, u32[]{:S(2)}) collective-permute-start(bf16[64,1024]{1,0:T(8,128)(2,1)} %bitcast.7), channel_id=1, source_target_pairs={{0,24},{4,28},{8,16},{12,20},{16,8},{20,12},{24,0},{28,4},{1,25},{... | collective-permute-start | bytes 393224 | tf_op jit(solution)/shard_map/ppermute | solution.py:19
  4.4 0.5 %collective-permute-start.5 = (bf16[64,1024]{1,0:T(8,128)(2,1)}, bf16[64,1024]{1,0:T(8,128)(2,1)S(1)}, u32[]{:S(2)}, u32[]{:S(2)}) collective-permute-start(bf16[64,1024]{1,0:T(8,128)(2,1)} %bitcast.8), channel_id=1, source_target_pairs={{0,16},{4,20},{8,24},{12,28},{16,0},{20,4},{24,8},{28,12},{1,17},{... | collective-permute-start | bytes 393224 | tf_op jit(solution)/shard_map/ppermute | solution.py:19
  4.9 0.1 collective-permute-start.3
  5.0 5.2 %prepare.1 = (bf16[1024,512]{1,0:T(8,128)(2,1)S(1)}, bf16[1024,1024]{1,0:T(8,128)(2,1)S(1)}, s32[256,128]{1,0:T(8,128)S(1)}) custom-call(bf16[512,1024]{1,0:T(8,128)(2,1)} %bitcast.15, s32[8192,128]{1,0:T(8,128)} %bitcast.13, s32[256,128]{1,0:T(8,128)} %bitcast.5), custom_call_target="tpu_custom_call" | custom-call | bytes 8388608 | tf_op jit(solution)/shard_map/prepare/pallas_call | solution.py:170
  10.2 0.0 collective-permute-done.7.refs_6_
  10.2 0.1 collective-permute-start.2
  10.3 0.9 %collective-permute-done.5.refs_4_ = bf16[64,1024]{1,0:T(8,128)(2,1)S(1)} collective-permute-done((bf16[64,1024]{1,0:T(8,128)(2,1)}, bf16[64,1024]{1,0:T(8,128)(2,1)S(1)}, u32[]{:S(2)}, u32[]{:S(2)}) %collective-permute-start.5) | collective-permute-done | bytes 131104 | tf_op jit(solution)/shard_map/ppermute | solution.py:19
  11.2 0.0 collective-permute-start.8
  11.2 0.3 collective-permute-done.3.refs_2_
  11.4 0.2 collective-permute-start.6
  11.7 0.3 collective-permute-start.4
  12.0 0.6 %collective-permute-done.8.refs_7_ = bf16[64,1024]{1,0:T(8,128)(2,1)S(1)} collective-permute-done((bf16[64,1024]{1,0:T(8,128)(2,1)S(1)}, bf16[64,1024]{1,0:T(8,128)(2,1)S(1)}, u32[]{:S(2)}, u32[]{:S(2)}) %collective-permute-start.8) | collective-permute-done | bytes 131104 | tf_op jit(solution)/shard_map/ppermute | solution.py:19
  12.5 0.3 collective-permute-done.6.refs_5_
  12.8 0.2 collective-permute-done.4.refs_3_
  13.0 23.5 %sketch.1 = (f32[32,128]{1,0:T(8,128)S(1)}, f32[32,128]{1,0:T(8,128)S(1)}, f32[32,128]{1,0:T(8,128)S(1)}, f32[32,128]{1,0:T(8,128)S(1)}) custom-call(bf16[1024,512]{1,0:T(8,128)(2,1)S(1)} %get-tuple-element.14.own_turned, bf16[1024,1024]{1,0:T(8,128)(2,1)S(1)} %get-tuple-element.15.own_signs, bf16[512,1024]{1,0:T(8,128)(2,1)S(1)} %collective-permute-done.other_acts, ...), custom_call_target="tpu_custom_call" | custom-call | tf_op jit(solution)/shard_map/sketch/pallas_call | solution.py:196
  36.5 1.9 %collective-permute-start.9 = (f32[32,128]{1,0:T(8,128)S(1)}, f32[32,128]{1,0:T(8,128)S(1)}, u32[]{:S(2)}, u32[]{:S(2)}) collective-permute-start(f32[32,128]{1,0:T(8,128)S(1)} %get-tuple-element.20), channel_id=1, source_target_pairs={{0,8},{4,12},{8,0},{12,4},{16,24},{20,28},{24,16},{28,20},{1,9},{5... | collective-permute-start | bytes 49160 | tf_op jit(solution)/shard_map/ppermute | solution.py:19
  38.5 1.5 %collective-permute-start.10 = (f32[32,128]{1,0:T(8,128)S(1)}, f32[32,128]{1,0:T(8,128)S(1)}, u32[]{:S(2)}, u32[]{:S(2)}) collective-permute-start(f32[32,128]{1,0:T(8,128)S(1)} %get-tuple-element.21), channel_id=1, source_target_pairs={{0,16},{4,20},{8,24},{12,28},{16,0},{20,4},{24,8},{28,12},{1,17},{... | collective-permute-start | bytes 49160 | tf_op jit(solution)/shard_map/ppermute | solution.py:19
  40.0 0.1 collective-permute-start.11
  40.1 0.2 collective-permute-done.9
  40.3 1.9 %collective-permute-done.10 = f32[32,128]{1,0:T(8,128)S(1)} collective-permute-done((f32[32,128]{1,0:T(8,128)S(1)}, f32[32,128]{1,0:T(8,128)S(1)}, u32[]{:S(2)}, u32[]{:S(2)}) %collective-permute-start.10) | collective-permute-done | bytes 16416 | tf_op jit(solution)/shard_map/ppermute | solution.py:19
  42.2 2.4 %collective-permute-done.11 = f32[32,128]{1,0:T(8,128)S(1)} collective-permute-done((f32[32,128]{1,0:T(8,128)S(1)}, f32[32,128]{1,0:T(8,128)S(1)}, u32[]{:S(2)}, u32[]{:S(2)}) %collective-permute-start.11) | collective-permute-done | bytes 16416 | tf_op jit(solution)/shard_map/ppermute | solution.py:19
  44.6 0.6 %add_add_fusion = f32[32,128]{1,0:T(8,128)} fusion(f32[32,128]{1,0:T(8,128)S(1)} %collective-permute-done.11, f32[32,128]{1,0:T(8,128)S(1)} %collective-permute-done.10, f32[32,128]{1,0:T(8,128)S(1)} %get-tuple-element.19, f32[32,128]{1,0:T(8,128)S(1)} %collective-permute-done.9), kind=kLoop, calls=%fused_computation | loop fusion | flops 12288 | bytes 81920 | tf_op jit(solution)/shard_map/add | solution.py:226
  (7 shorter events, 0.0 us)
Async XLA Ops:
  0.0 10.2 %copy-start.1 = (bf16[1,64,1024]{2,1,0:T(8,128)(2,1)S(1)}, bf16[1,64,1024]{2,1,0:T(8,128)(2,1)}, u32[]{:S(2)}) copy-start(bf16[1,64,1024]{2,1,0:T(8,128)(2,1)} %param.5) | copy-start | bytes 393220
  0.0 13.0 %copy-start = (s32[32768]{0:T(1024)S(1)}, s32[32768]{0:T(1024)}, u32[]{:S(2)}) copy-start(s32[32768]{0:T(1024)} %param.7) | copy-start | bytes 393220
  0.0 13.0 %collective-permute-start.1 = (s32[8192,128]{1,0:T(8,128)}, s32[8192,128]{1,0:T(8,128)S(1)}, u32[]{:S(2)}, u32[]{:S(2)}) collective-permute-start(s32[8192,128]{1,0:T(8,128)} %bitcast.12), channel_id=1, source_target_pairs={{0,4},{4,0},{8,12},{12,8},{16,20},{20,16},{24,28},{28,24},{1,5},{5... | collective-permute-start | bytes 12582920 | tf_op jit(solution)/shard_map/ppermute | solution.py:19
  0.5 12.6 %collective-permute-start = (bf16[512,1024]{1,0:T(8,128)(2,1)}, bf16[512,1024]{1,0:T(8,128)(2,1)S(1)}, u32[]{:S(2)}, u32[]{:S(2)}) collective-permute-start(bf16[512,1024]{1,0:T(8,128)(2,1)} %bitcast.14), channel_id=1, source_target_pairs={{0,4},{4,0},{8,12},{12,8},{16,20},{20,16},{24,28},{28,24},{1,5},{5... | collective-permute-start | bytes 3145736 | tf_op jit(solution)/shard_map/ppermute | solution.py:19
  0.5 9.6 %collective-permute-start.7 = (bf16[64,1024]{1,0:T(8,128)(2,1)}, bf16[64,1024]{1,0:T(8,128)(2,1)S(1)}, u32[]{:S(2)}, u32[]{:S(2)}) collective-permute-start(bf16[64,1024]{1,0:T(8,128)(2,1)} %bitcast.7), channel_id=1, source_target_pairs={{0,24},{4,28},{8,16},{12,20},{16,8},{20,12},{24,0},{28,4},{1,25},{... | collective-permute-start | bytes 393224 | tf_op jit(solution)/shard_map/ppermute | solution.py:19
  4.4 6.8 %collective-permute-start.5 = (bf16[64,1024]{1,0:T(8,128)(2,1)}, bf16[64,1024]{1,0:T(8,128)(2,1)S(1)}, u32[]{:S(2)}, u32[]{:S(2)}) collective-permute-start(bf16[64,1024]{1,0:T(8,128)(2,1)} %bitcast.8), channel_id=1, source_target_pairs={{0,16},{4,20},{8,24},{12,28},{16,0},{20,4},{24,8},{28,12},{1,17},{... | collective-permute-start | bytes 393224 | tf_op jit(solution)/shard_map/ppermute | solution.py:19
  4.9 6.5 %collective-permute-start.3 = (bf16[64,1024]{1,0:T(8,128)(2,1)}, bf16[64,1024]{1,0:T(8,128)(2,1)S(1)}, u32[]{:S(2)}, u32[]{:S(2)}) collective-permute-start(bf16[64,1024]{1,0:T(8,128)(2,1)} %bitcast.9), channel_id=1, source_target_pairs={{0,8},{4,12},{8,0},{12,4},{16,24},{20,28},{24,16},{28,20},{1,9},{5... | collective-permute-start | bytes 393224 | tf_op jit(solution)/shard_map/ppermute | solution.py:19
  10.2 1.5 %collective-permute-start.2 = (bf16[64,1024]{1,0:T(8,128)(2,1)S(1)}, bf16[64,1024]{1,0:T(8,128)(2,1)S(1)}, u32[]{:S(2)}, u32[]{:S(2)}) collective-permute-start(bf16[64,1024]{1,0:T(8,128)(2,1)S(1)} %bitcast.10), channel_id=1, source_target_pairs={{0,4},{4,0},{8,12},{12,8},{16,20},{20,16},{24,28},{28,24},{1,5},{5... | collective-permute-start | bytes 393224 | tf_op jit(solution)/shard_map/ppermute | solution.py:19
  11.2 1.3 %collective-permute-start.8 = (bf16[64,1024]{1,0:T(8,128)(2,1)S(1)}, bf16[64,1024]{1,0:T(8,128)(2,1)S(1)}, u32[]{:S(2)}, u32[]{:S(2)}) collective-permute-start(bf16[64,1024]{1,0:T(8,128)(2,1)S(1)} %collective-permute-done.7.refs_6_), channel_id=1, source_target_pairs={{0,4},{4,0},{8,12},{12,8},{16,20},{20,16},{24,28},{28,24},{1,5},{5... | collective-permute-start | bytes 393224 | tf_op jit(solution)/shard_map/ppermute | solution.py:19
  11.4 1.3 %collective-permute-start.6 = (bf16[64,1024]{1,0:T(8,128)(2,1)S(1)}, bf16[64,1024]{1,0:T(8,128)(2,1)S(1)}, u32[]{:S(2)}, u32[]{:S(2)}) collective-permute-start(bf16[64,1024]{1,0:T(8,128)(2,1)S(1)} %collective-permute-done.5.refs_4_), channel_id=1, source_target_pairs={{0,4},{4,0},{8,12},{12,8},{16,20},{20,16},{24,28},{28,24},{1,5},{5... | collective-permute-start | bytes 393224 | tf_op jit(solution)/shard_map/ppermute | solution.py:19
  11.7 1.3 %collective-permute-start.4 = (bf16[64,1024]{1,0:T(8,128)(2,1)S(1)}, bf16[64,1024]{1,0:T(8,128)(2,1)S(1)}, u32[]{:S(2)}, u32[]{:S(2)}) collective-permute-start(bf16[64,1024]{1,0:T(8,128)(2,1)S(1)} %collective-permute-done.3.refs_2_), channel_id=1, source_target_pairs={{0,4},{4,0},{8,12},{12,8},{16,20},{20,16},{24,28},{28,24},{1,5},{5... | collective-permute-start | bytes 393224 | tf_op jit(solution)/shard_map/ppermute | solution.py:19
  36.5 3.8 %collective-permute-start.9 = (f32[32,128]{1,0:T(8,128)S(1)}, f32[32,128]{1,0:T(8,128)S(1)}, u32[]{:S(2)}, u32[]{:S(2)}) collective-permute-start(f32[32,128]{1,0:T(8,128)S(1)} %get-tuple-element.20), channel_id=1, source_target_pairs={{0,8},{4,12},{8,0},{12,4},{16,24},{20,28},{24,16},{28,20},{1,9},{5... | collective-permute-start | bytes 49160 | tf_op jit(solution)/shard_map/ppermute | solution.py:19
  38.5 3.7 %collective-permute-start.10 = (f32[32,128]{1,0:T(8,128)S(1)}, f32[32,128]{1,0:T(8,128)S(1)}, u32[]{:S(2)}, u32[]{:S(2)}) collective-permute-start(f32[32,128]{1,0:T(8,128)S(1)} %get-tuple-element.21), channel_id=1, source_target_pairs={{0,16},{4,20},{8,24},{12,28},{16,0},{20,4},{24,8},{28,12},{1,17},{... | collective-permute-start | bytes 49160 | tf_op jit(solution)/shard_map/ppermute | solution.py:19
  40.0 4.6 %collective-permute-start.11 = (f32[32,128]{1,0:T(8,128)S(1)}, f32[32,128]{1,0:T(8,128)S(1)}, u32[]{:S(2)}, u32[]{:S(2)}) collective-permute-start(f32[32,128]{1,0:T(8,128)S(1)} %get-tuple-element.22), channel_id=1, source_target_pairs={{0,24},{4,28},{8,16},{12,20},{16,8},{20,12},{24,0},{28,4},{1,25},{... | collective-permute-start | bytes 49160 | tf_op jit(solution)/shard_map/ppermute | solution.py:19

commit v13 on v12

--- a/solution.py
+++ b/solution.py
@@ -10,6 +10,7 @@
 
 LANES = 128
 LANE_BITS = 7
+HALF_WORD = 16
 SIDE = 256
 SUBLANES = 8
 LIMIT = 40 * 1024 * 1024
@@ -58,7 +59,8 @@
     index = index_ref[...]
     at_row = ((index >> LANE_BITS) & (spread - 1)) * height + ((index // breadth) & (height - 1))
     half = (index // (breadth * height)) & 1
-    rows_ref[...] = half * (spread * height) + at_row
+    at_row = half * (spread * height) + at_row
+    rows_ref[...] = at_row | (pltpu.roll(at_row, LANES // 2, 1) << HALF_WORD)
 
 
 def sketch_kernel(parties, scale, own_turned, own_signs, other_acts, other_signs, index_ref, rows_hbm, *refs):
@@ -129,13 +131,16 @@
         for slot in range(depth):
             group = at * depth + slot
             choose(jnp.maximum(group - 1, 0), picked[slot - 1])
-            for first in range(0, LANES, SUBLANES):
-                at_rows = [rows_ref[group, first + k] for k in range(SUBLANES)]
-                lines = [jnp.broadcast_to(singles[row], (SUBLANES, LANES)) for row in at_rows]
-                merged = lines[0]
-                for k in range(1, SUBLANES):
-                    merged = jnp.where(sub_at[:SUBLANES] == k, lines[k], merged)
-                picked[slot][first : first + SUBLANES, :] = merged
+            for first in range(0, LANES // 2, SUBLANES):
+                words = [rows_ref[group, first + k] for k in range(SUBLANES)]
+                low = [word & ((1 << HALF_WORD) - 1) for word in words]
+                high = [word >> HALF_WORD for word in words]
+                for at_rows, to in ((low, first), (high, first + LANES // 2)):
+                    lines = [jnp.broadcast_to(singles[row], (SUBLANES, LANES)) for row in at_rows]
+                    merged = lines[0]
+                    for k in range(1, SUBLANES):
+                        merged = jnp.where(sub_at[:SUBLANES] == k, lines[k], merged)
+                    picked[slot][to : to + SUBLANES, :] = merged
         return carry
 
     lax.fori_loop(0, groups // depth, step, 0)

time: 45.5 us -> 49.3 us (1.084)
  Pallas kernels: 28.7 us -> 32.5 us
    pallas_call x1, Pallas kernels: 23.5 us -> 27.3 us  [on_device(): pl.pallas_call(functools.partial(sketch_kernel, parties, 1.0 / math.sqrt(...]
where the time goes in v13:
time: 49.3 us; the launch traced here: 49.1 us
  Pallas kernels  32.5 us (66%)
  starting transfers between devices  9.12 us (18%)
  waiting for transfers between devices  6.79 us (14%)
  other arithmetic  0.61 us (1%)
    pallas_call x1, Pallas kernels, on_device(): pl.pallas_call(functools.partial(sketch_kernel, parties, 1.0 / math.sqrt(...  27.3 us
    ppermute x12, starting transfers between devices, flipped(): lax.ppermute(x, axis, [(i, i ^ mask) for i in range(lax.axis_size(axis))])  9.12 us
    ppermute x12, waiting for transfers between devices, flipped(): lax.ppermute(x, axis, [(i, i ^ mask) for i in range(lax.axis_size(axis))])  6.79 us
    pallas_call x1, Pallas kernels, on_device(): pl.pallas_call(prepare_kernel, grid=(steps,), out_shape=[jax.ShapeDtypeSt...  5.19 us
  transfers between devices with their start and end apart: 12, of which 8 were waited for; matrix products, arithmetic and copies ran while one was open for 0% of the time, Pallas kernels for 11%

profile of v13, /device:TPU:0, one launch (start us, length us, event | category | flops | bytes accessed | tf_op | source)
XLA Modules:
  0.0 49.1 jit_solution(3633295514574874629)
XLA Ops:
  0.0 0.5 collective-permute-start.1
  0.5 0.1 collective-permute-start
  0.5 3.9 %collective-permute-start.7 = (bf16[64,1024]{1,0:T(8,128)(2,1)}, bf16[64,1024]{1,0:T(8,128)(2,1)S(1)}, u32[]{:S(2)}, u32[]{:S(2)}) collective-permute-start(bf16[64,1024]{1,0:T(8,128)(2,1)} %bitcast.7), channel_id=1, source_target_pairs={{0,24},{4,28},{8,16},{12,20},{16,8},{20,12},{24,0},{28,4},{1,25},{... | collective-permute-start | bytes 393224 | tf_op jit(solution)/shard_map/ppermute | solution.py:20
  4.4 0.5 %collective-permute-start.5 = (bf16[64,1024]{1,0:T(8,128)(2,1)}, bf16[64,1024]{1,0:T(8,128)(2,1)S(1)}, u32[]{:S(2)}, u32[]{:S(2)}) collective-permute-start(bf16[64,1024]{1,0:T(8,128)(2,1)} %bitcast.8), channel_id=1, source_target_pairs={{0,16},{4,20},{8,24},{12,28},{16,0},{20,4},{24,8},{28,12},{1,17},{... | collective-permute-start | bytes 393224 | tf_op jit(solution)/shard_map/ppermute | solution.py:20
  4.9 0.1 collective-permute-start.3
  5.0 5.2 %prepare.1 = (bf16[1024,512]{1,0:T(8,128)(2,1)S(1)}, bf16[1024,1024]{1,0:T(8,128)(2,1)S(1)}, s32[256,128]{1,0:T(8,128)S(1)}) custom-call(bf16[512,1024]{1,0:T(8,128)(2,1)} %bitcast.15, s32[8192,128]{1,0:T(8,128)} %bitcast.13, s32[256,128]{1,0:T(8,128)} %bitcast.5), custom_call_target="tpu_custom_call" | custom-call | bytes 8388608 | tf_op jit(solution)/shard_map/prepare/pallas_call | solution.py:175
  10.2 0.0 collective-permute-done.7.refs_6_
  10.2 0.1 collective-permute-start.2
  10.3 0.9 %collective-permute-done.5.refs_4_ = bf16[64,1024]{1,0:T(8,128)(2,1)S(1)} collective-permute-done((bf16[64,1024]{1,0:T(8,128)(2,1)}, bf16[64,1024]{1,0:T(8,128)(2,1)S(1)}, u32[]{:S(2)}, u32[]{:S(2)}) %collective-permute-start.5) | collective-permute-done | bytes 131104 | tf_op jit(solution)/shard_map/ppermute | solution.py:20
  11.2 0.0 collective-permute-start.8
  11.2 0.3 collective-permute-done.3.refs_2_
  11.4 0.2 collective-permute-start.6
  11.7 0.3 collective-permute-start.4
  12.0 0.6 %collective-permute-done.8.refs_7_ = bf16[64,1024]{1,0:T(8,128)(2,1)S(1)} collective-permute-done((bf16[64,1024]{1,0:T(8,128)(2,1)S(1)}, bf16[64,1024]{1,0:T(8,128)(2,1)S(1)}, u32[]{:S(2)}, u32[]{:S(2)}) %collective-permute-start.8) | collective-permute-done | bytes 131104 | tf_op jit(solution)/shard_map/ppermute | solution.py:20
  12.5 0.3 collective-permute-done.6.refs_5_
  12.8 0.2 collective-permute-done.4.refs_3_
  13.0 27.3 %sketch.1 = (f32[32,128]{1,0:T(8,128)S(1)}, f32[32,128]{1,0:T(8,128)S(1)}, f32[32,128]{1,0:T(8,128)S(1)}, f32[32,128]{1,0:T(8,128)S(1)}) custom-call(bf16[1024,512]{1,0:T(8,128)(2,1)S(1)} %get-tuple-element.14.own_turned, bf16[1024,1024]{1,0:T(8,128)(2,1)S(1)} %get-tuple-element.15.own_signs, bf16[512,1024]{1,0:T(8,128)(2,1)S(1)} %collective-permute-done.other_acts, ...), custom_call_target="tpu_custom_call" | custom-call | tf_op jit(solution)/shard_map/sketch/pallas_call | solution.py:201
  40.4 2.0 %collective-permute-start.9 = (f32[32,128]{1,0:T(8,128)S(1)}, f32[32,128]{1,0:T(8,128)S(1)}, u32[]{:S(2)}, u32[]{:S(2)}) collective-permute-start(f32[32,128]{1,0:T(8,128)S(1)} %get-tuple-element.20), channel_id=1, source_target_pairs={{0,8},{4,12},{8,0},{12,4},{16,24},{20,28},{24,16},{28,20},{1,9},{5... | collective-permute-start | bytes 49160 | tf_op jit(solution)/shard_map/ppermute | solution.py:20
  42.3 1.5 %collective-permute-start.10 = (f32[32,128]{1,0:T(8,128)S(1)}, f32[32,128]{1,0:T(8,128)S(1)}, u32[]{:S(2)}, u32[]{:S(2)}) collective-permute-start(f32[32,128]{1,0:T(8,128)S(1)} %get-tuple-element.21), channel_id=1, source_target_pairs={{0,16},{4,20},{8,24},{12,28},{16,0},{20,4},{24,8},{28,12},{1,17},{... | collective-permute-start | bytes 49160 | tf_op jit(solution)/shard_map/ppermute | solution.py:20
  43.8 0.1 collective-permute-start.11
  43.9 0.2 collective-permute-done.9
  44.2 1.9 %collective-permute-done.10 = f32[32,128]{1,0:T(8,128)S(1)} collective-permute-done((f32[32,128]{1,0:T(8,128)S(1)}, f32[32,128]{1,0:T(8,128)S(1)}, u32[]{:S(2)}, u32[]{:S(2)}) %collective-permute-start.10) | collective-permute-done | bytes 16416 | tf_op jit(solution)/shard_map/ppermute | solution.py:20
  46.1 2.4 %collective-permute-done.11 = f32[32,128]{1,0:T(8,128)S(1)} collective-permute-done((f32[32,128]{1,0:T(8,128)S(1)}, f32[32,128]{1,0:T(8,128)S(1)}, u32[]{:S(2)}, u32[]{:S(2)}) %collective-permute-start.11) | collective-permute-done | bytes 16416 | tf_op jit(solution)/shard_map/ppermute | solution.py:20
  48.5 0.6 %add_add_fusion = f32[32,128]{1,0:T(8,128)} fusion(f32[32,128]{1,0:T(8,128)S(1)} %collective-permute-done.11, f32[32,128]{1,0:T(8,128)S(1)} %collective-permute-done.10, f32[32,128]{1,0:T(8,128)S(1)} %get-tuple-element.19, f32[32,128]{1,0:T(8,128)S(1)} %collective-permute-done.9), kind=kLoop, calls=%fused_computation | loop fusion | flops 12288 | bytes 81920 | tf_op jit(solution)/shard_map/add | solution.py:231
  (7 shorter events, 0.0 us)
Async XLA Ops:
  0.0 10.2 %copy-start.1 = (bf16[1,64,1024]{2,1,0:T(8,128)(2,1)S(1)}, bf16[1,64,1024]{2,1,0:T(8,128)(2,1)}, u32[]{:S(2)}) copy-start(bf16[1,64,1024]{2,1,0:T(8,128)(2,1)} %param.5) | copy-start | bytes 393220
  0.0 13.0 %copy-start = (s32[32768]{0:T(1024)S(1)}, s32[32768]{0:T(1024)}, u32[]{:S(2)}) copy-start(s32[32768]{0:T(1024)} %param.7) | copy-start | bytes 393220
  0.0 13.0 %collective-permute-start.1 = (s32[8192,128]{1,0:T(8,128)}, s32[8192,128]{1,0:T(8,128)S(1)}, u32[]{:S(2)}, u32[]{:S(2)}) collective-permute-start(s32[8192,128]{1,0:T(8,128)} %bitcast.12), channel_id=1, source_target_pairs={{0,4},{4,0},{8,12},{12,8},{16,20},{20,16},{24,28},{28,24},{1,5},{5... | collective-permute-start | bytes 12582920 | tf_op jit(solution)/shard_map/ppermute | solution.py:20
  0.5 12.6 %collective-permute-start = (bf16[512,1024]{1,0:T(8,128)(2,1)}, bf16[512,1024]{1,0:T(8,128)(2,1)S(1)}, u32[]{:S(2)}, u32[]{:S(2)}) collective-permute-start(bf16[512,1024]{1,0:T(8,128)(2,1)} %bitcast.14), channel_id=1, source_target_pairs={{0,4},{4,0},{8,12},{12,8},{16,20},{20,16},{24,28},{28,24},{1,5},{5... | collective-permute-start | bytes 3145736 | tf_op jit(solution)/shard_map/ppermute | solution.py:20
  0.5 9.7 %collective-permute-start.7 = (bf16[64,1024]{1,0:T(8,128)(2,1)}, bf16[64,1024]{1,0:T(8,128)(2,1)S(1)}, u32[]{:S(2)}, u32[]{:S(2)}) collective-permute-start(bf16[64,1024]{1,0:T(8,128)(2,1)} %bitcast.7), channel_id=1, source_target_pairs={{0,24},{4,28},{8,16},{12,20},{16,8},{20,12},{24,0},{28,4},{1,25},{... | collective-permute-start | bytes 393224 | tf_op jit(solution)/shard_map/ppermute | solution.py:20
  4.4 6.8 %collective-permute-start.5 = (bf16[64,1024]{1,0:T(8,128)(2,1)}, bf16[64,1024]{1,0:T(8,128)(2,1)S(1)}, u32[]{:S(2)}, u32[]{:S(2)}) collective-permute-start(bf16[64,1024]{1,0:T(8,128)(2,1)} %bitcast.8), channel_id=1, source_target_pairs={{0,16},{4,20},{8,24},{12,28},{16,0},{20,4},{24,8},{28,12},{1,17},{... | collective-permute-start | bytes 393224 | tf_op jit(solution)/shard_map/ppermute | solution.py:20
  4.9 6.5 %collective-permute-start.3 = (bf16[64,1024]{1,0:T(8,128)(2,1)}, bf16[64,1024]{1,0:T(8,128)(2,1)S(1)}, u32[]{:S(2)}, u32[]{:S(2)}) collective-permute-start(bf16[64,1024]{1,0:T(8,128)(2,1)} %bitcast.9), channel_id=1, source_target_pairs={{0,8},{4,12},{8,0},{12,4},{16,24},{20,28},{24,16},{28,20},{1,9},{5... | collective-permute-start | bytes 393224 | tf_op jit(solution)/shard_map/ppermute | solution.py:20
  10.2 1.5 %collective-permute-start.2 = (bf16[64,1024]{1,0:T(8,128)(2,1)S(1)}, bf16[64,1024]{1,0:T(8,128)(2,1)S(1)}, u32[]{:S(2)}, u32[]{:S(2)}) collective-permute-start(bf16[64,1024]{1,0:T(8,128)(2,1)S(1)} %bitcast.10), channel_id=1, source_target_pairs={{0,4},{4,0},{8,12},{12,8},{16,20},{20,16},{24,28},{28,24},{1,5},{5... | collective-permute-start | bytes 393224 | tf_op jit(solution)/shard_map/ppermute | solution.py:20
  11.2 1.3 %collective-permute-start.8 = (bf16[64,1024]{1,0:T(8,128)(2,1)S(1)}, bf16[64,1024]{1,0:T(8,128)(2,1)S(1)}, u32[]{:S(2)}, u32[]{:S(2)}) collective-permute-start(bf16[64,1024]{1,0:T(8,128)(2,1)S(1)} %collective-permute-done.7.refs_6_), channel_id=1, source_target_pairs={{0,4},{4,0},{8,12},{12,8},{16,20},{20,16},{24,28},{28,24},{1,5},{5... | collective-permute-start | bytes 393224 | tf_op jit(solution)/shard_map/ppermute | solution.py:20
  11.4 1.3 %collective-permute-start.6 = (bf16[64,1024]{1,0:T(8,128)(2,1)S(1)}, bf16[64,1024]{1,0:T(8,128)(2,1)S(1)}, u32[]{:S(2)}, u32[]{:S(2)}) collective-permute-start(bf16[64,1024]{1,0:T(8,128)(2,1)S(1)} %collective-permute-done.5.refs_4_), channel_id=1, source_target_pairs={{0,4},{4,0},{8,12},{12,8},{16,20},{20,16},{24,28},{28,24},{1,5},{5... | collective-permute-start | bytes 393224 | tf_op jit(solution)/shard_map/ppermute | solution.py:20
  11.7 1.3 %collective-permute-start.4 = (bf16[64,1024]{1,0:T(8,128)(2,1)S(1)}, bf16[64,1024]{1,0:T(8,128)(2,1)S(1)}, u32[]{:S(2)}, u32[]{:S(2)}) collective-permute-start(bf16[64,1024]{1,0:T(8,128)(2,1)S(1)} %collective-permute-done.3.refs_2_), channel_id=1, source_target_pairs={{0,4},{4,0},{8,12},{12,8},{16,20},{20,16},{24,28},{28,24},{1,5},{5... | collective-permute-start | bytes 393224 | tf_op jit(solution)/shard_map/ppermute | solution.py:20
  40.4 3.8 %collective-permute-start.9 = (f32[32,128]{1,0:T(8,128)S(1)}, f32[32,128]{1,0:T(8,128)S(1)}, u32[]{:S(2)}, u32[]{:S(2)}) collective-permute-start(f32[32,128]{1,0:T(8,128)S(1)} %get-tuple-element.20), channel_id=1, source_target_pairs={{0,8},{4,12},{8,0},{12,4},{16,24},{20,28},{24,16},{28,20},{1,9},{5... | collective-permute-start | bytes 49160 | tf_op jit(solution)/shard_map/ppermute | solution.py:20
  42.3 3.7 %collective-permute-start.10 = (f32[32,128]{1,0:T(8,128)S(1)}, f32[32,128]{1,0:T(8,128)S(1)}, u32[]{:S(2)}, u32[]{:S(2)}) collective-permute-start(f32[32,128]{1,0:T(8,128)S(1)} %get-tuple-element.21), channel_id=1, source_target_pairs={{0,16},{4,20},{8,24},{12,28},{16,0},{20,4},{24,8},{28,12},{1,17},{... | collective-permute-start | bytes 49160 | tf_op jit(solution)/shard_map/ppermute | solution.py:20
  43.8 4.6 %collective-permute-start.11 = (f32[32,128]{1,0:T(8,128)S(1)}, f32[32,128]{1,0:T(8,128)S(1)}, u32[]{:S(2)}, u32[]{:S(2)}) collective-permute-start(f32[32,128]{1,0:T(8,128)S(1)} %get-tuple-element.22), channel_id=1, source_target_pairs={{0,24},{4,28},{8,16},{12,20},{16,8},{20,12},{24,0},{28,4},{1,25},{... | collective-permute-start | bytes 49160 | tf_op jit(solution)/shard_map/ppermute | solution.py:20

commit v14 on v13

--- a/solution.py
+++ b/solution.py
@@ -10,9 +10,9 @@
 
 LANES = 128
 LANE_BITS = 7
-HALF_WORD = 16
 SIDE = 256
 SUBLANES = 8
+DEPTH = 8
 LIMIT = 40 * 1024 * 1024
 
 
@@ -59,14 +59,13 @@
     index = index_ref[...]
     at_row = ((index >> LANE_BITS) & (spread - 1)) * height + ((index // breadth) & (height - 1))
     half = (index // (breadth * height)) & 1
-    at_row = half * (spread * height) + at_row
-    rows_ref[...] = at_row | (pltpu.roll(at_row, LANES // 2, 1) << HALF_WORD)
+    rows_ref[...] = half * (spread * height) + at_row
 
 
 def sketch_kernel(parties, scale, own_turned, own_signs, other_acts, other_signs, index_ref, rows_hbm, *refs):
     outs = parties // 2
     chunk_refs, out_refs, scratch = refs[:parties], refs[parties : parties + outs], refs[parties + outs :]
-    table, cots, other_turned, total, change, result, rows_ref, rows_sems, *picked = scratch
+    table, cots, other_turned, total, change, result, rows_even, rows_odd, rows_sems, *picked = scratch
     me = lax.axis_index("param")
     height, breadth = total.shape
     spread = breadth // LANES
@@ -76,13 +75,21 @@
     def start_of(out):
         return pl.multiple_of((me ^ (2 * out)) * share, share)
 
-    copies = []
-    for out in range(outs):
-        source = rows_hbm.at[pl.ds(start_of(out), share), :]
-        target = rows_ref.at[pl.ds(out * share, share), :]
-        copies.append(pltpu.make_async_copy(source, target, rows_sems.at[out]))
-    for copy in copies:
-        copy.start()
+    groups = share * outs
+    depth = len(picked)
+    last = groups // depth - 1
+
+    def fetch(batch):
+        group = jnp.minimum(batch, last) * depth
+        start = pl.multiple_of(start_of(group // share) + group % share, depth)
+        return pl.ds(start, depth)
+
+    def fetched(batch, parity_at):
+        target = (rows_even, rows_odd)[parity_at]
+        return pltpu.make_async_copy(rows_hbm.at[fetch(batch), :], target, rows_sems.at[parity_at])
+
+    fetched(0, 0).start()
+    fetched(1, 1).start()
 
     for distance in range(parties):
         start = pl.multiple_of((me ^ distance) * tokens, tokens)
@@ -115,10 +122,6 @@
                     at = (half * spread + col * pieces + piece) * height + row * SIDE
                     table[at : at + SIDE, :] = done[:, piece * LANES : (piece + 1) * LANES]
 
-    for copy in copies:
-        copy.wait()
-    groups = share * outs
-    depth = len(picked)
     singles = table.reshape(table.shape[0], 1, LANES)
     sub_at = lax.broadcasted_iota(jnp.int32, (LANES, LANES), 0)
 
@@ -128,22 +131,25 @@
         result[pl.ds(group, 1), :] = jnp.sum(chosen, axis=0, keepdims=True)
 
     def step(at, carry):
-        for slot in range(depth):
-            group = at * depth + slot
-            choose(jnp.maximum(group - 1, 0), picked[slot - 1])
-            for first in range(0, LANES // 2, SUBLANES):
-                words = [rows_ref[group, first + k] for k in range(SUBLANES)]
-                low = [word & ((1 << HALF_WORD) - 1) for word in words]
-                high = [word >> HALF_WORD for word in words]
-                for at_rows, to in ((low, first), (high, first + LANES // 2)):
+        for half, rows_ref in enumerate((rows_even, rows_odd)):
+            batch = 2 * at + half
+            fetched(batch, half).wait()
+            for slot in range(depth):
+                group = batch * depth + slot
+                choose(jnp.maximum(group - 1, 0), picked[slot - 1])
+                for first in range(0, LANES, SUBLANES):
+                    at_rows = [rows_ref[slot, first + k] for k in range(SUBLANES)]
                     lines = [jnp.broadcast_to(singles[row], (SUBLANES, LANES)) for row in at_rows]
                     merged = lines[0]
                     for k in range(1, SUBLANES):
                         merged = jnp.where(sub_at[:SUBLANES] == k, lines[k], merged)
-                    picked[slot][to : to + SUBLANES, :] = merged
+                    picked[slot][first : first + SUBLANES, :] = merged
+            fetched(batch + 2, half).start()
         return carry
 
-    lax.fori_loop(0, groups // depth, step, 0)
+    lax.fori_loop(0, groups // depth // 2, step, 0)
+    for half in range(2):
+        fetched(last, half).wait()
     choose(groups - 1, picked[-1])
 
     bits = (height * breadth).bit_length() - 1
@@ -210,10 +216,11 @@
             pltpu.VMEM((height, breadth), jnp.float32),
             pltpu.VMEM((height, breadth), jnp.float32),
             pltpu.VMEM((groups // 2, LANES), jnp.float32),
-            pltpu.SMEM((groups // 2, LANES), jnp.int32),
-            pltpu.SemaphoreType.DMA((outs,)),
+            pltpu.SMEM((DEPTH, LANES), jnp.int32),
+            pltpu.SMEM((DEPTH, LANES), jnp.int32),
+            pltpu.SemaphoreType.DMA((2,)),
         ]
-        + [pltpu.VMEM((LANES, LANES), jnp.float32)] * 8,
+        + [pltpu.VMEM((LANES, LANES), jnp.float32)] * DEPTH,
         compiler_params=pltpu.CompilerParams(vmem_limit_bytes=LIMIT),
         name="sketch",
     )(

time: 49.3 us -> 41.8 us (0.85)
  Pallas kernels: 32.5 us -> 25.1 us
    pallas_call x1, Pallas kernels: 27.3 us -> 19.9 us  [on_device(): pl.pallas_call(functools.partial(sketch_kernel, parties, 1.0 / math.sqrt(...]
  transfers between devices with their start and end apart: 12 -> 12, of which waited for: 8 -> 8; matrix products, arithmetic and copies ran while one was open for 0% -> 0% of each run, Pallas kernels for 11% -> 12%
where the time goes in v14:
time: 41.8 us; the launch traced here: 41.6 us
  Pallas kernels  25.1 us (60%)
  starting transfers between devices  9.12 us (22%)
  waiting for transfers between devices  6.79 us (16%)
  other arithmetic  0.61 us (1%)
    pallas_call x1, Pallas kernels, on_device(): pl.pallas_call(functools.partial(sketch_kernel, parties, 1.0 / math.sqrt(...  19.9 us
    ppermute x12, starting transfers between devices, flipped(): lax.ppermute(x, axis, [(i, i ^ mask) for i in range(lax.axis_size(axis))])  9.12 us
    ppermute x12, waiting for transfers between devices, flipped(): lax.ppermute(x, axis, [(i, i ^ mask) for i in range(lax.axis_size(axis))])  6.79 us
    pallas_call x1, Pallas kernels, on_device(): pl.pallas_call(prepare_kernel, grid=(steps,), out_shape=[jax.ShapeDtypeSt...  5.18 us
  transfers between devices with their start and end apart: 12, of which 8 were waited for; matrix products, arithmetic and copies ran while one was open for 0% of the time, Pallas kernels for 12%

profile of v14, /device:TPU:0, one launch (start us, length us, event | category | flops | bytes accessed | tf_op | source)
XLA Modules:
  0.0 41.6 jit_solution(18440961314065512205)
XLA Ops:
  0.0 0.5 %collective-permute-start.1 = (s32[8192,128]{1,0:T(8,128)}, s32[8192,128]{1,0:T(8,128)S(1)}, u32[]{:S(2)}, u32[]{:S(2)}) collective-permute-start(s32[8192,128]{1,0:T(8,128)} %bitcast.12), channel_id=1, source_target_pairs={{0,4},{4,0},{8,12},{12,8},{16,20},{20,16},{24,28},{28,24},{1,5},{5... | collective-permute-start | bytes 12582920 | tf_op jit(solution)/shard_map/ppermute | solution.py:20
  0.5 0.1 collective-permute-start
  0.5 3.9 %collective-permute-start.7 = (bf16[64,1024]{1,0:T(8,128)(2,1)}, bf16[64,1024]{1,0:T(8,128)(2,1)S(1)}, u32[]{:S(2)}, u32[]{:S(2)}) collective-permute-start(bf16[64,1024]{1,0:T(8,128)(2,1)} %bitcast.7), channel_id=1, source_target_pairs={{0,24},{4,28},{8,16},{12,20},{16,8},{20,12},{24,0},{28,4},{1,25},{... | collective-permute-start | bytes 393224 | tf_op jit(solution)/shard_map/ppermute | solution.py:20
  4.4 0.5 %collective-permute-start.5 = (bf16[64,1024]{1,0:T(8,128)(2,1)}, bf16[64,1024]{1,0:T(8,128)(2,1)S(1)}, u32[]{:S(2)}, u32[]{:S(2)}) collective-permute-start(bf16[64,1024]{1,0:T(8,128)(2,1)} %bitcast.8), channel_id=1, source_target_pairs={{0,16},{4,20},{8,24},{12,28},{16,0},{20,4},{24,8},{28,12},{1,17},{... | collective-permute-start | bytes 393224 | tf_op jit(solution)/shard_map/ppermute | solution.py:20
  4.9 0.1 collective-permute-start.3
  5.0 5.2 %prepare.1 = (bf16[1024,512]{1,0:T(8,128)(2,1)S(1)}, bf16[1024,1024]{1,0:T(8,128)(2,1)S(1)}, s32[256,128]{1,0:T(8,128)S(1)}) custom-call(bf16[512,1024]{1,0:T(8,128)(2,1)} %bitcast.15, s32[8192,128]{1,0:T(8,128)} %bitcast.13, s32[256,128]{1,0:T(8,128)} %bitcast.5), custom_call_target="tpu_custom_call" | custom-call | bytes 8388608 | tf_op jit(solution)/shard_map/prepare/pallas_call | solution.py:181
  10.2 0.1 collective-permute-start.2
  10.3 0.9 %collective-permute-done.5.refs_4_ = bf16[64,1024]{1,0:T(8,128)(2,1)S(1)} collective-permute-done((bf16[64,1024]{1,0:T(8,128)(2,1)}, bf16[64,1024]{1,0:T(8,128)(2,1)S(1)}, u32[]{:S(2)}, u32[]{:S(2)}) %collective-permute-start.5) | collective-permute-done | bytes 131104 | tf_op jit(solution)/shard_map/ppermute | solution.py:20
  11.2 0.0 collective-permute-start.8
  11.2 0.3 collective-permute-done.3.refs_2_
  11.4 0.2 collective-permute-start.6
  11.7 0.0 collective-permute-done.2.refs_1_
  11.7 0.3 collective-permute-start.4
  12.0 0.6 %collective-permute-done.8.refs_7_ = bf16[64,1024]{1,0:T(8,128)(2,1)S(1)} collective-permute-done((bf16[64,1024]{1,0:T(8,128)(2,1)S(1)}, bf16[64,1024]{1,0:T(8,128)(2,1)S(1)}, u32[]{:S(2)}, u32[]{:S(2)}) %collective-permute-start.8) | collective-permute-done | bytes 131104 | tf_op jit(solution)/shard_map/ppermute | solution.py:20
  12.5 0.3 collective-permute-done.6.refs_5_
  12.8 0.2 collective-permute-done.4.refs_3_
  13.0 19.9 %sketch.1 = (f32[32,128]{1,0:T(8,128)S(1)}, f32[32,128]{1,0:T(8,128)S(1)}, f32[32,128]{1,0:T(8,128)S(1)}, f32[32,128]{1,0:T(8,128)S(1)}) custom-call(bf16[1024,512]{1,0:T(8,128)(2,1)S(1)} %get-tuple-element.14.own_turned, bf16[1024,1024]{1,0:T(8,128)(2,1)S(1)} %get-tuple-element.15.own_signs, bf16[512,1024]{1,0:T(8,128)(2,1)S(1)} %collective-permute-done.other_acts, ...), custom_call_target="tpu_custom_call" | custom-call | tf_op jit(solution)/shard_map/sketch/pallas_call | solution.py:207
  32.9 1.9 %collective-permute-start.9 = (f32[32,128]{1,0:T(8,128)S(1)}, f32[32,128]{1,0:T(8,128)S(1)}, u32[]{:S(2)}, u32[]{:S(2)}) collective-permute-start(f32[32,128]{1,0:T(8,128)S(1)} %get-tuple-element.20), channel_id=1, source_target_pairs={{0,8},{4,12},{8,0},{12,4},{16,24},{20,28},{24,16},{28,20},{1,9},{5... | collective-permute-start | bytes 49160 | tf_op jit(solution)/shard_map/ppermute | solution.py:20
  34.9 1.5 %collective-permute-start.10 = (f32[32,128]{1,0:T(8,128)S(1)}, f32[32,128]{1,0:T(8,128)S(1)}, u32[]{:S(2)}, u32[]{:S(2)}) collective-permute-start(f32[32,128]{1,0:T(8,128)S(1)} %get-tuple-element.21), channel_id=1, source_target_pairs={{0,16},{4,20},{8,24},{12,28},{16,0},{20,4},{24,8},{28,12},{1,17},{... | collective-permute-start | bytes 49160 | tf_op jit(solution)/shard_map/ppermute | solution.py:20
  36.4 0.1 collective-permute-start.11
  36.5 0.2 collective-permute-done.9
  36.7 1.9 %collective-permute-done.10 = f32[32,128]{1,0:T(8,128)S(1)} collective-permute-done((f32[32,128]{1,0:T(8,128)S(1)}, f32[32,128]{1,0:T(8,128)S(1)}, u32[]{:S(2)}, u32[]{:S(2)}) %collective-permute-start.10) | collective-permute-done | bytes 16416 | tf_op jit(solution)/shard_map/ppermute | solution.py:20
  38.6 2.4 %collective-permute-done.11 = f32[32,128]{1,0:T(8,128)S(1)} collective-permute-done((f32[32,128]{1,0:T(8,128)S(1)}, f32[32,128]{1,0:T(8,128)S(1)}, u32[]{:S(2)}, u32[]{:S(2)}) %collective-permute-start.11) | collective-permute-done | bytes 16416 | tf_op jit(solution)/shard_map/ppermute | solution.py:20
  41.0 0.6 %add_add_fusion = f32[32,128]{1,0:T(8,128)} fusion(f32[32,128]{1,0:T(8,128)S(1)} %collective-permute-done.11, f32[32,128]{1,0:T(8,128)S(1)} %collective-permute-done.10, f32[32,128]{1,0:T(8,128)S(1)} %get-tuple-element.19, f32[32,128]{1,0:T(8,128)S(1)} %collective-permute-done.9), kind=kLoop, calls=%fused_computation | loop fusion | flops 12288 | bytes 81920 | tf_op jit(solution)/shard_map/add | solution.py:238
  (7 shorter events, 0.0 us)
Async XLA Ops:
  0.0 10.2 %copy-start.1 = (bf16[1,64,1024]{2,1,0:T(8,128)(2,1)S(1)}, bf16[1,64,1024]{2,1,0:T(8,128)(2,1)}, u32[]{:S(2)}) copy-start(bf16[1,64,1024]{2,1,0:T(8,128)(2,1)} %param.5) | copy-start | bytes 393220
  0.0 13.0 %copy-start = (s32[32768]{0:T(1024)S(1)}, s32[32768]{0:T(1024)}, u32[]{:S(2)}) copy-start(s32[32768]{0:T(1024)} %param.7) | copy-start | bytes 393220
  0.0 13.0 %collective-permute-start.1 = (s32[8192,128]{1,0:T(8,128)}, s32[8192,128]{1,0:T(8,128)S(1)}, u32[]{:S(2)}, u32[]{:S(2)}) collective-permute-start(s32[8192,128]{1,0:T(8,128)} %bitcast.12), channel_id=1, source_target_pairs={{0,4},{4,0},{8,12},{12,8},{16,20},{20,16},{24,28},{28,24},{1,5},{5... | collective-permute-start | bytes 12582920 | tf_op jit(solution)/shard_map/ppermute | solution.py:20
  0.5 12.6 %collective-permute-start = (bf16[512,1024]{1,0:T(8,128)(2,1)}, bf16[512,1024]{1,0:T(8,128)(2,1)S(1)}, u32[]{:S(2)}, u32[]{:S(2)}) collective-permute-start(bf16[512,1024]{1,0:T(8,128)(2,1)} %bitcast.14), channel_id=1, source_target_pairs={{0,4},{4,0},{8,12},{12,8},{16,20},{20,16},{24,28},{28,24},{1,5},{5... | collective-permute-start | bytes 3145736 | tf_op jit(solution)/shard_map/ppermute | solution.py:20
  0.5 9.6 %collective-permute-start.7 = (bf16[64,1024]{1,0:T(8,128)(2,1)}, bf16[64,1024]{1,0:T(8,128)(2,1)S(1)}, u32[]{:S(2)}, u32[]{:S(2)}) collective-permute-start(bf16[64,1024]{1,0:T(8,128)(2,1)} %bitcast.7), channel_id=1, source_target_pairs={{0,24},{4,28},{8,16},{12,20},{16,8},{20,12},{24,0},{28,4},{1,25},{... | collective-permute-start | bytes 393224 | tf_op jit(solution)/shard_map/ppermute | solution.py:20
  4.4 6.8 %collective-permute-start.5 = (bf16[64,1024]{1,0:T(8,128)(2,1)}, bf16[64,1024]{1,0:T(8,128)(2,1)S(1)}, u32[]{:S(2)}, u32[]{:S(2)}) collective-permute-start(bf16[64,1024]{1,0:T(8,128)(2,1)} %bitcast.8), channel_id=1, source_target_pairs={{0,16},{4,20},{8,24},{12,28},{16,0},{20,4},{24,8},{28,12},{1,17},{... | collective-permute-start | bytes 393224 | tf_op jit(solution)/shard_map/ppermute | solution.py:20
  4.9 6.5 %collective-permute-start.3 = (bf16[64,1024]{1,0:T(8,128)(2,1)}, bf16[64,1024]{1,0:T(8,128)(2,1)S(1)}, u32[]{:S(2)}, u32[]{:S(2)}) collective-permute-start(bf16[64,1024]{1,0:T(8,128)(2,1)} %bitcast.9), channel_id=1, source_target_pairs={{0,8},{4,12},{8,0},{12,4},{16,24},{20,28},{24,16},{28,20},{1,9},{5... | collective-permute-start | bytes 393224 | tf_op jit(solution)/shard_map/ppermute | solution.py:20
  10.2 1.5 %collective-permute-start.2 = (bf16[64,1024]{1,0:T(8,128)(2,1)S(1)}, bf16[64,1024]{1,0:T(8,128)(2,1)S(1)}, u32[]{:S(2)}, u32[]{:S(2)}) collective-permute-start(bf16[64,1024]{1,0:T(8,128)(2,1)S(1)} %bitcast.10), channel_id=1, source_target_pairs={{0,4},{4,0},{8,12},{12,8},{16,20},{20,16},{24,28},{28,24},{1,5},{5... | collective-permute-start | bytes 393224 | tf_op jit(solution)/shard_map/ppermute | solution.py:20
  11.2 1.3 %collective-permute-start.8 = (bf16[64,1024]{1,0:T(8,128)(2,1)S(1)}, bf16[64,1024]{1,0:T(8,128)(2,1)S(1)}, u32[]{:S(2)}, u32[]{:S(2)}) collective-permute-start(bf16[64,1024]{1,0:T(8,128)(2,1)S(1)} %collective-permute-done.7.refs_6_), channel_id=1, source_target_pairs={{0,4},{4,0},{8,12},{12,8},{16,20},{20,16},{24,28},{28,24},{1,5},{5... | collective-permute-start | bytes 393224 | tf_op jit(solution)/shard_map/ppermute | solution.py:20
  11.4 1.3 %collective-permute-start.6 = (bf16[64,1024]{1,0:T(8,128)(2,1)S(1)}, bf16[64,1024]{1,0:T(8,128)(2,1)S(1)}, u32[]{:S(2)}, u32[]{:S(2)}) collective-permute-start(bf16[64,1024]{1,0:T(8,128)(2,1)S(1)} %collective-permute-done.5.refs_4_), channel_id=1, source_target_pairs={{0,4},{4,0},{8,12},{12,8},{16,20},{20,16},{24,28},{28,24},{1,5},{5... | collective-permute-start | bytes 393224 | tf_op jit(solution)/shard_map/ppermute | solution.py:20
  11.7 1.3 %collective-permute-start.4 = (bf16[64,1024]{1,0:T(8,128)(2,1)S(1)}, bf16[64,1024]{1,0:T(8,128)(2,1)S(1)}, u32[]{:S(2)}, u32[]{:S(2)}) collective-permute-start(bf16[64,1024]{1,0:T(8,128)(2,1)S(1)} %collective-permute-done.3.refs_2_), channel_id=1, source_target_pairs={{0,4},{4,0},{8,12},{12,8},{16,20},{20,16},{24,28},{28,24},{1,5},{5... | collective-permute-start | bytes 393224 | tf_op jit(solution)/shard_map/ppermute | solution.py:20
  32.9 3.8 %collective-permute-start.9 = (f32[32,128]{1,0:T(8,128)S(1)}, f32[32,128]{1,0:T(8,128)S(1)}, u32[]{:S(2)}, u32[]{:S(2)}) collective-permute-start(f32[32,128]{1,0:T(8,128)S(1)} %get-tuple-element.20), channel_id=1, source_target_pairs={{0,8},{4,12},{8,0},{12,4},{16,24},{20,28},{24,16},{28,20},{1,9},{5... | collective-permute-start | bytes 49160 | tf_op jit(solution)/shard_map/ppermute | solution.py:20
  34.9 3.7 %collective-permute-start.10 = (f32[32,128]{1,0:T(8,128)S(1)}, f32[32,128]{1,0:T(8,128)S(1)}, u32[]{:S(2)}, u32[]{:S(2)}) collective-permute-start(f32[32,128]{1,0:T(8,128)S(1)} %get-tuple-element.21), channel_id=1, source_target_pairs={{0,16},{4,20},{8,24},{12,28},{16,0},{20,4},{24,8},{28,12},{1,17},{... | collective-permute-start | bytes 49160 | tf_op jit(solution)/shard_map/ppermute | solution.py:20
  36.4 4.6 %collective-permute-start.11 = (f32[32,128]{1,0:T(8,128)S(1)}, f32[32,128]{1,0:T(8,128)S(1)}, u32[]{:S(2)}, u32[]{:S(2)}) collective-permute-start(f32[32,128]{1,0:T(8,128)S(1)} %get-tuple-element.22), channel_id=1, source_target_pairs={{0,24},{4,28},{8,16},{12,20},{16,8},{20,12},{24,0},{28,4},{1,25},{... | collective-permute-start | bytes 49160 | tf_op jit(solution)/shard_map/ppermute | solution.py:20

commit v15 on v14

--- a/solution.py
+++ b/solution.py
@@ -12,7 +12,7 @@
 LANE_BITS = 7
 SIDE = 256
 SUBLANES = 8
-DEPTH = 8
+DEPTH = 16
 LIMIT = 40 * 1024 * 1024
 
 
@@ -94,16 +94,20 @@
     for distance in range(parties):
         start = pl.multiple_of((me ^ distance) * tokens, tokens)
         cots[pl.ds(start, tokens), :] = chunk_refs[distance][...]
-    other_turned[...] = other_acts[...].T
 
     row_at = lax.broadcasted_iota(jnp.int32, (SIDE, SIDE), 0)
     col_at = lax.broadcasted_iota(jnp.int32, (SIDE, SIDE), 1)
     hadamard = (1 - 2 * parity(row_at & col_at, 8)).astype(jnp.float32).astype(jnp.bfloat16)
+
+    tall = jnp.concatenate([hadamard, hadamard], axis=0)
+    wide = jnp.concatenate([hadamard, hadamard], axis=1)
 
     row_blocks, col_blocks, pieces = height // SIDE, breadth // SIDE, SIDE // LANES
     for col in range(col_blocks):
         cols = slice(col * SIDE, (col + 1) * SIDE)
         own = dot(own_turned[...], cots[:, cols]) * own_signs[:, cols].astype(jnp.float32)
+        if col == 0:
+            other_turned[...] = other_acts[...].T
         strips = [other_signs[pl.ds(col * pieces + piece, height, stride=spread), :] for piece in range(pieces)]
         other = dot(other_turned[...], cots[:, cols]) * jnp.concatenate(strips, axis=1).astype(jnp.float32)
         for signed, product in ((total, own + other), (change, own - other)):
@@ -115,9 +119,8 @@
             rows = slice(row * SIDE, (row + 1) * SIDE)
             parts = butterfly([signed[rows, col * SIDE : (col + 1) * SIDE] for col in range(col_blocks)])
             for col in range(col_blocks):
-                high, low = split(parts[col])
-                high, low = split(dot(high, hadamard) + dot(low, hadamard))
-                done = dot(hadamard, high) + dot(hadamard, low)
+                half_done = dot(jnp.concatenate(split(parts[col]), axis=1), tall)
+                done = dot(wide, jnp.concatenate(split(half_done), axis=0))
                 for piece in range(pieces):
                     at = (half * spread + col * pieces + piece) * height + row * SIDE
                     table[at : at + SIDE, :] = done[:, piece * LANES : (piece + 1) * LANES]
@@ -167,6 +170,7 @@
     groups = samples // LANES
     table_rows = height * breadth // LANES
     outs = parties // 2
+    depth = min(DEPTH, groups // parties)
     vmem = pl.BlockSpec(memory_space=pltpu.VMEM)
 
     chunks = {0: cotangents[0]}
@@ -216,11 +220,11 @@
             pltpu.VMEM((height, breadth), jnp.float32),
             pltpu.VMEM((height, breadth), jnp.float32),
             pltpu.VMEM((groups // 2, LANES), jnp.float32),
-            pltpu.SMEM((DEPTH, LANES), jnp.int32),
-            pltpu.SMEM((DEPTH, LANES), jnp.int32),
+            pltpu.SMEM((depth, LANES), jnp.int32),
+            pltpu.SMEM((depth, LANES), jnp.int32),
             pltpu.SemaphoreType.DMA((2,)),
         ]
-        + [pltpu.VMEM((LANES, LANES), jnp.float32)] * DEPTH,
+        + [pltpu.VMEM((LANES, LANES), jnp.float32)] * depth,
         compiler_params=pltpu.CompilerParams(vmem_limit_bytes=LIMIT),
         name="sketch",
     )(

time: 41.8 us -> 41.3 us (0.988)
  Pallas kernels: 25.1 us -> 24.5 us
    pallas_call x1, Pallas kernels: 19.9 us -> 19.4 us  [on_device(): pl.pallas_call(functools.partial(sketch_kernel, parties, 1.0 / math.sqrt(...]
  transfers between devices with their start and end apart: 12 -> 12, of which waited for: 8 -> 8; matrix products, arithmetic and copies ran while one was open for 0% -> 0% of each run, Pallas kernels for 12% -> 13%
where the time goes in v15:
time: 41.3 us; the launch traced here: 41.1 us
  Pallas kernels  24.5 us (59%)
  starting transfers between devices  9.12 us (22%)
  waiting for transfers between devices  6.79 us (16%)
  other arithmetic  0.61 us (1%)
    pallas_call x1, Pallas kernels, on_device(): pl.pallas_call(functools.partial(sketch_kernel, parties, 1.0 / math.sqrt(...  19.4 us
    ppermute x12, starting transfers between devices, flipped(): lax.ppermute(x, axis, [(i, i ^ mask) for i in range(lax.axis_size(axis))])  9.12 us
    ppermute x12, waiting for transfers between devices, flipped(): lax.ppermute(x, axis, [(i, i ^ mask) for i in range(lax.axis_size(axis))])  6.79 us
    pallas_call x1, Pallas kernels, on_device(): pl.pallas_call(prepare_kernel, grid=(steps,), out_shape=[jax.ShapeDtypeSt...  5.18 us
  transfers between devices with their start and end apart: 12, of which 8 were waited for; matrix products, arithmetic and copies ran while one was open for 0% of the time, Pallas kernels for 13%

profile of v15, /device:TPU:0, one launch (start us, length us, event | category | flops | bytes accessed | tf_op | source)
XLA Modules:
  0.0 41.1 jit_solution(18364464086228108494)
XLA Ops:
  0.0 0.5 %collective-permute-start.1 = (s32[8192,128]{1,0:T(8,128)}, s32[8192,128]{1,0:T(8,128)S(1)}, u32[]{:S(2)}, u32[]{:S(2)}) collective-permute-start(s32[8192,128]{1,0:T(8,128)} %bitcast.12), channel_id=1, source_target_pairs={{0,4},{4,0},{8,12},{12,8},{16,20},{20,16},{24,28},{28,24},{1,5},{5... | collective-permute-start | bytes 12582920 | tf_op jit(solution)/shard_map/ppermute | solution.py:20
  0.5 0.1 collective-permute-start
  0.5 3.9 %collective-permute-start.7 = (bf16[64,1024]{1,0:T(8,128)(2,1)}, bf16[64,1024]{1,0:T(8,128)(2,1)S(1)}, u32[]{:S(2)}, u32[]{:S(2)}) collective-permute-start(bf16[64,1024]{1,0:T(8,128)(2,1)} %bitcast.7), channel_id=1, source_target_pairs={{0,24},{4,28},{8,16},{12,20},{16,8},{20,12},{24,0},{28,4},{1,25},{... | collective-permute-start | bytes 393224 | tf_op jit(solution)/shard_map/ppermute | solution.py:20
  4.4 0.5 %collective-permute-start.5 = (bf16[64,1024]{1,0:T(8,128)(2,1)}, bf16[64,1024]{1,0:T(8,128)(2,1)S(1)}, u32[]{:S(2)}, u32[]{:S(2)}) collective-permute-start(bf16[64,1024]{1,0:T(8,128)(2,1)} %bitcast.8), channel_id=1, source_target_pairs={{0,16},{4,20},{8,24},{12,28},{16,0},{20,4},{24,8},{28,12},{1,17},{... | collective-permute-start | bytes 393224 | tf_op jit(solution)/shard_map/ppermute | solution.py:20
  4.9 0.1 collective-permute-start.3
  5.0 5.2 %prepare.1 = (bf16[1024,512]{1,0:T(8,128)(2,1)S(1)}, bf16[1024,1024]{1,0:T(8,128)(2,1)S(1)}, s32[256,128]{1,0:T(8,128)S(1)}) custom-call(bf16[512,1024]{1,0:T(8,128)(2,1)} %bitcast.15, s32[8192,128]{1,0:T(8,128)} %bitcast.13, s32[256,128]{1,0:T(8,128)} %bitcast.5), custom_call_target="tpu_custom_call" | custom-call | bytes 8388608 | tf_op jit(solution)/shard_map/prepare/pallas_call | solution.py:185
  10.2 0.1 collective-permute-start.2
  10.3 0.9 %collective-permute-done.5.refs_4_ = bf16[64,1024]{1,0:T(8,128)(2,1)S(1)} collective-permute-done((bf16[64,1024]{1,0:T(8,128)(2,1)}, bf16[64,1024]{1,0:T(8,128)(2,1)S(1)}, u32[]{:S(2)}, u32[]{:S(2)}) %collective-permute-start.5) | collective-permute-done | bytes 131104 | tf_op jit(solution)/shard_map/ppermute | solution.py:20
  11.2 0.0 collective-permute-start.8
  11.2 0.3 collective-permute-done.3.refs_2_
  11.4 0.2 collective-permute-start.6
  11.7 0.0 collective-permute-done.2.refs_1_
  11.7 0.3 collective-permute-start.4
  12.0 0.6 %collective-permute-done.8.refs_7_ = bf16[64,1024]{1,0:T(8,128)(2,1)S(1)} collective-permute-done((bf16[64,1024]{1,0:T(8,128)(2,1)S(1)}, bf16[64,1024]{1,0:T(8,128)(2,1)S(1)}, u32[]{:S(2)}, u32[]{:S(2)}) %collective-permute-start.8) | collective-permute-done | bytes 131104 | tf_op jit(solution)/shard_map/ppermute | solution.py:20
  12.5 0.3 collective-permute-done.6.refs_5_
  12.8 0.2 collective-permute-done.4.refs_3_
  13.0 19.4 %sketch.1 = (f32[32,128]{1,0:T(8,128)S(1)}, f32[32,128]{1,0:T(8,128)S(1)}, f32[32,128]{1,0:T(8,128)S(1)}, f32[32,128]{1,0:T(8,128)S(1)}) custom-call(bf16[1024,512]{1,0:T(8,128)(2,1)S(1)} %get-tuple-element.14.own_turned, bf16[1024,1024]{1,0:T(8,128)(2,1)S(1)} %get-tuple-element.15.own_signs, bf16[512,1024]{1,0:T(8,128)(2,1)S(1)} %collective-permute-done.other_acts, ...), custom_call_target="tpu_custom_call" | custom-call | tf_op jit(solution)/shard_map/sketch/pallas_call | solution.py:211
  32.4 1.9 %collective-permute-start.9 = (f32[32,128]{1,0:T(8,128)S(1)}, f32[32,128]{1,0:T(8,128)S(1)}, u32[]{:S(2)}, u32[]{:S(2)}) collective-permute-start(f32[32,128]{1,0:T(8,128)S(1)} %get-tuple-element.20), channel_id=1, source_target_pairs={{0,8},{4,12},{8,0},{12,4},{16,24},{20,28},{24,16},{28,20},{1,9},{5... | collective-permute-start | bytes 49160 | tf_op jit(solution)/shard_map/ppermute | solution.py:20
  34.4 1.5 %collective-permute-start.10 = (f32[32,128]{1,0:T(8,128)S(1)}, f32[32,128]{1,0:T(8,128)S(1)}, u32[]{:S(2)}, u32[]{:S(2)}) collective-permute-start(f32[32,128]{1,0:T(8,128)S(1)} %get-tuple-element.21), channel_id=1, source_target_pairs={{0,16},{4,20},{8,24},{12,28},{16,0},{20,4},{24,8},{28,12},{1,17},{... | collective-permute-start | bytes 49160 | tf_op jit(solution)/shard_map/ppermute | solution.py:20
  35.9 0.1 collective-permute-start.11
  36.0 0.2 collective-permute-done.9
  36.2 1.9 %collective-permute-done.10 = f32[32,128]{1,0:T(8,128)S(1)} collective-permute-done((f32[32,128]{1,0:T(8,128)S(1)}, f32[32,128]{1,0:T(8,128)S(1)}, u32[]{:S(2)}, u32[]{:S(2)}) %collective-permute-start.10) | collective-permute-done | bytes 16416 | tf_op jit(solution)/shard_map/ppermute | solution.py:20
  38.1 2.4 %collective-permute-done.11 = f32[32,128]{1,0:T(8,128)S(1)} collective-permute-done((f32[32,128]{1,0:T(8,128)S(1)}, f32[32,128]{1,0:T(8,128)S(1)}, u32[]{:S(2)}, u32[]{:S(2)}) %collective-permute-start.11) | collective-permute-done | bytes 16416 | tf_op jit(solution)/shard_map/ppermute | solution.py:20
  40.5 0.6 %add_add_fusion = f32[32,128]{1,0:T(8,128)} fusion(f32[32,128]{1,0:T(8,128)S(1)} %collective-permute-done.11, f32[32,128]{1,0:T(8,128)S(1)} %collective-permute-done.10, f32[32,128]{1,0:T(8,128)S(1)} %get-tuple-element.19, f32[32,128]{1,0:T(8,128)S(1)} %collective-permute-done.9), kind=kLoop, calls=%fused_computation | loop fusion | flops 12288 | bytes 81920 | tf_op jit(solution)/shard_map/add | solution.py:242
  (7 shorter events, 0.0 us)
Async XLA Ops:
  0.0 10.2 %copy-start.1 = (bf16[1,64,1024]{2,1,0:T(8,128)(2,1)S(1)}, bf16[1,64,1024]{2,1,0:T(8,128)(2,1)}, u32[]{:S(2)}) copy-start(bf16[1,64,1024]{2,1,0:T(8,128)(2,1)} %param.5) | copy-start | bytes 393220
  0.0 13.0 %copy-start = (s32[32768]{0:T(1024)S(1)}, s32[32768]{0:T(1024)}, u32[]{:S(2)}) copy-start(s32[32768]{0:T(1024)} %param.7) | copy-start | bytes 393220
  0.0 13.0 %collective-permute-start.1 = (s32[8192,128]{1,0:T(8,128)}, s32[8192,128]{1,0:T(8,128)S(1)}, u32[]{:S(2)}, u32[]{:S(2)}) collective-permute-start(s32[8192,128]{1,0:T(8,128)} %bitcast.12), channel_id=1, source_target_pairs={{0,4},{4,0},{8,12},{12,8},{16,20},{20,16},{24,28},{28,24},{1,5},{5... | collective-permute-start | bytes 12582920 | tf_op jit(solution)/shard_map/ppermute | solution.py:20
  0.5 12.6 %collective-permute-start = (bf16[512,1024]{1,0:T(8,128)(2,1)}, bf16[512,1024]{1,0:T(8,128)(2,1)S(1)}, u32[]{:S(2)}, u32[]{:S(2)}) collective-permute-start(bf16[512,1024]{1,0:T(8,128)(2,1)} %bitcast.14), channel_id=1, source_target_pairs={{0,4},{4,0},{8,12},{12,8},{16,20},{20,16},{24,28},{28,24},{1,5},{5... | collective-permute-start | bytes 3145736 | tf_op jit(solution)/shard_map/ppermute | solution.py:20
  0.5 9.6 %collective-permute-start.7 = (bf16[64,1024]{1,0:T(8,128)(2,1)}, bf16[64,1024]{1,0:T(8,128)(2,1)S(1)}, u32[]{:S(2)}, u32[]{:S(2)}) collective-permute-start(bf16[64,1024]{1,0:T(8,128)(2,1)} %bitcast.7), channel_id=1, source_target_pairs={{0,24},{4,28},{8,16},{12,20},{16,8},{20,12},{24,0},{28,4},{1,25},{... | collective-permute-start | bytes 393224 | tf_op jit(solution)/shard_map/ppermute | solution.py:20
  4.4 6.8 %collective-permute-start.5 = (bf16[64,1024]{1,0:T(8,128)(2,1)}, bf16[64,1024]{1,0:T(8,128)(2,1)S(1)}, u32[]{:S(2)}, u32[]{:S(2)}) collective-permute-start(bf16[64,1024]{1,0:T(8,128)(2,1)} %bitcast.8), channel_id=1, source_target_pairs={{0,16},{4,20},{8,24},{12,28},{16,0},{20,4},{24,8},{28,12},{1,17},{... | collective-permute-start | bytes 393224 | tf_op jit(solution)/shard_map/ppermute | solution.py:20
  4.9 6.5 %collective-permute-start.3 = (bf16[64,1024]{1,0:T(8,128)(2,1)}, bf16[64,1024]{1,0:T(8,128)(2,1)S(1)}, u32[]{:S(2)}, u32[]{:S(2)}) collective-permute-start(bf16[64,1024]{1,0:T(8,128)(2,1)} %bitcast.9), channel_id=1, source_target_pairs={{0,8},{4,12},{8,0},{12,4},{16,24},{20,28},{24,16},{28,20},{1,9},{5... | collective-permute-start | bytes 393224 | tf_op jit(solution)/shard_map/ppermute | solution.py:20
  10.2 1.5 %collective-permute-start.2 = (bf16[64,1024]{1,0:T(8,128)(2,1)S(1)}, bf16[64,1024]{1,0:T(8,128)(2,1)S(1)}, u32[]{:S(2)}, u32[]{:S(2)}) collective-permute-start(bf16[64,1024]{1,0:T(8,128)(2,1)S(1)} %bitcast.10), channel_id=1, source_target_pairs={{0,4},{4,0},{8,12},{12,8},{16,20},{20,16},{24,28},{28,24},{1,5},{5... | collective-permute-start | bytes 393224 | tf_op jit(solution)/shard_map/ppermute | solution.py:20
  11.2 1.3 %collective-permute-start.8 = (bf16[64,1024]{1,0:T(8,128)(2,1)S(1)}, bf16[64,1024]{1,0:T(8,128)(2,1)S(1)}, u32[]{:S(2)}, u32[]{:S(2)}) collective-permute-start(bf16[64,1024]{1,0:T(8,128)(2,1)S(1)} %collective-permute-done.7.refs_6_), channel_id=1, source_target_pairs={{0,4},{4,0},{8,12},{12,8},{16,20},{20,16},{24,28},{28,24},{1,5},{5... | collective-permute-start | bytes 393224 | tf_op jit(solution)/shard_map/ppermute | solution.py:20
  11.4 1.3 %collective-permute-start.6 = (bf16[64,1024]{1,0:T(8,128)(2,1)S(1)}, bf16[64,1024]{1,0:T(8,128)(2,1)S(1)}, u32[]{:S(2)}, u32[]{:S(2)}) collective-permute-start(bf16[64,1024]{1,0:T(8,128)(2,1)S(1)} %collective-permute-done.5.refs_4_), channel_id=1, source_target_pairs={{0,4},{4,0},{8,12},{12,8},{16,20},{20,16},{24,28},{28,24},{1,5},{5... | collective-permute-start | bytes 393224 | tf_op jit(solution)/shard_map/ppermute | solution.py:20
  11.7 1.3 %collective-permute-start.4 = (bf16[64,1024]{1,0:T(8,128)(2,1)S(1)}, bf16[64,1024]{1,0:T(8,128)(2,1)S(1)}, u32[]{:S(2)}, u32[]{:S(2)}) collective-permute-start(bf16[64,1024]{1,0:T(8,128)(2,1)S(1)} %collective-permute-done.3.refs_2_), channel_id=1, source_target_pairs={{0,4},{4,0},{8,12},{12,8},{16,20},{20,16},{24,28},{28,24},{1,5},{5... | collective-permute-start | bytes 393224 | tf_op jit(solution)/shard_map/ppermute | solution.py:20
  32.4 3.8 %collective-permute-start.9 = (f32[32,128]{1,0:T(8,128)S(1)}, f32[32,128]{1,0:T(8,128)S(1)}, u32[]{:S(2)}, u32[]{:S(2)}) collective-permute-start(f32[32,128]{1,0:T(8,128)S(1)} %get-tuple-element.20), channel_id=1, source_target_pairs={{0,8},{4,12},{8,0},{12,4},{16,24},{20,28},{24,16},{28,20},{1,9},{5... | collective-permute-start | bytes 49160 | tf_op jit(solution)/shard_map/ppermute | solution.py:20
  34.4 3.7 %collective-permute-start.10 = (f32[32,128]{1,0:T(8,128)S(1)}, f32[32,128]{1,0:T(8,128)S(1)}, u32[]{:S(2)}, u32[]{:S(2)}) collective-permute-start(f32[32,128]{1,0:T(8,128)S(1)} %get-tuple-element.21), channel_id=1, source_target_pairs={{0,16},{4,20},{8,24},{12,28},{16,0},{20,4},{24,8},{28,12},{1,17},{... | collective-permute-start | bytes 49160 | tf_op jit(solution)/shard_map/ppermute | solution.py:20
  35.9 4.6 %collective-permute-start.11 = (f32[32,128]{1,0:T(8,128)S(1)}, f32[32,128]{1,0:T(8,128)S(1)}, u32[]{:S(2)}, u32[]{:S(2)}) collective-permute-start(f32[32,128]{1,0:T(8,128)S(1)} %get-tuple-element.22), channel_id=1, source_target_pairs={{0,24},{4,28},{8,16},{12,20},{16,8},{20,12},{24,0},{28,4},{1,25},{... | collective-permute-start | bytes 49160 | tf_op jit(solution)/shard_map/ppermute | solution.py:20

commit v16 on v15

--- a/solution.py
+++ b/solution.py
@@ -13,7 +13,7 @@
 SIDE = 256
 SUBLANES = 8
 DEPTH = 16
-LIMIT = 40 * 1024 * 1024
+LIMIT = 24 * 1024 * 1024
 
 
 def flipped(x, axis, mask):
@@ -62,34 +62,85 @@
     rows_ref[...] = half * (spread * height) + at_row
 
 
+def gather(parties, scale, outs, table, index_ref, rows_hbm, out_refs, scratch):
+    result, rows_even, rows_odd, rows_sems, *picked = scratch
+    me = lax.axis_index("param")
+    share = index_ref.shape[0] // parties
+    groups = share * len(outs)
+    depth = len(picked)
+    last = groups // depth - 1
+    singles = table.reshape(table.shape[0], 1, LANES)
+    sub_at = lax.broadcasted_iota(jnp.int32, (LANES, LANES), 0)
+
+    def start_of(out):
+        return pl.multiple_of((me ^ (2 * out)) * share, share)
+
+    def place(group):
+        return start_of(outs[0] + group // share) + group % share
+
+    def fetched(batch, half):
+        start = pl.multiple_of(place(jnp.minimum(batch, last) * depth), depth)
+        target = (rows_even, rows_odd)[half]
+        return pltpu.make_async_copy(rows_hbm.at[pl.ds(start, depth), :], target, rows_sems.at[half])
+
+    def choose(group, rows):
+        lane = index_ref[pl.ds(place(group), 1), :] & (LANES - 1)
+        chosen = jnp.where(sub_at == lane, rows[...].T, 0.0)
+        result[pl.ds(group, 1), :] = jnp.sum(chosen, axis=0, keepdims=True)
+
+    def step(at, carry):
+        for half, rows_ref in enumerate((rows_even, rows_odd)):
+            batch = 2 * at + half
+            first_group = jnp.minimum(batch, last) * depth
+            fetched(batch, half).wait()
+            for slot in range(depth):
+                before = jnp.maximum(batch * depth - 1, 0) if slot == 0 else first_group + slot - 1
+                choose(before, picked[slot - 1])
+                for first in range(0, LANES, SUBLANES):
+                    at_rows = [rows_ref[slot, first + k] for k in range(SUBLANES)]
+                    lines = [jnp.broadcast_to(singles[row], (SUBLANES, LANES)) for row in at_rows]
+                    merged = lines[0]
+                    for k in range(1, SUBLANES):
+                        merged = jnp.where(sub_at[:SUBLANES] == k, lines[k], merged)
+                    picked[slot][first : first + SUBLANES, :] = merged
+            fetched(batch + 2, half).start()
+        return carry
+
+    def begin():
+        fetched(0, 0).start()
+        fetched(1, 1).start()
+
+    def finish():
+        lax.fori_loop(0, (last + 2) // 2, step, 0)
+        for half in range(2):
+            fetched(last, half).wait()
+        choose(groups - 1, picked[-1])
+        bits = ((table.shape[0] - SUBLANES) // 2 * LANES).bit_length() - 1
+        for at, (out, out_ref) in enumerate(zip(outs, out_refs)):
+            owner = index_ref[pl.ds(start_of(out), share), :] >> bits
+            sign = (1 - 2 * parity(owner & me, parties.bit_length() - 1)).astype(jnp.float32)
+            out_ref[...] = result[at * share : (at + 1) * share, :] * (sign * scale)
+
+    return begin, finish
+
+
+def own_kernel(parties, scale, table, index_ref, rows_hbm, out_ref, *scratch):
+    begin, finish = gather(parties, scale, [0], table, index_ref, rows_hbm, [out_ref], scratch)
+    begin()
+    finish()
+
+
 def sketch_kernel(parties, scale, own_turned, own_signs, other_acts, other_signs, index_ref, rows_hbm, *refs):
-    outs = parties // 2
-    chunk_refs, out_refs, scratch = refs[:parties], refs[parties : parties + outs], refs[parties + outs :]
-    table, cots, other_turned, total, change, result, rows_even, rows_odd, rows_sems, *picked = scratch
+    outs = list(range(1, parties // 2))
+    chunk_refs, table, refs = refs[:parties], refs[parties], refs[parties + 1 :]
+    out_refs, scratch = refs[: len(outs)], refs[len(outs) :]
+    cots, other_turned, total, change, *scratch = scratch
     me = lax.axis_index("param")
     height, breadth = total.shape
     spread = breadth // LANES
     tokens = chunk_refs[0].shape[0]
-    share = index_ref.shape[0] // parties
-
-    def start_of(out):
-        return pl.multiple_of((me ^ (2 * out)) * share, share)
-
-    groups = share * outs
-    depth = len(picked)
-    last = groups // depth - 1
-
-    def fetch(batch):
-        group = jnp.minimum(batch, last) * depth
-        start = pl.multiple_of(start_of(group // share) + group % share, depth)
-        return pl.ds(start, depth)
-
-    def fetched(batch, parity_at):
-        target = (rows_even, rows_odd)[parity_at]
-        return pltpu.make_async_copy(rows_hbm.at[fetch(batch), :], target, rows_sems.at[parity_at])
-
-    fetched(0, 0).start()
-    fetched(1, 1).start()
+    begin, finish = gather(parties, scale, outs, table, index_ref, rows_hbm, out_refs, scratch)
+    begin()
 
     for distance in range(parties):
         start = pl.multiple_of((me ^ distance) * tokens, tokens)
@@ -125,41 +176,7 @@
                     at = (half * spread + col * pieces + piece) * height + row * SIDE
                     table[at : at + SIDE, :] = done[:, piece * LANES : (piece + 1) * LANES]
 
-    singles = table.reshape(table.shape[0], 1, LANES)
-    sub_at = lax.broadcasted_iota(jnp.int32, (LANES, LANES), 0)
-
-    def choose(group, rows):
-        lane = index_ref[pl.ds(start_of(group // share) + group % share, 1), :] & (LANES - 1)
-        chosen = jnp.where(sub_at == lane, rows[...].T, 0.0)
-        result[pl.ds(group, 1), :] = jnp.sum(chosen, axis=0, keepdims=True)
-
-    def step(at, carry):
-        for half, rows_ref in enumerate((rows_even, rows_odd)):
-            batch = 2 * at + half
-            fetched(batch, half).wait()
-            for slot in range(depth):
-                group = batch * depth + slot
-                choose(jnp.maximum(group - 1, 0), picked[slot - 1])
-                for first in range(0, LANES, SUBLANES):
-                    at_rows = [rows_ref[slot, first + k] for k in range(SUBLANES)]
-                    lines = [jnp.broadcast_to(singles[row], (SUBLANES, LANES)) for row in at_rows]
-                    merged = lines[0]
-                    for k in range(1, SUBLANES):
-                        merged = jnp.where(sub_at[:SUBLANES] == k, lines[k], merged)
-                    picked[slot][first : first + SUBLANES, :] = merged
-            fetched(batch + 2, half).start()
-        return carry
-
-    lax.fori_loop(0, groups // depth // 2, step, 0)
-    for half in range(2):
-        fetched(last, half).wait()
-    choose(groups - 1, picked[-1])
-
-    bits = (height * breadth).bit_length() - 1
-    for out, out_ref in enumerate(out_refs):
-        owner = index_ref[pl.ds(start_of(out), share), :] >> bits
-        sign = (1 - 2 * parity(owner & me, parties.bit_length() - 1)).astype(jnp.float32)
-        out_ref[...] = result[out * share : (out + 1) * share, :] * (sign * scale)
+    finish()
 
 
 def on_device(activations, cotangents, signs, indices):
@@ -208,23 +225,30 @@
     for distance in range(0, parties, 2):
         chunks[distance + 1] = flipped(chunks[distance], "param", 1)
 
-    sums = pl.pallas_call(
-        functools.partial(sketch_kernel, parties, 1.0 / math.sqrt(height * breadth * parties)),
-        out_shape=[jax.ShapeDtypeStruct((groups // parties, LANES), jnp.float32)] * outs,
-        in_specs=[vmem] * 5 + [pl.BlockSpec(memory_space=pl.ANY)] + [vmem] * parties,
+    scale = 1.0 / math.sqrt(height * breadth * parties)
+    block = jax.ShapeDtypeStruct((groups // parties, LANES), jnp.float32)
+    any_place = pl.BlockSpec(memory_space=pl.ANY)
+
+    def gather_scratch(blocks):
+        return [
+            pltpu.VMEM((blocks * (groups // parties), LANES), jnp.float32),
+            pltpu.SMEM((depth, LANES), jnp.int32),
+            pltpu.SMEM((depth, LANES), jnp.int32),
+            pltpu.SemaphoreType.DMA((2,)),
+        ] + [pltpu.VMEM((LANES, LANES), jnp.float32)] * depth
+
+    table, *sums = pl.pallas_call(
+        functools.partial(sketch_kernel, parties, scale),
+        out_shape=[jax.ShapeDtypeStruct((2 * table_rows + SUBLANES, LANES), jnp.float32)] + [block] * (outs - 1),
+        in_specs=[vmem] * 5 + [any_place] + [vmem] * parties,
         out_specs=[vmem] * outs,
         scratch_shapes=[
-            pltpu.VMEM((2 * table_rows + SUBLANES, LANES), jnp.float32),
             pltpu.VMEM((tokens, breadth), jnp.bfloat16),
             pltpu.VMEM((height, tokens), jnp.bfloat16),
             pltpu.VMEM((height, breadth), jnp.float32),
             pltpu.VMEM((height, breadth), jnp.float32),
-            pltpu.VMEM((groups // 2, LANES), jnp.float32),
-            pltpu.SMEM((depth, LANES), jnp.int32),
-            pltpu.SMEM((depth, LANES), jnp.int32),
-            pltpu.SemaphoreType.DMA((2,)),
         ]
-        + [pltpu.VMEM((LANES, LANES), jnp.float32)] * depth,
+        + gather_scratch(outs - 1),
         compiler_params=pltpu.CompilerParams(vmem_limit_bytes=LIMIT),
         name="sketch",
     )(
@@ -236,10 +260,19 @@
         rows,
         *[chunks[d] for d in range(parties)],
     )
-
-    total = sums[0]
+    total = pl.pallas_call(
+        functools.partial(own_kernel, parties, scale),
+        out_shape=block,
+        in_specs=[vmem, vmem, any_place],
+        out_specs=vmem,
+        scratch_shapes=gather_scratch(1),
+        compiler_params=pltpu.CompilerParams(vmem_limit_bytes=LIMIT),
+        cost_estimate=pl.CostEstimate(flops=0, bytes_accessed=8 * height * breadth, transcendentals=0),
+        name="own",
+    )(table, index_rows, rows)
+
     for out in range(1, outs):
-        total = total + flipped(sums[out], "param", 2 * out)
+        total = total + flipped(sums[out - 1], "param", 2 * out)
     return total.reshape(1, samples // parties)
 
 

time: 41.3 us -> 39 us (0.944)
  waiting for transfers between devices: 6.79 us -> 3.06 us
  Pallas kernels: 24.5 us -> 25.9 us
    ppermute x12, waiting for transfers between devices: 6.79 us -> 3.06 us  [flipped(): lax.ppermute(x, axis, [(i, i ^ mask) for i in range(lax.axis_size(axis))])]
    pallas_call x1 -> x2, Pallas kernels: 19.4 us -> 20.8 us  [the longest x1 17 us: on_device(): pl.pallas_call(functools.partial(sketch_kernel, parties, scale), out_shap...]
  transfers between devices with their start and end apart: 12 -> 12, of which waited for: 8 -> 6; matrix products, arithmetic and copies ran while one was open for 0% -> 0% of each run, Pallas kernels for 13% -> 23%
where the time goes in v16:
time: 39 us; the launch traced here: 38.8 us
  Pallas kernels  25.9 us (66%)
  starting transfers between devices  9.12 us (23%)
  waiting for transfers between devices  3.06 us (8%)
  other arithmetic  0.61 us (2%)
    pallas_call x1, Pallas kernels, on_device(): pl.pallas_call(functools.partial(sketch_kernel, parties, scale), out_shap...  17 us
    ppermute x12, starting transfers between devices, flipped(): lax.ppermute(x, axis, [(i, i ^ mask) for i in range(lax.axis_size(axis))])  9.12 us
    pallas_call x1, Pallas kernels, on_device(): pl.pallas_call(prepare_kernel, grid=(steps,), out_shape=[jax.ShapeDtypeSt...  5.18 us
    pallas_call x1, Pallas kernels, on_device(): pl.pallas_call(functools.partial(own_kernel, parties, scale), out_shape=b...  3.71 us
    ppermute x12, waiting for transfers between devices, flipped(): lax.ppermute(x, axis, [(i, i ^ mask) for i in range(lax.axis_size(axis))])  3.06 us
  transfers between devices with their start and end apart: 12, of which 6 were waited for; matrix products, arithmetic and copies ran while one was open for 0% of the time, Pallas kernels for 23%

profile of v16, /device:TPU:0, one launch (start us, length us, event | category | flops | bytes accessed | tf_op | source)
XLA Modules:
  0.0 38.8 jit_solution(10656049743611781908)
XLA Ops:
  0.0 0.5 %collective-permute-start.1 = (s32[8192,128]{1,0:T(8,128)}, s32[8192,128]{1,0:T(8,128)S(1)}, u32[]{:S(2)}, u32[]{:S(2)}) collective-permute-start(s32[8192,128]{1,0:T(8,128)} %bitcast.13), channel_id=1, source_target_pairs={{0,4},{4,0},{8,12},{12,8},{16,20},{20,16},{24,28},{28,24},{1,5},{5... | collective-permute-start | bytes 12582920 | tf_op jit(solution)/shard_map/ppermute | solution.py:20
  0.5 0.1 collective-permute-start
  0.5 3.9 %collective-permute-start.7 = (bf16[64,1024]{1,0:T(8,128)(2,1)}, bf16[64,1024]{1,0:T(8,128)(2,1)S(1)}, u32[]{:S(2)}, u32[]{:S(2)}) collective-permute-start(bf16[64,1024]{1,0:T(8,128)(2,1)} %bitcast.8), channel_id=1, source_target_pairs={{0,24},{4,28},{8,16},{12,20},{16,8},{20,12},{24,0},{28,4},{1,25},{... | collective-permute-start | bytes 393224 | tf_op jit(solution)/shard_map/ppermute | solution.py:20
  4.4 0.5 %collective-permute-start.5 = (bf16[64,1024]{1,0:T(8,128)(2,1)}, bf16[64,1024]{1,0:T(8,128)(2,1)S(1)}, u32[]{:S(2)}, u32[]{:S(2)}) collective-permute-start(bf16[64,1024]{1,0:T(8,128)(2,1)} %bitcast.9), channel_id=1, source_target_pairs={{0,16},{4,20},{8,24},{12,28},{16,0},{20,4},{24,8},{28,12},{1,17},{... | collective-permute-start | bytes 393224 | tf_op jit(solution)/shard_map/ppermute | solution.py:20
  4.9 0.1 collective-permute-start.3
  5.0 5.2 %prepare.1 = (bf16[1024,512]{1,0:T(8,128)(2,1)S(1)}, bf16[1024,1024]{1,0:T(8,128)(2,1)S(1)}, s32[256,128]{1,0:T(8,128)S(1)}) custom-call(bf16[512,1024]{1,0:T(8,128)(2,1)} %bitcast.16, s32[8192,128]{1,0:T(8,128)} %bitcast.14, s32[256,128]{1,0:T(8,128)} %bitcast.5), custom_call_target="tpu_custom_call" | custom-call | bytes 8388608 | tf_op jit(solution)/shard_map/prepare/pallas_call | solution.py:202
  10.2 0.0 collective-permute-done.7.refs_6_
  10.2 0.1 collective-permute-start.2
  10.3 0.9 %collective-permute-done.5.refs_4_ = bf16[64,1024]{1,0:T(8,128)(2,1)S(1)} collective-permute-done((bf16[64,1024]{1,0:T(8,128)(2,1)}, bf16[64,1024]{1,0:T(8,128)(2,1)S(1)}, u32[]{:S(2)}, u32[]{:S(2)}) %collective-permute-start.5) | collective-permute-done | bytes 131104 | tf_op jit(solution)/shard_map/ppermute | solution.py:20
  11.2 0.0 collective-permute-start.8
  11.2 0.3 collective-permute-done.3.refs_2_
  11.4 0.2 collective-permute-start.6
  11.7 0.3 collective-permute-start.4
  12.0 0.6 %collective-permute-done.8.refs_7_ = bf16[64,1024]{1,0:T(8,128)(2,1)S(1)} collective-permute-done((bf16[64,1024]{1,0:T(8,128)(2,1)S(1)}, bf16[64,1024]{1,0:T(8,128)(2,1)S(1)}, u32[]{:S(2)}, u32[]{:S(2)}) %collective-permute-start.8) | collective-permute-done | bytes 131104 | tf_op jit(solution)/shard_map/ppermute | solution.py:20
  12.5 0.3 collective-permute-done.6.refs_5_
  12.8 0.2 collective-permute-done.4.refs_3_
  13.0 0.0 collective-permute-done.other_acts
  13.0 17.0 %sketch.1 = (f32[16392,128]{1,0:T(8,128)S(1)}, f32[32,128]{1,0:T(8,128)S(1)}, f32[32,128]{1,0:T(8,128)S(1)}, f32[32,128]{1,0:T(8,128)S(1)}) custom-call(bf16[1024,512]{1,0:T(8,128)(2,1)S(1)} %get-tuple-element.14.own_turned, bf16[1024,1024]{1,0:T(8,128)(2,1)S(1)} %get-tuple-element.15.own_signs, bf16[512,1024]{1,0:T(8,128)(2,1)S(1)} %collective-permute-done.other_acts, ...), custom_call_target="tpu_custom_call" | custom-call | tf_op jit(solution)/shard_map/sketch/pallas_call | solution.py:240
  30.1 1.9 %collective-permute-start.9 = (f32[32,128]{1,0:T(8,128)S(1)}, f32[32,128]{1,0:T(8,128)S(1)}, u32[]{:S(2)}, u32[]{:S(2)}) collective-permute-start(f32[32,128]{1,0:T(8,128)S(1)} %get-tuple-element.20), channel_id=1, source_target_pairs={{0,8},{4,12},{8,0},{12,4},{16,24},{20,28},{24,16},{28,20},{1,9},{5... | collective-permute-start | bytes 49160 | tf_op jit(solution)/shard_map/ppermute | solution.py:20
  32.0 1.5 %collective-permute-start.10 = (f32[32,128]{1,0:T(8,128)S(1)}, f32[32,128]{1,0:T(8,128)S(1)}, u32[]{:S(2)}, u32[]{:S(2)}) collective-permute-start(f32[32,128]{1,0:T(8,128)S(1)} %get-tuple-element.21), channel_id=1, source_target_pairs={{0,16},{4,20},{8,24},{12,28},{16,0},{20,4},{24,8},{28,12},{1,17},{... | collective-permute-start | bytes 49160 | tf_op jit(solution)/shard_map/ppermute | solution.py:20
  33.6 0.1 collective-permute-start.11
  33.6 3.7 %own.1 = f32[32,128]{1,0:T(8,128)S(1)} custom-call(f32[16392,128]{1,0:T(8,128)S(1)} %get-tuple-element.19.table, s32[256,128]{1,0:T(8,128)S(1)} %bitcast.7, s32[256,128]{1,0:T(8,128)S(1)} %get-tuple-element.17.rows_hbm), custom_call_target="tpu_custom_call" | custom-call | bytes 8388608 | tf_op jit(solution)/shard_map/own/pallas_call | solution.py:263
  37.4 0.8 %collective-permute-done.11 = f32[32,128]{1,0:T(8,128)S(1)} collective-permute-done((f32[32,128]{1,0:T(8,128)S(1)}, f32[32,128]{1,0:T(8,128)S(1)}, u32[]{:S(2)}, u32[]{:S(2)}) %collective-permute-start.11) | collective-permute-done | bytes 16416 | tf_op jit(solution)/shard_map/ppermute | solution.py:20
  38.2 0.6 %add_add_fusion = f32[32,128]{1,0:T(8,128)} fusion(f32[32,128]{1,0:T(8,128)S(1)} %collective-permute-done.11, f32[32,128]{1,0:T(8,128)S(1)} %collective-permute-done.10, f32[32,128]{1,0:T(8,128)S(1)} %own.1, f32[32,128]{1,0:T(8,128)S(1)} %collective-permute-done.9), kind=kLoop, calls=%fused_computation | loop fusion | flops 12288 | bytes 81920 | tf_op jit(solution)/shard_map/add | solution.py:275
  (8 shorter events, 0.0 us)
Async XLA Ops:
  0.0 10.2 %copy-start.1 = (bf16[1,64,1024]{2,1,0:T(8,128)(2,1)S(1)}, bf16[1,64,1024]{2,1,0:T(8,128)(2,1)}, u32[]{:S(2)}) copy-start(bf16[1,64,1024]{2,1,0:T(8,128)(2,1)} %param.5) | copy-start | bytes 393220
  0.0 13.0 %copy-start = (s32[32768]{0:T(1024)S(1)}, s32[32768]{0:T(1024)}, u32[]{:S(2)}) copy-start(s32[32768]{0:T(1024)} %param.7) | copy-start | bytes 393220
  0.0 13.0 %collective-permute-start.1 = (s32[8192,128]{1,0:T(8,128)}, s32[8192,128]{1,0:T(8,128)S(1)}, u32[]{:S(2)}, u32[]{:S(2)}) collective-permute-start(s32[8192,128]{1,0:T(8,128)} %bitcast.13), channel_id=1, source_target_pairs={{0,4},{4,0},{8,12},{12,8},{16,20},{20,16},{24,28},{28,24},{1,5},{5... | collective-permute-start | bytes 12582920 | tf_op jit(solution)/shard_map/ppermute | solution.py:20
  0.5 12.6 %collective-permute-start = (bf16[512,1024]{1,0:T(8,128)(2,1)}, bf16[512,1024]{1,0:T(8,128)(2,1)S(1)}, u32[]{:S(2)}, u32[]{:S(2)}) collective-permute-start(bf16[512,1024]{1,0:T(8,128)(2,1)} %bitcast.15), channel_id=1, source_target_pairs={{0,4},{4,0},{8,12},{12,8},{16,20},{20,16},{24,28},{28,24},{1,5},{5... | collective-permute-start | bytes 3145736 | tf_op jit(solution)/shard_map/ppermute | solution.py:20
  0.5 9.6 %collective-permute-start.7 = (bf16[64,1024]{1,0:T(8,128)(2,1)}, bf16[64,1024]{1,0:T(8,128)(2,1)S(1)}, u32[]{:S(2)}, u32[]{:S(2)}) collective-permute-start(bf16[64,1024]{1,0:T(8,128)(2,1)} %bitcast.8), channel_id=1, source_target_pairs={{0,24},{4,28},{8,16},{12,20},{16,8},{20,12},{24,0},{28,4},{1,25},{... | collective-permute-start | bytes 393224 | tf_op jit(solution)/shard_map/ppermute | solution.py:20
  4.4 6.8 %collective-permute-start.5 = (bf16[64,1024]{1,0:T(8,128)(2,1)}, bf16[64,1024]{1,0:T(8,128)(2,1)S(1)}, u32[]{:S(2)}, u32[]{:S(2)}) collective-permute-start(bf16[64,1024]{1,0:T(8,128)(2,1)} %bitcast.9), channel_id=1, source_target_pairs={{0,16},{4,20},{8,24},{12,28},{16,0},{20,4},{24,8},{28,12},{1,17},{... | collective-permute-start | bytes 393224 | tf_op jit(solution)/shard_map/ppermute | solution.py:20
  4.9 6.5 %collective-permute-start.3 = (bf16[64,1024]{1,0:T(8,128)(2,1)}, bf16[64,1024]{1,0:T(8,128)(2,1)S(1)}, u32[]{:S(2)}, u32[]{:S(2)}) collective-permute-start(bf16[64,1024]{1,0:T(8,128)(2,1)} %bitcast.10), channel_id=1, source_target_pairs={{0,8},{4,12},{8,0},{12,4},{16,24},{20,28},{24,16},{28,20},{1,9},{5... | collective-permute-start | bytes 393224 | tf_op jit(solution)/shard_map/ppermute | solution.py:20
  10.2 1.5 %collective-permute-start.2 = (bf16[64,1024]{1,0:T(8,128)(2,1)S(1)}, bf16[64,1024]{1,0:T(8,128)(2,1)S(1)}, u32[]{:S(2)}, u32[]{:S(2)}) collective-permute-start(bf16[64,1024]{1,0:T(8,128)(2,1)S(1)} %bitcast.11), channel_id=1, source_target_pairs={{0,4},{4,0},{8,12},{12,8},{16,20},{20,16},{24,28},{28,24},{1,5},{5... | collective-permute-start | bytes 393224 | tf_op jit(solution)/shard_map/ppermute | solution.py:20
  11.2 1.3 %collective-permute-start.8 = (bf16[64,1024]{1,0:T(8,128)(2,1)S(1)}, bf16[64,1024]{1,0:T(8,128)(2,1)S(1)}, u32[]{:S(2)}, u32[]{:S(2)}) collective-permute-start(bf16[64,1024]{1,0:T(8,128)(2,1)S(1)} %collective-permute-done.7.refs_6_), channel_id=1, source_target_pairs={{0,4},{4,0},{8,12},{12,8},{16,20},{20,16},{24,28},{28,24},{1,5},{5... | collective-permute-start | bytes 393224 | tf_op jit(solution)/shard_map/ppermute | solution.py:20
  11.4 1.3 %collective-permute-start.6 = (bf16[64,1024]{1,0:T(8,128)(2,1)S(1)}, bf16[64,1024]{1,0:T(8,128)(2,1)S(1)}, u32[]{:S(2)}, u32[]{:S(2)}) collective-permute-start(bf16[64,1024]{1,0:T(8,128)(2,1)S(1)} %collective-permute-done.5.refs_4_), channel_id=1, source_target_pairs={{0,4},{4,0},{8,12},{12,8},{16,20},{20,16},{24,28},{28,24},{1,5},{5... | collective-permute-start | bytes 393224 | tf_op jit(solution)/shard_map/ppermute | solution.py:20
  11.7 1.3 %collective-permute-start.4 = (bf16[64,1024]{1,0:T(8,128)(2,1)S(1)}, bf16[64,1024]{1,0:T(8,128)(2,1)S(1)}, u32[]{:S(2)}, u32[]{:S(2)}) collective-permute-start(bf16[64,1024]{1,0:T(8,128)(2,1)S(1)} %collective-permute-done.3.refs_2_), channel_id=1, source_target_pairs={{0,4},{4,0},{8,12},{12,8},{16,20},{20,16},{24,28},{28,24},{1,5},{5... | collective-permute-start | bytes 393224 | tf_op jit(solution)/shard_map/ppermute | solution.py:20
  30.1 7.3 %collective-permute-start.9 = (f32[32,128]{1,0:T(8,128)S(1)}, f32[32,128]{1,0:T(8,128)S(1)}, u32[]{:S(2)}, u32[]{:S(2)}) collective-permute-start(f32[32,128]{1,0:T(8,128)S(1)} %get-tuple-element.20), channel_id=1, source_target_pairs={{0,8},{4,12},{8,0},{12,4},{16,24},{20,28},{24,16},{28,20},{1,9},{5... | collective-permute-start | bytes 49160 | tf_op jit(solution)/shard_map/ppermute | solution.py:20
  32.0 5.3 %collective-permute-start.10 = (f32[32,128]{1,0:T(8,128)S(1)}, f32[32,128]{1,0:T(8,128)S(1)}, u32[]{:S(2)}, u32[]{:S(2)}) collective-permute-start(f32[32,128]{1,0:T(8,128)S(1)} %get-tuple-element.21), channel_id=1, source_target_pairs={{0,16},{4,20},{8,24},{12,28},{16,0},{20,4},{24,8},{28,12},{1,17},{... | collective-permute-start | bytes 49160 | tf_op jit(solution)/shard_map/ppermute | solution.py:20
  33.6 4.6 %collective-permute-start.11 = (f32[32,128]{1,0:T(8,128)S(1)}, f32[32,128]{1,0:T(8,128)S(1)}, u32[]{:S(2)}, u32[]{:S(2)}) collective-permute-start(f32[32,128]{1,0:T(8,128)S(1)} %get-tuple-element.22), channel_id=1, source_target_pairs={{0,24},{4,28},{8,16},{12,20},{16,8},{20,12},{24,0},{28,4},{1,25},{... | collective-permute-start | bytes 49160 | tf_op jit(solution)/shard_map/ppermute | solution.py:20

commit v17 on v16

--- a/solution.py
+++ b/solution.py
@@ -169,9 +169,11 @@
         for row in range(row_blocks):
             rows = slice(row * SIDE, (row + 1) * SIDE)
             parts = butterfly([signed[rows, col * SIDE : (col + 1) * SIDE] for col in range(col_blocks)])
+            stacked = jnp.concatenate(parts, axis=0)
+            high, low = split(dot(jnp.concatenate(split(stacked), axis=1), tall))
             for col in range(col_blocks):
-                half_done = dot(jnp.concatenate(split(parts[col]), axis=1), tall)
-                done = dot(wide, jnp.concatenate(split(half_done), axis=0))
+                block = slice(col * SIDE, (col + 1) * SIDE)
+                done = dot(wide, jnp.concatenate([high[block], low[block]], axis=0))
                 for piece in range(pieces):
                     at = (half * spread + col * pieces + piece) * height + row * SIDE
                     table[at : at + SIDE, :] = done[:, piece * LANES : (piece + 1) * LANES]

time: 39 us -> 39.3 us (level)
  no operation moved by 1% of the time
where the time goes in v17:
time: 39.3 us; the launch traced here: 39.1 us
  Pallas kernels  26.2 us (67%)
  starting transfers between devices  9.12 us (23%)
  waiting for transfers between devices  3.06 us (8%)
  other arithmetic  0.61 us (2%)
    pallas_call x1, Pallas kernels, on_device(): pl.pallas_call(functools.partial(sketch_kernel, parties, scale), out_shap...  17.3 us
    ppermute x12, starting transfers between devices, flipped(): lax.ppermute(x, axis, [(i, i ^ mask) for i in range(lax.axis_size(axis))])  9.12 us
    pallas_call x1, Pallas kernels, on_device(): pl.pallas_call(prepare_kernel, grid=(steps,), out_shape=[jax.ShapeDtypeSt...  5.18 us
    pallas_call x1, Pallas kernels, on_device(): pl.pallas_call(functools.partial(own_kernel, parties, scale), out_shape=b...  3.71 us
    ppermute x12, waiting for transfers between devices, flipped(): lax.ppermute(x, axis, [(i, i ^ mask) for i in range(lax.axis_size(axis))])  3.06 us
  transfers between devices with their start and end apart: 12, of which 6 were waited for; matrix products, arithmetic and copies ran while one was open for 0% of the time, Pallas kernels for 23%

profile of v17, /device:TPU:0, one launch (start us, length us, event | category | flops | bytes accessed | tf_op | source)
XLA Modules:
  0.0 39.1 jit_solution(18285235275355832443)
XLA Ops:
  0.0 0.5 %collective-permute-start.1 = (s32[8192,128]{1,0:T(8,128)}, s32[8192,128]{1,0:T(8,128)S(1)}, u32[]{:S(2)}, u32[]{:S(2)}) collective-permute-start(s32[8192,128]{1,0:T(8,128)} %bitcast.13), channel_id=1, source_target_pairs={{0,4},{4,0},{8,12},{12,8},{16,20},{20,16},{24,28},{28,24},{1,5},{5... | collective-permute-start | bytes 12582920 | tf_op jit(solution)/shard_map/ppermute | solution.py:20
  0.5 0.1 collective-permute-start
  0.5 3.9 %collective-permute-start.7 = (bf16[64,1024]{1,0:T(8,128)(2,1)}, bf16[64,1024]{1,0:T(8,128)(2,1)S(1)}, u32[]{:S(2)}, u32[]{:S(2)}) collective-permute-start(bf16[64,1024]{1,0:T(8,128)(2,1)} %bitcast.8), channel_id=1, source_target_pairs={{0,24},{4,28},{8,16},{12,20},{16,8},{20,12},{24,0},{28,4},{1,25},{... | collective-permute-start | bytes 393224 | tf_op jit(solution)/shard_map/ppermute | solution.py:20
  4.4 0.5 %collective-permute-start.5 = (bf16[64,1024]{1,0:T(8,128)(2,1)}, bf16[64,1024]{1,0:T(8,128)(2,1)S(1)}, u32[]{:S(2)}, u32[]{:S(2)}) collective-permute-start(bf16[64,1024]{1,0:T(8,128)(2,1)} %bitcast.9), channel_id=1, source_target_pairs={{0,16},{4,20},{8,24},{12,28},{16,0},{20,4},{24,8},{28,12},{1,17},{... | collective-permute-start | bytes 393224 | tf_op jit(solution)/shard_map/ppermute | solution.py:20
  4.9 0.1 collective-permute-start.3
  5.0 5.2 %prepare.1 = (bf16[1024,512]{1,0:T(8,128)(2,1)S(1)}, bf16[1024,1024]{1,0:T(8,128)(2,1)S(1)}, s32[256,128]{1,0:T(8,128)S(1)}) custom-call(bf16[512,1024]{1,0:T(8,128)(2,1)} %bitcast.16, s32[8192,128]{1,0:T(8,128)} %bitcast.14, s32[256,128]{1,0:T(8,128)} %bitcast.5), custom_call_target="tpu_custom_call" | custom-call | bytes 8388608 | tf_op jit(solution)/shard_map/prepare/pallas_call | solution.py:204
  10.2 0.0 collective-permute-done.7.refs_6_
  10.2 0.1 collective-permute-start.2
  10.3 0.9 %collective-permute-done.5.refs_4_ = bf16[64,1024]{1,0:T(8,128)(2,1)S(1)} collective-permute-done((bf16[64,1024]{1,0:T(8,128)(2,1)}, bf16[64,1024]{1,0:T(8,128)(2,1)S(1)}, u32[]{:S(2)}, u32[]{:S(2)}) %collective-permute-start.5) | collective-permute-done | bytes 131104 | tf_op jit(solution)/shard_map/ppermute | solution.py:20
  11.2 0.0 collective-permute-start.8
  11.2 0.3 collective-permute-done.3.refs_2_
  11.4 0.2 collective-permute-start.6
  11.7 0.0 collective-permute-done.2.refs_1_
  11.7 0.3 collective-permute-start.4
  12.0 0.6 %collective-permute-done.8.refs_7_ = bf16[64,1024]{1,0:T(8,128)(2,1)S(1)} collective-permute-done((bf16[64,1024]{1,0:T(8,128)(2,1)S(1)}, bf16[64,1024]{1,0:T(8,128)(2,1)S(1)}, u32[]{:S(2)}, u32[]{:S(2)}) %collective-permute-start.8) | collective-permute-done | bytes 131104 | tf_op jit(solution)/shard_map/ppermute | solution.py:20
  12.5 0.3 collective-permute-done.6.refs_5_
  12.8 0.2 collective-permute-done.4.refs_3_
  13.0 17.3 %sketch.1 = (f32[16392,128]{1,0:T(8,128)S(1)}, f32[32,128]{1,0:T(8,128)S(1)}, f32[32,128]{1,0:T(8,128)S(1)}, f32[32,128]{1,0:T(8,128)S(1)}) custom-call(bf16[1024,512]{1,0:T(8,128)(2,1)S(1)} %get-tuple-element.14.own_turned, bf16[1024,1024]{1,0:T(8,128)(2,1)S(1)} %get-tuple-element.15.own_signs, bf16[512,1024]{1,0:T(8,128)(2,1)S(1)} %collective-permute-done.other_acts, ...), custom_call_target="tpu_custom_call" | custom-call | tf_op jit(solution)/shard_map/sketch/pallas_call | solution.py:242
  30.3 1.9 %collective-permute-start.9 = (f32[32,128]{1,0:T(8,128)S(1)}, f32[32,128]{1,0:T(8,128)S(1)}, u32[]{:S(2)}, u32[]{:S(2)}) collective-permute-start(f32[32,128]{1,0:T(8,128)S(1)} %get-tuple-element.20), channel_id=1, source_target_pairs={{0,8},{4,12},{8,0},{12,4},{16,24},{20,28},{24,16},{28,20},{1,9},{5... | collective-permute-start | bytes 49160 | tf_op jit(solution)/shard_map/ppermute | solution.py:20
  32.3 1.5 %collective-permute-start.10 = (f32[32,128]{1,0:T(8,128)S(1)}, f32[32,128]{1,0:T(8,128)S(1)}, u32[]{:S(2)}, u32[]{:S(2)}) collective-permute-start(f32[32,128]{1,0:T(8,128)S(1)} %get-tuple-element.21), channel_id=1, source_target_pairs={{0,16},{4,20},{8,24},{12,28},{16,0},{20,4},{24,8},{28,12},{1,17},{... | collective-permute-start | bytes 49160 | tf_op jit(solution)/shard_map/ppermute | solution.py:20
  33.8 0.1 collective-permute-start.11
  33.9 3.7 %own.1 = f32[32,128]{1,0:T(8,128)S(1)} custom-call(f32[16392,128]{1,0:T(8,128)S(1)} %get-tuple-element.19.table, s32[256,128]{1,0:T(8,128)S(1)} %bitcast.7, s32[256,128]{1,0:T(8,128)S(1)} %get-tuple-element.17.rows_hbm), custom_call_target="tpu_custom_call" | custom-call | bytes 8388608 | tf_op jit(solution)/shard_map/own/pallas_call | solution.py:265
  37.6 0.8 %collective-permute-done.11 = f32[32,128]{1,0:T(8,128)S(1)} collective-permute-done((f32[32,128]{1,0:T(8,128)S(1)}, f32[32,128]{1,0:T(8,128)S(1)}, u32[]{:S(2)}, u32[]{:S(2)}) %collective-permute-start.11) | collective-permute-done | bytes 16416 | tf_op jit(solution)/shard_map/ppermute | solution.py:20
  38.5 0.6 %add_add_fusion = f32[32,128]{1,0:T(8,128)} fusion(f32[32,128]{1,0:T(8,128)S(1)} %collective-permute-done.11, f32[32,128]{1,0:T(8,128)S(1)} %collective-permute-done.10, f32[32,128]{1,0:T(8,128)S(1)} %own.1, f32[32,128]{1,0:T(8,128)S(1)} %collective-permute-done.9), kind=kLoop, calls=%fused_computation | loop fusion | flops 12288 | bytes 81920 | tf_op jit(solution)/shard_map/add | solution.py:277
  (8 shorter events, 0.0 us)
Async XLA Ops:
  0.0 10.2 %copy-start.1 = (bf16[1,64,1024]{2,1,0:T(8,128)(2,1)S(1)}, bf16[1,64,1024]{2,1,0:T(8,128)(2,1)}, u32[]{:S(2)}) copy-start(bf16[1,64,1024]{2,1,0:T(8,128)(2,1)} %param.5) | copy-start | bytes 393220
  0.0 13.0 %copy-start = (s32[32768]{0:T(1024)S(1)}, s32[32768]{0:T(1024)}, u32[]{:S(2)}) copy-start(s32[32768]{0:T(1024)} %param.7) | copy-start | bytes 393220
  0.0 13.0 %collective-permute-start.1 = (s32[8192,128]{1,0:T(8,128)}, s32[8192,128]{1,0:T(8,128)S(1)}, u32[]{:S(2)}, u32[]{:S(2)}) collective-permute-start(s32[8192,128]{1,0:T(8,128)} %bitcast.13), channel_id=1, source_target_pairs={{0,4},{4,0},{8,12},{12,8},{16,20},{20,16},{24,28},{28,24},{1,5},{5... | collective-permute-start | bytes 12582920 | tf_op jit(solution)/shard_map/ppermute | solution.py:20
  0.5 12.6 %collective-permute-start = (bf16[512,1024]{1,0:T(8,128)(2,1)}, bf16[512,1024]{1,0:T(8,128)(2,1)S(1)}, u32[]{:S(2)}, u32[]{:S(2)}) collective-permute-start(bf16[512,1024]{1,0:T(8,128)(2,1)} %bitcast.15), channel_id=1, source_target_pairs={{0,4},{4,0},{8,12},{12,8},{16,20},{20,16},{24,28},{28,24},{1,5},{5... | collective-permute-start | bytes 3145736 | tf_op jit(solution)/shard_map/ppermute | solution.py:20
  0.5 9.6 %collective-permute-start.7 = (bf16[64,1024]{1,0:T(8,128)(2,1)}, bf16[64,1024]{1,0:T(8,128)(2,1)S(1)}, u32[]{:S(2)}, u32[]{:S(2)}) collective-permute-start(bf16[64,1024]{1,0:T(8,128)(2,1)} %bitcast.8), channel_id=1, source_target_pairs={{0,24},{4,28},{8,16},{12,20},{16,8},{20,12},{24,0},{28,4},{1,25},{... | collective-permute-start | bytes 393224 | tf_op jit(solution)/shard_map/ppermute | solution.py:20
  4.4 6.8 %collective-permute-start.5 = (bf16[64,1024]{1,0:T(8,128)(2,1)}, bf16[64,1024]{1,0:T(8,128)(2,1)S(1)}, u32[]{:S(2)}, u32[]{:S(2)}) collective-permute-start(bf16[64,1024]{1,0:T(8,128)(2,1)} %bitcast.9), channel_id=1, source_target_pairs={{0,16},{4,20},{8,24},{12,28},{16,0},{20,4},{24,8},{28,12},{1,17},{... | collective-permute-start | bytes 393224 | tf_op jit(solution)/shard_map/ppermute | solution.py:20
  4.9 6.5 %collective-permute-start.3 = (bf16[64,1024]{1,0:T(8,128)(2,1)}, bf16[64,1024]{1,0:T(8,128)(2,1)S(1)}, u32[]{:S(2)}, u32[]{:S(2)}) collective-permute-start(bf16[64,1024]{1,0:T(8,128)(2,1)} %bitcast.10), channel_id=1, source_target_pairs={{0,8},{4,12},{8,0},{12,4},{16,24},{20,28},{24,16},{28,20},{1,9},{5... | collective-permute-start | bytes 393224 | tf_op jit(solution)/shard_map/ppermute | solution.py:20
  10.2 1.5 %collective-permute-start.2 = (bf16[64,1024]{1,0:T(8,128)(2,1)S(1)}, bf16[64,1024]{1,0:T(8,128)(2,1)S(1)}, u32[]{:S(2)}, u32[]{:S(2)}) collective-permute-start(bf16[64,1024]{1,0:T(8,128)(2,1)S(1)} %bitcast.11), channel_id=1, source_target_pairs={{0,4},{4,0},{8,12},{12,8},{16,20},{20,16},{24,28},{28,24},{1,5},{5... | collective-permute-start | bytes 393224 | tf_op jit(solution)/shard_map/ppermute | solution.py:20
  11.2 1.3 %collective-permute-start.8 = (bf16[64,1024]{1,0:T(8,128)(2,1)S(1)}, bf16[64,1024]{1,0:T(8,128)(2,1)S(1)}, u32[]{:S(2)}, u32[]{:S(2)}) collective-permute-start(bf16[64,1024]{1,0:T(8,128)(2,1)S(1)} %collective-permute-done.7.refs_6_), channel_id=1, source_target_pairs={{0,4},{4,0},{8,12},{12,8},{16,20},{20,16},{24,28},{28,24},{1,5},{5... | collective-permute-start | bytes 393224 | tf_op jit(solution)/shard_map/ppermute | solution.py:20
  11.4 1.3 %collective-permute-start.6 = (bf16[64,1024]{1,0:T(8,128)(2,1)S(1)}, bf16[64,1024]{1,0:T(8,128)(2,1)S(1)}, u32[]{:S(2)}, u32[]{:S(2)}) collective-permute-start(bf16[64,1024]{1,0:T(8,128)(2,1)S(1)} %collective-permute-done.5.refs_4_), channel_id=1, source_target_pairs={{0,4},{4,0},{8,12},{12,8},{16,20},{20,16},{24,28},{28,24},{1,5},{5... | collective-permute-start | bytes 393224 | tf_op jit(solution)/shard_map/ppermute | solution.py:20
  11.7 1.3 %collective-permute-start.4 = (bf16[64,1024]{1,0:T(8,128)(2,1)S(1)}, bf16[64,1024]{1,0:T(8,128)(2,1)S(1)}, u32[]{:S(2)}, u32[]{:S(2)}) collective-permute-start(bf16[64,1024]{1,0:T(8,128)(2,1)S(1)} %collective-permute-done.3.refs_2_), channel_id=1, source_target_pairs={{0,4},{4,0},{8,12},{12,8},{16,20},{20,16},{24,28},{28,24},{1,5},{5... | collective-permute-start | bytes 393224 | tf_op jit(solution)/shard_map/ppermute | solution.py:20
  30.3 7.3 %collective-permute-start.9 = (f32[32,128]{1,0:T(8,128)S(1)}, f32[32,128]{1,0:T(8,128)S(1)}, u32[]{:S(2)}, u32[]{:S(2)}) collective-permute-start(f32[32,128]{1,0:T(8,128)S(1)} %get-tuple-element.20), channel_id=1, source_target_pairs={{0,8},{4,12},{8,0},{12,4},{16,24},{20,28},{24,16},{28,20},{1,9},{5... | collective-permute-start | bytes 49160 | tf_op jit(solution)/shard_map/ppermute | solution.py:20
  32.3 5.3 %collective-permute-start.10 = (f32[32,128]{1,0:T(8,128)S(1)}, f32[32,128]{1,0:T(8,128)S(1)}, u32[]{:S(2)}, u32[]{:S(2)}) collective-permute-start(f32[32,128]{1,0:T(8,128)S(1)} %get-tuple-element.21), channel_id=1, source_target_pairs={{0,16},{4,20},{8,24},{12,28},{16,0},{20,4},{24,8},{28,12},{1,17},{... | collective-permute-start | bytes 49160 | tf_op jit(solution)/shard_map/ppermute | solution.py:20
  33.8 4.6 %collective-permute-start.11 = (f32[32,128]{1,0:T(8,128)S(1)}, f32[32,128]{1,0:T(8,128)S(1)}, u32[]{:S(2)}, u32[]{:S(2)}) collective-permute-start(f32[32,128]{1,0:T(8,128)S(1)} %get-tuple-element.22), channel_id=1, source_target_pairs={{0,24},{4,28},{8,16},{12,20},{16,8},{20,12},{24,0},{28,4},{1,25},{... | collective-permute-start | bytes 49160 | tf_op jit(solution)/shard_map/ppermute | solution.py:20

commit v18 on v16

--- a/solution.py
+++ b/solution.py
@@ -48,18 +48,35 @@
     return jnp.dot(left, right, preferred_element_type=jnp.float32)
 
 
-def prepare_kernel(acts_ref, signs_ref, index_ref, turned_ref, signs_out_ref, rows_ref):
-    rows, breadth = signs_out_ref.shape
+def prepare_kernel(acts_hbm, signs_hbm, index_hbm, turned_ref, signs_out_ref, rows_ref, acts_ref, signs_ref, index_ref, sems):
+    height, breadth = signs_out_ref.shape
     spread = breadth // LANES
-    for piece in range(spread):
-        part = signs_ref[pl.ds(piece, rows, stride=spread), :]
-        signs_out_ref[:, piece * LANES : (piece + 1) * LANES] = part.astype(jnp.float32).astype(jnp.bfloat16)
-    turned_ref[...] = acts_ref[...].T
-    height = rows * pl.num_programs(0)
+    index_load = pltpu.make_async_copy(index_hbm, index_ref, sems.at[0])
+    sign_loads, acts_loads = [], []
+    for at in range(height // LANES):
+        piece = pl.ds(at * LANES * spread, LANES * spread)
+        sign_loads.append(pltpu.make_async_copy(signs_hbm.at[piece, :], signs_ref.at[piece, :], sems.at[1 + at]))
+    for at in range(height // SIDE):
+        piece = pl.ds(at * SIDE, SIDE)
+        sem = sems.at[1 + height // LANES + at]
+        acts_loads.append(pltpu.make_async_copy(acts_hbm.at[:, piece], acts_ref.at[:, piece], sem))
+    for load in [index_load] + sign_loads + acts_loads:
+        load.start()
+
+    index_load.wait()
     index = index_ref[...]
     at_row = ((index >> LANE_BITS) & (spread - 1)) * height + ((index // breadth) & (height - 1))
     half = (index // (breadth * height)) & 1
     rows_ref[...] = half * (spread * height) + at_row
+    for at, load in enumerate(sign_loads):
+        load.wait()
+        for strip in range(spread):
+            part = signs_ref[pl.ds(at * LANES * spread + strip, LANES, stride=spread), :]
+            part = part.astype(jnp.float32).astype(jnp.bfloat16)
+            signs_out_ref[at * LANES : (at + 1) * LANES, strip * LANES : (strip + 1) * LANES] = part
+    for at, load in enumerate(acts_loads):
+        load.wait()
+        turned_ref[at * SIDE : (at + 1) * SIDE, :] = acts_ref[:, at * SIDE : (at + 1) * SIDE].T
 
 
 def gather(parties, scale, outs, table, index_ref, rows_hbm, out_refs, scratch):
@@ -198,24 +215,20 @@
     index_rows = indices.reshape(groups, LANES)
     other_acts, other_signs = flipped(acts, "param", 1), flipped(sign_rows, "param", 1)
 
-    steps = height // LANES
     turned, sign_matrix, rows = pl.pallas_call(
         prepare_kernel,
-        grid=(steps,),
         out_shape=[
             jax.ShapeDtypeStruct((height, tokens), jnp.bfloat16),
             jax.ShapeDtypeStruct((height, breadth), jnp.bfloat16),
             jax.ShapeDtypeStruct((groups, LANES), jnp.int32),
         ],
-        in_specs=[
-            pl.BlockSpec((tokens, LANES), lambda at: (0, at)),
-            pl.BlockSpec((table_rows // steps, LANES), lambda at: (at, 0)),
-            pl.BlockSpec((groups // steps, LANES), lambda at: (at, 0)),
-        ],
-        out_specs=[
-            pl.BlockSpec((LANES, tokens), lambda at: (at, 0)),
-            pl.BlockSpec((LANES, breadth), lambda at: (at, 0)),
-            pl.BlockSpec((groups // steps, LANES), lambda at: (at, 0)),
+        in_specs=[pl.BlockSpec(memory_space=pl.ANY)] * 3,
+        out_specs=[vmem] * 3,
+        scratch_shapes=[
+            pltpu.VMEM((tokens, height), jnp.bfloat16),
+            pltpu.VMEM((table_rows, LANES), jnp.int32),
+            pltpu.VMEM((groups, LANES), jnp.int32),
+            pltpu.SemaphoreType.DMA((1 + height // LANES + height // SIDE,)),
         ],
         compiler_params=pltpu.CompilerParams(vmem_limit_bytes=LIMIT),
         cost_estimate=pl.CostEstimate(flops=0, bytes_accessed=8 * height * breadth, transcendentals=0),

time: 39 us -> 38.3 us (0.982)
  Pallas kernels: 25.9 us -> 23.9 us
  waiting for transfers between devices: 3.06 us -> 4.58 us
    pallas_call x1, Pallas kernels: 5.18 us -> 2.94 us  [on_device(): pl.pallas_call(prepare_kernel, out_shape=[jax.ShapeDtypeStruct((height, t...]
    ppermute x12, waiting for transfers between devices: 3.06 us -> 4.58 us  [flipped(): lax.ppermute(x, axis, [(i, i ^ mask) for i in range(lax.axis_size(axis))])]
  transfers between devices with their start and end apart: 12 -> 12, of which waited for: 6 -> 6; matrix products, arithmetic and copies ran while one was open for 0% -> 0% of each run, Pallas kernels for 23% -> 17%
where the time goes in v18:
time: 38.3 us; the launch traced here: 38.2 us
  Pallas kernels  23.9 us (62%)
  starting transfers between devices  9.05 us (24%)
  waiting for transfers between devices  4.58 us (12%)
  other arithmetic  0.61 us (2%)
    pallas_call x1, Pallas kernels, on_device(): pl.pallas_call(functools.partial(sketch_kernel, parties, scale), out_shap...  17.2 us
    ppermute x12, starting transfers between devices, flipped(): lax.ppermute(x, axis, [(i, i ^ mask) for i in range(lax.axis_size(axis))])  9.05 us
    ppermute x12, waiting for transfers between devices, flipped(): lax.ppermute(x, axis, [(i, i ^ mask) for i in range(lax.axis_size(axis))])  4.58 us
    pallas_call x1, Pallas kernels, on_device(): pl.pallas_call(functools.partial(own_kernel, parties, scale), out_shape=b...  3.71 us
    pallas_call x1, Pallas kernels, on_device(): pl.pallas_call(prepare_kernel, out_shape=[jax.ShapeDtypeStruct((height, t...  2.94 us
  transfers between devices with their start and end apart: 12, of which 6 were waited for; matrix products, arithmetic and copies ran while one was open for 0% of the time, Pallas kernels for 17%

profile of v18, /device:TPU:0, one launch (start us, length us, event | category | flops | bytes accessed | tf_op | source)
XLA Modules:
  0.0 38.2 jit_solution(6702837711312474784)
XLA Ops:
  0.0 0.5 %collective-permute-start.1 = (s32[8192,128]{1,0:T(8,128)}, s32[8192,128]{1,0:T(8,128)S(1)}, u32[]{:S(2)}, u32[]{:S(2)}) collective-permute-start(s32[8192,128]{1,0:T(8,128)} %bitcast.13), channel_id=1, source_target_pairs={{0,4},{4,0},{8,12},{12,8},{16,20},{20,16},{24,28},{28,24},{1,5},{5... | collective-permute-start | bytes 12582920 | tf_op jit(solution)/shard_map/ppermute | solution.py:20
  0.5 0.1 collective-permute-start
  0.5 3.9 %collective-permute-start.7 = (bf16[64,1024]{1,0:T(8,128)(2,1)}, bf16[64,1024]{1,0:T(8,128)(2,1)S(1)}, u32[]{:S(2)}, u32[]{:S(2)}) collective-permute-start(bf16[64,1024]{1,0:T(8,128)(2,1)} %bitcast.8), channel_id=1, source_target_pairs={{0,24},{4,28},{8,16},{12,20},{16,8},{20,12},{24,0},{28,4},{1,25},{... | collective-permute-start | bytes 393224 | tf_op jit(solution)/shard_map/ppermute | solution.py:20
  4.4 0.5 %collective-permute-start.5 = (bf16[64,1024]{1,0:T(8,128)(2,1)}, bf16[64,1024]{1,0:T(8,128)(2,1)S(1)}, u32[]{:S(2)}, u32[]{:S(2)}) collective-permute-start(bf16[64,1024]{1,0:T(8,128)(2,1)} %bitcast.9), channel_id=1, source_target_pairs={{0,16},{4,20},{8,24},{12,28},{16,0},{20,4},{24,8},{28,12},{1,17},{... | collective-permute-start | bytes 393224 | tf_op jit(solution)/shard_map/ppermute | solution.py:20
  4.9 0.1 collective-permute-start.3
  5.0 2.9 %prepare.1 = (bf16[1024,512]{1,0:T(8,128)(2,1)S(1)}, bf16[1024,1024]{1,0:T(8,128)(2,1)S(1)}, s32[256,128]{1,0:T(8,128)S(1)}) custom-call(bf16[512,1024]{1,0:T(8,128)(2,1)} %bitcast.16, s32[8192,128]{1,0:T(8,128)} %bitcast.14, s32[256,128]{1,0:T(8,128)} %bitcast.5), custom_call_target="tpu_custom_call" | custom-call | bytes 8388608 | tf_op jit(solution)/shard_map/prepare/pallas_call | solution.py:218
  7.9 0.7 %collective-permute-done.7.refs_6_ = bf16[64,1024]{1,0:T(8,128)(2,1)S(1)} collective-permute-done((bf16[64,1024]{1,0:T(8,128)(2,1)}, bf16[64,1024]{1,0:T(8,128)(2,1)S(1)}, u32[]{:S(2)}, u32[]{:S(2)}) %collective-permute-start.7) | collective-permute-done | bytes 131104 | tf_op jit(solution)/shard_map/ppermute | solution.py:20
  8.6 0.0 collective-permute-start.2
  8.7 2.5 %collective-permute-done.5.refs_4_ = bf16[64,1024]{1,0:T(8,128)(2,1)S(1)} collective-permute-done((bf16[64,1024]{1,0:T(8,128)(2,1)}, bf16[64,1024]{1,0:T(8,128)(2,1)S(1)}, u32[]{:S(2)}, u32[]{:S(2)}) %collective-permute-start.5) | collective-permute-done | bytes 131104 | tf_op jit(solution)/shard_map/ppermute | solution.py:20
  11.2 0.0 collective-permute-start.8
  11.2 0.3 collective-permute-done.3.refs_2_
  11.4 0.2 collective-permute-start.6
  11.7 0.0 collective-permute-done.2.refs_1_
  11.7 0.3 collective-permute-start.4
  12.0 0.6 %collective-permute-done.8.refs_7_ = bf16[64,1024]{1,0:T(8,128)(2,1)S(1)} collective-permute-done((bf16[64,1024]{1,0:T(8,128)(2,1)S(1)}, bf16[64,1024]{1,0:T(8,128)(2,1)S(1)}, u32[]{:S(2)}, u32[]{:S(2)}) %collective-permute-start.8) | collective-permute-done | bytes 131104 | tf_op jit(solution)/shard_map/ppermute | solution.py:20
  12.5 0.3 collective-permute-done.6.refs_5_
  12.8 0.2 collective-permute-done.4.refs_3_
  13.0 17.2 %sketch.1 = (f32[16392,128]{1,0:T(8,128)S(1)}, f32[32,128]{1,0:T(8,128)S(1)}, f32[32,128]{1,0:T(8,128)S(1)}, f32[32,128]{1,0:T(8,128)S(1)}) custom-call(bf16[1024,512]{1,0:T(8,128)(2,1)S(1)} %get-tuple-element.14.own_turned, bf16[1024,1024]{1,0:T(8,128)(2,1)S(1)} %get-tuple-element.15.own_signs, bf16[512,1024]{1,0:T(8,128)(2,1)S(1)} %collective-permute-done.other_acts, ...), custom_call_target="tpu_custom_call" | custom-call | tf_op jit(solution)/shard_map/sketch/pallas_call | solution.py:253
  30.3 1.7 %collective-permute-start.9 = (f32[32,128]{1,0:T(8,128)S(1)}, f32[32,128]{1,0:T(8,128)S(1)}, u32[]{:S(2)}, u32[]{:S(2)}) collective-permute-start(f32[32,128]{1,0:T(8,128)S(1)} %get-tuple-element.20), channel_id=1, source_target_pairs={{0,8},{4,12},{8,0},{12,4},{16,24},{20,28},{24,16},{28,20},{1,9},{5... | collective-permute-start | bytes 49160 | tf_op jit(solution)/shard_map/ppermute | solution.py:20
  32.0 0.6 %collective-permute-start.10 = (f32[32,128]{1,0:T(8,128)S(1)}, f32[32,128]{1,0:T(8,128)S(1)}, u32[]{:S(2)}, u32[]{:S(2)}) collective-permute-start(f32[32,128]{1,0:T(8,128)S(1)} %get-tuple-element.21), channel_id=1, source_target_pairs={{0,16},{4,20},{8,24},{12,28},{16,0},{20,4},{24,8},{28,12},{1,17},{... | collective-permute-start | bytes 49160 | tf_op jit(solution)/shard_map/ppermute | solution.py:20
  32.6 1.2 %collective-permute-start.11 = (f32[32,128]{1,0:T(8,128)S(1)}, f32[32,128]{1,0:T(8,128)S(1)}, u32[]{:S(2)}, u32[]{:S(2)}) collective-permute-start(f32[32,128]{1,0:T(8,128)S(1)} %get-tuple-element.22), channel_id=1, source_target_pairs={{0,24},{4,28},{8,16},{12,20},{16,8},{20,12},{24,0},{28,4},{1,25},{... | collective-permute-start | bytes 49160 | tf_op jit(solution)/shard_map/ppermute | solution.py:20
  33.8 3.7 %own.1 = f32[32,128]{1,0:T(8,128)S(1)} custom-call(f32[16392,128]{1,0:T(8,128)S(1)} %get-tuple-element.19.table, s32[256,128]{1,0:T(8,128)S(1)} %bitcast.7, s32[256,128]{1,0:T(8,128)S(1)} %get-tuple-element.17.rows_hbm), custom_call_target="tpu_custom_call" | custom-call | bytes 8388608 | tf_op jit(solution)/shard_map/own/pallas_call | solution.py:276
  37.6 0.0 collective-permute-done.10
  37.6 0.6 %add_add_fusion = f32[32,128]{1,0:T(8,128)} fusion(f32[32,128]{1,0:T(8,128)S(1)} %collective-permute-done.11, f32[32,128]{1,0:T(8,128)S(1)} %collective-permute-done.10, f32[32,128]{1,0:T(8,128)S(1)} %own.1, f32[32,128]{1,0:T(8,128)S(1)} %collective-permute-done.9), kind=kLoop, calls=%fused_computation | loop fusion | flops 12288 | bytes 81920 | tf_op jit(solution)/shard_map/add | solution.py:288
  (8 shorter events, 0.0 us)
Async XLA Ops:
  0.0 8.6 %copy-start.1 = (bf16[1,64,1024]{2,1,0:T(8,128)(2,1)S(1)}, bf16[1,64,1024]{2,1,0:T(8,128)(2,1)}, u32[]{:S(2)}) copy-start(bf16[1,64,1024]{2,1,0:T(8,128)(2,1)} %param.5) | copy-start | bytes 393220
  0.0 13.0 %copy-start = (s32[32768]{0:T(1024)S(1)}, s32[32768]{0:T(1024)}, u32[]{:S(2)}) copy-start(s32[32768]{0:T(1024)} %param.7) | copy-start | bytes 393220
  0.0 13.0 %collective-permute-start.1 = (s32[8192,128]{1,0:T(8,128)}, s32[8192,128]{1,0:T(8,128)S(1)}, u32[]{:S(2)}, u32[]{:S(2)}) collective-permute-start(s32[8192,128]{1,0:T(8,128)} %bitcast.13), channel_id=1, source_target_pairs={{0,4},{4,0},{8,12},{12,8},{16,20},{20,16},{24,28},{28,24},{1,5},{5... | collective-permute-start | bytes 12582920 | tf_op jit(solution)/shard_map/ppermute | solution.py:20
  0.5 12.6 %collective-permute-start = (bf16[512,1024]{1,0:T(8,128)(2,1)}, bf16[512,1024]{1,0:T(8,128)(2,1)S(1)}, u32[]{:S(2)}, u32[]{:S(2)}) collective-permute-start(bf16[512,1024]{1,0:T(8,128)(2,1)} %bitcast.15), channel_id=1, source_target_pairs={{0,4},{4,0},{8,12},{12,8},{16,20},{20,16},{24,28},{28,24},{1,5},{5... | collective-permute-start | bytes 3145736 | tf_op jit(solution)/shard_map/ppermute | solution.py:20
  0.5 8.1 %collective-permute-start.7 = (bf16[64,1024]{1,0:T(8,128)(2,1)}, bf16[64,1024]{1,0:T(8,128)(2,1)S(1)}, u32[]{:S(2)}, u32[]{:S(2)}) collective-permute-start(bf16[64,1024]{1,0:T(8,128)(2,1)} %bitcast.8), channel_id=1, source_target_pairs={{0,24},{4,28},{8,16},{12,20},{16,8},{20,12},{24,0},{28,4},{1,25},{... | collective-permute-start | bytes 393224 | tf_op jit(solution)/shard_map/ppermute | solution.py:20
  4.4 6.8 %collective-permute-start.5 = (bf16[64,1024]{1,0:T(8,128)(2,1)}, bf16[64,1024]{1,0:T(8,128)(2,1)S(1)}, u32[]{:S(2)}, u32[]{:S(2)}) collective-permute-start(bf16[64,1024]{1,0:T(8,128)(2,1)} %bitcast.9), channel_id=1, source_target_pairs={{0,16},{4,20},{8,24},{12,28},{16,0},{20,4},{24,8},{28,12},{1,17},{... | collective-permute-start | bytes 393224 | tf_op jit(solution)/shard_map/ppermute | solution.py:20
  4.9 6.5 %collective-permute-start.3 = (bf16[64,1024]{1,0:T(8,128)(2,1)}, bf16[64,1024]{1,0:T(8,128)(2,1)S(1)}, u32[]{:S(2)}, u32[]{:S(2)}) collective-permute-start(bf16[64,1024]{1,0:T(8,128)(2,1)} %bitcast.10), channel_id=1, source_target_pairs={{0,8},{4,12},{8,0},{12,4},{16,24},{20,28},{24,16},{28,20},{1,9},{5... | collective-permute-start | bytes 393224 | tf_op jit(solution)/shard_map/ppermute | solution.py:20
  8.6 3.0 %collective-permute-start.2 = (bf16[64,1024]{1,0:T(8,128)(2,1)S(1)}, bf16[64,1024]{1,0:T(8,128)(2,1)S(1)}, u32[]{:S(2)}, u32[]{:S(2)}) collective-permute-start(bf16[64,1024]{1,0:T(8,128)(2,1)S(1)} %bitcast.11), channel_id=1, source_target_pairs={{0,4},{4,0},{8,12},{12,8},{16,20},{20,16},{24,28},{28,24},{1,5},{5... | collective-permute-start | bytes 393224 | tf_op jit(solution)/shard_map/ppermute | solution.py:20
  11.2 1.3 %collective-permute-start.8 = (bf16[64,1024]{1,0:T(8,128)(2,1)S(1)}, bf16[64,1024]{1,0:T(8,128)(2,1)S(1)}, u32[]{:S(2)}, u32[]{:S(2)}) collective-permute-start(bf16[64,1024]{1,0:T(8,128)(2,1)S(1)} %collective-permute-done.7.refs_6_), channel_id=1, source_target_pairs={{0,4},{4,0},{8,12},{12,8},{16,20},{20,16},{24,28},{28,24},{1,5},{5... | collective-permute-start | bytes 393224 | tf_op jit(solution)/shard_map/ppermute | solution.py:20
  11.4 1.3 %collective-permute-start.6 = (bf16[64,1024]{1,0:T(8,128)(2,1)S(1)}, bf16[64,1024]{1,0:T(8,128)(2,1)S(1)}, u32[]{:S(2)}, u32[]{:S(2)}) collective-permute-start(bf16[64,1024]{1,0:T(8,128)(2,1)S(1)} %collective-permute-done.5.refs_4_), channel_id=1, source_target_pairs={{0,4},{4,0},{8,12},{12,8},{16,20},{20,16},{24,28},{28,24},{1,5},{5... | collective-permute-start | bytes 393224 | tf_op jit(solution)/shard_map/ppermute | solution.py:20
  11.7 1.3 %collective-permute-start.4 = (bf16[64,1024]{1,0:T(8,128)(2,1)S(1)}, bf16[64,1024]{1,0:T(8,128)(2,1)S(1)}, u32[]{:S(2)}, u32[]{:S(2)}) collective-permute-start(bf16[64,1024]{1,0:T(8,128)(2,1)S(1)} %collective-permute-done.3.refs_2_), channel_id=1, source_target_pairs={{0,4},{4,0},{8,12},{12,8},{16,20},{20,16},{24,28},{28,24},{1,5},{5... | collective-permute-start | bytes 393224 | tf_op jit(solution)/shard_map/ppermute | solution.py:20
  30.3 7.3 %collective-permute-start.9 = (f32[32,128]{1,0:T(8,128)S(1)}, f32[32,128]{1,0:T(8,128)S(1)}, u32[]{:S(2)}, u32[]{:S(2)}) collective-permute-start(f32[32,128]{1,0:T(8,128)S(1)} %get-tuple-element.20), channel_id=1, source_target_pairs={{0,8},{4,12},{8,0},{12,4},{16,24},{20,28},{24,16},{28,20},{1,9},{5... | collective-permute-start | bytes 49160 | tf_op jit(solution)/shard_map/ppermute | solution.py:20
  32.0 5.5 %collective-permute-start.10 = (f32[32,128]{1,0:T(8,128)S(1)}, f32[32,128]{1,0:T(8,128)S(1)}, u32[]{:S(2)}, u32[]{:S(2)}) collective-permute-start(f32[32,128]{1,0:T(8,128)S(1)} %get-tuple-element.21), channel_id=1, source_target_pairs={{0,16},{4,20},{8,24},{12,28},{16,0},{20,4},{24,8},{28,12},{1,17},{... | collective-permute-start | bytes 49160 | tf_op jit(solution)/shard_map/ppermute | solution.py:20
  32.6 4.9 %collective-permute-start.11 = (f32[32,128]{1,0:T(8,128)S(1)}, f32[32,128]{1,0:T(8,128)S(1)}, u32[]{:S(2)}, u32[]{:S(2)}) collective-permute-start(f32[32,128]{1,0:T(8,128)S(1)} %get-tuple-element.22), channel_id=1, source_target_pairs={{0,24},{4,28},{8,16},{12,20},{16,8},{20,12},{24,0},{28,4},{1,25},{... | collective-permute-start | bytes 49160 | tf_op jit(solution)/shard_map/ppermute | solution.py:20

commit v19 on v18

--- a/solution.py
+++ b/solution.py
@@ -48,7 +48,8 @@
     return jnp.dot(left, right, preferred_element_type=jnp.float32)
 
 
-def prepare_kernel(acts_hbm, signs_hbm, index_hbm, turned_ref, signs_out_ref, rows_ref, acts_ref, signs_ref, index_ref, sems):
+def prepare_kernel(other_acts, acts_hbm, signs_hbm, index_hbm, *refs):
+    other_turned, turned_ref, signs_out_ref, rows_ref, acts_ref, signs_ref, index_ref, sems = refs
     height, breadth = signs_out_ref.shape
     spread = breadth // LANES
     index_load = pltpu.make_async_copy(index_hbm, index_ref, sems.at[0])
@@ -63,6 +64,7 @@
     for load in [index_load] + sign_loads + acts_loads:
         load.start()
 
+    other_turned[...] = other_acts[...].T
     index_load.wait()
     index = index_ref[...]
     at_row = ((index >> LANE_BITS) & (spread - 1)) * height + ((index // breadth) & (height - 1))
@@ -147,11 +149,11 @@
     finish()
 
 
-def sketch_kernel(parties, scale, own_turned, own_signs, other_acts, other_signs, index_ref, rows_hbm, *refs):
+def sketch_kernel(parties, scale, own_turned, own_signs, other_turned, other_signs, index_ref, rows_hbm, *refs):
     outs = list(range(1, parties // 2))
     chunk_refs, table, refs = refs[:parties], refs[parties], refs[parties + 1 :]
     out_refs, scratch = refs[: len(outs)], refs[len(outs) :]
-    cots, other_turned, total, change, *scratch = scratch
+    cots, total, change, *scratch = scratch
     me = lax.axis_index("param")
     height, breadth = total.shape
     spread = breadth // LANES
@@ -174,8 +176,6 @@
     for col in range(col_blocks):
         cols = slice(col * SIDE, (col + 1) * SIDE)
         own = dot(own_turned[...], cots[:, cols]) * own_signs[:, cols].astype(jnp.float32)
-        if col == 0:
-            other_turned[...] = other_acts[...].T
         strips = [other_signs[pl.ds(col * pieces + piece, height, stride=spread), :] for piece in range(pieces)]
         other = dot(other_turned[...], cots[:, cols]) * jnp.concatenate(strips, axis=1).astype(jnp.float32)
         for signed, product in ((total, own + other), (change, own - other)):
@@ -215,15 +215,16 @@
     index_rows = indices.reshape(groups, LANES)
     other_acts, other_signs = flipped(acts, "param", 1), flipped(sign_rows, "param", 1)
 
-    turned, sign_matrix, rows = pl.pallas_call(
+    other_turned, turned, sign_matrix, rows = pl.pallas_call(
         prepare_kernel,
         out_shape=[
+            jax.ShapeDtypeStruct((height, tokens), jnp.bfloat16),
             jax.ShapeDtypeStruct((height, tokens), jnp.bfloat16),
             jax.ShapeDtypeStruct((height, breadth), jnp.bfloat16),
             jax.ShapeDtypeStruct((groups, LANES), jnp.int32),
         ],
-        in_specs=[pl.BlockSpec(memory_space=pl.ANY)] * 3,
-        out_specs=[vmem] * 3,
+        in_specs=[vmem] + [pl.BlockSpec(memory_space=pl.ANY)] * 3,
+        out_specs=[vmem] * 4,
         scratch_shapes=[
             pltpu.VMEM((tokens, height), jnp.bfloat16),
             pltpu.VMEM((table_rows, LANES), jnp.int32),
@@ -233,8 +234,10 @@
         compiler_params=pltpu.CompilerParams(vmem_limit_bytes=LIMIT),
         cost_estimate=pl.CostEstimate(flops=0, bytes_accessed=8 * height * breadth, transcendentals=0),
         name="prepare",
-    )(*[pltpu.with_memory_space_constraint(x, pltpu.HBM) for x in (acts, sign_rows, index_rows)])
-    chunks[0], rows = lax.optimization_barrier((chunks[0], rows))
+    )(other_acts, *[pltpu.with_memory_space_constraint(x, pltpu.HBM) for x in (acts, sign_rows, index_rows)])
+    held = list(range(0, parties, 2))
+    rows, *passed = lax.optimization_barrier((rows, *[chunks[d] for d in held]))
+    chunks.update(zip(held, passed))
     for distance in range(0, parties, 2):
         chunks[distance + 1] = flipped(chunks[distance], "param", 1)
 
@@ -257,7 +260,6 @@
         out_specs=[vmem] * outs,
         scratch_shapes=[
             pltpu.VMEM((tokens, breadth), jnp.bfloat16),
-            pltpu.VMEM((height, tokens), jnp.bfloat16),
             pltpu.VMEM((height, breadth), jnp.float32),
             pltpu.VMEM((height, breadth), jnp.float32),
         ]
@@ -267,7 +269,7 @@
     )(
         turned,
         sign_matrix,
-        other_acts,
+        other_turned,
         other_signs,
         index_rows,
         rows,

time: 38.3 us -> 41.1 us (1.073)
  waiting for transfers between devices: 4.58 us -> 6.07 us
  starting transfers between devices: 9.05 us -> 10.3 us
    ppermute x12, waiting for transfers between devices: 4.58 us -> 6.07 us  [flipped(): lax.ppermute(x, axis, [(i, i ^ mask) for i in range(lax.axis_size(axis))])]
    ppermute x12, starting transfers between devices: 9.05 us -> 10.3 us  [flipped(): lax.ppermute(x, axis, [(i, i ^ mask) for i in range(lax.axis_size(axis))])]
  transfers between devices with their start and end apart: 12 -> 12, of which waited for: 6 -> 6; matrix products, arithmetic and copies ran while one was open for 0% -> 0% of each run, Pallas kernels for 17% -> 16%
where the time goes in v19:
time: 41.1 us; the launch traced here: 40.9 us
  Pallas kernels  23.8 us (58%)
  starting transfers between devices  10.3 us (25%)
  waiting for transfers between devices  6.07 us (15%)
  other arithmetic  0.61 us (1%)
    pallas_call x1, Pallas kernels, on_device(): pl.pallas_call(functools.partial(sketch_kernel, parties, scale), out_shap...  17.2 us
    ppermute x12, starting transfers between devices, flipped(): lax.ppermute(x, axis, [(i, i ^ mask) for i in range(lax.axis_size(axis))])  10.3 us
    ppermute x12, waiting for transfers between devices, flipped(): lax.ppermute(x, axis, [(i, i ^ mask) for i in range(lax.axis_size(axis))])  6.07 us
    pallas_call x1, Pallas kernels, on_device(): pl.pallas_call(functools.partial(own_kernel, parties, scale), out_shape=b...  3.71 us
    pallas_call x1, Pallas kernels, on_device(): pl.pallas_call(prepare_kernel, out_shape=[jax.ShapeDtypeStruct((height, t...  2.94 us
  transfers between devices with their start and end apart: 12, of which 6 were waited for; matrix products, arithmetic and copies ran while one was open for 0% of the time, Pallas kernels for 16%

profile of v19, /device:TPU:0, one launch (start us, length us, event | category | flops | bytes accessed | tf_op | source)
XLA Modules:
  0.0 40.9 jit_solution(4178358001860979847)
XLA Ops:
  0.0 0.5 %collective-permute-start.1 = (s32[8192,128]{1,0:T(8,128)}, s32[8192,128]{1,0:T(8,128)S(1)}, u32[]{:S(2)}, u32[]{:S(2)}) collective-permute-start(s32[8192,128]{1,0:T(8,128)} %bitcast.13), channel_id=1, source_target_pairs={{0,4},{4,0},{8,12},{12,8},{16,20},{20,16},{24,28},{28,24},{1,5},{5... | collective-permute-start | bytes 12582920 | tf_op jit(solution)/shard_map/ppermute | solution.py:20
  0.5 0.1 collective-permute-start
  0.5 3.9 %collective-permute-start.4 = (bf16[64,1024]{1,0:T(8,128)(2,1)}, bf16[64,1024]{1,0:T(8,128)(2,1)S(1)}, u32[]{:S(2)}, u32[]{:S(2)}) collective-permute-start(bf16[64,1024]{1,0:T(8,128)(2,1)} %bitcast.8), channel_id=1, source_target_pairs={{0,24},{4,28},{8,16},{12,20},{16,8},{20,12},{24,0},{28,4},{1,25},{... | collective-permute-start | bytes 393224 | tf_op jit(solution)/shard_map/ppermute | solution.py:20
  4.4 0.5 %collective-permute-start.3 = (bf16[64,1024]{1,0:T(8,128)(2,1)}, bf16[64,1024]{1,0:T(8,128)(2,1)S(1)}, u32[]{:S(2)}, u32[]{:S(2)}) collective-permute-start(bf16[64,1024]{1,0:T(8,128)(2,1)} %bitcast.9), channel_id=1, source_target_pairs={{0,16},{4,20},{8,24},{12,28},{16,0},{20,4},{24,8},{28,12},{1,17},{... | collective-permute-start | bytes 393224 | tf_op jit(solution)/shard_map/ppermute | solution.py:20
  4.9 0.1 collective-permute-start.2
  5.0 4.0 %collective-permute-done.other_acts = bf16[512,1024]{1,0:T(8,128)(2,1)S(1)} collective-permute-done((bf16[512,1024]{1,0:T(8,128)(2,1)}, bf16[512,1024]{1,0:T(8,128)(2,1)S(1)}, u32[]{:S(2)}, u32[]{:S(2)}) %collective-permute-start) | collective-permute-done | bytes 1048608 | tf_op jit(solution)/shard_map/ppermute | solution.py:20
  9.0 2.9 %prepare.1 = (bf16[1024,512]{1,0:T(8,128)(2,1)S(1)}, bf16[1024,512]{1,0:T(8,128)(2,1)S(1)}, bf16[1024,1024]{1,0:T(8,128)(2,1)S(1)}, s32[256,128]{1,0:T(8,128)S(1)}) custom-call(bf16[512,1024]{1,0:T(8,128)(2,1)S(1)} %collective-permute-done.other_acts, bf16[512,1024]{1,0:T(8,128)(2,1)} %bitcast.16, s32[8192,128]{1,0:T(8,128)} %bitcast.14, s32[256,128]{1,0:T(8,128)} %bitcast.5), custom_call_target="tpu_custom_call" | custom-call | bytes 8388608 | tf_op jit(solution)/shard_map/prepare/pallas_call | solution.py:218
  11.9 0.0 collective-permute-done.4.refs_6_
  11.9 0.0 collective-permute-done.2.refs_2_
  11.9 0.4 %collective-permute-start.5 = (bf16[64,1024]{1,0:T(8,128)(2,1)S(1)}, bf16[64,1024]{1,0:T(8,128)(2,1)S(1)}, u32[]{:S(2)}, u32[]{:S(2)}) collective-permute-start(bf16[64,1024]{1,0:T(8,128)(2,1)S(1)} %bitcast.11), channel_id=1, source_target_pairs={{0,4},{4,0},{8,12},{12,8},{16,20},{20,16},{24,28},{28,24},{1,5},{5... | collective-permute-start | bytes 393224 | tf_op jit(solution)/shard_map/ppermute | solution.py:20
  12.4 0.1 collective-permute-start.6
  12.5 0.4 collective-permute-start.7
  12.9 0.1 collective-permute-start.8
  13.0 0.3 collective-permute-done.5.refs_1_
  13.4 0.4 collective-permute-done.6.refs_3_
  13.7 0.2 collective-permute-done.7.refs_5_
  13.9 0.3 collective-permute-done.8.refs_7_
  14.2 17.2 %sketch.1 = (f32[16392,128]{1,0:T(8,128)S(1)}, f32[32,128]{1,0:T(8,128)S(1)}, f32[32,128]{1,0:T(8,128)S(1)}, f32[32,128]{1,0:T(8,128)S(1)}) custom-call(bf16[1024,512]{1,0:T(8,128)(2,1)S(1)} %get-tuple-element.18.own_turned, bf16[1024,1024]{1,0:T(8,128)(2,1)S(1)} %get-tuple-element.19.own_signs, bf16[1024,512]{1,0:T(8,128)(2,1)S(1)} %get-tuple-element.20.other_turned, ...), custom_call_target="tpu_custom_call" | custom-call | tf_op jit(solution)/shard_map/sketch/pallas_call | solution.py:256
  31.4 2.7 %collective-permute-start.9 = (f32[32,128]{1,0:T(8,128)S(1)}, f32[32,128]{1,0:T(8,128)S(1)}, u32[]{:S(2)}, u32[]{:S(2)}) collective-permute-start(f32[32,128]{1,0:T(8,128)S(1)} %get-tuple-element.28), channel_id=1, source_target_pairs={{0,8},{4,12},{8,0},{12,4},{16,24},{20,28},{24,16},{28,20},{1,9},{5... | collective-permute-start | bytes 49160 | tf_op jit(solution)/shard_map/ppermute | solution.py:20
  34.2 1.5 %collective-permute-start.10 = (f32[32,128]{1,0:T(8,128)S(1)}, f32[32,128]{1,0:T(8,128)S(1)}, u32[]{:S(2)}, u32[]{:S(2)}) collective-permute-start(f32[32,128]{1,0:T(8,128)S(1)} %get-tuple-element.29), channel_id=1, source_target_pairs={{0,16},{4,20},{8,24},{12,28},{16,0},{20,4},{24,8},{28,12},{1,17},{... | collective-permute-start | bytes 49160 | tf_op jit(solution)/shard_map/ppermute | solution.py:20
  35.7 0.0 collective-permute-start.11
  35.7 3.7 %own.1 = f32[32,128]{1,0:T(8,128)S(1)} custom-call(f32[16392,128]{1,0:T(8,128)S(1)} %get-tuple-element.27.table, s32[256,128]{1,0:T(8,128)S(1)} %bitcast.7, s32[256,128]{1,0:T(8,128)S(1)} %get-tuple-element.22.rows_hbm), custom_call_target="tpu_custom_call" | custom-call | bytes 8388608 | tf_op jit(solution)/shard_map/own/pallas_call | solution.py:278
  39.5 0.9 %collective-permute-done.11 = f32[32,128]{1,0:T(8,128)S(1)} collective-permute-done((f32[32,128]{1,0:T(8,128)S(1)}, f32[32,128]{1,0:T(8,128)S(1)}, u32[]{:S(2)}, u32[]{:S(2)}) %collective-permute-start.11) | collective-permute-done | bytes 16416 | tf_op jit(solution)/shard_map/ppermute | solution.py:20
  40.3 0.6 %add_add_fusion = f32[32,128]{1,0:T(8,128)} fusion(f32[32,128]{1,0:T(8,128)S(1)} %collective-permute-done.11, f32[32,128]{1,0:T(8,128)S(1)} %collective-permute-done.10, f32[32,128]{1,0:T(8,128)S(1)} %own.1, f32[32,128]{1,0:T(8,128)S(1)} %collective-permute-done.9), kind=kLoop, calls=%fused_computation | loop fusion | flops 12288 | bytes 81920 | tf_op jit(solution)/shard_map/add | solution.py:290
  (8 shorter events, 0.0 us)
Async XLA Ops:
  0.0 11.9 %copy-start.1 = (bf16[1,64,1024]{2,1,0:T(8,128)(2,1)S(1)}, bf16[1,64,1024]{2,1,0:T(8,128)(2,1)}, u32[]{:S(2)}) copy-start(bf16[1,64,1024]{2,1,0:T(8,128)(2,1)} %param.5) | copy-start | bytes 393220
  0.0 14.2 %copy-start = (s32[32768]{0:T(1024)S(1)}, s32[32768]{0:T(1024)}, u32[]{:S(2)}) copy-start(s32[32768]{0:T(1024)} %param.7) | copy-start | bytes 393220
  0.0 14.2 %collective-permute-start.1 = (s32[8192,128]{1,0:T(8,128)}, s32[8192,128]{1,0:T(8,128)S(1)}, u32[]{:S(2)}, u32[]{:S(2)}) collective-permute-start(s32[8192,128]{1,0:T(8,128)} %bitcast.13), channel_id=1, source_target_pairs={{0,4},{4,0},{8,12},{12,8},{16,20},{20,16},{24,28},{28,24},{1,5},{5... | collective-permute-start | bytes 12582920 | tf_op jit(solution)/shard_map/ppermute | solution.py:20
  0.5 8.5 %collective-permute-start = (bf16[512,1024]{1,0:T(8,128)(2,1)}, bf16[512,1024]{1,0:T(8,128)(2,1)S(1)}, u32[]{:S(2)}, u32[]{:S(2)}) collective-permute-start(bf16[512,1024]{1,0:T(8,128)(2,1)} %bitcast.15), channel_id=1, source_target_pairs={{0,4},{4,0},{8,12},{12,8},{16,20},{20,16},{24,28},{28,24},{1,5},{5... | collective-permute-start | bytes 3145736 | tf_op jit(solution)/shard_map/ppermute | solution.py:20
  0.5 11.4 %collective-permute-start.4 = (bf16[64,1024]{1,0:T(8,128)(2,1)}, bf16[64,1024]{1,0:T(8,128)(2,1)S(1)}, u32[]{:S(2)}, u32[]{:S(2)}) collective-permute-start(bf16[64,1024]{1,0:T(8,128)(2,1)} %bitcast.8), channel_id=1, source_target_pairs={{0,24},{4,28},{8,16},{12,20},{16,8},{20,12},{24,0},{28,4},{1,25},{... | collective-permute-start | bytes 393224 | tf_op jit(solution)/shard_map/ppermute | solution.py:20
  4.4 7.5 %collective-permute-start.3 = (bf16[64,1024]{1,0:T(8,128)(2,1)}, bf16[64,1024]{1,0:T(8,128)(2,1)S(1)}, u32[]{:S(2)}, u32[]{:S(2)}) collective-permute-start(bf16[64,1024]{1,0:T(8,128)(2,1)} %bitcast.9), channel_id=1, source_target_pairs={{0,16},{4,20},{8,24},{12,28},{16,0},{20,4},{24,8},{28,12},{1,17},{... | collective-permute-start | bytes 393224 | tf_op jit(solution)/shard_map/ppermute | solution.py:20
  4.9 7.0 %collective-permute-start.2 = (bf16[64,1024]{1,0:T(8,128)(2,1)}, bf16[64,1024]{1,0:T(8,128)(2,1)S(1)}, u32[]{:S(2)}, u32[]{:S(2)}) collective-permute-start(bf16[64,1024]{1,0:T(8,128)(2,1)} %bitcast.10), channel_id=1, source_target_pairs={{0,8},{4,12},{8,0},{12,4},{16,24},{20,28},{24,16},{28,20},{1,9},{5... | collective-permute-start | bytes 393224 | tf_op jit(solution)/shard_map/ppermute | solution.py:20
  11.9 1.4 %collective-permute-start.5 = (bf16[64,1024]{1,0:T(8,128)(2,1)S(1)}, bf16[64,1024]{1,0:T(8,128)(2,1)S(1)}, u32[]{:S(2)}, u32[]{:S(2)}) collective-permute-start(bf16[64,1024]{1,0:T(8,128)(2,1)S(1)} %bitcast.11), channel_id=1, source_target_pairs={{0,4},{4,0},{8,12},{12,8},{16,20},{20,16},{24,28},{28,24},{1,5},{5... | collective-permute-start | bytes 393224 | tf_op jit(solution)/shard_map/ppermute | solution.py:20
  12.4 1.3 %collective-permute-start.6 = (bf16[64,1024]{1,0:T(8,128)(2,1)S(1)}, bf16[64,1024]{1,0:T(8,128)(2,1)S(1)}, u32[]{:S(2)}, u32[]{:S(2)}) collective-permute-start(bf16[64,1024]{1,0:T(8,128)(2,1)S(1)} %collective-permute-done.2.refs_2_), channel_id=1, source_target_pairs={{0,4},{4,0},{8,12},{12,8},{16,20},{20,16},{24,28},{28,24},{1,5},{5... | collective-permute-start | bytes 393224 | tf_op jit(solution)/shard_map/ppermute | solution.py:20
  12.5 1.4 %collective-permute-start.7 = (bf16[64,1024]{1,0:T(8,128)(2,1)S(1)}, bf16[64,1024]{1,0:T(8,128)(2,1)S(1)}, u32[]{:S(2)}, u32[]{:S(2)}) collective-permute-start(bf16[64,1024]{1,0:T(8,128)(2,1)S(1)} %collective-permute-done.3.refs_4_), channel_id=1, source_target_pairs={{0,4},{4,0},{8,12},{12,8},{16,20},{20,16},{24,28},{28,24},{1,5},{5... | collective-permute-start | bytes 393224 | tf_op jit(solution)/shard_map/ppermute | solution.py:20
  12.9 1.3 %collective-permute-start.8 = (bf16[64,1024]{1,0:T(8,128)(2,1)S(1)}, bf16[64,1024]{1,0:T(8,128)(2,1)S(1)}, u32[]{:S(2)}, u32[]{:S(2)}) collective-permute-start(bf16[64,1024]{1,0:T(8,128)(2,1)S(1)} %collective-permute-done.4.refs_6_), channel_id=1, source_target_pairs={{0,4},{4,0},{8,12},{12,8},{16,20},{20,16},{24,28},{28,24},{1,5},{5... | collective-permute-start | bytes 393224 | tf_op jit(solution)/shard_map/ppermute | solution.py:20
  31.4 8.0 %collective-permute-start.9 = (f32[32,128]{1,0:T(8,128)S(1)}, f32[32,128]{1,0:T(8,128)S(1)}, u32[]{:S(2)}, u32[]{:S(2)}) collective-permute-start(f32[32,128]{1,0:T(8,128)S(1)} %get-tuple-element.28), channel_id=1, source_target_pairs={{0,8},{4,12},{8,0},{12,4},{16,24},{20,28},{24,16},{28,20},{1,9},{5... | collective-permute-start | bytes 49160 | tf_op jit(solution)/shard_map/ppermute | solution.py:20
  34.2 5.3 %collective-permute-start.10 = (f32[32,128]{1,0:T(8,128)S(1)}, f32[32,128]{1,0:T(8,128)S(1)}, u32[]{:S(2)}, u32[]{:S(2)}) collective-permute-start(f32[32,128]{1,0:T(8,128)S(1)} %get-tuple-element.29), channel_id=1, source_target_pairs={{0,16},{4,20},{8,24},{12,28},{16,0},{20,4},{24,8},{28,12},{1,17},{... | collective-permute-start | bytes 49160 | tf_op jit(solution)/shard_map/ppermute | solution.py:20
  35.7 4.6 %collective-permute-start.11 = (f32[32,128]{1,0:T(8,128)S(1)}, f32[32,128]{1,0:T(8,128)S(1)}, u32[]{:S(2)}, u32[]{:S(2)}) collective-permute-start(f32[32,128]{1,0:T(8,128)S(1)} %get-tuple-element.30), channel_id=1, source_target_pairs={{0,24},{4,28},{8,16},{12,20},{16,8},{20,12},{24,0},{28,4},{1,25},{... | collective-permute-start | bytes 49160 | tf_op jit(solution)/shard_map/ppermute | solution.py:20
